TPU v7x, 32 devices: a whole 2x2x4 slice. The times are simulated.
32 devices in a mesh: node: 8 (over y, x, core), local: 4 (over z).
Axes of the slice: x: 2, y: 2, z: 4, core: 2. Of those that a mesh axis runs over, the one named last changes fastest.
Arguments:
- tokens: bfloat16 [4096, 4096], P(('node', 'local')), may hold values from -8 to 8
- norm_gain: bfloat16 [4096], replicated, may hold values from 0.25 to 1.75
- routes: int32 [4096, 8], P(('node', 'local')), may hold values from 0 to 31, as said below
- route_gates: float32 [4096, 8], P(('node', 'local')), may hold values from 0.35 to 1
- placement: int32 [32], replicated, may hold values from 0 to 31, each once
- gate_weight: bfloat16 [32, 4096, 768], P(('node', 'local')), may hold values from -0.09375 to 0.09375
- up_weight: bfloat16 [32, 4096, 768], P(('node', 'local')), may hold values from -0.09375 to 0.09375
- down_weight: bfloat16 [32, 768, 4096], P(('node', 'local')), may hold values from -0.21875 to 0.21875
Outputs:
- moe_output: bfloat16 [4096, 4096], P(('node', 'local'))
Inputs may be any that keep to these rules, and one draw needn't show every extreme that they name: `routes`: each token names 8 different experts. In every aligned block of 32 tokens of one device, each expert is named at most 12 times; at every block position some expert is named exactly 12 times by that block of every device.
All inputs are finite; a program needn't handle non-finite values.
Results may differ from a plain program's by a relative error of at most 0.0076.
Values may be sent and summed in bfloat16 or wider, within the bound.
No kernel may reach another device: no remote copies, remote signals or barrier semaphores. Data moves between devices by JAX's collectives and lax.ppermute only.
A program may use at most 128 MiB of HBM per device.

v0:
```python
import jax
import jax.numpy as jnp
from jax import lax
from jax.sharding import PartitionSpec as P

BLOCK_TOK = 32


EPSILON = 1e-06


def body(tokens, norm_gain, routes, route_gates, placement, gate_weight, up_weight, down_weight):
    node_count = lax.axis_size("node")
    local_count = lax.axis_size("local")
    devices = node_count * local_count
    experts = placement.shape[0]
    tok_rows, features = tokens.shape
    top_count = routes.shape[1]
    blocks = tok_rows // BLOCK_TOK
    per_expert = BLOCK_TOK * top_count // experts
    capacity = per_expert * 3 // 2
    slot_count = devices * capacity
    values = tokens.astype(jnp.float32)
    rescale = lax.rsqrt(jnp.mean(values * values, axis=-1, keepdims=True) + EPSILON)
    normed = (values * rescale * norm_gain.astype(jnp.float32)).astype(jnp.bfloat16)
    combine_weight = (route_gates / jnp.sum(route_gates, axis=-1, keepdims=True)).astype(
        jnp.bfloat16
    )
    expert_ids = jnp.arange(experts, dtype=jnp.int32)
    holder = jnp.sum(
        jnp.where(placement[None, :] == expert_ids[:, None], expert_ids[None, :], 0), axis=1
    )
    target = jnp.sum(
        jnp.where(routes[:, :, None] == expert_ids[None, None, :], holder[None, None, :], 0),
        axis=-1,
    )
    block_ids = routes.reshape(blocks, BLOCK_TOK * top_count)
    matches = (block_ids[:, :, None] == expert_ids[None, None, :]).astype(jnp.int32)
    position = jnp.sum((jnp.cumsum(matches, axis=1) - matches) * matches, axis=-1)
    column = target.reshape(blocks, BLOCK_TOK, top_count) * capacity + position.reshape(
        blocks, BLOCK_TOK, top_count
    )
    slot_ids = jnp.arange(slot_count, dtype=jnp.int32)
    matched = column[..., None] == slot_ids[None, None, None, :]
    spread = jnp.any(matched, axis=2).astype(jnp.bfloat16)
    block_weight = combine_weight.reshape(blocks, BLOCK_TOK, top_count)
    combine_table = jnp.sum(
        jnp.where(matched, block_weight[..., None], jnp.zeros((), jnp.bfloat16)), axis=2
    )
    pieces = []
    for block_index in range(blocks):
        picked = normed[block_index * BLOCK_TOK : (block_index + 1) * BLOCK_TOK]
        outbound = jnp.einsum(
            "ts,td->sd", spread[block_index], picked, preferred_element_type=jnp.float32
        )
        outgoing_arrived = lax.all_to_all(
            outbound.astype(jnp.bfloat16).reshape(devices, capacity, features),
            ("node", "local"),
            split_axis=0,
            concat_axis=0,
            tiled=True,
        )
        arrived = outgoing_arrived.reshape(slot_count, features)
        gate_pre = jnp.dot(arrived, gate_weight[0], preferred_element_type=jnp.float32)
        up_pre = jnp.dot(arrived, up_weight[0], preferred_element_type=jnp.float32)
        hidden = (jax.nn.silu(gate_pre) * up_pre).astype(jnp.bfloat16)
        returning_landed = lax.all_to_all(
            jnp.dot(hidden, down_weight[0], preferred_element_type=jnp.float32)
            .astype(jnp.bfloat16)
            .reshape(devices, capacity, features),
            ("node", "local"),
            split_axis=0,
            concat_axis=0,
            tiled=True,
        )
        landed = returning_landed.reshape(slot_count, features)
        mixed = jnp.dot(combine_table[block_index], landed, preferred_element_type=jnp.float32)
        pieces.append(mixed.astype(jnp.bfloat16))
    return jnp.concatenate(pieces, axis=0)


def solution(mesh):
    in_specs = (
        P(("node", "local"), None),
        P(),
        P(("node", "local"), None),
        P(("node", "local"), None),
        P(),
        P(("node", "local"), None, None),
        P(("node", "local"), None, None),
        P(("node", "local"), None, None),
    )
    out_specs = P(("node", "local"), None)
    return jax.shard_map(body, mesh=mesh, in_specs=in_specs, out_specs=out_specs, check_vma=False)
```

profile of v0, /device:TPU:9, one launch (start us, length us, event | category | flops | bytes accessed | tf_op | source)
XLA Modules:
  0.0 806.8 jit_solution(4800610494909259517)
XLA Ops:
  0.0 0.9 copy.18
  1.1 0.8 select_reduce_fusion.1
  1.8 1.5 fusion.36
  3.4 0.8 select_reduce_fusion
  4.2 0.7 convert_element_type.74
  5.0 2.3 reduce-window.6
  7.4 0.1 copy.20
  7.6 0.1 fusion.84
  7.8 0.5 fusion.39
  8.4 0.3 fusion.38
  8.7 1.0 copy-done.3
  9.7 1.0 convolution_convert_fusion
  10.7 2.7 reshape.104
  13.4 6.4 all-to-all-start.6
  19.9 2.0 convolution_convert_fusion.1
  21.8 2.7 reshape.100
  24.6 89.4 %all-to-all-done.6 = bf16[32,12,4096]{2,1,0:T(8,128)(2,1)} async-done(((bf16[32,12,4096]{2,1,0:T(8,128)(2,1)}), bf16[32,12,4096]{2,1,0:T(8,128)(2,1)}, u32[]{:S(2)}, u32[]{:S(2)}) %all-to-all-start.6) | async-done | bytes 3145760 | tf_op jit(solution)/shard_map/all_to_all | solution.py:56
  113.9 3.9 all-to-all-start.4
  117.8 2.0 convolution_convert_fusion.2
  119.8 2.7 reshape.96
  122.5 89.4 %all-to-all-done.4 = bf16[32,12,4096]{2,1,0:T(8,128)(2,1)} async-done(((bf16[32,12,4096]{2,1,0:T(8,128)(2,1)}), bf16[32,12,4096]{2,1,0:T(8,128)(2,1)}, u32[]{:S(2)}, u32[]{:S(2)}) %all-to-all-start.4) | async-done | bytes 3145760 | tf_op jit(solution)/shard_map/all_to_all | solution.py:56
  211.9 3.9 all-to-all-start.2
  215.7 2.0 convolution_convert_fusion.3
  217.7 2.7 reshape.92
  220.4 89.4 %all-to-all-done.2 = bf16[32,12,4096]{2,1,0:T(8,128)(2,1)} async-done(((bf16[32,12,4096]{2,1,0:T(8,128)(2,1)}), bf16[32,12,4096]{2,1,0:T(8,128)(2,1)}, u32[]{:S(2)}, u32[]{:S(2)}) %all-to-all-start.2) | async-done | bytes 3145760 | tf_op jit(solution)/shard_map/all_to_all | solution.py:56
  309.8 4.6 all-to-all-start
  314.4 4.0 reshape.105
  318.4 6.4 fusion.16
  324.7 13.3 %fusion.33 = bf16[384,4096]{1,0:T(8,128)(2,1)} fusion(bf16[1,768,4096]{2,1,0:T(8,128)(2,1)} %param.15, bf16[384,4096]{1,0:T(8,128)(2,1)S(1)} %reshape.105, bf16[1,4096,768]{2,1,0:T(8,128)(2,1)} %param.14, f32[384,768]{1,0:T(8,128)} %fusion.16), kind=kOutput, calls=%fused_computation.31 | convolution fusion | flops 4835180544 | bytes 20054016 | tf_op jit(solution)/shard_map/dot_general | solution.py:68
  338.1 5.5 reshape.106
  343.5 64.7 %all-to-all-done = bf16[32,12,4096]{2,1,0:T(8,128)(2,1)} async-done(((bf16[32,12,4096]{2,1,0:T(8,128)(2,1)}), bf16[32,12,4096]{2,1,0:T(8,128)(2,1)}, u32[]{:S(2)}, u32[]{:S(2)}) %all-to-all-start) | async-done | bytes 3145760 | tf_op jit(solution)/shard_map/all_to_all | solution.py:56
  408.2 4.2 all-to-all-start.7
  412.5 4.0 reshape.101
  416.4 6.4 fusion.18
  422.8 13.3 %fusion.30 = bf16[384,4096]{1,0:T(8,128)(2,1)} fusion(bf16[1,768,4096]{2,1,0:T(8,128)(2,1)} %param.15, bf16[384,4096]{1,0:T(8,128)(2,1)S(1)} %reshape.101, bf16[1,4096,768]{2,1,0:T(8,128)(2,1)} %param.14, f32[384,768]{1,0:T(8,128)} %fusion.18), kind=kOutput, calls=%fused_computation.30 | convolution fusion | flops 4835180544 | bytes 20054016 | tf_op jit(solution)/shard_map/dot_general | solution.py:68
  436.1 5.5 reshape.102
  441.6 64.7 %all-to-all-done.7 = bf16[32,12,4096]{2,1,0:T(8,128)(2,1)} async-done(((bf16[32,12,4096]{2,1,0:T(8,128)(2,1)}), bf16[32,12,4096]{2,1,0:T(8,128)(2,1)}, u32[]{:S(2)}, u32[]{:S(2)}) %all-to-all-start.7) | async-done | bytes 3145760 | tf_op jit(solution)/shard_map/all_to_all | solution.py:67
  506.3 4.3 all-to-all-start.5
  510.6 4.0 reshape.97
  514.6 6.4 fusion.20
  520.9 13.4 %fusion.27 = bf16[384,4096]{1,0:T(8,128)(2,1)} fusion(bf16[1,768,4096]{2,1,0:T(8,128)(2,1)} %param.15, bf16[384,4096]{1,0:T(8,128)(2,1)S(1)} %reshape.97, bf16[1,4096,768]{2,1,0:T(8,128)(2,1)} %param.14, f32[384,768]{1,0:T(8,128)} %fusion.20), kind=kOutput, calls=%fused_computation.29 | convolution fusion | flops 4835180544 | bytes 20054016 | tf_op jit(solution)/shard_map/dot_general | solution.py:68
  534.3 5.5 reshape.98
  539.8 64.6 %all-to-all-done.5 = bf16[32,12,4096]{2,1,0:T(8,128)(2,1)} async-done(((bf16[32,12,4096]{2,1,0:T(8,128)(2,1)}), bf16[32,12,4096]{2,1,0:T(8,128)(2,1)}, u32[]{:S(2)}, u32[]{:S(2)}) %all-to-all-start.5) | async-done | bytes 3145760 | tf_op jit(solution)/shard_map/all_to_all | solution.py:67
  604.4 4.3 all-to-all-start.3
  608.7 4.0 reshape.93
  612.7 6.4 fusion.22
  619.1 13.3 %fusion.24 = bf16[384,4096]{1,0:T(8,128)(2,1)} fusion(bf16[1,768,4096]{2,1,0:T(8,128)(2,1)} %param.15, bf16[384,4096]{1,0:T(8,128)(2,1)S(1)} %reshape.93, bf16[1,4096,768]{2,1,0:T(8,128)(2,1)} %param.14, f32[384,768]{1,0:T(8,128)} %fusion.22), kind=kOutput, calls=%fused_computation.28 | convolution fusion | flops 4835180544 | bytes 20054016 | tf_op jit(solution)/shard_map/dot_general | solution.py:68
  632.4 5.5 reshape.94
  637.9 64.7 %all-to-all-done.3 = bf16[32,12,4096]{2,1,0:T(8,128)(2,1)} async-done(((bf16[32,12,4096]{2,1,0:T(8,128)(2,1)}), bf16[32,12,4096]{2,1,0:T(8,128)(2,1)}, u32[]{:S(2)}, u32[]{:S(2)}) %all-to-all-start.3) | async-done | bytes 3145760 | tf_op jit(solution)/shard_map/all_to_all | solution.py:67
  702.6 3.9 all-to-all-start.1
  706.5 0.1 copy.26
  706.6 0.6 fusion.65
  707.2 4.0 reshape.107
  711.2 5.6 reshape.103
  716.8 5.6 reshape.99
  722.3 0.6 convolution_convert_fusion.4
  723.0 1.2 copy-done
  724.2 1.4 convolution_convert_fusion.5
  725.6 1.3 convolution_convert_fusion.6
  726.9 73.6 %all-to-all-done.1 = bf16[32,12,4096]{2,1,0:T(8,128)(2,1)} async-done(((bf16[32,12,4096]{2,1,0:T(8,128)(2,1)}), bf16[32,12,4096]{2,1,0:T(8,128)(2,1)}, u32[]{:S(2)}, u32[]{:S(2)}) %all-to-all-start.1) | async-done | bytes 3145760 | tf_op jit(solution)/shard_map/all_to_all | solution.py:67
  800.5 4.0 reshape.95
  804.5 0.7 convolution_convert_fusion.7
  805.2 0.3 copy-done.4
  805.5 1.0 pad_maximum_fusion
  (25 shorter events, 0.7 us)
Async XLA Ops:
  0.0 8.4 %copy-start.2 = (bf16[128,4096]{1,0:T(8,128)(2,1)S(1)}, bf16[128,4096]{1,0:T(8,128)(2,1)}, u32[]{:S(2)}) copy-start(bf16[128,4096]{1,0:T(8,128)(2,1)} %param.8) | copy-start | bytes 3145732
  8.7 1.0 copy-start.3
  13.4 100.5 %all-to-all-start.6 = ((bf16[32,12,4096]{2,1,0:T(8,128)(2,1)}), bf16[32,12,4096]{2,1,0:T(8,128)(2,1)}, u32[]{:S(2)}, u32[]{:S(2)}) async-start(bf16[32,12,4096]{2,1,0:T(8,128)(2,1)} %reshape.104), calls=%async_computation.6 | async-start | bytes 8388608 | tf_op jit(solution)/shard_map/all_to_all | solution.py:56
  113.9 97.9 %all-to-all-start.4 = ((bf16[32,12,4096]{2,1,0:T(8,128)(2,1)}), bf16[32,12,4096]{2,1,0:T(8,128)(2,1)}, u32[]{:S(2)}, u32[]{:S(2)}) async-start(bf16[32,12,4096]{2,1,0:T(8,128)(2,1)} %reshape.100), calls=%async_computation.4 | async-start | bytes 8388608 | tf_op jit(solution)/shard_map/all_to_all | solution.py:56
  211.9 97.9 %all-to-all-start.2 = ((bf16[32,12,4096]{2,1,0:T(8,128)(2,1)}), bf16[32,12,4096]{2,1,0:T(8,128)(2,1)}, u32[]{:S(2)}, u32[]{:S(2)}) async-start(bf16[32,12,4096]{2,1,0:T(8,128)(2,1)} %reshape.96), calls=%async_computation.2 | async-start | bytes 8388608 | tf_op jit(solution)/shard_map/all_to_all | solution.py:56
  309.8 98.4 %all-to-all-start = ((bf16[32,12,4096]{2,1,0:T(8,128)(2,1)}), bf16[32,12,4096]{2,1,0:T(8,128)(2,1)}, u32[]{:S(2)}, u32[]{:S(2)}) async-start(bf16[32,12,4096]{2,1,0:T(8,128)(2,1)} %reshape.92), calls=%async_computation | async-start | bytes 8388608 | tf_op jit(solution)/shard_map/all_to_all | solution.py:56
  408.2 98.1 %all-to-all-start.7 = ((bf16[32,12,4096]{2,1,0:T(8,128)(2,1)}), bf16[32,12,4096]{2,1,0:T(8,128)(2,1)}, u32[]{:S(2)}, u32[]{:S(2)}) async-start(bf16[32,12,4096]{2,1,0:T(8,128)(2,1)} %reshape.106), calls=%async_computation.7 | async-start | bytes 8388608 | tf_op jit(solution)/shard_map/all_to_all | solution.py:67
  506.3 98.1 %all-to-all-start.5 = ((bf16[32,12,4096]{2,1,0:T(8,128)(2,1)}), bf16[32,12,4096]{2,1,0:T(8,128)(2,1)}, u32[]{:S(2)}, u32[]{:S(2)}) async-start(bf16[32,12,4096]{2,1,0:T(8,128)(2,1)} %reshape.102), calls=%async_computation.5 | async-start | bytes 8388608 | tf_op jit(solution)/shard_map/all_to_all | solution.py:67
  604.4 98.2 %all-to-all-start.3 = ((bf16[32,12,4096]{2,1,0:T(8,128)(2,1)}), bf16[32,12,4096]{2,1,0:T(8,128)(2,1)}, u32[]{:S(2)}, u32[]{:S(2)}) async-start(bf16[32,12,4096]{2,1,0:T(8,128)(2,1)} %reshape.98), calls=%async_computation.3 | async-start | bytes 8388608 | tf_op jit(solution)/shard_map/all_to_all | solution.py:67
  637.9 68.5 %copy-start.6 = (f32[128,8]{0,1:T(8,128)S(1)}, f32[128,8]{0,1:T(8,128)}, u32[]{:S(2)}) copy-start(f32[128,8]{0,1:T(8,128)} %param.11) | copy-start | bytes 12292
  702.6 97.9 %all-to-all-start.1 = ((bf16[32,12,4096]{2,1,0:T(8,128)(2,1)}), bf16[32,12,4096]{2,1,0:T(8,128)(2,1)}, u32[]{:S(2)}, u32[]{:S(2)}) async-start(bf16[32,12,4096]{2,1,0:T(8,128)(2,1)} %reshape.94), calls=%async_computation.1 | async-start | bytes 8388608 | tf_op jit(solution)/shard_map/all_to_all | solution.py:67
  722.3 1.9 copy-start
  722.3 3.2 copy-start.1
  804.5 1.0 copy-start.4
  804.5 1.0 copy-start.5
where the time goes:
time: 814 us; the launch traced here: 807 us
  waiting for transfers between devices  600 us (74%)
  matrix products  89.8 us (11%)
  local copies, waits for them, and re-layouts  72 us (9%)
  starting transfers between devices  35.4 us (4%)
  other arithmetic  8.77 us (1%)
    all_to_all x4, waiting for transfers between devices, body(): lax.all_to_all(outbound.astype(jnp.bfloat16).reshape(devices, capacity, f...  333 us
    all_to_all x4, waiting for transfers between devices, body(): lax.all_to_all(jnp.dot(hidden, down_weight[0], preferred_element_type=jnp...  268 us
    dot_general x4, matrix products, body(): jnp.dot(hidden, down_weight[0], preferred_element_type=jnp.float32)  53.3 us
    dot_general x4, matrix products, body(): jnp.dot(arrived, gate_weight[0], preferred_element_type=jnp.float32)  25.6 us
    reshape x4, local copies, waits for them, and re-layouts, body(): returning_landed = lax.all_to_all(jnp.dot(hidden, down_weight[0], preferr...  22 us
    reshape x4, local copies, waits for them, and re-layouts, body(): landed = returning_landed.reshape(slot_count, features)  19.1 us
    all_to_all x4, starting transfers between devices, body(): lax.all_to_all(outbound.astype(jnp.bfloat16).reshape(devices, capacity, f...  18.7 us
    all_to_all x4, starting transfers between devices, body(): lax.all_to_all(jnp.dot(hidden, down_weight[0], preferred_element_type=jnp...  16.6 us
  transfers between devices with their start and end apart: 8, of which 8 were waited for; matrix products, arithmetic and copies ran while one was open for 19% of the time, Pallas kernels for 0%

commit v1 on v0

v1 whole, which is shorter than its diff:
```python
import jax
import jax.numpy as jnp
from jax import lax
from jax.sharding import PartitionSpec as P

BLOCK_TOK = 32
EPSILON = 1e-06
AXES = ("node", "local")


def body(tokens, norm_gain, routes, route_gates, placement, gate_weight, up_weight, down_weight):
    nodes, locals_ = lax.axis_size("node"), lax.axis_size("local")
    experts = placement.shape[0]
    tok_rows, features = tokens.shape
    top_count = routes.shape[1]
    blocks = tok_rows // BLOCK_TOK
    capacity = BLOCK_TOK * top_count // experts * 3 // 2
    slots = nodes * locals_ * capacity
    values = tokens.astype(jnp.float32)
    rescale = lax.rsqrt(jnp.mean(values * values, axis=-1, keepdims=True) + EPSILON)
    normed = (values * rescale * norm_gain.astype(jnp.float32)).astype(jnp.bfloat16)
    combine_weight = (route_gates / jnp.sum(route_gates, axis=-1, keepdims=True)).astype(
        jnp.bfloat16
    )
    held = routes[:, :, None] == placement[None, None, :]
    table = jnp.sum(
        jnp.where(held, combine_weight[:, :, None], jnp.zeros((), jnp.bfloat16)), axis=1
    )
    column = lax.all_gather(table, "local", axis=0, tiled=True)
    column = column.reshape(locals_, blocks, BLOCK_TOK, nodes, locals_)
    mine = lax.dynamic_index_in_dim(column, lax.axis_index("local"), 4, keepdims=False)
    mask = (mine > 0).astype(jnp.int32)
    rank = jnp.cumsum(mask, axis=2) - mask
    first = (
        jnp.arange(nodes, dtype=jnp.int32)[None, :] * locals_
        + jnp.arange(locals_, dtype=jnp.int32)[:, None]
    ) * capacity
    place = jnp.where(mask > 0, rank + first[:, None, None, :], -1)
    slot_ids = jnp.arange(slots, dtype=jnp.int32)
    matched = place[..., None] == slot_ids
    spread = jnp.any(matched, axis=3).astype(jnp.bfloat16)
    mixing = jnp.sum(
        jnp.where(matched, mine[..., None], jnp.zeros((), jnp.bfloat16)), axis=3
    )
    pieces = []
    for block in range(blocks):
        rows = normed[block * BLOCK_TOK : (block + 1) * BLOCK_TOK]
        gathered = lax.all_gather(rows, "local", axis=0, tiled=True)
        outbound = jnp.einsum(
            "ts,td->sd",
            spread[:, block].reshape(-1, slots),
            gathered,
            preferred_element_type=jnp.float32,
        ).astype(jnp.bfloat16)
        arrived = lax.all_to_all(outbound, "node", 0, 0, tiled=True)
        gate_pre = jnp.dot(arrived, gate_weight[0], preferred_element_type=jnp.float32)
        up_pre = jnp.dot(arrived, up_weight[0], preferred_element_type=jnp.float32)
        hidden = (jax.nn.silu(gate_pre) * up_pre).astype(jnp.bfloat16)
        out = jnp.dot(hidden, down_weight[0], preferred_element_type=jnp.float32).astype(jnp.bfloat16)
        landed = lax.all_to_all(out, "node", 0, 0, tiled=True)
        mixed = jnp.dot(
            mixing[:, block].reshape(-1, slots), landed, preferred_element_type=jnp.float32
        ).astype(jnp.bfloat16)
        pieces.append(lax.psum_scatter(mixed, "local", scatter_dimension=0, tiled=True))
    return jnp.concatenate(pieces, axis=0)


def solution(mesh):
    rows = P(AXES, None)
    stacked = P(AXES, None, None)
    in_specs = (rows, P(), rows, rows, P(), stacked, stacked, stacked)
    return jax.shard_map(body, mesh=mesh, in_specs=in_specs, out_specs=rows, check_vma=False)
```

time: 814 us -> 427 us (0.52)
  the two profiles are of different devices: /device:TPU:9 before, /device:TPU:0 now
where the time goes in v1:
time: 427 us; the launch traced here: 420 us
  waiting for transfers between devices  229 us (54%)
  matrix products  109 us (26%)
  starting transfers between devices  34 us (8%)
  between operations  14 us (3%)
  blocking collectives  13.6 us (3%)
  other arithmetic  12.2 us (3%)
  local copies, waits for them, and re-layouts  8.48 us (2%)
    all_gather x4, waiting for transfers between devices, body(): gathered = lax.all_gather(rows, 'local', axis=0, tiled=True)  98.6 us
    all_to_all x4, waiting for transfers between devices, body(): landed = lax.all_to_all(out, 'node', 0, 0, tiled=True)  74 us
    dot_general x4, matrix products, body(): jnp.dot(hidden, down_weight[0], preferred_element_type=jnp.float32)  55.8 us
    all_to_all x4, waiting for transfers between devices, body(): arrived = lax.all_to_all(outbound, 'node', 0, 0, tiled=True)  29.3 us
    dot_general x4, matrix products, body(): jnp.dot(arrived, gate_weight[0], preferred_element_type=jnp.float32)  28.7 us
    reduce_scatter x4, waiting for transfers between devices, body(): lax.psum_scatter(mixed, 'local', scatter_dimension=0, tiled=True)  25.1 us
    all_to_all x4, starting transfers between devices, body(): arrived = lax.all_to_all(outbound, 'node', 0, 0, tiled=True)  17.5 us
    all_to_all x4, starting transfers between devices, body(): landed = lax.all_to_all(out, 'node', 0, 0, tiled=True)  15.7 us
  transfers between devices with their start and end apart: 16, of which 13 were waited for; matrix products, arithmetic and copies ran while one was open for 28% of the time, Pallas kernels for 0%

profile of v1, /device:TPU:0, one launch (start us, length us, event | category | flops | bytes accessed | tf_op | source)
XLA Modules:
  0.0 420.1 jit_solution(2900260143515139498)
XLA Ops:
  6.5 0.7 convert_element_type.73
  7.3 1.5 fusion.41
  8.8 1.6 fusion.43
  10.4 1.0 fusion.92
  11.4 0.1 fusion.86
  11.5 13.6 %all_gather.15 = bf16[512,32]{0,1:T(8,128)(2,1)S(1)} all-gather(bf16[128,32]{0,1:T(8,128)(2,1)S(1)} %fusion.86), channel_id=1, replica_groups=mesh['node'=8,'local'=4] {'local'}, dimensions={0}, use_global_device_ids=true | all-gather | bytes 40960 | tf_op jit(solution)/shard_map/all_gather | solution.py:29
  25.2 0.1 reshape.57
  25.3 0.9 copy.25
  26.2 0.8 fusion.45
  27.1 3.1 copy.23
  30.2 2.1 fusion.24
  32.3 0.1 fusion.94
  32.3 9.8 %all-gather.5.cloned.1.call-done = bf16[128,4096]{1,0:T(8,128)(2,1)} async-done(((bf16[32,4096]{1,0:T(8,128)(2,1)}), bf16[128,4096]{1,0:T(8,128)(2,1)}) %all-gather.5.cloned.1.call-update) | async-done | bytes 1048592 | tf_op jit(solution)/shard_map/all_gather | solution.py:48
  42.2 3.9 convolution_convert_fusion.3
  46.1 3.7 all-to-all-start
  49.7 0.0 all-gather.7.cloned.1.call-start
  49.8 0.7 all-gather.7.cloned.1.call-update
  50.5 29.7 %all-gather.7.cloned.1.call-done = bf16[128,4096]{1,0:T(8,128)(2,1)} async-done(((bf16[32,4096]{1,0:T(8,128)(2,1)}), bf16[128,4096]{1,0:T(8,128)(2,1)}) %all-gather.7.cloned.1.call-update) | async-done | bytes 1048592 | tf_op jit(solution)/shard_map/all_gather | solution.py:48
  80.2 3.9 convolution_convert_fusion.2
  84.1 3.5 all-to-all-done
  87.6 4.5 %all-to-all-start.2 = ((bf16[8,48,4096]{2,1,0:T(8,128)(2,1)}), bf16[8,48,4096]{2,1,0:T(8,128)(2,1)}, u32[]{:S(2)}, u32[]{:S(2)}) async-start(bf16[8,48,4096]{2,1,0:T(8,128)(2,1)} %bitcast.15), calls=%async_computation.3 | async-start | bytes 6291456 | tf_op jit(solution)/shard_map/all_to_all | solution.py:55
  92.1 0.0 all-gather.9.cloned.1.call-start
  92.1 0.7 all-gather.9.cloned.1.call-update
  92.8 29.6 %all-gather.9.cloned.1.call-done = bf16[128,4096]{1,0:T(8,128)(2,1)} async-done(((bf16[32,4096]{1,0:T(8,128)(2,1)}), bf16[128,4096]{1,0:T(8,128)(2,1)}) %all-gather.9.cloned.1.call-update) | async-done | bytes 1048592 | tf_op jit(solution)/shard_map/all_gather | solution.py:48
  122.4 3.9 convolution_convert_fusion.1
  126.3 3.6 all-to-all-done.2
  129.9 4.4 %all-to-all-start.4 = ((bf16[8,48,4096]{2,1,0:T(8,128)(2,1)}), bf16[8,48,4096]{2,1,0:T(8,128)(2,1)}, u32[]{:S(2)}, u32[]{:S(2)}) async-start(bf16[8,48,4096]{2,1,0:T(8,128)(2,1)} %bitcast.21), calls=%async_computation.6 | async-start | bytes 6291456 | tf_op jit(solution)/shard_map/all_to_all | solution.py:55
  134.4 0.0 all-gather.11.cloned.1.call-start
  134.4 0.5 all-gather.11.cloned.1.call-update
  135.0 29.5 %all-gather.11.cloned.1.call-done = bf16[128,4096]{1,0:T(8,128)(2,1)} async-done(((bf16[32,4096]{1,0:T(8,128)(2,1)}), bf16[128,4096]{1,0:T(8,128)(2,1)}) %all-gather.11.cloned.1.call-update) | async-done | bytes 1048592 | tf_op jit(solution)/shard_map/all_gather | solution.py:48
  164.5 3.9 convolution_convert_fusion
  168.4 3.9 all-to-all-done.4
  172.3 5.0 %all-to-all-start.6 = ((bf16[8,48,4096]{2,1,0:T(8,128)(2,1)}), bf16[8,48,4096]{2,1,0:T(8,128)(2,1)}, u32[]{:S(2)}, u32[]{:S(2)}) async-start(bf16[8,48,4096]{2,1,0:T(8,128)(2,1)} %bitcast.27), calls=%async_computation.9 | async-start | bytes 6291456 | tf_op jit(solution)/shard_map/all_to_all | solution.py:55
  177.3 6.4 %fusion.22 = f32[384,768]{1,0:T(8,128)} fusion(bf16[384,4096]{1,0:T(8,128)(2,1)S(1)} %bitcast.116, bf16[1,4096,768]{2,1,0:T(8,128)(2,1)} %param.13), kind=kOutput, calls=%fused_computation.22 | convolution fusion | flops 2415919104 | bytes 10616832 | tf_op jit(solution)/shard_map/dot_general | solution.py:56
  183.7 13.3 %fusion.26 = bf16[384,4096]{1,0:T(8,128)(2,1)} fusion(bf16[1,768,4096]{2,1,0:T(8,128)(2,1)} %param.15, bf16[384,4096]{1,0:T(8,128)(2,1)S(1)} %bitcast.117, bf16[1,4096,768]{2,1,0:T(8,128)(2,1)} %param.14, f32[384,768]{1,0:T(8,128)} %fusion.22), kind=kOutput, calls=%fused_computation.27 | convolution fusion | flops 4835180544 | bytes 20054016 | tf_op jit(solution)/shard_map/dot_general | solution.py:59
  196.9 18.2 %all-to-all-done.6 = bf16[8,48,4096]{2,1,0:T(8,128)(2,1)} async-done(((bf16[8,48,4096]{2,1,0:T(8,128)(2,1)}), bf16[8,48,4096]{2,1,0:T(8,128)(2,1)}, u32[]{:S(2)}, u32[]{:S(2)}) %all-to-all-start.6) | async-done | bytes 3145760 | tf_op jit(solution)/shard_map/all_to_all | solution.py:55
  215.2 3.8 all-to-all-start.1
  219.0 0.9 copy.24
  219.9 3.0 fusion.40
  222.9 7.4 %fusion.20 = f32[384,768]{1,0:T(8,128)} fusion(bf16[384,4096]{1,0:T(8,128)(2,1)} %bitcast.16, bf16[1,4096,768]{2,1,0:T(8,128)(2,1)} %param.13), kind=kOutput, calls=%fused_computation.20 | convolution fusion | flops 2415919104 | bytes 10616832 | tf_op jit(solution)/shard_map/dot_general | solution.py:56
  230.3 14.2 %fusion.29 = bf16[384,4096]{1,0:T(8,128)(2,1)} fusion(bf16[1,768,4096]{2,1,0:T(8,128)(2,1)} %param.15, bf16[384,4096]{1,0:T(8,128)(2,1)} %bitcast.16, bf16[1,4096,768]{2,1,0:T(8,128)(2,1)} %param.14, f32[384,768]{1,0:T(8,128)} %fusion.20), kind=kOutput, calls=%fused_computation.28 | convolution fusion | flops 4835180544 | bytes 20054016 | tf_op jit(solution)/shard_map/dot_general | solution.py:59
  244.4 12.4 %all-to-all-done.1 = bf16[8,48,4096]{2,1,0:T(8,128)(2,1)S(1)} async-done(((bf16[8,48,4096]{2,1,0:T(8,128)(2,1)}), bf16[8,48,4096]{2,1,0:T(8,128)(2,1)S(1)}, u32[]{:S(2)}, u32[]{:S(2)}) %all-to-all-start.1) | async-done | bytes 3145760 | tf_op jit(solution)/shard_map/all_to_all | solution.py:60
  256.8 1.7 copy-done
  258.5 3.6 all-to-all-start.3
  262.2 0.3 reduce-scatter.5.cloned.1.call-start
  262.4 0.7 fusion.93
  263.1 7.5 %fusion.18 = f32[384,768]{1,0:T(8,128)} fusion(bf16[384,4096]{1,0:T(8,128)(2,1)} %bitcast.22, bf16[1,4096,768]{2,1,0:T(8,128)(2,1)} %param.13), kind=kOutput, calls=%fused_computation.18 | convolution fusion | flops 2415919104 | bytes 10616832 | tf_op jit(solution)/shard_map/dot_general | solution.py:56
  270.7 1.7 convolution_convert_fusion.7
  272.4 14.2 %fusion.32 = bf16[384,4096]{1,0:T(8,128)(2,1)} fusion(bf16[1,768,4096]{2,1,0:T(8,128)(2,1)} %param.15, bf16[384,4096]{1,0:T(8,128)(2,1)} %bitcast.22, bf16[1,4096,768]{2,1,0:T(8,128)(2,1)} %param.14, f32[384,768]{1,0:T(8,128)} %fusion.18), kind=kOutput, calls=%fused_computation.29 | convolution fusion | flops 4835180544 | bytes 20054016 | tf_op jit(solution)/shard_map/dot_general | solution.py:59
  286.6 13.4 %all-to-all-done.3 = bf16[8,48,4096]{2,1,0:T(8,128)(2,1)S(1)} async-done(((bf16[8,48,4096]{2,1,0:T(8,128)(2,1)}), bf16[8,48,4096]{2,1,0:T(8,128)(2,1)S(1)}, u32[]{:S(2)}, u32[]{:S(2)}) %all-to-all-start.3) | async-done | bytes 3145760 | tf_op jit(solution)/shard_map/all_to_all | solution.py:60
  300.0 4.4 %all-to-all-start.5 = ((bf16[8,48,4096]{2,1,0:T(8,128)(2,1)}), bf16[8,48,4096]{2,1,0:T(8,128)(2,1)}, u32[]{:S(2)}, u32[]{:S(2)}) async-start(bf16[8,48,4096]{2,1,0:T(8,128)(2,1)} %bitcast.119), calls=%async_computation.7 | async-start | bytes 6291456 | tf_op jit(solution)/shard_map/all_to_all | solution.py:60
  304.4 0.3 reduce-scatter.7.cloned.1.call-start
  304.7 7.4 %fusion.16 = f32[384,768]{1,0:T(8,128)} fusion(bf16[384,4096]{1,0:T(8,128)(2,1)} %bitcast.28, bf16[1,4096,768]{2,1,0:T(8,128)(2,1)} %param.13), kind=kOutput, calls=%fused_computation.16 | convolution fusion | flops 2415919104 | bytes 10616832 | tf_op jit(solution)/shard_map/dot_general | solution.py:56
  312.1 1.7 convolution_convert_fusion.6
  313.9 14.2 %fusion.35 = bf16[384,4096]{1,0:T(8,128)(2,1)} fusion(bf16[1,768,4096]{2,1,0:T(8,128)(2,1)} %param.15, bf16[384,4096]{1,0:T(8,128)(2,1)} %bitcast.28, bf16[1,4096,768]{2,1,0:T(8,128)(2,1)} %param.14, f32[384,768]{1,0:T(8,128)} %fusion.16), kind=kOutput, calls=%fused_computation.30 | convolution fusion | flops 4835180544 | bytes 20054016 | tf_op jit(solution)/shard_map/dot_general | solution.py:59
  328.1 14.2 %all-to-all-done.5 = bf16[8,48,4096]{2,1,0:T(8,128)(2,1)} async-done(((bf16[8,48,4096]{2,1,0:T(8,128)(2,1)}), bf16[8,48,4096]{2,1,0:T(8,128)(2,1)}, u32[]{:S(2)}, u32[]{:S(2)}) %all-to-all-start.5) | async-done | bytes 3145760 | tf_op jit(solution)/shard_map/all_to_all | solution.py:60
  342.3 3.8 all-to-all-start.7
  346.1 0.0 reduce-scatter.9.cloned.1.call-start
  346.2 3.6 convolution_convert_fusion.5
  349.8 0.0 reduce-scatter.11.cloned.1.call-start
  349.9 34.0 %all-to-all-done.7 = bf16[8,48,4096]{2,1,0:T(8,128)(2,1)S(1)} async-done(((bf16[8,48,4096]{2,1,0:T(8,128)(2,1)}), bf16[8,48,4096]{2,1,0:T(8,128)(2,1)S(1)}, u32[]{:S(2)}, u32[]{:S(2)}) %all-to-all-start.7) | async-done | bytes 3145760 | tf_op jit(solution)/shard_map/all_to_all | solution.py:60
  383.9 1.7 convolution_convert_fusion.4
  385.7 25.0 %reduce-scatter.11.cloned.1.call-done = bf16[32,4096]{1,0:T(8,128)(2,1)} async-done(((bf16[128,4096]{1,0:T(8,128)(2,1)}), bf16[32,4096]{1,0:T(8,128)(2,1)}) %reduce-scatter.11.cloned.1.call-update) | async-done | bytes 262160 | tf_op jit(solution)/shard_map/reduce_scatter | solution.py:64
  410.7 2.2 pad_maximum_fusion
  (34 shorter events, 0.2 us)
Async XLA Ops:
  6.5 4.9 %copy-start.7 = (f32[128,8]{0,1:T(8,128)S(1)}, f32[128,8]{0,1:T(8,128)}, u32[]{:S(2)}) copy-start(f32[128,8]{0,1:T(8,128)} %param.11) | copy-start | bytes 12292
  6.5 4.9 %copy-start.8 = (s32[128,8]{0,1:T(8,128)S(1)}, s32[128,8]{0,1:T(8,128)}, u32[]{:S(2)}) copy-start(s32[128,8]{0,1:T(8,128)} %param.10) | copy-start | bytes 12292
  6.5 4.9 %copy-start.9 = (s32[32]{0:T(128)S(1)}, s32[32]{0:T(128)}, u32[]{:S(2)}) copy-start(s32[32]{0:T(128)} %param.12) | copy-start | bytes 388
  6.5 35.6 %all-gather.5.cloned.1.call-start = ((), (), s32[]{:S(2)}) async-start(), calls=%async_computation.12 | async-start | bytes 1310720 | tf_op jit(solution)/shard_map/all_gather | solution.py:48
  25.3 0.9 copy-start.6
  46.1 41.5 %all-to-all-start = ((bf16[8,48,4096]{2,1,0:T(8,128)(2,1)}), bf16[8,48,4096]{2,1,0:T(8,128)(2,1)S(1)}, u32[]{:S(2)}, u32[]{:S(2)}) async-start(bf16[8,48,4096]{2,1,0:T(8,128)(2,1)} %bitcast.6), calls=%async_computation | async-start | bytes 6291456 | tf_op jit(solution)/shard_map/all_to_all | solution.py:55
  49.7 30.5 %all-gather.7.cloned.1.call-start = ((), (), s32[]{:S(2)}) async-start(), calls=%async_computation.14 | async-start | bytes 1310720 | tf_op jit(solution)/shard_map/all_gather | solution.py:48
  87.6 42.4 %all-to-all-start.2 = ((bf16[8,48,4096]{2,1,0:T(8,128)(2,1)}), bf16[8,48,4096]{2,1,0:T(8,128)(2,1)}, u32[]{:S(2)}, u32[]{:S(2)}) async-start(bf16[8,48,4096]{2,1,0:T(8,128)(2,1)} %bitcast.15), calls=%async_computation.3 | async-start | bytes 6291456 | tf_op jit(solution)/shard_map/all_to_all | solution.py:55
  92.1 30.4 %all-gather.9.cloned.1.call-start = ((), (), s32[]{:S(2)}) async-start(), calls=%async_computation.16 | async-start | bytes 1310720 | tf_op jit(solution)/shard_map/all_gather | solution.py:48
  129.9 42.3 %all-to-all-start.4 = ((bf16[8,48,4096]{2,1,0:T(8,128)(2,1)}), bf16[8,48,4096]{2,1,0:T(8,128)(2,1)}, u32[]{:S(2)}, u32[]{:S(2)}) async-start(bf16[8,48,4096]{2,1,0:T(8,128)(2,1)} %bitcast.21), calls=%async_computation.6 | async-start | bytes 6291456 | tf_op jit(solution)/shard_map/all_to_all | solution.py:55
  134.4 30.1 %all-gather.11.cloned.1.call-start = ((), (), s32[]{:S(2)}) async-start(), calls=%async_computation.18 | async-start | bytes 1310720 | tf_op jit(solution)/shard_map/all_gather | solution.py:48
  172.3 42.9 %all-to-all-start.6 = ((bf16[8,48,4096]{2,1,0:T(8,128)(2,1)}), bf16[8,48,4096]{2,1,0:T(8,128)(2,1)}, u32[]{:S(2)}, u32[]{:S(2)}) async-start(bf16[8,48,4096]{2,1,0:T(8,128)(2,1)} %bitcast.27), calls=%async_computation.9 | async-start | bytes 6291456 | tf_op jit(solution)/shard_map/all_to_all | solution.py:55
  215.2 41.6 %all-to-all-start.1 = ((bf16[8,48,4096]{2,1,0:T(8,128)(2,1)}), bf16[8,48,4096]{2,1,0:T(8,128)(2,1)S(1)}, u32[]{:S(2)}, u32[]{:S(2)}) async-start(bf16[8,48,4096]{2,1,0:T(8,128)(2,1)} %bitcast.121), calls=%async_computation.1 | async-start | bytes 6291456 | tf_op jit(solution)/shard_map/all_to_all | solution.py:60
  256.8 1.7 copy-start
  256.8 5.6 %copy-start.2 = (bf16[4,4,32,384]{3,2,1,0:T(8,128)(2,1)S(1)}, bf16[4,4,32,384]{3,2,1,0:T(8,128)(2,1)}, u32[]{:S(2)}) copy-start(bf16[4,4,32,384]{3,2,1,0:T(8,128)(2,1)} %fusion.40) | copy-start | bytes 1179652
  258.5 41.5 %all-to-all-start.3 = ((bf16[8,48,4096]{2,1,0:T(8,128)(2,1)}), bf16[8,48,4096]{2,1,0:T(8,128)(2,1)S(1)}, u32[]{:S(2)}, u32[]{:S(2)}) async-start(bf16[8,48,4096]{2,1,0:T(8,128)(2,1)} %bitcast.118), calls=%async_computation.4 | async-start | bytes 6291456 | tf_op jit(solution)/shard_map/all_to_all | solution.py:60
  262.2 123.5 %reduce-scatter.5.cloned.1.call-start = ((), (), s32[]{:S(2)}) async-start(), calls=%async_computation.13 | async-start | bytes 1310720 | tf_op jit(solution)/shard_map/reduce_scatter | solution.py:64
  263.1 7.5 %copy-start.1 = (bf16[8,48,4096]{2,1,0:T(8,128)(2,1)S(1)}, bf16[8,48,4096]{2,1,0:T(8,128)(2,1)}, u32[]{:S(2)}) copy-start(bf16[8,48,4096]{2,1,0:T(8,128)(2,1)} %copy-done) | copy-start | bytes 9437188
  300.0 42.3 %all-to-all-start.5 = ((bf16[8,48,4096]{2,1,0:T(8,128)(2,1)}), bf16[8,48,4096]{2,1,0:T(8,128)(2,1)}, u32[]{:S(2)}, u32[]{:S(2)}) async-start(bf16[8,48,4096]{2,1,0:T(8,128)(2,1)} %bitcast.119), calls=%async_computation.7 | async-start | bytes 6291456 | tf_op jit(solution)/shard_map/all_to_all | solution.py:60
  304.4 81.3 %reduce-scatter.7.cloned.1.call-start = ((), (), s32[]{:S(2)}) async-start(), calls=%async_computation.15 | async-start | bytes 1310720 | tf_op jit(solution)/shard_map/reduce_scatter | solution.py:64
  304.7 7.4 %copy-start.5 = (bf16[4,1,32,384]{3,2,1,0:T(8,128)(2,1)S(1)}, bf16[4,1,32,384]{3,2,1,0:T(8,128)(2,1)}, u32[]{:S(2)}) copy-start(bf16[4,1,32,384]{3,2,1,0:T(8,128)(2,1)} %get-tuple-element.12) | copy-start | bytes 294916
  342.3 3.9 copy-start.4
  342.3 41.6 %all-to-all-start.7 = ((bf16[8,48,4096]{2,1,0:T(8,128)(2,1)}), bf16[8,48,4096]{2,1,0:T(8,128)(2,1)S(1)}, u32[]{:S(2)}, u32[]{:S(2)}) async-start(bf16[8,48,4096]{2,1,0:T(8,128)(2,1)} %bitcast.120), calls=%async_computation.10 | async-start | bytes 6291456 | tf_op jit(solution)/shard_map/all_to_all | solution.py:60
  346.1 37.8 %copy-start.3 = (bf16[4,1,32,384]{3,2,1,0:T(8,128)(2,1)S(1)}, bf16[4,1,32,384]{3,2,1,0:T(8,128)(2,1)}, u32[]{:S(2)}) copy-start(bf16[4,1,32,384]{3,2,1,0:T(8,128)(2,1)} %get-tuple-element.10) | copy-start | bytes 294916
  346.1 39.6 %reduce-scatter.9.cloned.1.call-start = ((), (), s32[]{:S(2)}) async-start(), calls=%async_computation.17 | async-start | bytes 1310720 | tf_op jit(solution)/shard_map/reduce_scatter | solution.py:64
  349.8 60.9 %reduce-scatter.11.cloned.1.call-start = ((), (), s32[]{:S(2)}) async-start(), calls=%async_computation.19 | async-start | bytes 1310720 | tf_op jit(solution)/shard_map/reduce_scatter | solution.py:64
Sparse Core Ops, SparseCore 0:
  11.5 30.6 all-gather.4
  52.1 28.0 all-gather.6
  94.5 27.9 all-gather.8
  136.5 27.9 all-gather.10
  272.5 27.1 reduce-scatter.4
  314.0 27.0 reduce-scatter.6
  350.0 27.1 reduce-scatter.8
  385.7 24.9 reduce-scatter.10

commit v2 on v1

v2 whole, which is shorter than its diff:
```python
import jax
import jax.numpy as jnp
import numpy as np
from jax import lax
from jax.experimental import pallas as pl
from jax.experimental.pallas import tpu as pltpu
from jax.sharding import PartitionSpec as P

BLOCK_TOK = 32
EPSILON = 1e-06
AXES = ("node", "local")
LANES = 128
BF16, F32 = jnp.bfloat16, jnp.float32


def fence(*arrays):
    def kernel(*refs):
        pass

    anywhere = pl.BlockSpec(memory_space=pl.ANY)
    return pl.pallas_call(
        kernel,
        out_shape=[jax.ShapeDtypeStruct(a.shape, a.dtype) for a in arrays],
        in_specs=[anywhere] * len(arrays),
        out_specs=[anywhere] * len(arrays),
        input_output_aliases={i: i for i in range(len(arrays))},
    )(*arrays)


def swap(array, axis, bits):
    size = lax.axis_size(axis)
    return lax.ppermute(array, axis, [(i, i ^ bits) for i in range(size)])


def swaps(parts, axis, first, last):
    return [swap(parts[k], axis, k) for k in range(first, last)]


def bit_order(size, last_first):
    bits = [1 << i for i in range(size.bit_length() - 1)]
    return bits[:1] + bits[:0:-1] if last_first else bits


def gather_doubling(array, axis, bits):
    for bit in bits:
        array = jnp.concatenate([array, swap(array, axis, bit)])
    return array


def gathered_from(bits):
    found = [0]
    for bit in bits:
        found += [k ^ bit for k in found]
    return np.array(found)


def sum_halving(array, axis, bits):
    for bit in bits[::-1]:
        keep, give = jnp.split(array, 2)
        array = keep + swap(give.astype(BF16), axis, bit).astype(F32)
    return array.astype(BF16)


def relative(array, axis, dim):
    size = lax.axis_size(axis)
    order = jnp.arange(size, dtype=jnp.int32) ^ lax.axis_index(axis)
    pick = (order[:, None] == jnp.arange(size, dtype=jnp.int32)).astype(array.dtype)
    return jnp.moveaxis(jnp.tensordot(pick, array, ((1,), (dim,))), 0, dim)


def tables(known, capacity, gather_axis, exchange_axis, by_bits):
    group, peers = lax.axis_size(gather_axis), lax.axis_size(exchange_axis)
    experts = group * peers
    slots = experts * capacity
    known = known[:, :experts].reshape(
        group, BLOCK_TOK, lax.axis_size("node"), lax.axis_size("local")
    )
    at = 3 if gather_axis == "local" else 2
    known = lax.dynamic_index_in_dim(known, lax.axis_index(gather_axis), at, keepdims=False)
    if by_bits:
        known = relative(known, exchange_axis, 2)
    mask = (known > 0).astype(jnp.int32)
    rank = jnp.cumsum(mask, axis=1) - mask
    first = (
        jnp.arange(peers, dtype=jnp.int32)[None, :] * group
        + jnp.arange(group, dtype=jnp.int32)[:, None]
    ) * capacity
    place = jnp.where(mask > 0, rank + first[:, None, :], -1)
    matched = place[..., None] == jnp.arange(slots, dtype=jnp.int32)
    spread = jnp.any(matched, axis=2).astype(BF16)
    mixing = jnp.sum(jnp.where(matched, known[..., None], jnp.zeros((), BF16)), axis=2)
    return spread, mixing


def pick_rows(spread, rows):
    flat = spread.reshape(-1, spread.shape[-1])
    return jnp.einsum("ts,td->sd", flat, rows, preferred_element_type=F32).astype(BF16)


def mix_rows(mixing, landed):
    flat = mixing.reshape(-1, mixing.shape[-1])
    return jnp.dot(flat, landed, preferred_element_type=F32)


def expert_kernel(x_ref, gate_ref, up_ref, down_ref, out_ref, total):
    step = pl.program_id(0)
    x = x_ref[...]
    gate_pre = jnp.dot(x, gate_ref[...], preferred_element_type=F32)
    up_pre = jnp.dot(x, up_ref[...], preferred_element_type=F32)
    hidden = (gate_pre / (1 + jnp.exp(-gate_pre)) * up_pre).astype(BF16)
    part = jnp.dot(hidden, down_ref[...], preferred_element_type=F32)

    @pl.when(step == 0)
    def _():
        total[...] = part

    @pl.when(step > 0)
    def _():
        total[...] += part

    @pl.when(step == pl.num_programs(0) - 1)
    def _():
        out_ref[...] = total[...].astype(BF16)


def expert(arrived, gate_weight, up_weight, down_weight):
    rows, features = arrived.shape
    hidden = gate_weight.shape[1]
    tile = 256
    return pl.pallas_call(
        expert_kernel,
        grid=(hidden // tile,),
        out_shape=jax.ShapeDtypeStruct((rows, features), BF16),
        in_specs=[
            pl.BlockSpec((rows, features), lambda i: (0, 0)),
            pl.BlockSpec((features, tile), lambda i: (0, i)),
            pl.BlockSpec((features, tile), lambda i: (0, i)),
            pl.BlockSpec((tile, features), lambda i: (i, 0)),
        ],
        out_specs=pl.BlockSpec((rows, features), lambda i: (0, 0)),
        scratch_shapes=[pltpu.VMEM((rows, features), F32)],
        compiler_params=pltpu.CompilerParams(vmem_limit_bytes=44 * 2**20),
        cost_estimate=pl.CostEstimate(
            flops=6 * rows * features * hidden,
            bytes_accessed=6 * features * hidden + 4 * rows * features,
            transcendentals=rows * hidden,
        ),
    )(arrived, gate_weight, up_weight, down_weight)


def to_experts(rows):
    return lax.all_to_all(rows, "node", 0, 0, tiled=True)


def body(tokens, norm_gain, routes, route_gates, placement, gate_weight, up_weight, down_weight):
    experts = placement.shape[0]
    tok_rows, features = tokens.shape
    top_count = routes.shape[1]
    capacity = BLOCK_TOK * top_count // experts * 3 // 2
    half = features // 2
    values = tokens.astype(F32)
    rescale = lax.rsqrt(jnp.mean(values * values, axis=-1, keepdims=True) + EPSILON)
    normed = (values * rescale * norm_gain.astype(F32)).astype(BF16)
    combine_weight = (route_gates / jnp.sum(route_gates, axis=-1, keepdims=True)).astype(BF16)
    held = routes[:, :, None] == placement[None, None, :]
    table = jnp.sum(jnp.where(held, combine_weight[:, :, None], jnp.zeros((), BF16)), axis=1)
    weights = (gate_weight[0], up_weight[0], down_weight[0])
    sent = jnp.concatenate([normed, jnp.pad(table, ((0, 0), (0, -experts % LANES)))], axis=1)
    sent0, sent1, sent2, sent3 = jnp.split(sent, tok_rows // BLOCK_TOK)

    peers = lax.axis_size("local")
    cut = max(peers - 1, 1)

    def gather(rows, first, last):
        return swaps([rows] * peers, "local", first, last)

    def along_local(parts):
        gathered = jnp.concatenate(parts)
        spread, mixing = tables(gathered[:, features:], capacity, "local", "node", False)
        return pick_rows(spread, gathered[:, :features]), mixing

    def sums_out(mixed):
        own, *parts = jnp.split(mixed, peers)
        return own, [part.astype(BF16) for part in parts]

    def total(own, parts):
        for part in parts:
            own = own + part.astype(F32)
        return own.astype(BF16)

    nodes = lax.axis_size("node")
    bits_a, bits_b = bit_order(nodes, False), bit_order(nodes, True)
    order_a, order_b = gathered_from(bits_a), gathered_from(bits_b)
    near0 = gather(sent0, 1, peers)
    near = jnp.concatenate([sent3, swap(sent3, "node", bits_a[0])])
    rows_a = gather_doubling(near[:, :half], "node", bits_a[1:])
    rows_b = gather_doubling(near[:, half:], "node", bits_b[1:])
    back = np.argsort(order_b)
    known = rows_b[:, half:].reshape(nodes, BLOCK_TOK, -1)
    known = jnp.concatenate([known[int(k)] for k in back])
    spread3, mixing3 = tables(known, capacity, "node", "local", True)
    spread3b = jnp.stack([spread3[int(k)] for k in order_b])
    mixing3b = jnp.stack([mixing3[int(k)] for k in order_b])
    sent1, *near0 = fence(sent1, *near0)
    near1 = gather(sent1, 1, cut)
    outbound0, mixing0 = along_local([sent0] + near0)
    outbound3 = jnp.concatenate(
        [pick_rows(spread3, rows_a), pick_rows(spread3b, rows_b[:, :half])], axis=1
    )

    outbound0, outbound3, sent1, sent2, *near1 = fence(outbound0, outbound3, sent1, sent2, *near1)
    arrived0 = to_experts(outbound0)
    near1 += gather(sent1, cut, peers)
    own3, *parts = jnp.split(outbound3, peers)
    arrived3 = swaps([own3] + parts, "local", 1, cut)
    outbound1, mixing1 = along_local([sent1] + near1)

    arrived0, outbound1, sent2, last3, *arrived3 = fence(
        arrived0, outbound1, sent2, parts[-1], *arrived3
    )
    arrived1 = to_experts(outbound1)
    near2 = gather(sent2, 1, peers)
    last3 = jnp.split(last3, 2)
    arrived3.append(swap(last3[0], "local", peers - 1))
    out0 = expert(arrived0, *weights)
    out0, sent2, *near2 = fence(out0, sent2, *near2)
    outbound2, mixing2 = along_local([sent2] + near2)

    arrived1, outbound2, out0, last3, *arrived3 = fence(
        arrived1, outbound2, out0, last3[1], *arrived3
    )
    arrived2 = to_experts(outbound2)
    arrived3.append(swap(last3, "local", peers - 1))
    out1 = expert(arrived1, *weights)
    out1, *arrived3 = fence(out1, *arrived3)
    out3 = expert(jnp.concatenate([own3] + arrived3), *weights)

    arrived2, out0, out1, out3 = fence(arrived2, out0, out1, out3)
    landed0 = to_experts(out0)
    own3, *parts = jnp.split(out3, peers)
    landed3 = swaps([own3] + parts, "local", 1, cut)
    out2 = expert(arrived2, *weights)

    landed0, out1, out2, last3, *landed3 = fence(landed0, out1, out2, parts[-1], *landed3)
    landed1 = to_experts(out1)
    last3 = jnp.split(last3, 2)
    landed3.append(swap(last3[0], "local", peers - 1))
    sum0, parts0 = sums_out(mix_rows(mixing0, landed0))
    parts0 = swaps([None] + parts0, "local", 1, peers)

    landed1, out2, last3, *rest = fence(landed1, out2, last3[1], *landed3, *parts0)
    landed3, parts0 = rest[: len(landed3)], rest[len(landed3) :]
    landed2 = to_experts(out2)
    landed3.append(swap(last3, "local", peers - 1))
    piece0 = total(sum0, parts0)
    sum1, parts1 = sums_out(mix_rows(mixing1, landed1))
    parts1 = swaps([None] + parts1, "local", 1, peers)
    landed3 = jnp.concatenate([own3] + landed3)
    mixed3a = mix_rows(mixing3, landed3[:, :half])
    mixed3b = mix_rows(mixing3b, landed3[:, half:])

    landed2, mixed3a, mixed3b, piece0, *parts1 = fence(
        landed2, mixed3a, mixed3b, piece0, *parts1
    )
    sum2, parts2 = sums_out(mix_rows(mixing2, landed2))
    mixed3a, mixed3b, *parts2 = fence(mixed3a, mixed3b, *parts2)
    parts2 = swaps([None] + parts2, "local", 1, peers)
    piece1 = total(sum1, parts1)
    piece3 = jnp.concatenate(
        [sum_halving(mixed3a, "node", bits_a), sum_halving(mixed3b, "node", bits_b)], axis=1
    )
    piece2 = total(sum2, parts2)
    return jnp.concatenate([piece0, piece1, piece2, piece3], axis=0)


def solution(mesh):
    rows = P(AXES, None)
    stacked = P(AXES, None, None)
    in_specs = (rows, P(), rows, rows, P(), stacked, stacked, stacked)
    return jax.shard_map(body, mesh=mesh, in_specs=in_specs, out_specs=rows, check_vma=False)
```

time: 427 us -> 406 us (0.951)
  the two profiles are of different devices: /device:TPU:0 before, /device:TPU:9 now
where the time goes in v2:
time: 406 us; the launch traced here: 405 us
  waiting for transfers between devices  153 us (38%)
  starting transfers between devices  86.6 us (21%)
  local copies, waits for them, and re-layouts  57.8 us (14%)
  Pallas kernels  53.2 us (13%)
  other arithmetic  27 us (7%)
  matrix products  26.4 us (7%)
    ppermute x37, waiting for transfers between devices, swap(): return lax.ppermute(array, axis, [(i, i ^ bits) for i in range(size)])  149 us
    pallas_call x4, Pallas kernels, expert(): pl.pallas_call(expert_kernel, grid=(hidden // tile,), out_shape=jax.Shape...  53.2 us
    ppermute x37, starting transfers between devices, swap(): return lax.ppermute(array, axis, [(i, i ^ bits) for i in range(size)])  49 us
    all_to_all x6, starting transfers between devices, to_experts(): return lax.all_to_all(rows, 'node', 0, 0, tiled=True)  37.6 us
    unnamed x150, local copies, waits for them, and re-layouts  37.1 us
    dot_general x5, matrix products, mix_rows(): return jnp.dot(flat, landed, preferred_element_type=F32)  13.8 us
    dot_general x5, matrix products, pick_rows(): jnp.einsum('ts,td->sd', flat, rows, preferred_element_type=F32).astype(BF16)  11.8 us
  transfers between devices with their start and end apart: 43, of which 22 were waited for; matrix products, arithmetic and copies ran while one was open for 19% of the time, Pallas kernels for 13%

profile of v2, /device:TPU:9, one launch (start us, length us, event | category | flops | bytes accessed | tf_op | source)
XLA Modules:
  0.0 404.7 jit_solution(17213893166247659150)
XLA Ops:
  4.5 1.6 fusion.3
  13.0 13.2 %collective-permute-done.2.refs_3_ = bf16[32,4224]{1,0:T(8,128)(2,1)S(1)} collective-permute-done((bf16[32,4224]{1,0:T(8,128)(2,1)S(1)}, bf16[32,4224]{1,0:T(8,128)(2,1)S(1)}, u32[]{:S(2)}, u32[]{:S(2)}) %collective-permute-start.2) | collective-permute-done | bytes 270368 | tf_op jit(solution)/shard_map/ppermute | solution.py:32
  26.2 4.7 %collective-permute-done.1.refs_2_ = bf16[32,4224]{1,0:T(8,128)(2,1)S(1)} collective-permute-done((bf16[32,4224]{1,0:T(8,128)(2,1)S(1)}, bf16[32,4224]{1,0:T(8,128)(2,1)S(1)}, u32[]{:S(2)}, u32[]{:S(2)}) %collective-permute-start.1) | collective-permute-done | bytes 270368 | tf_op jit(solution)/shard_map/ppermute | solution.py:32
  31.7 3.1 collective-permute-start.9
  40.5 2.9 collective-permute-done.4
  45.2 2.7 convolution_convert_fusion.2.refs_0_
  50.0 5.5 %collective-permute-done.5 = bf16[128,2176]{1,0:T(8,128)(2,1)S(1)} collective-permute-done((bf16[128,2176]{1,0:T(8,128)(2,1)S(1)}, bf16[128,2176]{1,0:T(8,128)(2,1)S(1)}, u32[]{:S(2)}, u32[]{:S(2)}) %collective-permute-start.5) | collective-permute-done | bytes 557088 | tf_op jit(solution)/shard_map/ppermute | solution.py:32
  57.5 1.9 fusion.103
  60.3 1.7 convolution_convert_fusion.3
  62.6 2.1 pad_maximum_fusion.refs_1_
  65.6 7.6 %all-to-all-start = ((bf16[8,48,4096]{2,1,0:T(8,128)(2,1)}), bf16[8,48,4096]{2,1,0:T(8,128)(2,1)S(1)}, u32[]{:S(2)}, u32[]{:S(2)}) async-start(bf16[8,48,4096]{2,1,0:T(8,128)(2,1)} %bitcast.71), calls=%async_computation | async-start | bytes 6291456 | tf_op jit(solution)/shard_map/all_to_all | solution.py:152
  73.6 3.6 slice_dynamic-update-slice_fusion.1
  77.3 2.9 collective-permute-start.12
  80.2 23.6 %collective-permute-done.10 = bf16[32,4224]{1,0:T(8,128)(2,1)S(1)} collective-permute-done((bf16[32,4224]{1,0:T(8,128)(2,1)S(1)}, bf16[32,4224]{1,0:T(8,128)(2,1)S(1)}, u32[]{:S(2)}, u32[]{:S(2)}) %collective-permute-start.10) | collective-permute-done | bytes 270368 | tf_op jit(solution)/shard_map/ppermute | solution.py:32
  107.0 1.8 copy.130
  109.4 4.0 convolution_convert_fusion.1.refs_1_
  113.4 5.6 %collective-permute-done.12.refs_5_ = bf16[96,4096]{1,0:T(8,128)(2,1)} collective-permute-done((bf16[96,4096]{1,0:T(8,128)(2,1)}, bf16[96,4096]{1,0:T(8,128)(2,1)}, u32[]{:S(2)}, u32[]{:S(2)}) %collective-permute-start.12) | collective-permute-done | bytes 786464 | tf_op jit(solution)/shard_map/ppermute | solution.py:32
  119.0 1.8 copy-done.3
  121.7 4.0 collective-permute-start.14
  125.7 6.1 %all-to-all-start.1 = ((bf16[8,48,4096]{2,1,0:T(8,128)(2,1)}), bf16[8,48,4096]{2,1,0:T(8,128)(2,1)}, u32[]{:S(2)}, u32[]{:S(2)}) async-start(bf16[8,48,4096]{2,1,0:T(8,128)(2,1)} %bitcast.68), calls=%async_computation.1 | async-start | bytes 6291456 | tf_op jit(solution)/shard_map/all_to_all | solution.py:152
  131.9 2.0 fusion.96
  134.4 12.9 %shard_map.85.refs_0_ = bf16[384,4096]{1,0:T(8,128)(2,1)S(1)} custom-call(bf16[384,4096]{1,0:T(8,128)(2,1)S(1)} %copy-done.4, bf16[4096,768]{1,0:T(8,128)(2,1)} %bitcast.91, bf16[4096,768]{1,0:T(8,128)(2,1)} %bitcast.95, bf16[768,4096]{1,0:T(8,128)(2,1)} %bitcast.99), custom_call_target="tpu_custom_call" | custom-call | flops 7247757312 | bytes 25165824 | tf_op jit(solution)/shard_map/pallas_call | solution.py:130
  147.3 1.6 copy-done
  148.9 3.8 collective-permute-done.14.refs_3_
  159.4 2.8 convolution_convert_fusion.refs_1_
  162.3 3.9 all-to-all-done.1
  166.2 7.4 %all-to-all-start.2 = ((bf16[8,48,4096]{2,1,0:T(8,128)(2,1)}), bf16[8,48,4096]{2,1,0:T(8,128)(2,1)S(1)}, u32[]{:S(2)}, u32[]{:S(2)}) async-start(bf16[8,48,4096]{2,1,0:T(8,128)(2,1)} %bitcast.70), calls=%async_computation.2 | async-start | bytes 6291456 | tf_op jit(solution)/shard_map/all_to_all | solution.py:152
  174.0 14.4 %shard_map.88.refs_0_ = bf16[384,4096]{1,0:T(8,128)(2,1)S(1)} custom-call(bf16[384,4096]{1,0:T(8,128)(2,1)} %get-tuple-element.92.x_ref, bf16[4096,768]{1,0:T(8,128)(2,1)} %bitcast.92, bf16[4096,768]{1,0:T(8,128)(2,1)} %bitcast.96, bf16[768,4096]{1,0:T(8,128)(2,1)} %bitcast.100), custom_call_target="tpu_custom_call" | custom-call | flops 7247757312 | bytes 25165824 | tf_op jit(solution)/shard_map/pallas_call | solution.py:130
  188.5 1.6 copy-done.1
  190.1 2.2 collective-permute-done.17.refs_4_
  193.1 2.1 constant_dynamic-update-slice_fusion.11
  195.2 2.1 constant_dynamic-update-slice_fusion.10
  198.8 1.9 copy-done.9
  200.7 12.9 %shard_map.90.refs_3_ = bf16[384,4096]{1,0:T(8,128)(2,1)S(1)} custom-call(bf16[384,4096]{1,0:T(8,128)(2,1)S(1)} %copy-done.9, bf16[4096,768]{1,0:T(8,128)(2,1)} %bitcast.93, bf16[4096,768]{1,0:T(8,128)(2,1)} %bitcast.97, bf16[768,4096]{1,0:T(8,128)(2,1)} %bitcast.101), custom_call_target="tpu_custom_call" | custom-call | flops 7247757312 | bytes 25165824 | tf_op jit(solution)/shard_map/pallas_call | solution.py:130
  213.7 1.6 copy-done.7
  215.3 1.7 copy-done.5
  217.1 5.8 %all-to-all-start.3 = ((bf16[8,48,4096]{2,1,0:T(8,128)(2,1)}), bf16[8,48,4096]{2,1,0:T(8,128)(2,1)}, u32[]{:S(2)}, u32[]{:S(2)}) async-start(bf16[8,48,4096]{2,1,0:T(8,128)(2,1)} %bitcast.63), calls=%async_computation.3 | async-start | bytes 6291456 | tf_op jit(solution)/shard_map/all_to_all | solution.py:152
  228.9 12.9 %shard_map.92.refs_2_ = bf16[384,4096]{1,0:T(8,128)(2,1)S(1)} custom-call(bf16[384,4096]{1,0:T(8,128)(2,1)S(1)} %copy-done.6, bf16[4096,768]{1,0:T(8,128)(2,1)} %bitcast.94, bf16[4096,768]{1,0:T(8,128)(2,1)} %bitcast.98, bf16[768,4096]{1,0:T(8,128)(2,1)} %bitcast.102), custom_call_target="tpu_custom_call" | custom-call | flops 7247757312 | bytes 25165824 | tf_op jit(solution)/shard_map/pallas_call | solution.py:130
  241.8 1.7 copy-done.2
  243.6 16.8 %collective-permute-done.19.refs_5_ = bf16[96,4096]{1,0:T(8,128)(2,1)S(1)} collective-permute-done((bf16[96,4096]{1,0:T(8,128)(2,1)S(1)}, bf16[96,4096]{1,0:T(8,128)(2,1)S(1)}, u32[]{:S(2)}, u32[]{:S(2)}) %collective-permute-start.19) | collective-permute-done | bytes 786464 | tf_op jit(solution)/shard_map/ppermute | solution.py:32
  260.4 1.7 collective-permute-done.18.refs_4_
  262.9 5.2 %all-to-all-start.4 = ((bf16[8,48,4096]{2,1,0:T(8,128)(2,1)}), bf16[8,48,4096]{2,1,0:T(8,128)(2,1)S(1)}, u32[]{:S(2)}, u32[]{:S(2)}) async-start(bf16[8,48,4096]{2,1,0:T(8,128)(2,1)} %bitcast.64), calls=%async_computation.4 | async-start | bytes 6291456 | tf_op jit(solution)/shard_map/all_to_all | solution.py:152
  270.6 2.1 fusion.95
  273.7 4.0 fusion.100
  279.1 3.5 collective-permute-start.22
  285.8 23.2 %collective-permute-done.23.refs_8_ = bf16[32,4096]{1,0:T(8,128)(2,1)} collective-permute-done((bf16[32,4096]{1,0:T(8,128)(2,1)}, bf16[32,4096]{1,0:T(8,128)(2,1)}, u32[]{:S(2)}, u32[]{:S(2)}) %collective-permute-start.23) | collective-permute-done | bytes 262176 | tf_op jit(solution)/shard_map/ppermute | solution.py:32
  309.0 4.4 %collective-permute-done.22.refs_7_ = bf16[32,4096]{1,0:T(8,128)(2,1)} collective-permute-done((bf16[32,4096]{1,0:T(8,128)(2,1)}, bf16[32,4096]{1,0:T(8,128)(2,1)}, u32[]{:S(2)}, u32[]{:S(2)}) %collective-permute-start.22) | collective-permute-done | bytes 262176 | tf_op jit(solution)/shard_map/ppermute | solution.py:32
  313.5 1.7 copy-done.12
  315.2 5.4 %all-to-all-start.5 = ((bf16[8,48,4096]{2,1,0:T(8,128)(2,1)}), bf16[8,48,4096]{2,1,0:T(8,128)(2,1)}, u32[]{:S(2)}, u32[]{:S(2)}) async-start(bf16[8,48,4096]{2,1,0:T(8,128)(2,1)} %bitcast.65), calls=%async_computation.5 | async-start | bytes 6291456 | tf_op jit(solution)/shard_map/all_to_all | solution.py:152
  321.1 3.2 fusion.101
  325.4 4.9 %collective-permute-start.26 = (bf16[32,4096]{1,0:T(8,128)(2,1)S(1)}, bf16[32,4096]{1,0:T(8,128)(2,1)S(1)}, u32[]{:S(2)}, u32[]{:S(2)}) collective-permute-start(bf16[32,4096]{1,0:T(8,128)(2,1)S(1)} %get-tuple-element.149), channel_id=1, source_target_pairs={{0,2},{1,3},{2,0},{3,1},{4,6},{5,7},{6,4},{7,5},{8,10},{9,11},{10,... | collective-permute-start | bytes 786440 | tf_op jit(solution)/shard_map/ppermute | solution.py:32
  330.4 2.1 fusion.68.refs_3_
  333.6 17.0 %collective-permute-done.24 = bf16[48,4096]{1,0:T(8,128)(2,1)S(1)} collective-permute-done((bf16[48,4096]{1,0:T(8,128)(2,1)S(1)}, bf16[48,4096]{1,0:T(8,128)(2,1)S(1)}, u32[]{:S(2)}, u32[]{:S(2)}) %collective-permute-start.24) | collective-permute-done | bytes 393248 | tf_op jit(solution)/shard_map/ppermute | solution.py:32
  350.6 2.0 fusion.4.refs_2_
  352.7 2.0 fusion.6.refs_1_
  356.2 3.7 collective-permute-done.26.refs_5_
  361.6 2.6 fusion.102
  365.1 3.0 collective-permute-start.28
  377.6 1.8 collective-permute-done.29
  379.4 12.1 %collective-permute-done.30 = bf16[32,4096]{1,0:T(8,128)(2,1)S(1)} collective-permute-done((bf16[32,4096]{1,0:T(8,128)(2,1)}, bf16[32,4096]{1,0:T(8,128)(2,1)S(1)}, u32[]{:S(2)}, u32[]{:S(2)}) %collective-permute-start.30) | collective-permute-done | bytes 262176 | tf_op jit(solution)/shard_map/ppermute | solution.py:32
  391.8 1.6 collective-permute-start.35
  394.9 2.8 collective-permute-done.35
  397.8 3.1 collective-permute-start.36
  401.0 1.7 collective-permute-start.33
  (284 shorter events, 76.3 us)
Async XLA Ops:
  7.1 19.1 %collective-permute-start.2 = (bf16[32,4224]{1,0:T(8,128)(2,1)S(1)}, bf16[32,4224]{1,0:T(8,128)(2,1)S(1)}, u32[]{:S(2)}, u32[]{:S(2)}) collective-permute-start(bf16[32,4224]{1,0:T(8,128)(2,1)S(1)} %get-tuple-element.144), channel_id=1, source_target_pairs={{0,3},{1,2},{2,1},{3,0},{4,7},{5,6},{6,5},{7,4},{8,11},{9,10},{10,... | collective-permute-start | bytes 811016 | tf_op jit(solution)/shard_map/ppermute | solution.py:32
  8.4 22.5 %collective-permute-start.1 = (bf16[32,4224]{1,0:T(8,128)(2,1)S(1)}, bf16[32,4224]{1,0:T(8,128)(2,1)S(1)}, u32[]{:S(2)}, u32[]{:S(2)}) collective-permute-start(bf16[32,4224]{1,0:T(8,128)(2,1)S(1)} %get-tuple-element.144), channel_id=1, source_target_pairs={{0,2},{1,3},{2,0},{3,1},{4,6},{5,7},{6,4},{7,5},{8,10},{9,11},{10,... | collective-permute-start | bytes 811016 | tf_op jit(solution)/shard_map/ppermute | solution.py:32
  9.4 21.5 %collective-permute-start = (bf16[32,4224]{1,0:T(8,128)(2,1)S(1)}, bf16[32,4224]{1,0:T(8,128)(2,1)S(1)}, u32[]{:S(2)}, u32[]{:S(2)}) collective-permute-start(bf16[32,4224]{1,0:T(8,128)(2,1)S(1)} %get-tuple-element.144), channel_id=1, source_target_pairs={{0,1},{1,0},{2,3},{3,2},{4,5},{5,4},{6,7},{7,6},{8,9},{9,8},{10,11... | collective-permute-start | bytes 811016 | tf_op jit(solution)/shard_map/ppermute | solution.py:32
  10.6 24.2 %collective-permute-start.3 = (bf16[32,4224]{1,0:T(8,128)(2,1)S(1)}, bf16[32,4224]{1,0:T(8,128)(2,1)S(1)}, u32[]{:S(2)}, u32[]{:S(2)}) collective-permute-start(bf16[32,4224]{1,0:T(8,128)(2,1)S(1)} %get-tuple-element.142), channel_id=1, source_target_pairs={{0,4},{4,0},{8,12},{12,8},{16,20},{20,16},{24,28},{28,24},{1,5},{5... | collective-permute-start | bytes 811016 | tf_op jit(solution)/shard_map/ppermute | solution.py:32
  11.8 26.7 %copy-start.62 = (s32[4,8]{1,0:T(4,128)}, s32[4,8]{1,0:T(4,128)S(1)}, u32[]{:S(2)}) copy-start(s32[4,8]{1,0:T(4,128)S(1)} %add_multiply_fusion.1) | copy-start | bytes 388
  31.7 33.0 %collective-permute-start.9 = (bf16[32,4224]{1,0:T(8,128)(2,1)}, bf16[32,4224]{1,0:T(8,128)(2,1)S(1)}, u32[]{:S(2)}, u32[]{:S(2)}) collective-permute-start(bf16[32,4224]{1,0:T(8,128)(2,1)} %get-tuple-element.72.refs_2_), channel_id=1, source_target_pairs={{0,2},{1,3},{2,0},{3,1},{4,6},{5,7},{6,4},{7,5},{8,10},{9,11},{10,... | collective-permute-start | bytes 811016 | tf_op jit(solution)/shard_map/ppermute | solution.py:32
  34.8 29.9 %collective-permute-start.8 = (bf16[32,4224]{1,0:T(8,128)(2,1)}, bf16[32,4224]{1,0:T(8,128)(2,1)S(1)}, u32[]{:S(2)}, u32[]{:S(2)}) collective-permute-start(bf16[32,4224]{1,0:T(8,128)(2,1)} %get-tuple-element.72.refs_2_), channel_id=1, source_target_pairs={{0,1},{1,0},{2,3},{3,2},{4,5},{5,4},{6,7},{7,6},{8,9},{9,8},{10,11... | collective-permute-start | bytes 811016 | tf_op jit(solution)/shard_map/ppermute | solution.py:32
  34.8 13.1 %collective-permute-start.6 = (bf16[64,2048]{1,0:T(8,128)(2,1)S(1)}, bf16[64,2048]{1,0:T(8,128)(2,1)S(1)}, u32[]{:S(2)}, u32[]{:S(2)}) collective-permute-start(bf16[64,2048]{1,0:T(8,128)(2,1)S(1)} %pad_maximum_fusion.13), channel_id=1, source_target_pairs={{0,8},{4,12},{8,0},{12,4},{16,24},{20,28},{24,16},{28,20},{1,9},{5... | collective-permute-start | bytes 786440 | tf_op jit(solution)/shard_map/ppermute | solution.py:32
  37.1 8.1 %copy-start.40 = (bf16[32,4224]{1,0:T(8,128)(2,1)S(1)}, bf16[32,4224]{1,0:T(8,128)(2,1)}, u32[]{:S(2)}) copy-start(bf16[32,4224]{1,0:T(8,128)(2,1)} %get-tuple-element.71) | copy-start | bytes 811012
  37.1 8.1 %copy-start.42 = (bf16[32,4224]{1,0:T(8,128)(2,1)S(1)}, bf16[32,4224]{1,0:T(8,128)(2,1)}, u32[]{:S(2)}) copy-start(bf16[32,4224]{1,0:T(8,128)(2,1)} %get-tuple-element.70) | copy-start | bytes 811012
  37.1 8.1 %copy-start.44 = (bf16[32,4224]{1,0:T(8,128)(2,1)S(1)}, bf16[32,4224]{1,0:T(8,128)(2,1)}, u32[]{:S(2)}) copy-start(bf16[32,4224]{1,0:T(8,128)(2,1)} %get-tuple-element.69) | copy-start | bytes 811012
  37.1 6.2 %collective-permute-start.4 = (bf16[64,2176]{1,0:T(8,128)(2,1)S(1)}, bf16[64,2176]{1,0:T(8,128)(2,1)}, u32[]{:S(2)}, u32[]{:S(2)}) collective-permute-start(bf16[64,2176]{1,0:T(8,128)(2,1)S(1)} %fusion.72), channel_id=1, source_target_pairs={{0,16},{4,20},{8,24},{12,28},{16,0},{20,4},{24,8},{28,12},{1,17},{... | collective-permute-start | bytes 835592 | tf_op jit(solution)/shard_map/ppermute | solution.py:32
  40.5 7.5 %copy-start.52 = (s32[4,32,8,1]{2,1,0,3:T(8,128)}, s32[4,32,8,1]{2,1,0,3:T(8,128)S(1)}, u32[]{:S(2)}) copy-start(s32[4,32,8,1]{2,1,0,3:T(8,128)S(1)} %copy.129) | copy-start | bytes 12292
  44.3 11.2 %collective-permute-start.5 = (bf16[128,2176]{1,0:T(8,128)(2,1)S(1)}, bf16[128,2176]{1,0:T(8,128)(2,1)S(1)}, u32[]{:S(2)}, u32[]{:S(2)}) collective-permute-start(bf16[128,2176]{1,0:T(8,128)(2,1)S(1)} %pad_maximum_fusion.11), channel_id=1, source_target_pairs={{0,8},{4,12},{8,0},{12,4},{16,24},{20,28},{24,16},{28,20},{1,9},{5... | collective-permute-start | bytes 1671176 | tf_op jit(solution)/shard_map/ppermute | solution.py:32
  47.9 11.6 %copy-start.66 = (s32[8,4]{1,0:T(8,128)S(1)}, s32[8,4]{1,0:T(8,128)}, u32[]{:S(2)}) copy-start(s32[8,4]{1,0:T(8,128)} %add_multiply_fusion) | copy-start | bytes 388
  48.0 14.0 %collective-permute-start.7 = (bf16[128,2048]{1,0:T(8,128)(2,1)S(1)}, bf16[128,2048]{1,0:T(8,128)(2,1)S(1)}, u32[]{:S(2)}, u32[]{:S(2)}) collective-permute-start(bf16[128,2048]{1,0:T(8,128)(2,1)S(1)} %pad_maximum_fusion.12), channel_id=1, source_target_pairs={{0,16},{4,20},{8,24},{12,28},{16,0},{20,4},{24,8},{28,12},{1,17},{... | collective-permute-start | bytes 1572872 | tf_op jit(solution)/shard_map/ppermute | solution.py:32
  65.6 7.6 %copy-start.19 = (bf16[32,4224]{1,0:T(8,128)(2,1)S(1)}, bf16[32,4224]{1,0:T(8,128)(2,1)}, u32[]{:S(2)}) copy-start(bf16[32,4224]{1,0:T(8,128)(2,1)} %get-tuple-element.74) | copy-start | bytes 811012
  65.6 53.4 %all-to-all-start = ((bf16[8,48,4096]{2,1,0:T(8,128)(2,1)}), bf16[8,48,4096]{2,1,0:T(8,128)(2,1)S(1)}, u32[]{:S(2)}, u32[]{:S(2)}) async-start(bf16[8,48,4096]{2,1,0:T(8,128)(2,1)} %bitcast.71), calls=%async_computation | async-start | bytes 6291456 | tf_op jit(solution)/shard_map/all_to_all | solution.py:152
  73.2 30.7 %collective-permute-start.10 = (bf16[32,4224]{1,0:T(8,128)(2,1)S(1)}, bf16[32,4224]{1,0:T(8,128)(2,1)S(1)}, u32[]{:S(2)}, u32[]{:S(2)}) collective-permute-start(bf16[32,4224]{1,0:T(8,128)(2,1)S(1)} %copy-done.19), channel_id=1, source_target_pairs={{0,3},{1,2},{2,1},{3,0},{4,7},{5,6},{6,5},{7,4},{8,11},{9,10},{10,... | collective-permute-start | bytes 811016 | tf_op jit(solution)/shard_map/ppermute | solution.py:32
  77.2 28.7 %copy-start.63 = (s32[4,8]{1,0:T(4,128)S(1)}, s32[4,8]{1,0:T(4,128)}, u32[]{:S(2)}) copy-start(s32[4,8]{1,0:T(4,128)} %copy-done.62) | copy-start | bytes 388
  77.3 41.7 %collective-permute-start.12 = (bf16[96,4096]{1,0:T(8,128)(2,1)}, bf16[96,4096]{1,0:T(8,128)(2,1)}, u32[]{:S(2)}, u32[]{:S(2)}) collective-permute-start(bf16[96,4096]{1,0:T(8,128)(2,1)} %get-tuple-element.138), channel_id=1, source_target_pairs={{0,2},{1,3},{2,0},{3,1},{4,6},{5,7},{6,4},{7,5},{8,10},{9,11},{10,... | collective-permute-start | bytes 2359304 | tf_op jit(solution)/shard_map/ppermute | solution.py:32
  80.2 38.8 %collective-permute-start.11 = (bf16[96,4096]{1,0:T(8,128)(2,1)}, bf16[96,4096]{1,0:T(8,128)(2,1)}, u32[]{:S(2)}, u32[]{:S(2)}) collective-permute-start(bf16[96,4096]{1,0:T(8,128)(2,1)} %get-tuple-element.139), channel_id=1, source_target_pairs={{0,1},{1,0},{2,3},{3,2},{4,5},{5,4},{6,7},{7,6},{8,9},{9,8},{10,11... | collective-permute-start | bytes 2359304 | tf_op jit(solution)/shard_map/ppermute | solution.py:32
  120.7 28.2 %collective-permute-start.15 = (bf16[32,4224]{1,0:T(8,128)(2,1)}, bf16[32,4224]{1,0:T(8,128)(2,1)}, u32[]{:S(2)}, u32[]{:S(2)}) collective-permute-start(bf16[32,4224]{1,0:T(8,128)(2,1)} %get-tuple-element.81.refs_1_), channel_id=1, source_target_pairs={{0,3},{1,2},{2,1},{3,0},{4,7},{5,6},{6,5},{7,4},{8,11},{9,10},{10,... | collective-permute-start | bytes 811016 | tf_op jit(solution)/shard_map/ppermute | solution.py:32
  121.7 30.9 %collective-permute-start.14 = (bf16[32,4224]{1,0:T(8,128)(2,1)}, bf16[32,4224]{1,0:T(8,128)(2,1)}, u32[]{:S(2)}, u32[]{:S(2)}) collective-permute-start(bf16[32,4224]{1,0:T(8,128)(2,1)} %get-tuple-element.81.refs_1_), channel_id=1, source_target_pairs={{0,2},{1,3},{2,0},{3,1},{4,6},{5,7},{6,4},{7,5},{8,10},{9,11},{10,... | collective-permute-start | bytes 811016 | tf_op jit(solution)/shard_map/ppermute | solution.py:32
  125.7 26.9 %collective-permute-start.13 = (bf16[32,4224]{1,0:T(8,128)(2,1)}, bf16[32,4224]{1,0:T(8,128)(2,1)}, u32[]{:S(2)}, u32[]{:S(2)}) collective-permute-start(bf16[32,4224]{1,0:T(8,128)(2,1)} %get-tuple-element.81.refs_1_), channel_id=1, source_target_pairs={{0,1},{1,0},{2,3},{3,2},{4,5},{5,4},{6,7},{7,6},{8,9},{9,8},{10,11... | collective-permute-start | bytes 811016 | tf_op jit(solution)/shard_map/ppermute | solution.py:32
  125.7 8.6 %copy-start.4 = (bf16[384,4096]{1,0:T(8,128)(2,1)S(1)}, bf16[384,4096]{1,0:T(8,128)(2,1)}, u32[]{:S(2)}) copy-start(bf16[384,4096]{1,0:T(8,128)(2,1)} %get-tuple-element.80.x_ref) | copy-start | bytes 9437188
  125.7 40.4 %all-to-all-start.1 = ((bf16[8,48,4096]{2,1,0:T(8,128)(2,1)}), bf16[8,48,4096]{2,1,0:T(8,128)(2,1)}, u32[]{:S(2)}, u32[]{:S(2)}) async-start(bf16[8,48,4096]{2,1,0:T(8,128)(2,1)} %bitcast.68), calls=%async_computation.1 | async-start | bytes 6291456 | tf_op jit(solution)/shard_map/all_to_all | solution.py:152
  133.9 28.3 %collective-permute-start.16 = (bf16[48,4096]{1,0:T(8,128)(2,1)}, bf16[48,4096]{1,0:T(8,128)(2,1)S(1)}, u32[]{:S(2)}, u32[]{:S(2)}) collective-permute-start(bf16[48,4096]{1,0:T(8,128)(2,1)} %get-tuple-element.156), channel_id=1, source_target_pairs={{0,3},{1,2},{2,1},{3,0},{4,7},{5,6},{6,5},{7,4},{8,11},{9,10},{10,... | collective-permute-start | bytes 1179656 | tf_op jit(solution)/shard_map/ppermute | solution.py:32
  166.2 7.4 %copy-start.31 = (bf16[48,4096]{1,0:T(8,128)(2,1)S(1)}, bf16[48,4096]{1,0:T(8,128)(2,1)}, u32[]{:S(2)}) copy-start(bf16[48,4096]{1,0:T(8,128)(2,1)} %get-tuple-element.96) | copy-start | bytes 1179652
  166.2 49.1 %all-to-all-start.2 = ((bf16[8,48,4096]{2,1,0:T(8,128)(2,1)}), bf16[8,48,4096]{2,1,0:T(8,128)(2,1)S(1)}, u32[]{:S(2)}, u32[]{:S(2)}) async-start(bf16[8,48,4096]{2,1,0:T(8,128)(2,1)} %bitcast.70), calls=%async_computation.2 | async-start | bytes 6291456 | tf_op jit(solution)/shard_map/all_to_all | solution.py:152
  173.6 18.7 %collective-permute-start.17 = (bf16[48,4096]{1,0:T(8,128)(2,1)S(1)}, bf16[48,4096]{1,0:T(8,128)(2,1)S(1)}, u32[]{:S(2)}, u32[]{:S(2)}) collective-permute-start(bf16[48,4096]{1,0:T(8,128)(2,1)S(1)} %copy-done.31), channel_id=1, source_target_pairs={{0,3},{1,2},{2,1},{3,0},{4,7},{5,6},{6,5},{7,4},{8,11},{9,10},{10,... | collective-permute-start | bytes 1179656 | tf_op jit(solution)/shard_map/ppermute | solution.py:32
  217.1 7.9 %copy-start.8 = (bf16[384,4096]{1,0:T(8,128)(2,1)S(1)}, bf16[384,4096]{1,0:T(8,128)(2,1)}, u32[]{:S(2)}) copy-start(bf16[384,4096]{1,0:T(8,128)(2,1)} %get-tuple-element.105) | copy-start | bytes 9437188
  217.1 45.0 %all-to-all-start.3 = ((bf16[8,48,4096]{2,1,0:T(8,128)(2,1)}), bf16[8,48,4096]{2,1,0:T(8,128)(2,1)}, u32[]{:S(2)}, u32[]{:S(2)}) async-start(bf16[8,48,4096]{2,1,0:T(8,128)(2,1)} %bitcast.63), calls=%async_computation.3 | async-start | bytes 6291456 | tf_op jit(solution)/shard_map/all_to_all | solution.py:152
  226.3 34.1 %collective-permute-start.19 = (bf16[96,4096]{1,0:T(8,128)(2,1)S(1)}, bf16[96,4096]{1,0:T(8,128)(2,1)S(1)}, u32[]{:S(2)}, u32[]{:S(2)}) collective-permute-start(bf16[96,4096]{1,0:T(8,128)(2,1)S(1)} %get-tuple-element.134), channel_id=1, source_target_pairs={{0,2},{1,3},{2,0},{3,1},{4,6},{5,7},{6,4},{7,5},{8,10},{9,11},{10,... | collective-permute-start | bytes 2359304 | tf_op jit(solution)/shard_map/ppermute | solution.py:32
  226.9 35.1 %collective-permute-start.18 = (bf16[96,4096]{1,0:T(8,128)(2,1)S(1)}, bf16[96,4096]{1,0:T(8,128)(2,1)S(1)}, u32[]{:S(2)}, u32[]{:S(2)}) collective-permute-start(bf16[96,4096]{1,0:T(8,128)(2,1)S(1)} %get-tuple-element.135), channel_id=1, source_target_pairs={{0,1},{1,0},{2,3},{3,2},{4,5},{5,4},{6,7},{7,6},{8,9},{9,8},{10,11... | collective-permute-start | bytes 2359304 | tf_op jit(solution)/shard_map/ppermute | solution.py:32
  262.9 6.9 %copy-start.23 = (bf16[4,32,8,1]{3,2,1,0:T(8,128)(2,1)S(1)}, bf16[4,32,8,1]{3,2,1,0:T(8,128)(2,1)}, u32[]{:S(2)}) copy-start(bf16[4,32,8,1]{3,2,1,0:T(8,128)(2,1)} %copy-done.22) | copy-start | bytes 6148
  262.9 50.5 %all-to-all-start.4 = ((bf16[8,48,4096]{2,1,0:T(8,128)(2,1)}), bf16[8,48,4096]{2,1,0:T(8,128)(2,1)S(1)}, u32[]{:S(2)}, u32[]{:S(2)}) async-start(bf16[8,48,4096]{2,1,0:T(8,128)(2,1)} %bitcast.64), calls=%async_computation.4 | async-start | bytes 6291456 | tf_op jit(solution)/shard_map/all_to_all | solution.py:152
  272.7 40.8 %collective-permute-start.20 = (bf16[48,4096]{1,0:T(8,128)(2,1)}, bf16[48,4096]{1,0:T(8,128)(2,1)}, u32[]{:S(2)}, u32[]{:S(2)}) collective-permute-start(bf16[48,4096]{1,0:T(8,128)(2,1)} %get-tuple-element.154), channel_id=1, source_target_pairs={{0,3},{1,2},{2,1},{3,0},{4,7},{5,6},{6,5},{7,4},{8,11},{9,10},{10,... | collective-permute-start | bytes 1179656 | tf_op jit(solution)/shard_map/ppermute | solution.py:32
  273.7 8.8 %copy-start.55 = (s32[4,32,8,1]{2,1,0,3:T(8,128)S(1)}, s32[4,32,8,1]{2,1,0,3:T(8,128)}, u32[]{:S(2)}) copy-start(s32[4,32,8,1]{2,1,0,3:T(8,128)} %copy-done.54) | copy-start | bytes 12292
  273.7 10.0 %copy-start.25 = (bf16[4,32,8,1]{3,2,1,0:T(8,128)(2,1)S(1)}, bf16[4,32,8,1]{3,2,1,0:T(8,128)(2,1)}, u32[]{:S(2)}) copy-start(bf16[4,32,8,1]{3,2,1,0:T(8,128)(2,1)} %copy-done.24) | copy-start | bytes 6148
  278.6 30.4 %collective-permute-start.23 = (bf16[32,4096]{1,0:T(8,128)(2,1)}, bf16[32,4096]{1,0:T(8,128)(2,1)}, u32[]{:S(2)}, u32[]{:S(2)}) collective-permute-start(bf16[32,4096]{1,0:T(8,128)(2,1)} %get-tuple-element.151), channel_id=1, source_target_pairs={{0,3},{1,2},{2,1},{3,0},{4,7},{5,6},{6,5},{7,4},{8,11},{9,10},{10,... | collective-permute-start | bytes 786440 | tf_op jit(solution)/shard_map/ppermute | solution.py:32
  279.1 34.4 %collective-permute-start.22 = (bf16[32,4096]{1,0:T(8,128)(2,1)}, bf16[32,4096]{1,0:T(8,128)(2,1)}, u32[]{:S(2)}, u32[]{:S(2)}) collective-permute-start(bf16[32,4096]{1,0:T(8,128)(2,1)} %get-tuple-element.152), channel_id=1, source_target_pairs={{0,2},{1,3},{2,0},{3,1},{4,6},{5,7},{6,4},{7,5},{8,10},{9,11},{10,... | collective-permute-start | bytes 786440 | tf_op jit(solution)/shard_map/ppermute | solution.py:32
  282.5 30.9 %collective-permute-start.21 = (bf16[32,4096]{1,0:T(8,128)(2,1)}, bf16[32,4096]{1,0:T(8,128)(2,1)}, u32[]{:S(2)}, u32[]{:S(2)}) collective-permute-start(bf16[32,4096]{1,0:T(8,128)(2,1)} %get-tuple-element.153), channel_id=1, source_target_pairs={{0,1},{1,0},{2,3},{3,2},{4,5},{5,4},{6,7},{7,6},{8,9},{9,8},{10,11... | collective-permute-start | bytes 786440 | tf_op jit(solution)/shard_map/ppermute | solution.py:32
  315.2 44.7 %all-to-all-start.5 = ((bf16[8,48,4096]{2,1,0:T(8,128)(2,1)}), bf16[8,48,4096]{2,1,0:T(8,128)(2,1)}, u32[]{:S(2)}, u32[]{:S(2)}) async-start(bf16[8,48,4096]{2,1,0:T(8,128)(2,1)} %bitcast.65), calls=%async_computation.5 | async-start | bytes 6291456 | tf_op jit(solution)/shard_map/all_to_all | solution.py:152
  320.6 29.9 %collective-permute-start.24 = (bf16[48,4096]{1,0:T(8,128)(2,1)S(1)}, bf16[48,4096]{1,0:T(8,128)(2,1)S(1)}, u32[]{:S(2)}, u32[]{:S(2)}) collective-permute-start(bf16[48,4096]{1,0:T(8,128)(2,1)S(1)} %copy-done.32), channel_id=1, source_target_pairs={{0,3},{1,2},{2,1},{3,0},{4,7},{5,6},{6,5},{7,4},{8,11},{9,10},{10,... | collective-permute-start | bytes 1179656 | tf_op jit(solution)/shard_map/ppermute | solution.py:32
  321.1 9.2 %copy-start.18 = (bf16[384,4096]{1,0:T(8,128)(2,1)S(1)}, bf16[384,4096]{1,0:T(8,128)(2,1)}, u32[]{:S(2)}) copy-start(bf16[384,4096]{1,0:T(8,128)(2,1)} %get-tuple-element.133) | copy-start | bytes 9437188
  324.3 31.9 %collective-permute-start.27 = (bf16[32,4096]{1,0:T(8,128)(2,1)S(1)}, bf16[32,4096]{1,0:T(8,128)(2,1)S(1)}, u32[]{:S(2)}, u32[]{:S(2)}) collective-permute-start(bf16[32,4096]{1,0:T(8,128)(2,1)S(1)} %get-tuple-element.148), channel_id=1, source_target_pairs={{0,3},{1,2},{2,1},{3,0},{4,7},{5,6},{6,5},{7,4},{8,11},{9,10},{10,... | collective-permute-start | bytes 786440 | tf_op jit(solution)/shard_map/ppermute | solution.py:32
  325.4 34.5 %collective-permute-start.26 = (bf16[32,4096]{1,0:T(8,128)(2,1)S(1)}, bf16[32,4096]{1,0:T(8,128)(2,1)S(1)}, u32[]{:S(2)}, u32[]{:S(2)}) collective-permute-start(bf16[32,4096]{1,0:T(8,128)(2,1)S(1)} %get-tuple-element.149), channel_id=1, source_target_pairs={{0,2},{1,3},{2,0},{3,1},{4,6},{5,7},{6,4},{7,5},{8,10},{9,11},{10,... | collective-permute-start | bytes 786440 | tf_op jit(solution)/shard_map/ppermute | solution.py:32
  330.3 29.6 %collective-permute-start.25 = (bf16[32,4096]{1,0:T(8,128)(2,1)S(1)}, bf16[32,4096]{1,0:T(8,128)(2,1)S(1)}, u32[]{:S(2)}, u32[]{:S(2)}) collective-permute-start(bf16[32,4096]{1,0:T(8,128)(2,1)S(1)} %get-tuple-element.150), channel_id=1, source_target_pairs={{0,1},{1,0},{2,3},{3,2},{4,5},{5,4},{6,7},{7,6},{8,9},{9,8},{10,11... | collective-permute-start | bytes 786440 | tf_op jit(solution)/shard_map/ppermute | solution.py:32
  330.4 20.2 %copy-start.51 = (bf16[8,32,384]{2,1,0:T(8,128)(2,1)S(1)}, bf16[8,32,384]{2,1,0:T(8,128)(2,1)}, u32[]{:S(2)}) copy-start(bf16[8,32,384]{2,1,0:T(8,128)(2,1)} %pad_maximum_fusion.15) | copy-start | bytes 589828
  365.1 9.8 %copy-start.46 = (bf16[32,4096]{1,0:T(8,128)(2,1)S(1)}, bf16[32,4096]{1,0:T(8,128)(2,1)}, u32[]{:S(2)}) copy-start(bf16[32,4096]{1,0:T(8,128)(2,1)} %get-tuple-element.124) | copy-start | bytes 786436
  365.1 9.8 %copy-start.48 = (bf16[32,4096]{1,0:T(8,128)(2,1)S(1)}, bf16[32,4096]{1,0:T(8,128)(2,1)}, u32[]{:S(2)}) copy-start(bf16[32,4096]{1,0:T(8,128)(2,1)} %get-tuple-element.123) | copy-start | bytes 786436
  365.1 9.8 %copy-start.50 = (bf16[32,4096]{1,0:T(8,128)(2,1)S(1)}, bf16[32,4096]{1,0:T(8,128)(2,1)}, u32[]{:S(2)}) copy-start(bf16[32,4096]{1,0:T(8,128)(2,1)} %get-tuple-element.122) | copy-start | bytes 786436
  365.1 12.5 %collective-permute-start.28 = (bf16[32,4096]{1,0:T(8,128)(2,1)}, bf16[32,4096]{1,0:T(8,128)(2,1)S(1)}, u32[]{:S(2)}, u32[]{:S(2)}) collective-permute-start(bf16[32,4096]{1,0:T(8,128)(2,1)} %get-tuple-element.128), channel_id=1, source_target_pairs={{0,1},{1,0},{2,3},{3,2},{4,5},{5,4},{6,7},{7,6},{8,9},{9,8},{10,11... | collective-permute-start | bytes 786440 | tf_op jit(solution)/shard_map/ppermute | solution.py:32
  368.1 11.3 %collective-permute-start.29 = (bf16[32,4096]{1,0:T(8,128)(2,1)}, bf16[32,4096]{1,0:T(8,128)(2,1)S(1)}, u32[]{:S(2)}, u32[]{:S(2)}) collective-permute-start(bf16[32,4096]{1,0:T(8,128)(2,1)} %get-tuple-element.129), channel_id=1, source_target_pairs={{0,2},{1,3},{2,0},{3,1},{4,6},{5,7},{6,4},{7,5},{8,10},{9,11},{10,... | collective-permute-start | bytes 786440 | tf_op jit(solution)/shard_map/ppermute | solution.py:32
  368.4 23.2 %collective-permute-start.30 = (bf16[32,4096]{1,0:T(8,128)(2,1)}, bf16[32,4096]{1,0:T(8,128)(2,1)S(1)}, u32[]{:S(2)}, u32[]{:S(2)}) collective-permute-start(bf16[32,4096]{1,0:T(8,128)(2,1)} %get-tuple-element.130), channel_id=1, source_target_pairs={{0,3},{1,2},{2,1},{3,0},{4,7},{5,6},{6,5},{7,4},{8,11},{9,10},{10,... | collective-permute-start | bytes 786440 | tf_op jit(solution)/shard_map/ppermute | solution.py:32
  370.7 21.0 %copy-start.10 = (f32[256,2048]{1,0:T(8,128)S(1)}, f32[256,2048]{1,0:T(8,128)}, u32[]{:S(2)}) copy-start(f32[256,2048]{1,0:T(8,128)} %get-tuple-element.132) | copy-start | bytes 6291460
  372.1 19.5 %collective-permute-start.34 = (bf16[128,2048]{1,0:T(8,128)(2,1)S(1)}, bf16[128,2048]{1,0:T(8,128)(2,1)S(1)}, u32[]{:S(2)}, u32[]{:S(2)}) collective-permute-start(bf16[128,2048]{1,0:T(8,128)(2,1)S(1)} %split.240), channel_id=1, source_target_pairs={{0,8},{4,12},{8,0},{12,4},{16,24},{20,28},{24,16},{28,20},{1,9},{5... | collective-permute-start | bytes 1572872 | tf_op jit(solution)/shard_map/ppermute | solution.py:32
  373.6 19.9 %collective-permute-start.31 = (bf16[128,2048]{1,0:T(8,128)(2,1)S(1)}, bf16[128,2048]{1,0:T(8,128)(2,1)S(1)}, u32[]{:S(2)}, u32[]{:S(2)}) collective-permute-start(bf16[128,2048]{1,0:T(8,128)(2,1)S(1)} %split.241), channel_id=1, source_target_pairs={{0,16},{4,20},{8,24},{12,28},{16,0},{20,4},{24,8},{28,12},{1,17},{... | collective-permute-start | bytes 1572872 | tf_op jit(solution)/shard_map/ppermute | solution.py:32
  391.8 5.9 %collective-permute-start.35 = (bf16[64,2048]{1,0:T(8,128)(2,1)S(1)}, bf16[64,2048]{1,0:T(8,128)(2,1)S(1)}, u32[]{:S(2)}, u32[]{:S(2)}) collective-permute-start(bf16[64,2048]{1,0:T(8,128)(2,1)S(1)} %split.242), channel_id=1, source_target_pairs={{0,16},{4,20},{8,24},{12,28},{16,0},{20,4},{24,8},{28,12},{1,17},{... | collective-permute-start | bytes 786440 | tf_op jit(solution)/shard_map/ppermute | solution.py:32
  393.6 10.0 %copy-start.28 = (bf16[32,4096]{1,0:T(8,128)(2,1)S(1)}, bf16[32,4096]{1,0:T(8,128)(2,1)}, u32[]{:S(2)}) copy-start(bf16[32,4096]{1,0:T(8,128)(2,1)} %get-tuple-element.121) | copy-start | bytes 786436
  393.6 7.2 %collective-permute-start.32 = (bf16[64,2048]{1,0:T(8,128)(2,1)S(1)}, bf16[64,2048]{1,0:T(8,128)(2,1)S(1)}, u32[]{:S(2)}, u32[]{:S(2)}) collective-permute-start(bf16[64,2048]{1,0:T(8,128)(2,1)S(1)} %split.243), channel_id=1, source_target_pairs={{0,8},{4,12},{8,0},{12,4},{16,24},{20,28},{24,16},{28,20},{1,9},{5... | collective-permute-start | bytes 786440 | tf_op jit(solution)/shard_map/ppermute | solution.py:32
  397.8 4.9 %collective-permute-start.36 = (bf16[32,2048]{1,0:T(8,128)(2,1)S(1)}, bf16[32,2048]{1,0:T(8,128)(2,1)S(1)}, u32[]{:S(2)}, u32[]{:S(2)}) collective-permute-start(bf16[32,2048]{1,0:T(8,128)(2,1)S(1)} %split.244), channel_id=1, source_target_pairs={{0,4},{4,0},{8,12},{12,8},{16,20},{20,16},{24,28},{28,24},{1,5},{5... | collective-permute-start | bytes 393224 | tf_op jit(solution)/shard_map/ppermute | solution.py:32
  401.0 2.7 collective-permute-start.33
  (47 other events, 134.6 us)

commit v3 on v1

v3 whole, which is shorter than its diff:
```python
import functools

import jax
import jax.numpy as jnp
import numpy as np
from jax import lax
from jax.experimental import pallas as pl
from jax.experimental.pallas import tpu as pltpu
from jax.sharding import PartitionSpec as P

BLOCK_TOK = 32
EPSILON = 1e-06
AXES = ("node", "local")
LANES = 128
TILES = 4
BF16, F32, I32 = jnp.bfloat16, jnp.float32, jnp.int32
ANYWHERE = pl.BlockSpec(memory_space=pl.ANY)
PARAMS = pltpu.CompilerParams(vmem_limit_bytes=60 * 2**20)


def fence(arrays, after):
    token = sum(a[:16, :LANES].astype(F32) for a in after)

    def kernel(*refs):
        pass

    return pl.pallas_call(
        kernel,
        out_shape=[jax.ShapeDtypeStruct(a.shape, a.dtype) for a in arrays],
        in_specs=[ANYWHERE] * (len(arrays) + 1),
        out_specs=[ANYWHERE] * len(arrays),
        input_output_aliases={i: i for i in range(len(arrays))},
    )(*arrays, token)


def swap(array, axis, bits):
    size = lax.axis_size(axis)
    return lax.ppermute(array, axis, [(i, i ^ bits) for i in range(size)])


def swaps(parts, axis, first, last):
    return [swap(parts[k], axis, k) for k in range(first, last)]


def bit_order(size, last_first):
    bits = [1 << i for i in range(size.bit_length() - 1)]
    return bits[:1] + bits[:0:-1] if last_first else bits


def gather_doubling(array, axis, bits):
    for bit in bits:
        array = jnp.concatenate([array, swap(array, axis, bit)])
    return array


def gathered_from(bits):
    found = [0]
    for bit in bits:
        found += [k ^ bit for k in found]
    return found


def sum_halving(keep, give, axis, bits):
    for step, bit in enumerate(bits[::-1]):
        if step:
            keep, give = jnp.split(keep, 2)
        keep = keep + swap(give.astype(BF16), axis, bit).astype(F32)
    return keep.astype(BF16)


def below(rows):
    at = np.arange(rows)
    same = at[:, None] // BLOCK_TOK == at[None, :] // BLOCK_TOK
    return jnp.asarray((same & (at[None, :] < at[:, None])).astype(np.float32), BF16)


def choose(table, lane, own, turn, before):
    select = lax.broadcasted_iota(I32, (table.shape[1], lane.shape[1]), 0) == lane
    weight = jnp.dot(table, select.astype(BF16), preferred_element_type=F32)
    mask = jnp.where(weight > 0, own.astype(F32), 0.0)
    rank = jnp.dot(before, mask.astype(BF16), preferred_element_type=F32)
    place = jnp.where(rank == turn, mask, 0.0)
    return place.astype(BF16), (place * weight).astype(BF16)


def gather_rows(place, rows):
    return lax.dot_general(
        place, rows, (((0,), (0,)), ((), ())), preferred_element_type=F32
    ).astype(BF16)


def pick_kernel(count, *refs):
    parts, refs = refs[:count], refs[count:]
    tables, refs = refs[:count], refs[count:]
    lane, own, turn, before, out, mixing, place = refs

    @pl.when(pl.program_id(0) == 0)
    def _():
        table = jnp.concatenate([t[...] for t in tables])
        place[...], mixing[...] = choose(table, lane[...], own[...], turn[...], before[...])

    out[...] = gather_rows(place[...], jnp.concatenate([p[...] for p in parts]))


def whole_block(array):
    return pl.BlockSpec(array.shape, lambda j: (0,) * array.ndim)


def pick(parts, lane, own, turn, features):
    slots = lane.shape[1]
    rows = len(parts) * BLOCK_TOK
    tile = features // TILES
    before = below(rows)
    small = (lane, own, turn, before)
    return pl.pallas_call(
        functools.partial(pick_kernel, len(parts)),
        grid=(TILES,),
        out_shape=[
            jax.ShapeDtypeStruct((slots, features), BF16),
            jax.ShapeDtypeStruct((rows, slots), BF16),
        ],
        in_specs=[pl.BlockSpec((BLOCK_TOK, tile), lambda j: (0, j))] * len(parts)
        + [pl.BlockSpec((BLOCK_TOK, LANES), lambda j: (0, features // LANES))] * len(parts)
        + [whole_block(a) for a in small],
        out_specs=[
            pl.BlockSpec((slots, tile), lambda j: (0, j)),
            pl.BlockSpec((rows, slots), lambda j: (0, 0)),
        ],
        scratch_shapes=[pltpu.VMEM((rows, slots), BF16)],
        compiler_params=PARAMS,
        cost_estimate=pl.CostEstimate(
            flops=2 * rows * slots * features,
            bytes_accessed=2 * (rows + slots) * features,
            transcendentals=0,
        ),
    )(*parts, *parts, *small)


def pick_cross_kernel(order, cuts, a_ref, b_ref, table, lane, own_a, own_b, turn, before, *refs):
    outs, (mixing_a, mixing_b, place_a, place_b) = refs[:-4], refs[-4:]
    step = pl.program_id(0)

    @pl.when(step == 0)
    def _():
        known = table[...]
        place_b[...], mixing_b[...] = choose(known, lane[...], own_b[...], turn[...], before[...])
        back = [order.index(k) * BLOCK_TOK for k in range(len(order))]
        known = jnp.concatenate([known[at : at + BLOCK_TOK] for at in back])
        place_a[...], mixing_a[...] = choose(known, lane[...], own_a[...], turn[...], before[...])

    def store(place, rows):
        result = gather_rows(place, rows)
        for out, first, last in zip(outs, cuts[:-1], cuts[1:]):
            out[...] = result[first:last]

    @pl.when(step < TILES // 2)
    def _():
        store(place_a[...], a_ref[...])

    @pl.when(step >= TILES // 2)
    def _():
        store(place_b[...], b_ref[...])


def in_first_half(shape):
    return pl.BlockSpec(shape, lambda j: (0, jnp.minimum(j, TILES // 2 - 1)))


def in_second_half(shape):
    return pl.BlockSpec(shape, lambda j: (0, jnp.maximum(j - TILES // 2, 0)))


def pick_cross(rows_a, rows_b, order_b, lane, own_a, own_b, turn, features, cuts):
    slots = lane.shape[1]
    rows = rows_a.shape[0]
    tile = features // TILES
    small = (lane, own_a, own_b, turn, below(rows))
    sizes = [last - first for first, last in zip(cuts[:-1], cuts[1:])]
    results = pl.pallas_call(
        functools.partial(pick_cross_kernel, order_b, cuts),
        grid=(TILES,),
        out_shape=[jax.ShapeDtypeStruct((size, features), BF16) for size in sizes]
        + [jax.ShapeDtypeStruct((rows, slots), BF16)] * 2,
        in_specs=[
            in_first_half((rows, tile)),
            in_second_half((rows, tile)),
            pl.BlockSpec((rows, LANES), lambda j: (0, features // 2 // LANES)),
        ]
        + [whole_block(a) for a in small],
        out_specs=[pl.BlockSpec((size, tile), lambda j: (0, j)) for size in sizes]
        + [pl.BlockSpec((rows, slots), lambda j: (0, 0))] * 2,
        scratch_shapes=[pltpu.VMEM((rows, slots), BF16)] * 2,
        compiler_params=PARAMS,
        cost_estimate=pl.CostEstimate(
            flops=2 * rows * slots * features,
            bytes_accessed=2 * (rows + slots) * features,
            transcendentals=0,
        ),
    )(rows_a, rows_b, rows_b, *small)
    return list(results[:-2]), results[-2], results[-1]


def mix_kernel(mixing, landed, own, *outs):
    result = jnp.dot(mixing[...], landed[...], preferred_element_type=F32)
    own[...] = result[:BLOCK_TOK]
    for k, out in enumerate(outs):
        out[...] = result[(k + 1) * BLOCK_TOK : (k + 2) * BLOCK_TOK].astype(BF16)


def mix(mixing, landed):
    rows, slots = mixing.shape
    features = landed.shape[1]
    tile = features // TILES
    count = rows // BLOCK_TOK
    own, *parts = pl.pallas_call(
        mix_kernel,
        grid=(TILES,),
        out_shape=[jax.ShapeDtypeStruct((BLOCK_TOK, features), F32)]
        + [jax.ShapeDtypeStruct((BLOCK_TOK, features), BF16)] * (count - 1),
        in_specs=[whole_block(mixing), pl.BlockSpec((slots, tile), lambda j: (0, j))],
        out_specs=[pl.BlockSpec((BLOCK_TOK, tile), lambda j: (0, j))] * count,
        compiler_params=PARAMS,
        cost_estimate=pl.CostEstimate(
            flops=2 * rows * slots * features,
            bytes_accessed=2 * (rows + slots) * features,
            transcendentals=0,
        ),
    )(mixing, landed)
    return own, [None] + parts


def mix_cross_kernel(mixing_a, mixing_b, *refs):
    landed, (keep_a, give_a, keep_b, give_b) = refs[:-4], refs[-4:]
    step = pl.program_id(0)
    half = keep_a.shape[0]
    rows = jnp.concatenate([part[...] for part in landed])

    def store(mixing, keep, give):
        result = jnp.dot(mixing[...], rows, preferred_element_type=F32)
        keep[...] = result[:half]
        give[...] = result[half:].astype(BF16)

    @pl.when(step < TILES // 2)
    def _():
        store(mixing_a, keep_a, give_a)

    @pl.when(step >= TILES // 2)
    def _():
        store(mixing_b, keep_b, give_b)


def mix_cross(mixing_a, mixing_b, landed):
    rows, slots = mixing_a.shape
    features = landed[0].shape[1]
    tile = features // TILES
    shape = (rows // 2, features // 2)
    return pl.pallas_call(
        mix_cross_kernel,
        grid=(TILES,),
        out_shape=[jax.ShapeDtypeStruct(shape, F32), jax.ShapeDtypeStruct(shape, BF16)] * 2,
        in_specs=[whole_block(mixing_a), whole_block(mixing_b)]
        + [pl.BlockSpec((part.shape[0], tile), lambda j: (0, j)) for part in landed],
        out_specs=[in_first_half((rows // 2, tile))] * 2 + [in_second_half((rows // 2, tile))] * 2,
        compiler_params=PARAMS,
        cost_estimate=pl.CostEstimate(
            flops=2 * rows * slots * features,
            bytes_accessed=2 * (rows + slots) * features,
            transcendentals=0,
        ),
    )(mixing_a, mixing_b, *landed)


def expert_kernel(count, *refs):
    parts, (gate_ref, up_ref, down_ref), outs = refs[:count], refs[count : count + 3], refs[count + 3 : -2]
    x_ref, total = refs[-2:]
    step = pl.program_id(0)

    @pl.when(step == 0)
    def _():
        x_ref[...] = jnp.concatenate([part[...] for part in parts])

    x = x_ref[...]
    gate_pre = jnp.dot(x, gate_ref[...], preferred_element_type=F32)
    up_pre = jnp.dot(x, up_ref[...], preferred_element_type=F32)
    hidden = (gate_pre / (1 + jnp.exp(-gate_pre)) * up_pre).astype(BF16)
    part = jnp.dot(hidden, down_ref[...], preferred_element_type=F32)

    @pl.when(step == 0)
    def _():
        total[...] = part

    @pl.when(step > 0)
    def _():
        total[...] += part

    @pl.when(step == pl.num_programs(0) - 1)
    def _():
        at = 0
        for out in outs:
            out[...] = total[at : at + out.shape[0]].astype(BF16)
            at += out.shape[0]


def expert(parts, gate_weight, up_weight, down_weight):
    rows = sum(part.shape[0] for part in parts)
    features, hidden = gate_weight.shape
    tile = 256
    return pl.pallas_call(
        functools.partial(expert_kernel, len(parts)),
        grid=(hidden // tile,),
        out_shape=[jax.ShapeDtypeStruct(part.shape, BF16) for part in parts],
        in_specs=[whole_block(part) for part in parts]
        + [
            pl.BlockSpec((features, tile), lambda i: (0, i)),
            pl.BlockSpec((features, tile), lambda i: (0, i)),
            pl.BlockSpec((tile, features), lambda i: (i, 0)),
        ],
        out_specs=[whole_block(part) for part in parts],
        scratch_shapes=[pltpu.VMEM((rows, features), BF16), pltpu.VMEM((rows, features), F32)],
        compiler_params=PARAMS,
        cost_estimate=pl.CostEstimate(
            flops=6 * rows * features * hidden,
            bytes_accessed=6 * features * hidden + 4 * rows * features,
            transcendentals=rows * hidden,
        ),
    )(*parts, gate_weight, up_weight, down_weight)


def to_experts(rows):
    return lax.all_to_all(rows, "node", 0, 0, tiled=True)


def total(own, parts):
    for part in parts:
        own = own + part.astype(F32)
    return own.astype(BF16)


def body(tokens, norm_gain, routes, route_gates, placement, gate_weight, up_weight, down_weight):
    nodes, peers = lax.axis_size("node"), lax.axis_size("local")
    node, local = lax.axis_index("node"), lax.axis_index("local")
    experts = placement.shape[0]
    tok_rows, features = tokens.shape
    top_count = routes.shape[1]
    capacity = BLOCK_TOK * top_count // experts * 3 // 2
    slots = experts * capacity
    half = features // 2
    values = tokens.astype(F32)
    rescale = lax.rsqrt(jnp.mean(values * values, axis=-1, keepdims=True) + EPSILON)
    normed = (values * rescale * norm_gain.astype(F32)).astype(BF16)
    combine_weight = (route_gates / jnp.sum(route_gates, axis=-1, keepdims=True)).astype(BF16)
    held = routes[:, :, None] == placement[None, None, :]
    table = jnp.sum(jnp.where(held, combine_weight[:, :, None], jnp.zeros((), BF16)), axis=1)
    weights = (gate_weight[0], up_weight[0], down_weight[0])
    sent = jnp.concatenate([normed, jnp.pad(table, ((0, 0), (0, -experts % LANES)))], axis=1)
    sent0, sent1, sent2, sent3 = jnp.split(sent, tok_rows // BLOCK_TOK)

    bits_a, bits_b = bit_order(nodes, False), bit_order(nodes, True)
    order_a, order_b = gathered_from(bits_a), gathered_from(bits_b)
    slot = np.arange(slots)
    turn = jnp.asarray(slot[None, :] % capacity, F32)
    near_group = slot // capacity % peers
    near_lane = jnp.asarray(slot[None, :] // (capacity * peers) * peers, I32) + local
    near_own = (np.arange(peers * BLOCK_TOK)[:, None] // BLOCK_TOK == near_group).astype(np.float32)
    near_own = jnp.asarray(near_own, BF16)
    cross_group = slot // capacity % nodes
    cross_lane = (jnp.asarray(slot[None, :] // (capacity * nodes), I32) ^ local) + node * peers
    cross_own = [
        jnp.asarray((np.repeat(order, BLOCK_TOK)[:, None] == cross_group).astype(np.float32), BF16)
        for order in (order_a, order_b)
    ]
    cuts = [slots // peers * k for k in range(peers)] + [slots - slots // peers // 2, slots]

    def gather(rows, first, last):
        return swaps([rows] * peers, "local", first, last)

    def pick_near(rows, near):
        return pick([rows] + near, near_lane, near_own, turn, features)

    near0 = gather(sent0, 1, peers)
    pair = jnp.concatenate([sent3, swap(sent3, "node", bits_a[0])])
    rows_a = gather_doubling(pair[:, :half], "node", bits_a[1:])
    rows_b = gather_doubling(pair[:, half:], "node", bits_b[1:])
    (sent1,) = fence([sent1], near0 + [rows_a, rows_b])
    near1 = gather(sent1, 1, peers - 1)
    outbound0, mixing0 = pick_near(sent0, near0)

    outbound0, sent1, rows_a, rows_b = fence([outbound0, sent1, rows_a, rows_b], near1)
    arrived0 = to_experts(outbound0)
    near1 += gather(sent1, peers - 1, peers)
    outbound3, mixing3a, mixing3b = pick_cross(
        rows_a, rows_b, order_b, cross_lane, *cross_own, turn, features, cuts
    )
    arrived3 = outbound3[:1] + swaps(outbound3, "local", 1, peers - 1)
    outbound1, mixing1 = pick_near(sent1, near1)

    outbound1, sent2, first3, last3 = fence(
        [outbound1, sent2] + outbound3[-2:], [arrived0] + arrived3[1:]
    )
    arrived1 = to_experts(outbound1)
    near2 = gather(sent2, 1, peers)
    arrived3.append(swap(first3, "local", peers - 1))
    (out0,) = expert([arrived0], *weights)
    outbound2, mixing2 = pick_near(sent2, near2)

    outbound2, last3 = fence([outbound2, last3], [arrived1, out0, arrived3[-1]])
    arrived2 = to_experts(outbound2)
    arrived3.append(swap(last3, "local", peers - 1))
    (out1,) = expert([arrived1], *weights)
    arrived3[-1], = fence([arrived3[-1]], [out1])
    out3 = list(expert(arrived3, *weights))

    out0, *out3 = fence([out0] + out3, [arrived2, out1])
    landed0 = to_experts(out0)
    landed3 = out3[:1] + swaps(out3, "local", 1, peers - 1)
    (out2,) = expert([arrived2], *weights)

    out1, first3, last3 = fence([out1] + out3[-2:], [landed0, out2] + landed3[1:])
    landed1 = to_experts(out1)
    landed3.append(swap(first3, "local", peers - 1))
    sum0, parts0 = mix(mixing0, landed0)
    parts0 = swaps(parts0, "local", 1, peers)

    out2, last3 = fence([out2, last3], [landed1, landed3[-1]] + parts0)
    landed2 = to_experts(out2)
    landed3.append(swap(last3, "local", peers - 1))
    sum1, parts1 = mix(mixing1, landed1)
    parts1 = swaps(parts1, "local", 1, peers)
    piece0 = total(sum0, parts0)
    cross = mix_cross(mixing3a, mixing3b, landed3)

    landed2, *cross = fence([landed2] + list(cross), parts1)
    sum2, parts2 = mix(mixing2, landed2)
    cross = fence(list(cross), parts2[1:])
    parts2 = swaps(parts2, "local", 1, peers)
    piece1 = total(sum1, parts1)
    piece3 = jnp.concatenate(
        [sum_halving(*cross[:2], "node", bits_a), sum_halving(*cross[2:], "node", bits_b)], axis=1
    )
    piece2 = total(sum2, parts2)
    return jnp.concatenate([piece0, piece1, piece2, piece3], axis=0)


def solution(mesh):
    rows = P(AXES, None)
    stacked = P(AXES, None, None)
    in_specs = (rows, P(), rows, rows, P(), stacked, stacked, stacked)
    return jax.shard_map(body, mesh=mesh, in_specs=in_specs, out_specs=rows, check_vma=False)
```

time: 427 us -> 405 us (0.948)
  the two profiles are of different devices: /device:TPU:0 before, /device:TPU:9 now
where the time goes in v3:
time: 405 us; the launch traced here: 403 us
  waiting for transfers between devices  192 us (47%)
  Pallas kernels  105 us (26%)
  starting transfers between devices  72.3 us (18%)
  other arithmetic  26.6 us (7%)
  local copies, waits for them, and re-layouts  6.78 us (2%)
    ppermute x37, waiting for transfers between devices, swap(): return lax.ppermute(array, axis, [(i, i ^ bits) for i in range(size)])  192 us
    pallas_call x4, Pallas kernels, expert(): pl.pallas_call(functools.partial(expert_kernel, len(parts)), grid=(hidden...  65.2 us
    ppermute x37, starting transfers between devices, swap(): return lax.ppermute(array, axis, [(i, i ^ bits) for i in range(size)])  41.5 us
    all_to_all x6, starting transfers between devices, to_experts(): return lax.all_to_all(rows, 'node', 0, 0, tiled=True)  30.8 us
    pallas_call x3, Pallas kernels, pick(): pl.pallas_call(functools.partial(pick_kernel, len(parts)), grid=(TILES,),...  15.1 us
    pallas_call x3, Pallas kernels, mix(): pl.pallas_call(mix_kernel, grid=(TILES,), out_shape=[jax.ShapeDtypeStruct...  13.4 us
    add x9, other arithmetic, fence(): token = sum((a[:16, :LANES].astype(F32) for a in after))  11 us
  transfers between devices with their start and end apart: 43, of which 23 were waited for; matrix products, arithmetic and copies ran while one was open for 3% of the time, Pallas kernels for 25%

profile of v3, /device:TPU:9, one launch (start us, length us, event | category | flops | bytes accessed | tf_op | source)
XLA Modules:
  0.0 403.2 jit_solution(3408264546569034343)
XLA Ops:
  0.0 1.5 fusion.1
  4.5 1.6 fusion.3
  7.8 1.3 collective-permute-start.2
  11.3 1.3 collective-permute-start.4
  12.6 1.3 collective-permute-start.6
  13.9 13.6 %collective-permute-done.2.refs_3_.refs_7_ = bf16[32,4224]{1,0:T(8,128)(2,1)S(1)} collective-permute-done((bf16[32,4224]{1,0:T(8,128)(2,1)S(1)}, bf16[32,4224]{1,0:T(8,128)(2,1)S(1)}, u32[]{:S(2)}, u32[]{:S(2)}) %collective-permute-start.2) | collective-permute-done | bytes 270368 | tf_op jit(solution)/shard_map/ppermute | solution.py:38
  27.5 4.9 %collective-permute-done.1.refs_2_.refs_6_ = bf16[32,4224]{1,0:T(8,128)(2,1)S(1)} collective-permute-done((bf16[32,4224]{1,0:T(8,128)(2,1)S(1)}, bf16[32,4224]{1,0:T(8,128)(2,1)S(1)}, u32[]{:S(2)}, u32[]{:S(2)}) %collective-permute-start.1) | collective-permute-done | bytes 270368 | tf_op jit(solution)/shard_map/ppermute | solution.py:38
  33.0 3.1 collective-permute-start.9
  38.3 1.3 collective-permute-start.7
  40.1 5.0 %shard_map.172 = (bf16[384,4096]{1,0:T(8,128)(2,1)}, bf16[128,384]{1,0:T(8,128)(2,1)}) custom-call(bf16[32,4224]{1,0:T(8,128)(2,1)} %copy-done.10, bf16[32,4224]{1,0:T(8,128)(2,1)} %copy-done.17, bf16[32,4224]{1,0:T(8,128)(2,1)} %copy-done.16, bf16[32,4224]{1,0:T(8,128)(2,1)} %copy-done.15, bf16[32,4224]{1,0:T(8,128)(2,1)} %copy-done.10, ...), custom_call_target="tpu_custom_call" | custom-call | flops 402653184 | bytes 4194304 | tf_op jit(solution)/shard_map/pallas_call | solution.py:115
  45.2 2.0 collective-permute-done.9.refs_2_.refs_6_
  48.0 1.6 collective-permute-done.5
  49.6 2.1 pad_maximum_fusion.1.refs_2_
  52.9 5.7 %all-to-all-start = ((bf16[8,48,4096]{2,1,0:T(8,128)(2,1)}), bf16[8,48,4096]{2,1,0:T(8,128)(2,1)S(1)}, u32[]{:S(2)}, u32[]{:S(2)}) async-start(bf16[8,48,4096]{2,1,0:T(8,128)(2,1)} %bitcast.25), calls=%async_computation | async-start | bytes 6291456 | tf_op jit(solution)/shard_map/all_to_all | solution.py:330
  59.2 5.9 %shard_map.176 = (bf16[96,4096]{1,0:T(8,128)(2,1)}, bf16[96,4096]{1,0:T(8,128)(2,1)}, bf16[96,4096]{1,0:T(8,128)(2,1)}, bf16[48,4096]{1,0:T(8,128)(2,1)}, bf16[4...) custom-call(bf16[256,2048]{1,0:T(8,128)(2,1)} %get-tuple-element.72.a_ref, ...), custom_call_target="tpu_custom_call" | custom-call | flops 805306368 | bytes 5242880 | tf_op jit(solution)/shard_map/pallas_call | solution.py:179
  65.1 1.5 collective-permute-start.10
  66.7 1.3 collective-permute-start.12
  67.9 46.1 %collective-permute-done.12.refs_3_.refs_7_ = bf16[32,4224]{1,0:T(8,128)(2,1)S(1)} collective-permute-done((bf16[32,4224]{1,0:T(8,128)(2,1)S(1)}, bf16[32,4224]{1,0:T(8,128)(2,1)S(1)}, u32[]{:S(2)}, u32[]{:S(2)}) %collective-permute-start.12) | collective-permute-done | bytes 270368 | tf_op jit(solution)/shard_map/ppermute | solution.py:38
  114.8 5.0 %shard_map.177 = (bf16[384,4096]{1,0:T(8,128)(2,1)}, bf16[128,384]{1,0:T(8,128)(2,1)}) custom-call(bf16[32,4224]{1,0:T(8,128)(2,1)} %get-tuple-element.77.refs_0_.refs_4_, bf16[32,4224]{1,0:T(8,128)(2,1)} %copy-done.14, bf16[32,4224]{1,0:T(8,128)(2,1)} %copy-done.13, bf16[32,4224]{1,0:T(8,128)(2,1)} %copy-done.21, ...), custom_call_target="tpu_custom_call" | custom-call | flops 402653184 | bytes 4194304 | tf_op jit(solution)/shard_map/pallas_call | solution.py:115
  119.8 1.6 convert_add_fusion.8.refs_4_
  121.6 5.4 %all-to-all-start.1 = ((bf16[8,48,4096]{2,1,0:T(8,128)(2,1)}), bf16[8,48,4096]{2,1,0:T(8,128)(2,1)}, u32[]{:S(2)}, u32[]{:S(2)}) async-start(bf16[8,48,4096]{2,1,0:T(8,128)(2,1)} %bitcast.23), calls=%async_computation.1 | async-start | bytes 6291456 | tf_op jit(solution)/shard_map/all_to_all | solution.py:330
  127.2 2.4 collective-permute-start.14
  129.8 16.3 %shard_map.175.refs_0_ = bf16[384,4096]{1,0:T(8,128)(2,1)} custom-call(bf16[384,4096]{1,0:T(8,128)(2,1)} %bitcast.27, bf16[4096,768]{1,0:T(8,128)(2,1)} %bitcast.30, bf16[4096,768]{1,0:T(8,128)(2,1)} %bitcast.34, bf16[768,4096]{1,0:T(8,128)(2,1)} %bitcast.38), custom_call_target="tpu_custom_call" | custom-call | flops 7247757312 | bytes 25165824 | tf_op jit(solution)/shard_map/pallas_call | solution.py:308
  146.1 8.9 %collective-permute-done.15.refs_2_.refs_6_ = bf16[32,4224]{1,0:T(8,128)(2,1)S(1)} collective-permute-done((bf16[32,4224]{1,0:T(8,128)(2,1)S(1)}, bf16[32,4224]{1,0:T(8,128)(2,1)S(1)}, u32[]{:S(2)}, u32[]{:S(2)}) %collective-permute-start.15) | collective-permute-done | bytes 270368 | tf_op jit(solution)/shard_map/ppermute | solution.py:38
  156.4 5.0 %shard_map.179 = (bf16[384,4096]{1,0:T(8,128)(2,1)}, bf16[128,384]{1,0:T(8,128)(2,1)}) custom-call(bf16[32,4224]{1,0:T(8,128)(2,1)} %get-tuple-element.82.refs_0_.refs_4_, bf16[32,4224]{1,0:T(8,128)(2,1)} %copy-done.20, bf16[32,4224]{1,0:T(8,128)(2,1)} %copy-done.19, bf16[32,4224]{1,0:T(8,128)(2,1)} %copy-done.18, ...), custom_call_target="tpu_custom_call" | custom-call | flops 402653184 | bytes 4194304 | tf_op jit(solution)/shard_map/pallas_call | solution.py:115
  161.4 3.1 collective-permute-done.13.refs_3_
  164.5 1.3 convert_add_fusion.7.refs_2_
  165.8 4.4 %all-to-all-start.2 = ((bf16[8,48,4096]{2,1,0:T(8,128)(2,1)}), bf16[8,48,4096]{2,1,0:T(8,128)(2,1)S(1)}, u32[]{:S(2)}, u32[]{:S(2)}) async-start(bf16[8,48,4096]{2,1,0:T(8,128)(2,1)} %bitcast.24), calls=%async_computation.2 | async-start | bytes 6291456 | tf_op jit(solution)/shard_map/all_to_all | solution.py:330
  171.4 16.3 %shard_map.181.refs_0_ = bf16[384,4096]{1,0:T(8,128)(2,1)} custom-call(bf16[384,4096]{1,0:T(8,128)(2,1)} %bitcast.6.refs_0_, bf16[4096,768]{1,0:T(8,128)(2,1)} %bitcast.31, bf16[4096,768]{1,0:T(8,128)(2,1)} %bitcast.35, bf16[768,4096]{1,0:T(8,128)(2,1)} %bitcast.39), custom_call_target="tpu_custom_call" | custom-call | flops 7247757312 | bytes 25165824 | tf_op jit(solution)/shard_map/pallas_call | solution.py:308
  187.7 1.3 slice_convert_fusion.4.refs_1_
  189.7 16.3 %shard_map.183 = (bf16[96,4096]{1,0:T(8,128)(2,1)}, bf16[96,4096]{1,0:T(8,128)(2,1)}, bf16[96,4096]{1,0:T(8,128)(2,1)}, bf16[48,4096]{1,0:T(8,128)(2,1)}, bf16[48,4096]{1,0:T(8,128)(2,1)}) custom-call(bf16[96,4096]{1,0:T(8,128)(2,1)} %get-tuple-element.74.refs_0_, bf16[96,4096]{1,0:T(8,128)(2,1)} %collective-permute-done.10.refs_1_, ...), custom_call_target="tpu_custom_call" | custom-call | flops 7247757312 | bytes 25165824 | tf_op jit(solution)/shard_map/pallas_call | solution.py:308
  206.0 1.6 convert_add_fusion.6.refs_6_
  207.7 5.6 %all-to-all-start.3 = ((bf16[8,48,4096]{2,1,0:T(8,128)(2,1)}), bf16[8,48,4096]{2,1,0:T(8,128)(2,1)S(1)}, u32[]{:S(2)}, u32[]{:S(2)}) async-start(bf16[8,48,4096]{2,1,0:T(8,128)(2,1)} %bitcast.17), calls=%async_computation.3 | async-start | bytes 6291456 | tf_op jit(solution)/shard_map/all_to_all | solution.py:330
  213.4 2.4 collective-permute-start.22
  215.7 16.4 %shard_map.186.refs_0_ = bf16[384,4096]{1,0:T(8,128)(2,1)} custom-call(bf16[384,4096]{1,0:T(8,128)(2,1)} %bitcast.29, bf16[4096,768]{1,0:T(8,128)(2,1)} %bitcast.33, bf16[4096,768]{1,0:T(8,128)(2,1)} %bitcast.37, bf16[768,4096]{1,0:T(8,128)(2,1)} %bitcast.41), custom_call_target="tpu_custom_call" | custom-call | flops 7247757312 | bytes 25165824 | tf_op jit(solution)/shard_map/pallas_call | solution.py:308
  232.1 15.3 %collective-permute-done.21.refs_1_ = bf16[96,4096]{1,0:T(8,128)(2,1)} collective-permute-done((bf16[96,4096]{1,0:T(8,128)(2,1)}, bf16[96,4096]{1,0:T(8,128)(2,1)}, u32[]{:S(2)}, u32[]{:S(2)}) %collective-permute-start.21) | collective-permute-done | bytes 786464 | tf_op jit(solution)/shard_map/ppermute | solution.py:38
  247.4 3.1 collective-permute-done.22.refs_2_
  250.5 1.6 convert_add_fusion.5.refs_3_
  252.1 5.0 %all-to-all-start.4 = ((bf16[8,48,4096]{2,1,0:T(8,128)(2,1)}), bf16[8,48,4096]{2,1,0:T(8,128)(2,1)S(1)}, u32[]{:S(2)}, u32[]{:S(2)}) async-start(bf16[8,48,4096]{2,1,0:T(8,128)(2,1)} %bitcast.16), calls=%async_computation.4 | async-start | bytes 6291456 | tf_op jit(solution)/shard_map/all_to_all | solution.py:330
  257.8 4.3 %shard_map.185 = (f32[32,4096]{1,0:T(8,128)}, bf16[32,4096]{1,0:T(8,128)(2,1)}, bf16[32,4096]{1,0:T(8,128)(2,1)}, bf16[32,4096]{1,0:T(8,128)(2,1)}) custom-call(bf16[128,384]{1,0:T(8,128)(2,1)} %get-tuple-element.69.mixing, bf16[384,4096]{1,0:T(8,128)(2,1)} %bitcast.22), custom_call_target="tpu_custom_call" | custom-call | flops 402653184 | bytes 4194304 | tf_op jit(solution)/shard_map/pallas_call | solution.py:215
  262.1 2.8 collective-permute-start.18
  266.2 9.4 %collective-permute-done.18 = bf16[32,4096]{1,0:T(8,128)(2,1)S(1)} collective-permute-done((bf16[32,4096]{1,0:T(8,128)(2,1)}, bf16[32,4096]{1,0:T(8,128)(2,1)S(1)}, u32[]{:S(2)}, u32[]{:S(2)}) %collective-permute-start.18) | collective-permute-done | bytes 262176 | tf_op jit(solution)/shard_map/ppermute | solution.py:38
  275.7 15.9 %collective-permute-done.19 = bf16[32,4096]{1,0:T(8,128)(2,1)S(1)} collective-permute-done((bf16[32,4096]{1,0:T(8,128)(2,1)}, bf16[32,4096]{1,0:T(8,128)(2,1)S(1)}, u32[]{:S(2)}, u32[]{:S(2)}) %collective-permute-start.19) | collective-permute-done | bytes 262176 | tf_op jit(solution)/shard_map/ppermute | solution.py:38
  291.5 7.2 %collective-permute-done.20 = bf16[32,4096]{1,0:T(8,128)(2,1)S(1)} collective-permute-done((bf16[32,4096]{1,0:T(8,128)(2,1)}, bf16[32,4096]{1,0:T(8,128)(2,1)S(1)}, u32[]{:S(2)}, u32[]{:S(2)}) %collective-permute-start.20) | collective-permute-done | bytes 262176 | tf_op jit(solution)/shard_map/ppermute | solution.py:38
  299.4 1.6 convert_add_fusion.4.refs_2_
  301.1 4.7 %all-to-all-start.5 = ((bf16[8,48,4096]{2,1,0:T(8,128)(2,1)}), bf16[8,48,4096]{2,1,0:T(8,128)(2,1)S(1)}, u32[]{:S(2)}, u32[]{:S(2)}) async-start(bf16[8,48,4096]{2,1,0:T(8,128)(2,1)} %bitcast.18), calls=%async_computation.5 | async-start | bytes 6291456 | tf_op jit(solution)/shard_map/all_to_all | solution.py:330
  305.8 4.5 %shard_map.188 = (f32[32,4096]{1,0:T(8,128)}, bf16[32,4096]{1,0:T(8,128)(2,1)}, bf16[32,4096]{1,0:T(8,128)(2,1)}, bf16[32,4096]{1,0:T(8,128)(2,1)}) custom-call(bf16[128,384]{1,0:T(8,128)(2,1)} %get-tuple-element.98.mixing, bf16[384,4096]{1,0:T(8,128)(2,1)} %bitcast.20), custom_call_target="tpu_custom_call" | custom-call | flops 402653184 | bytes 4194304 | tf_op jit(solution)/shard_map/pallas_call | solution.py:215
  310.3 1.9 collective-permute-start.24
  313.6 1.4 add_convert_fusion.2
  315.0 6.4 %collective-permute-done.23 = bf16[32,4096]{1,0:T(8,128)(2,1)S(1)} collective-permute-done((bf16[32,4096]{1,0:T(8,128)(2,1)}, bf16[32,4096]{1,0:T(8,128)(2,1)S(1)}, u32[]{:S(2)}, u32[]{:S(2)}) %collective-permute-start.23) | collective-permute-done | bytes 262176 | tf_op jit(solution)/shard_map/ppermute | solution.py:38
  321.4 3.1 collective-permute-done.24
  324.4 20.1 %collective-permute-done.25 = bf16[32,4096]{1,0:T(8,128)(2,1)S(1)} collective-permute-done((bf16[32,4096]{1,0:T(8,128)(2,1)}, bf16[32,4096]{1,0:T(8,128)(2,1)S(1)}, u32[]{:S(2)}, u32[]{:S(2)}) %collective-permute-start.25) | collective-permute-done | bytes 262176 | tf_op jit(solution)/shard_map/ppermute | solution.py:38
  345.2 7.8 %collective-permute-done.27.refs_4_ = bf16[48,4096]{1,0:T(8,128)(2,1)S(1)} collective-permute-done((bf16[48,4096]{1,0:T(8,128)(2,1)S(1)}, bf16[48,4096]{1,0:T(8,128)(2,1)S(1)}, u32[]{:S(2)}, u32[]{:S(2)}) %collective-permute-start.27) | collective-permute-done | bytes 393248 | tf_op jit(solution)/shard_map/ppermute | solution.py:38
  353.7 5.7 %shard_map.190 = (f32[128,2048]{1,0:T(8,128)}, bf16[128,2048]{1,0:T(8,128)(2,1)}, f32[128,2048]{1,0:T(8,128)}, bf16[128,2048]{1,0:T(8,128)(2,1)}) custom-call(bf16[256,384]{1,0:T(8,128)(2,1)} %get-tuple-element.112.mixing_a, bf16[256,384]{1,0:T(8,128)(2,1)} %get-tuple-element.113.mixing_b, bf16[96,4096]{1,0:T(8,128)(2,1)} %get-tuple-element.114.refs_0_, ...), custom_call_target="tpu_custom_call" | custom-call | flops 805306368 | bytes 5242880 | tf_op jit(solution)/shard_map/pallas_call | solution.py:257
  359.4 1.6 copy-done
  361.1 4.6 %shard_map.192 = (f32[32,4096]{1,0:T(8,128)}, bf16[32,4096]{1,0:T(8,128)(2,1)}, bf16[32,4096]{1,0:T(8,128)(2,1)}, bf16[32,4096]{1,0:T(8,128)(2,1)}) custom-call(bf16[128,384]{1,0:T(8,128)(2,1)} %get-tuple-element.108.mixing, bf16[384,4096]{1,0:T(8,128)(2,1)} %get-tuple-element.120.landed), custom_call_target="tpu_custom_call" | custom-call | flops 402653184 | bytes 4194304 | tf_op jit(solution)/shard_map/pallas_call | solution.py:215
  365.6 1.9 collective-permute-start.29
  368.4 1.3 convert_add_fusion.2.refs_4_
  372.0 2.6 collective-permute-done.28
  374.5 4.0 collective-permute-done.29
  378.6 11.8 %collective-permute-done.30 = bf16[32,4096]{1,0:T(8,128)(2,1)S(1)} collective-permute-done((bf16[32,4096]{1,0:T(8,128)(2,1)}, bf16[32,4096]{1,0:T(8,128)(2,1)S(1)}, u32[]{:S(2)}, u32[]{:S(2)}) %collective-permute-start.30) | collective-permute-done | bytes 262176 | tf_op jit(solution)/shard_map/ppermute | solution.py:38
  392.8 3.1 collective-permute-done.32
  396.0 3.6 collective-permute-start.33
  399.6 1.5 collective-permute-start.36
  (160 shorter events, 30.9 us)
Async XLA Ops:
  7.1 31.2 %copy-start.10 = (bf16[32,4224]{1,0:T(8,128)(2,1)}, bf16[32,4224]{1,0:T(8,128)(2,1)S(1)}, u32[]{:S(2)}) copy-start(bf16[32,4224]{1,0:T(8,128)(2,1)S(1)} %get-tuple-element.136.refs_0_.refs_4_) | copy-start | bytes 811012
  7.1 4.2 %collective-permute-start.3 = (bf16[32,4224]{1,0:T(8,128)(2,1)S(1)}, bf16[32,4224]{1,0:T(8,128)(2,1)S(1)}, u32[]{:S(2)}, u32[]{:S(2)}) collective-permute-start(bf16[32,4224]{1,0:T(8,128)(2,1)S(1)} %get-tuple-element.134), channel_id=1, source_target_pairs={{0,4},{4,0},{8,12},{12,8},{16,20},{20,16},{24,28},{28,24},{1,5},{5... | collective-permute-start | bytes 811016 | tf_op jit(solution)/shard_map/ppermute | solution.py:38
  7.8 19.7 %collective-permute-start.2 = (bf16[32,4224]{1,0:T(8,128)(2,1)S(1)}, bf16[32,4224]{1,0:T(8,128)(2,1)S(1)}, u32[]{:S(2)}, u32[]{:S(2)}) collective-permute-start(bf16[32,4224]{1,0:T(8,128)(2,1)S(1)} %get-tuple-element.136.refs_0_.refs_4_), channel_id=1, source_target_pairs={{0,3},{1,2},{2,1},{3,0},{4,7},{5,6},{6,5},{7,4},{8,11},{9,10},{10,... | collective-permute-start | bytes 811016 | tf_op jit(solution)/shard_map/ppermute | solution.py:38
  9.1 23.3 %collective-permute-start.1 = (bf16[32,4224]{1,0:T(8,128)(2,1)S(1)}, bf16[32,4224]{1,0:T(8,128)(2,1)S(1)}, u32[]{:S(2)}, u32[]{:S(2)}) collective-permute-start(bf16[32,4224]{1,0:T(8,128)(2,1)S(1)} %get-tuple-element.136.refs_0_.refs_4_), channel_id=1, source_target_pairs={{0,2},{1,3},{2,0},{3,1},{4,6},{5,7},{6,4},{7,5},{8,10},{9,11},{10,... | collective-permute-start | bytes 811016 | tf_op jit(solution)/shard_map/ppermute | solution.py:38
  10.1 22.3 %collective-permute-start = (bf16[32,4224]{1,0:T(8,128)(2,1)S(1)}, bf16[32,4224]{1,0:T(8,128)(2,1)S(1)}, u32[]{:S(2)}, u32[]{:S(2)}) collective-permute-start(bf16[32,4224]{1,0:T(8,128)(2,1)S(1)} %get-tuple-element.136.refs_0_.refs_4_), channel_id=1, source_target_pairs={{0,1},{1,0},{2,3},{3,2},{4,5},{5,4},{6,7},{7,6},{8,9},{9,8},{10,11... | collective-permute-start | bytes 811016 | tf_op jit(solution)/shard_map/ppermute | solution.py:38
  11.3 28.3 %copy-start.34 = (s32[1,384]{1,0:T(1,128)S(1)}, s32[1,384]{1,0:T(1,128)}, u32[]{:S(2)}) copy-start(s32[1,384]{1,0:T(1,128)} %constant.40.clone) | copy-start | bytes 4612
  11.3 24.8 %collective-permute-start.4 = (bf16[64,2048]{1,0:T(8,128)(2,1)S(1)}, bf16[64,2048]{1,0:T(8,128)(2,1)S(1)}, u32[]{:S(2)}, u32[]{:S(2)}) collective-permute-start(bf16[64,2048]{1,0:T(8,128)(2,1)S(1)} %pad_maximum_fusion.5), channel_id=1, source_target_pairs={{0,8},{4,12},{8,0},{12,4},{16,24},{20,28},{24,16},{28,20},{1,9},{5... | collective-permute-start | bytes 786440 | tf_op jit(solution)/shard_map/ppermute | solution.py:38
  12.6 25.6 %collective-permute-start.6 = (bf16[64,2176]{1,0:T(8,128)(2,1)S(1)}, bf16[64,2176]{1,0:T(8,128)(2,1)S(1)}, u32[]{:S(2)}, u32[]{:S(2)}) collective-permute-start(bf16[64,2176]{1,0:T(8,128)(2,1)S(1)} %pad_maximum_fusion.4), channel_id=1, source_target_pairs={{0,16},{4,20},{8,24},{12,28},{16,0},{20,4},{24,8},{28,12},{1,17},{... | collective-permute-start | bytes 835592 | tf_op jit(solution)/shard_map/ppermute | solution.py:38
  27.5 12.6 %copy-start.15 = (bf16[32,4224]{1,0:T(8,128)(2,1)}, bf16[32,4224]{1,0:T(8,128)(2,1)S(1)}, u32[]{:S(2)}) copy-start(bf16[32,4224]{1,0:T(8,128)(2,1)S(1)} %collective-permute-done.2.refs_3_.refs_7_) | copy-start | bytes 811012
  32.4 7.8 %copy-start.16 = (bf16[32,4224]{1,0:T(8,128)(2,1)}, bf16[32,4224]{1,0:T(8,128)(2,1)S(1)}, u32[]{:S(2)}) copy-start(bf16[32,4224]{1,0:T(8,128)(2,1)S(1)} %collective-permute-done.1.refs_2_.refs_6_) | copy-start | bytes 811012
  32.4 7.8 %copy-start.17 = (bf16[32,4224]{1,0:T(8,128)(2,1)}, bf16[32,4224]{1,0:T(8,128)(2,1)S(1)}, u32[]{:S(2)}) copy-start(bf16[32,4224]{1,0:T(8,128)(2,1)S(1)} %collective-permute-done.refs_1_.refs_5_) | copy-start | bytes 811012
  33.0 14.2 %collective-permute-start.9 = (bf16[32,4224]{1,0:T(8,128)(2,1)}, bf16[32,4224]{1,0:T(8,128)(2,1)S(1)}, u32[]{:S(2)}, u32[]{:S(2)}) collective-permute-start(bf16[32,4224]{1,0:T(8,128)(2,1)} %shard_map.173.refs_1_), channel_id=1, source_target_pairs={{0,2},{1,3},{2,0},{3,1},{4,6},{5,7},{6,4},{7,5},{8,10},{9,11},{10,... | collective-permute-start | bytes 811016 | tf_op jit(solution)/shard_map/ppermute | solution.py:38
  36.1 11.2 %collective-permute-start.8 = (bf16[32,4224]{1,0:T(8,128)(2,1)}, bf16[32,4224]{1,0:T(8,128)(2,1)S(1)}, u32[]{:S(2)}, u32[]{:S(2)}) collective-permute-start(bf16[32,4224]{1,0:T(8,128)(2,1)} %shard_map.173.refs_1_), channel_id=1, source_target_pairs={{0,1},{1,0},{2,3},{3,2},{4,5},{5,4},{6,7},{7,6},{8,9},{9,8},{10,11... | collective-permute-start | bytes 811016 | tf_op jit(solution)/shard_map/ppermute | solution.py:38
  37.0 12.7 %collective-permute-start.5 = (bf16[128,2048]{1,0:T(8,128)(2,1)}, bf16[128,2048]{1,0:T(8,128)(2,1)}, u32[]{:S(2)}, u32[]{:S(2)}) collective-permute-start(bf16[128,2048]{1,0:T(8,128)(2,1)} %pad_maximum_fusion.3), channel_id=1, source_target_pairs={{0,16},{4,20},{8,24},{12,28},{16,0},{20,4},{24,8},{28,12},{1,17},{... | collective-permute-start | bytes 1572872 | tf_op jit(solution)/shard_map/ppermute | solution.py:38
  38.3 13.5 %collective-permute-start.7 = (bf16[128,2176]{1,0:T(8,128)(2,1)S(1)}, bf16[128,2176]{1,0:T(8,128)(2,1)S(1)}, u32[]{:S(2)}, u32[]{:S(2)}) collective-permute-start(bf16[128,2176]{1,0:T(8,128)(2,1)S(1)} %pad_maximum_fusion.2), channel_id=1, source_target_pairs={{0,8},{4,12},{8,0},{12,4},{16,24},{20,28},{24,16},{28,20},{1,9},{5... | collective-permute-start | bytes 1671176 | tf_op jit(solution)/shard_map/ppermute | solution.py:38
  47.2 5.7 %copy-start.13 = (bf16[32,4224]{1,0:T(8,128)(2,1)}, bf16[32,4224]{1,0:T(8,128)(2,1)S(1)}, u32[]{:S(2)}) copy-start(bf16[32,4224]{1,0:T(8,128)(2,1)S(1)} %collective-permute-done.9.refs_2_.refs_6_) | copy-start | bytes 811012
  52.9 5.7 %copy-start.35 = (s32[1,384]{1,0:T(1,128)S(1)}, s32[1,384]{1,0:T(1,128)}, u32[]{:S(2)}) copy-start(s32[1,384]{1,0:T(1,128)} %constant.42.clone) | copy-start | bytes 4612
  52.9 66.9 %all-to-all-start = ((bf16[8,48,4096]{2,1,0:T(8,128)(2,1)}), bf16[8,48,4096]{2,1,0:T(8,128)(2,1)S(1)}, u32[]{:S(2)}, u32[]{:S(2)}) async-start(bf16[8,48,4096]{2,1,0:T(8,128)(2,1)} %bitcast.25), calls=%async_computation | async-start | bytes 6291456 | tf_op jit(solution)/shard_map/all_to_all | solution.py:330
  58.6 8.1 %copy-start.5 = (bf16[32,4224]{1,0:T(8,128)(2,1)S(1)}, bf16[32,4224]{1,0:T(8,128)(2,1)}, u32[]{:S(2)}) copy-start(bf16[32,4224]{1,0:T(8,128)(2,1)} %get-tuple-element.77.refs_0_.refs_4_) | copy-start | bytes 811012
  65.1 54.7 %collective-permute-start.10 = (bf16[96,4096]{1,0:T(8,128)(2,1)}, bf16[96,4096]{1,0:T(8,128)(2,1)}, u32[]{:S(2)}, u32[]{:S(2)}) collective-permute-start(bf16[96,4096]{1,0:T(8,128)(2,1)} %get-tuple-element.75), channel_id=1, source_target_pairs={{0,1},{1,0},{2,3},{3,2},{4,5},{5,4},{6,7},{7,6},{8,9},{9,8},{10,11... | collective-permute-start | bytes 2359304 | tf_op jit(solution)/shard_map/ppermute | solution.py:38
  66.7 53.1 %collective-permute-start.11 = (bf16[96,4096]{1,0:T(8,128)(2,1)}, bf16[96,4096]{1,0:T(8,128)(2,1)}, u32[]{:S(2)}, u32[]{:S(2)}) collective-permute-start(bf16[96,4096]{1,0:T(8,128)(2,1)} %get-tuple-element.76), channel_id=1, source_target_pairs={{0,2},{1,3},{2,0},{3,1},{4,6},{5,7},{6,4},{7,5},{8,10},{9,11},{10,... | collective-permute-start | bytes 2359304 | tf_op jit(solution)/shard_map/ppermute | solution.py:38
  66.7 47.4 %collective-permute-start.12 = (bf16[32,4224]{1,0:T(8,128)(2,1)S(1)}, bf16[32,4224]{1,0:T(8,128)(2,1)S(1)}, u32[]{:S(2)}, u32[]{:S(2)}) collective-permute-start(bf16[32,4224]{1,0:T(8,128)(2,1)S(1)} %copy-done.5), channel_id=1, source_target_pairs={{0,3},{1,2},{2,1},{3,0},{4,7},{5,6},{6,5},{7,4},{8,11},{9,10},{10,... | collective-permute-start | bytes 811016 | tf_op jit(solution)/shard_map/ppermute | solution.py:38
  121.6 42.9 %all-to-all-start.1 = ((bf16[8,48,4096]{2,1,0:T(8,128)(2,1)}), bf16[8,48,4096]{2,1,0:T(8,128)(2,1)}, u32[]{:S(2)}, u32[]{:S(2)}) async-start(bf16[8,48,4096]{2,1,0:T(8,128)(2,1)} %bitcast.23), calls=%async_computation.1 | async-start | bytes 6291456 | tf_op jit(solution)/shard_map/all_to_all | solution.py:330
  126.9 19.1 %collective-permute-start.16 = (bf16[32,4224]{1,0:T(8,128)(2,1)S(1)}, bf16[32,4224]{1,0:T(8,128)(2,1)S(1)}, u32[]{:S(2)}, u32[]{:S(2)}) collective-permute-start(bf16[32,4224]{1,0:T(8,128)(2,1)S(1)} %copy-done.6), channel_id=1, source_target_pairs={{0,3},{1,2},{2,1},{3,0},{4,7},{5,6},{6,5},{7,4},{8,11},{9,10},{10,... | collective-permute-start | bytes 811016 | tf_op jit(solution)/shard_map/ppermute | solution.py:38
  127.2 27.8 %collective-permute-start.15 = (bf16[32,4224]{1,0:T(8,128)(2,1)S(1)}, bf16[32,4224]{1,0:T(8,128)(2,1)S(1)}, u32[]{:S(2)}, u32[]{:S(2)}) collective-permute-start(bf16[32,4224]{1,0:T(8,128)(2,1)S(1)} %copy-done.6), channel_id=1, source_target_pairs={{0,2},{1,3},{2,0},{3,1},{4,6},{5,7},{6,4},{7,5},{8,10},{9,11},{10,... | collective-permute-start | bytes 811016 | tf_op jit(solution)/shard_map/ppermute | solution.py:38
  127.2 27.8 %collective-permute-start.14 = (bf16[32,4224]{1,0:T(8,128)(2,1)S(1)}, bf16[32,4224]{1,0:T(8,128)(2,1)S(1)}, u32[]{:S(2)}, u32[]{:S(2)}) collective-permute-start(bf16[32,4224]{1,0:T(8,128)(2,1)S(1)} %copy-done.6), channel_id=1, source_target_pairs={{0,1},{1,0},{2,3},{3,2},{4,5},{5,4},{6,7},{7,6},{8,9},{9,8},{10,11... | collective-permute-start | bytes 811016 | tf_op jit(solution)/shard_map/ppermute | solution.py:38
  129.6 34.9 %collective-permute-start.13 = (bf16[48,4096]{1,0:T(8,128)(2,1)}, bf16[48,4096]{1,0:T(8,128)(2,1)S(1)}, u32[]{:S(2)}, u32[]{:S(2)}) collective-permute-start(bf16[48,4096]{1,0:T(8,128)(2,1)} %get-tuple-element.81), channel_id=1, source_target_pairs={{0,3},{1,2},{2,1},{3,0},{4,7},{5,6},{6,5},{7,4},{8,11},{9,10},{10,... | collective-permute-start | bytes 1179656 | tf_op jit(solution)/shard_map/ppermute | solution.py:38
  146.1 8.9 %copy-start.18 = (bf16[32,4224]{1,0:T(8,128)(2,1)}, bf16[32,4224]{1,0:T(8,128)(2,1)S(1)}, u32[]{:S(2)}) copy-start(bf16[32,4224]{1,0:T(8,128)(2,1)S(1)} %collective-permute-done.16.refs_3_.refs_7_) | copy-start | bytes 811012
  165.8 40.2 %all-to-all-start.2 = ((bf16[8,48,4096]{2,1,0:T(8,128)(2,1)}), bf16[8,48,4096]{2,1,0:T(8,128)(2,1)S(1)}, u32[]{:S(2)}, u32[]{:S(2)}) async-start(bf16[8,48,4096]{2,1,0:T(8,128)(2,1)} %bitcast.24), calls=%async_computation.2 | async-start | bytes 6291456 | tf_op jit(solution)/shard_map/all_to_all | solution.py:330
  170.2 19.5 %collective-permute-start.17 = (bf16[48,4096]{1,0:T(8,128)(2,1)S(1)}, bf16[48,4096]{1,0:T(8,128)(2,1)}, u32[]{:S(2)}, u32[]{:S(2)}) collective-permute-start(bf16[48,4096]{1,0:T(8,128)(2,1)S(1)} %copy-done.11), channel_id=1, source_target_pairs={{0,3},{1,2},{2,1},{3,0},{4,7},{5,6},{6,5},{7,4},{8,11},{9,10},{10,... | collective-permute-start | bytes 1179656 | tf_op jit(solution)/shard_map/ppermute | solution.py:38
  207.7 42.7 %all-to-all-start.3 = ((bf16[8,48,4096]{2,1,0:T(8,128)(2,1)}), bf16[8,48,4096]{2,1,0:T(8,128)(2,1)S(1)}, u32[]{:S(2)}, u32[]{:S(2)}) async-start(bf16[8,48,4096]{2,1,0:T(8,128)(2,1)} %bitcast.17), calls=%async_computation.3 | async-start | bytes 6291456 | tf_op jit(solution)/shard_map/all_to_all | solution.py:330
  213.4 34.0 %collective-permute-start.21 = (bf16[96,4096]{1,0:T(8,128)(2,1)}, bf16[96,4096]{1,0:T(8,128)(2,1)}, u32[]{:S(2)}, u32[]{:S(2)}) collective-permute-start(bf16[96,4096]{1,0:T(8,128)(2,1)} %get-tuple-element.101), channel_id=1, source_target_pairs={{0,1},{1,0},{2,3},{3,2},{4,5},{5,4},{6,7},{7,6},{8,9},{9,8},{10,11... | collective-permute-start | bytes 2359304 | tf_op jit(solution)/shard_map/ppermute | solution.py:38
  213.4 37.1 %collective-permute-start.22 = (bf16[96,4096]{1,0:T(8,128)(2,1)}, bf16[96,4096]{1,0:T(8,128)(2,1)}, u32[]{:S(2)}, u32[]{:S(2)}) collective-permute-start(bf16[96,4096]{1,0:T(8,128)(2,1)} %get-tuple-element.102), channel_id=1, source_target_pairs={{0,2},{1,3},{2,0},{3,1},{4,6},{5,7},{6,4},{7,5},{8,10},{9,11},{10,... | collective-permute-start | bytes 2359304 | tf_op jit(solution)/shard_map/ppermute | solution.py:38
  252.1 47.3 %all-to-all-start.4 = ((bf16[8,48,4096]{2,1,0:T(8,128)(2,1)}), bf16[8,48,4096]{2,1,0:T(8,128)(2,1)S(1)}, u32[]{:S(2)}, u32[]{:S(2)}) async-start(bf16[8,48,4096]{2,1,0:T(8,128)(2,1)} %bitcast.16), calls=%async_computation.4 | async-start | bytes 6291456 | tf_op jit(solution)/shard_map/all_to_all | solution.py:330
  257.1 42.3 %collective-permute-start.26 = (bf16[48,4096]{1,0:T(8,128)(2,1)S(1)}, bf16[48,4096]{1,0:T(8,128)(2,1)}, u32[]{:S(2)}, u32[]{:S(2)}) collective-permute-start(bf16[48,4096]{1,0:T(8,128)(2,1)S(1)} %copy-done.12), channel_id=1, source_target_pairs={{0,3},{1,2},{2,1},{3,0},{4,7},{5,6},{6,5},{7,4},{8,11},{9,10},{10,... | collective-permute-start | bytes 1179656 | tf_op jit(solution)/shard_map/ppermute | solution.py:38
  262.1 13.5 %collective-permute-start.18 = (bf16[32,4096]{1,0:T(8,128)(2,1)}, bf16[32,4096]{1,0:T(8,128)(2,1)S(1)}, u32[]{:S(2)}, u32[]{:S(2)}) collective-permute-start(bf16[32,4096]{1,0:T(8,128)(2,1)} %get-tuple-element.95), channel_id=1, source_target_pairs={{0,1},{1,0},{2,3},{3,2},{4,5},{5,4},{6,7},{7,6},{8,9},{9,8},{10,11... | collective-permute-start | bytes 786440 | tf_op jit(solution)/shard_map/ppermute | solution.py:38
  265.0 26.6 %collective-permute-start.19 = (bf16[32,4096]{1,0:T(8,128)(2,1)}, bf16[32,4096]{1,0:T(8,128)(2,1)S(1)}, u32[]{:S(2)}, u32[]{:S(2)}) collective-permute-start(bf16[32,4096]{1,0:T(8,128)(2,1)} %get-tuple-element.96), channel_id=1, source_target_pairs={{0,2},{1,3},{2,0},{3,1},{4,6},{5,7},{6,4},{7,5},{8,10},{9,11},{10,... | collective-permute-start | bytes 786440 | tf_op jit(solution)/shard_map/ppermute | solution.py:38
  265.0 33.7 %collective-permute-start.20 = (bf16[32,4096]{1,0:T(8,128)(2,1)}, bf16[32,4096]{1,0:T(8,128)(2,1)S(1)}, u32[]{:S(2)}, u32[]{:S(2)}) collective-permute-start(bf16[32,4096]{1,0:T(8,128)(2,1)} %get-tuple-element.97), channel_id=1, source_target_pairs={{0,3},{1,2},{2,1},{3,0},{4,7},{5,6},{6,5},{7,4},{8,11},{9,10},{10,... | collective-permute-start | bytes 786440 | tf_op jit(solution)/shard_map/ppermute | solution.py:38
  275.7 23.1 %copy-start.31 = (bf16[32,4096]{1,0:T(8,128)(2,1)}, bf16[32,4096]{1,0:T(8,128)(2,1)S(1)}, u32[]{:S(2)}) copy-start(bf16[32,4096]{1,0:T(8,128)(2,1)S(1)} %collective-permute-done.18) | copy-start | bytes 786436
  291.5 7.2 %copy-start.32 = (bf16[32,4096]{1,0:T(8,128)(2,1)}, bf16[32,4096]{1,0:T(8,128)(2,1)S(1)}, u32[]{:S(2)}) copy-start(bf16[32,4096]{1,0:T(8,128)(2,1)S(1)} %collective-permute-done.19) | copy-start | bytes 786436
  301.1 58.4 %all-to-all-start.5 = ((bf16[8,48,4096]{2,1,0:T(8,128)(2,1)}), bf16[8,48,4096]{2,1,0:T(8,128)(2,1)S(1)}, u32[]{:S(2)}, u32[]{:S(2)}) async-start(bf16[8,48,4096]{2,1,0:T(8,128)(2,1)} %bitcast.18), calls=%async_computation.5 | async-start | bytes 6291456 | tf_op jit(solution)/shard_map/all_to_all | solution.py:330
  305.8 7.2 %copy-start.7 = (bf16[48,4096]{1,0:T(8,128)(2,1)S(1)}, bf16[48,4096]{1,0:T(8,128)(2,1)}, u32[]{:S(2)}) copy-start(bf16[48,4096]{1,0:T(8,128)(2,1)} %get-tuple-element.115) | copy-start | bytes 1179652
  310.3 11.1 %collective-permute-start.23 = (bf16[32,4096]{1,0:T(8,128)(2,1)}, bf16[32,4096]{1,0:T(8,128)(2,1)S(1)}, u32[]{:S(2)}, u32[]{:S(2)}) collective-permute-start(bf16[32,4096]{1,0:T(8,128)(2,1)} %get-tuple-element.105), channel_id=1, source_target_pairs={{0,1},{1,0},{2,3},{3,2},{4,5},{5,4},{6,7},{7,6},{8,9},{9,8},{10,11... | collective-permute-start | bytes 786440 | tf_op jit(solution)/shard_map/ppermute | solution.py:38
  310.3 14.2 %collective-permute-start.24 = (bf16[32,4096]{1,0:T(8,128)(2,1)}, bf16[32,4096]{1,0:T(8,128)(2,1)S(1)}, u32[]{:S(2)}, u32[]{:S(2)}) collective-permute-start(bf16[32,4096]{1,0:T(8,128)(2,1)} %get-tuple-element.106), channel_id=1, source_target_pairs={{0,2},{1,3},{2,0},{3,1},{4,6},{5,7},{6,4},{7,5},{8,10},{9,11},{10,... | collective-permute-start | bytes 786440 | tf_op jit(solution)/shard_map/ppermute | solution.py:38
  312.1 32.4 %collective-permute-start.25 = (bf16[32,4096]{1,0:T(8,128)(2,1)}, bf16[32,4096]{1,0:T(8,128)(2,1)S(1)}, u32[]{:S(2)}, u32[]{:S(2)}) collective-permute-start(bf16[32,4096]{1,0:T(8,128)(2,1)} %get-tuple-element.107), channel_id=1, source_target_pairs={{0,3},{1,2},{2,1},{3,0},{4,7},{5,6},{6,5},{7,4},{8,11},{9,10},{10,... | collective-permute-start | bytes 786440 | tf_op jit(solution)/shard_map/ppermute | solution.py:38
  312.9 40.1 %collective-permute-start.27 = (bf16[48,4096]{1,0:T(8,128)(2,1)S(1)}, bf16[48,4096]{1,0:T(8,128)(2,1)S(1)}, u32[]{:S(2)}, u32[]{:S(2)}) collective-permute-start(bf16[48,4096]{1,0:T(8,128)(2,1)S(1)} %copy-done.7), channel_id=1, source_target_pairs={{0,3},{1,2},{2,1},{3,0},{4,7},{5,6},{6,5},{7,4},{8,11},{9,10},{10,... | collective-permute-start | bytes 1179656 | tf_op jit(solution)/shard_map/ppermute | solution.py:38
  321.3 32.4 %copy-start.25 = (bf16[32,4096]{1,0:T(8,128)(2,1)}, bf16[32,4096]{1,0:T(8,128)(2,1)S(1)}, u32[]{:S(2)}) copy-start(bf16[32,4096]{1,0:T(8,128)(2,1)S(1)} %collective-permute-done.23) | copy-start | bytes 786436
  324.4 29.3 %copy-start.27 = (bf16[32,4096]{1,0:T(8,128)(2,1)}, bf16[32,4096]{1,0:T(8,128)(2,1)S(1)}, u32[]{:S(2)}) copy-start(bf16[32,4096]{1,0:T(8,128)(2,1)S(1)} %collective-permute-done.24) | copy-start | bytes 786436
  344.6 9.2 %copy-start.29 = (bf16[32,4096]{1,0:T(8,128)(2,1)}, bf16[32,4096]{1,0:T(8,128)(2,1)S(1)}, u32[]{:S(2)}) copy-start(bf16[32,4096]{1,0:T(8,128)(2,1)S(1)} %collective-permute-done.25) | copy-start | bytes 786436
  361.1 7.2 %copy-start.22 = (f32[32,4096]{1,0:T(8,128)S(1)}, f32[32,4096]{1,0:T(8,128)}, u32[]{:S(2)}) copy-start(f32[32,4096]{1,0:T(8,128)} %get-tuple-element.104) | copy-start | bytes 1572868
  361.1 7.2 %copy-start.26 = (bf16[32,4096]{1,0:T(8,128)(2,1)S(1)}, bf16[32,4096]{1,0:T(8,128)(2,1)}, u32[]{:S(2)}) copy-start(bf16[32,4096]{1,0:T(8,128)(2,1)} %copy-done.25) | copy-start | bytes 786436
  361.1 7.2 %copy-start.28 = (bf16[32,4096]{1,0:T(8,128)(2,1)S(1)}, bf16[32,4096]{1,0:T(8,128)(2,1)}, u32[]{:S(2)}) copy-start(bf16[32,4096]{1,0:T(8,128)(2,1)} %copy-done.27) | copy-start | bytes 786436
  361.1 7.2 %copy-start.30 = (bf16[32,4096]{1,0:T(8,128)(2,1)S(1)}, bf16[32,4096]{1,0:T(8,128)(2,1)}, u32[]{:S(2)}) copy-start(bf16[32,4096]{1,0:T(8,128)(2,1)} %copy-done.29) | copy-start | bytes 786436
  365.6 8.9 %collective-permute-start.28 = (bf16[32,4096]{1,0:T(8,128)(2,1)}, bf16[32,4096]{1,0:T(8,128)(2,1)S(1)}, u32[]{:S(2)}, u32[]{:S(2)}) collective-permute-start(bf16[32,4096]{1,0:T(8,128)(2,1)} %get-tuple-element.122), channel_id=1, source_target_pairs={{0,1},{1,0},{2,3},{3,2},{4,5},{5,4},{6,7},{7,6},{8,9},{9,8},{10,11... | collective-permute-start | bytes 786440 | tf_op jit(solution)/shard_map/ppermute | solution.py:38
  365.6 12.9 %collective-permute-start.29 = (bf16[32,4096]{1,0:T(8,128)(2,1)}, bf16[32,4096]{1,0:T(8,128)(2,1)S(1)}, u32[]{:S(2)}, u32[]{:S(2)}) collective-permute-start(bf16[32,4096]{1,0:T(8,128)(2,1)} %get-tuple-element.123), channel_id=1, source_target_pairs={{0,2},{1,3},{2,0},{3,1},{4,6},{5,7},{6,4},{7,5},{8,10},{9,11},{10,... | collective-permute-start | bytes 786440 | tf_op jit(solution)/shard_map/ppermute | solution.py:38
  367.5 22.8 %collective-permute-start.30 = (bf16[32,4096]{1,0:T(8,128)(2,1)}, bf16[32,4096]{1,0:T(8,128)(2,1)S(1)}, u32[]{:S(2)}, u32[]{:S(2)}) collective-permute-start(bf16[32,4096]{1,0:T(8,128)(2,1)} %get-tuple-element.124), channel_id=1, source_target_pairs={{0,3},{1,2},{2,1},{3,0},{4,7},{5,6},{6,5},{7,4},{8,11},{9,10},{10,... | collective-permute-start | bytes 786440 | tf_op jit(solution)/shard_map/ppermute | solution.py:38
  368.3 22.0 %copy-start.23 = (f32[32,4096]{1,0:T(8,128)S(1)}, f32[32,4096]{1,0:T(8,128)}, u32[]{:S(2)}) copy-start(f32[32,4096]{1,0:T(8,128)} %get-tuple-element.121) | copy-start | bytes 1572868
  369.8 20.7 %copy-start.3 = (f32[128,2048]{1,0:T(8,128)S(1)}, f32[128,2048]{1,0:T(8,128)}, u32[]{:S(2)}) copy-start(f32[128,2048]{1,0:T(8,128)} %get-tuple-element.129) | copy-start | bytes 3145732
  369.8 20.7 %collective-permute-start.31 = (bf16[128,2048]{1,0:T(8,128)(2,1)}, bf16[128,2048]{1,0:T(8,128)(2,1)S(1)}, u32[]{:S(2)}, u32[]{:S(2)}) collective-permute-start(bf16[128,2048]{1,0:T(8,128)(2,1)} %get-tuple-element.130), channel_id=1, source_target_pairs={{0,16},{4,20},{8,24},{12,28},{16,0},{20,4},{24,8},{28,12},{1,17},{... | collective-permute-start | bytes 1572872 | tf_op jit(solution)/shard_map/ppermute | solution.py:38
  370.8 20.7 %collective-permute-start.34 = (bf16[128,2048]{1,0:T(8,128)(2,1)}, bf16[128,2048]{1,0:T(8,128)(2,1)S(1)}, u32[]{:S(2)}, u32[]{:S(2)}) collective-permute-start(bf16[128,2048]{1,0:T(8,128)(2,1)} %get-tuple-element.132), channel_id=1, source_target_pairs={{0,8},{4,12},{8,0},{12,4},{16,24},{20,28},{24,16},{28,20},{1,9},{5... | collective-permute-start | bytes 1572872 | tf_op jit(solution)/shard_map/ppermute | solution.py:38
  390.6 5.3 %collective-permute-start.32 = (bf16[64,2048]{1,0:T(8,128)(2,1)S(1)}, bf16[64,2048]{1,0:T(8,128)(2,1)S(1)}, u32[]{:S(2)}, u32[]{:S(2)}) collective-permute-start(bf16[64,2048]{1,0:T(8,128)(2,1)S(1)} %split.77), channel_id=1, source_target_pairs={{0,8},{4,12},{8,0},{12,4},{16,24},{20,28},{24,16},{28,20},{1,9},{5... | collective-permute-start | bytes 786440 | tf_op jit(solution)/shard_map/ppermute | solution.py:38
  391.7 7.8 %collective-permute-start.35 = (bf16[64,2048]{1,0:T(8,128)(2,1)S(1)}, bf16[64,2048]{1,0:T(8,128)(2,1)S(1)}, u32[]{:S(2)}, u32[]{:S(2)}) collective-permute-start(bf16[64,2048]{1,0:T(8,128)(2,1)S(1)} %split.76), channel_id=1, source_target_pairs={{0,16},{4,20},{8,24},{12,28},{16,0},{20,4},{24,8},{28,12},{1,17},{... | collective-permute-start | bytes 786440 | tf_op jit(solution)/shard_map/ppermute | solution.py:38
  396.0 5.1 %collective-permute-start.33 = (bf16[32,2048]{1,0:T(8,128)(2,1)S(1)}, bf16[32,2048]{1,0:T(8,128)(2,1)S(1)}, u32[]{:S(2)}, u32[]{:S(2)}) collective-permute-start(bf16[32,2048]{1,0:T(8,128)(2,1)S(1)} %split.79), channel_id=1, source_target_pairs={{0,4},{4,0},{8,12},{12,8},{16,20},{20,16},{24,28},{28,24},{1,5},{5... | collective-permute-start | bytes 393224 | tf_op jit(solution)/shard_map/ppermute | solution.py:38
  399.6 2.5 collective-permute-start.36
  (16 other events, 34.9 us)

commit v4 on v3

--- a/solution.py
+++ b/solution.py
@@ -47,6 +47,13 @@
     return bits[:1] + bits[:0:-1] if last_first else bits
 
 
+def chain_step(arrays, axis, step):
+    size = lax.axis_size(axis)
+    rightward = [(i, i + 1) for i in range(step - 1, size - 1)]
+    leftward = [(size - 1 - i, size - 2 - i) for i in range(step - 1, size - 1)]
+    return [lax.ppermute(a, axis, way) for a, way in zip(arrays, (rightward, leftward))]
+
+
 def gather_doubling(array, axis, bits):
     for bit in bits:
         array = jnp.concatenate([array, swap(array, axis, bit)])
@@ -74,10 +81,10 @@
     return jnp.asarray((same & (at[None, :] < at[:, None])).astype(np.float32), BF16)
 
 
-def choose(table, lane, own, turn, before):
+def choose(table, lane, row_group, slot_group, turn, before):
     select = lax.broadcasted_iota(I32, (table.shape[1], lane.shape[1]), 0) == lane
     weight = jnp.dot(table, select.astype(BF16), preferred_element_type=F32)
-    mask = jnp.where(weight > 0, own.astype(F32), 0.0)
+    mask = jnp.where((weight > 0) & (row_group == slot_group), 1.0, 0.0)
     rank = jnp.dot(before, mask.astype(BF16), preferred_element_type=F32)
     place = jnp.where(rank == turn, mask, 0.0)
     return place.astype(BF16), (place * weight).astype(BF16)
@@ -92,12 +99,15 @@
 def pick_kernel(count, *refs):
     parts, refs = refs[:count], refs[count:]
     tables, refs = refs[:count], refs[count:]
-    lane, own, turn, before, out, mixing, place = refs
+    lane, row_group, slot_group, turn, before, order, out, mixing, place = refs
 
     @pl.when(pl.program_id(0) == 0)
     def _():
         table = jnp.concatenate([t[...] for t in tables])
-        place[...], mixing[...] = choose(table, lane[...], own[...], turn[...], before[...])
+        place[...], weights = choose(
+            table, lane[...], row_group[...], slot_group[...], turn[...], before[...]
+        )
+        mixing[...] = jnp.dot(order[...], weights, preferred_element_type=F32).astype(BF16)
 
     out[...] = gather_rows(place[...], jnp.concatenate([p[...] for p in parts]))
 
@@ -106,25 +116,24 @@
     return pl.BlockSpec(array.shape, lambda j: (0,) * array.ndim)
 
 
-def pick(parts, lane, own, turn, features):
+def pick(parts, block, lane, row_group, slot_group, turn, order, features):
     slots = lane.shape[1]
     rows = len(parts) * BLOCK_TOK
     tile = features // TILES
-    before = below(rows)
-    small = (lane, own, turn, before)
+    small = (lane, row_group, slot_group, turn, below(rows), order)
     return pl.pallas_call(
         functools.partial(pick_kernel, len(parts)),
         grid=(TILES,),
         out_shape=[
             jax.ShapeDtypeStruct((slots, features), BF16),
-            jax.ShapeDtypeStruct((rows, slots), BF16),
+            jax.ShapeDtypeStruct((order.shape[0], slots), BF16),
         ],
-        in_specs=[pl.BlockSpec((BLOCK_TOK, tile), lambda j: (0, j))] * len(parts)
-        + [pl.BlockSpec((BLOCK_TOK, LANES), lambda j: (0, features // LANES))] * len(parts)
+        in_specs=[pl.BlockSpec((BLOCK_TOK, tile), lambda j: (block, j))] * len(parts)
+        + [pl.BlockSpec((BLOCK_TOK, LANES), lambda j: (block, features // LANES))] * len(parts)
         + [whole_block(a) for a in small],
         out_specs=[
             pl.BlockSpec((slots, tile), lambda j: (0, j)),
-            pl.BlockSpec((rows, slots), lambda j: (0, 0)),
+            pl.BlockSpec((order.shape[0], slots), lambda j: (0, 0)),
         ],
         scratch_shapes=[pltpu.VMEM((rows, slots), BF16)],
         compiler_params=PARAMS,
@@ -136,30 +145,32 @@
     )(*parts, *parts, *small)
 
 
-def pick_cross_kernel(order, cuts, a_ref, b_ref, table, lane, own_a, own_b, turn, before, *refs):
-    outs, (mixing_a, mixing_b, place_a, place_b) = refs[:-4], refs[-4:]
+def pick_cross_kernel(order, cuts, a0, a1, b0, b1, t0, t1, *refs):
+    lane, group_a, group_b, slot_group, turn, before = refs[:6]
+    outs, (mixing_a, mixing_b, place_a, place_b) = refs[6:-4], refs[-4:]
     step = pl.program_id(0)
 
     @pl.when(step == 0)
     def _():
-        known = table[...]
-        place_b[...], mixing_b[...] = choose(known, lane[...], own_b[...], turn[...], before[...])
+        known = jnp.concatenate([t0[...], t1[...]])
+        common = slot_group[...], turn[...], before[...]
+        place_b[...], mixing_b[...] = choose(known, lane[...], group_b[...], *common)
         back = [order.index(k) * BLOCK_TOK for k in range(len(order))]
         known = jnp.concatenate([known[at : at + BLOCK_TOK] for at in back])
-        place_a[...], mixing_a[...] = choose(known, lane[...], own_a[...], turn[...], before[...])
-
-    def store(place, rows):
-        result = gather_rows(place, rows)
+        place_a[...], mixing_a[...] = choose(known, lane[...], group_a[...], *common)
+
+    def store(place, first_rows, last_rows):
+        result = gather_rows(place[...], jnp.concatenate([first_rows[...], last_rows[...]]))
         for out, first, last in zip(outs, cuts[:-1], cuts[1:]):
             out[...] = result[first:last]
 
     @pl.when(step < TILES // 2)
     def _():
-        store(place_a[...], a_ref[...])
+        store(place_a, a0, a1)
 
     @pl.when(step >= TILES // 2)
     def _():
-        store(place_b[...], b_ref[...])
+        store(place_b, b0, b1)
 
 
 def in_first_half(shape):
@@ -170,22 +181,21 @@
     return pl.BlockSpec(shape, lambda j: (0, jnp.maximum(j - TILES // 2, 0)))
 
 
-def pick_cross(rows_a, rows_b, order_b, lane, own_a, own_b, turn, features, cuts):
+def pick_cross(rows_a, rows_b, order_b, lane, group_a, group_b, slot_group, turn, features, cuts):
     slots = lane.shape[1]
-    rows = rows_a.shape[0]
+    part = rows_a[0].shape[0]
+    rows = 2 * part
     tile = features // TILES
-    small = (lane, own_a, own_b, turn, below(rows))
+    small = (lane, group_a, group_b, slot_group, turn, below(rows))
     sizes = [last - first for first, last in zip(cuts[:-1], cuts[1:])]
     results = pl.pallas_call(
         functools.partial(pick_cross_kernel, order_b, cuts),
         grid=(TILES,),
         out_shape=[jax.ShapeDtypeStruct((size, features), BF16) for size in sizes]
         + [jax.ShapeDtypeStruct((rows, slots), BF16)] * 2,
-        in_specs=[
-            in_first_half((rows, tile)),
-            in_second_half((rows, tile)),
-            pl.BlockSpec((rows, LANES), lambda j: (0, features // 2 // LANES)),
-        ]
+        in_specs=[in_first_half((part, tile))] * 2
+        + [in_second_half((part, tile))] * 2
+        + [pl.BlockSpec((part, LANES), lambda j: (0, features // 2 // LANES))] * 2
         + [whole_block(a) for a in small],
         out_specs=[pl.BlockSpec((size, tile), lambda j: (0, j)) for size in sizes]
         + [pl.BlockSpec((rows, slots), lambda j: (0, 0))] * 2,
@@ -196,7 +206,7 @@
             bytes_accessed=2 * (rows + slots) * features,
             transcendentals=0,
         ),
-    )(rows_a, rows_b, rows_b, *small)
+    )(*rows_a, *rows_b, *rows_b, *small)
     return list(results[:-2]), results[-2], results[-1]
 
 
@@ -271,13 +281,16 @@
 
 
 def expert_kernel(count, *refs):
-    parts, (gate_ref, up_ref, down_ref), outs = refs[:count], refs[count : count + 3], refs[count + 3 : -2]
-    x_ref, total = refs[-2:]
+    parts, (gate_ref, up_ref, down_ref) = refs[:count], refs[count : count + 3]
+    outs, (joined, total) = refs[count + 3 : -2], refs[-2:]
     step = pl.program_id(0)
-
-    @pl.when(step == 0)
-    def _():
-        x_ref[...] = jnp.concatenate([part[...] for part in parts])
+    x_ref = parts[0] if count == 1 else joined
+
+    if count > 1:
+
+        @pl.when(step == 0)
+        def _():
+            joined[...] = jnp.concatenate([part[...] for part in parts])
 
     x = x_ref[...]
     gate_pre = jnp.dot(x, gate_ref[...], preferred_element_type=F32)
@@ -316,7 +329,10 @@
             pl.BlockSpec((tile, features), lambda i: (i, 0)),
         ],
         out_specs=[whole_block(part) for part in parts],
-        scratch_shapes=[pltpu.VMEM((rows, features), BF16), pltpu.VMEM((rows, features), F32)],
+        scratch_shapes=[
+            pltpu.VMEM((rows if len(parts) > 1 else 16, features), BF16),
+            pltpu.VMEM((rows, features), F32),
+        ],
         compiler_params=PARAMS,
         cost_estimate=pl.CostEstimate(
             flops=6 * rows * features * hidden,
@@ -326,6 +342,32 @@
     )(*parts, gate_weight, up_weight, down_weight)
 
 
+def prepare_kernel(tokens, gain, routes, gates, placement, *outs):
+    scale = gain[...].astype(F32)
+    chosen = gates[...] / jnp.sum(gates[...], axis=-1, keepdims=True)
+    for block, out in enumerate(outs):
+        at = slice(block * BLOCK_TOK, (block + 1) * BLOCK_TOK)
+        values = tokens[at].astype(F32)
+        rescale = lax.rsqrt(jnp.mean(values * values, axis=-1, keepdims=True) + EPSILON)
+        out[:, : values.shape[1]] = (values * rescale * scale).astype(BF16)
+        table = jnp.zeros((BLOCK_TOK, placement.shape[1]), F32)
+        for k in range(routes.shape[1]):
+            held = routes[at, k : k + 1] == placement[...]
+            table = jnp.where(held, chosen[at, k : k + 1], table)
+        out[:, values.shape[1] :] = table.astype(BF16)
+
+
+def prepare(tokens, norm_gain, routes, route_gates, placement):
+    rows, features = tokens.shape
+    lanes = -(-placement.shape[0] // LANES) * LANES
+    padded = jnp.pad(placement, (0, lanes - placement.shape[0]), constant_values=-1)
+    return pl.pallas_call(
+        prepare_kernel,
+        out_shape=[jax.ShapeDtypeStruct((BLOCK_TOK, features + lanes), BF16)] * (rows // BLOCK_TOK),
+        compiler_params=PARAMS,
+    )(tokens, norm_gain[None], routes, route_gates, padded[None])
+
+
 def to_experts(rows):
     return lax.all_to_all(rows, "node", 0, 0, tiled=True)
 
@@ -340,88 +382,101 @@
     nodes, peers = lax.axis_size("node"), lax.axis_size("local")
     node, local = lax.axis_index("node"), lax.axis_index("local")
     experts = placement.shape[0]
-    tok_rows, features = tokens.shape
-    top_count = routes.shape[1]
-    capacity = BLOCK_TOK * top_count // experts * 3 // 2
+    features = tokens.shape[1]
+    capacity = BLOCK_TOK * routes.shape[1] // experts * 3 // 2
     slots = experts * capacity
     half = features // 2
-    values = tokens.astype(F32)
-    rescale = lax.rsqrt(jnp.mean(values * values, axis=-1, keepdims=True) + EPSILON)
-    normed = (values * rescale * norm_gain.astype(F32)).astype(BF16)
-    combine_weight = (route_gates / jnp.sum(route_gates, axis=-1, keepdims=True)).astype(BF16)
-    held = routes[:, :, None] == placement[None, None, :]
-    table = jnp.sum(jnp.where(held, combine_weight[:, :, None], jnp.zeros((), BF16)), axis=1)
     weights = (gate_weight[0], up_weight[0], down_weight[0])
-    sent = jnp.concatenate([normed, jnp.pad(table, ((0, 0), (0, -experts % LANES)))], axis=1)
-    sent0, sent1, sent2, sent3 = jnp.split(sent, tok_rows // BLOCK_TOK)
+    sent0, sent1, sent2, sent3 = prepare(tokens, norm_gain, routes, route_gates, placement)
 
     bits_a, bits_b = bit_order(nodes, False), bit_order(nodes, True)
     order_a, order_b = gathered_from(bits_a), gathered_from(bits_b)
     slot = np.arange(slots)
     turn = jnp.asarray(slot[None, :] % capacity, F32)
-    near_group = slot // capacity % peers
+    near_group = jnp.asarray(slot[None, :] // capacity % peers, I32)
     near_lane = jnp.asarray(slot[None, :] // (capacity * peers) * peers, I32) + local
-    near_own = (np.arange(peers * BLOCK_TOK)[:, None] // BLOCK_TOK == near_group).astype(np.float32)
-    near_own = jnp.asarray(near_own, BF16)
-    cross_group = slot // capacity % nodes
+    cross_group = jnp.asarray(slot[None, :] // capacity % nodes, I32)
     cross_lane = (jnp.asarray(slot[None, :] // (capacity * nodes), I32) ^ local) + node * peers
-    cross_own = [
-        jnp.asarray((np.repeat(order, BLOCK_TOK)[:, None] == cross_group).astype(np.float32), BF16)
-        for order in (order_a, order_b)
-    ]
-    cuts = [slots // peers * k for k in range(peers)] + [slots - slots // peers // 2, slots]
-
-    def gather(rows, first, last):
-        return swaps([rows] * peers, "local", first, last)
-
-    def pick_near(rows, near):
-        return pick([rows] + near, near_lane, near_own, turn, features)
-
-    near0 = gather(sent0, 1, peers)
+
+    def by_token(groups):
+        return jnp.repeat(jnp.asarray(groups, I32), BLOCK_TOK)[:, None]
+
+    bits = by_token(np.arange(peers))
+    steps = np.array([0] + [s for d in range(1, peers) for s in (-d, d)])
+    source = local + jnp.asarray(steps, I32)
+    chain_bits = by_token(jnp.where((source >= 0) & (source < peers), source ^ local, -1))
+    within = np.arange(peers * BLOCK_TOK)[:, None] % BLOCK_TOK
+    chain_within = np.arange(len(steps) * BLOCK_TOK)[None, :] % BLOCK_TOK
+    chain_order = (bits == chain_bits.T) & jnp.asarray(within == chain_within)
+    chain_order = chain_order.astype(BF16)
+    same_order = jnp.asarray(np.eye(peers * BLOCK_TOK, dtype=np.float32), BF16)
+    size = slots // peers
+    cuts = [size * k for k in range(peers - 1)]
+    cuts += [cuts[-1] + size * 2 // 3, size * (peers - 1), slots - size // 3, slots]
+
+    near0 = swaps([sent0] * peers, "local", 1, peers)
     pair = jnp.concatenate([sent3, swap(sent3, "node", bits_a[0])])
-    rows_a = gather_doubling(pair[:, :half], "node", bits_a[1:])
-    rows_b = gather_doubling(pair[:, half:], "node", bits_b[1:])
-    (sent1,) = fence([sent1], near0 + [rows_a, rows_b])
-    near1 = gather(sent1, 1, peers - 1)
-    outbound0, mixing0 = pick_near(sent0, near0)
-
-    outbound0, sent1, rows_a, rows_b = fence([outbound0, sent1, rows_a, rows_b], near1)
+    rows_a = gather_doubling(pair[:, :half], "node", bits_a[1:-1])
+    rows_b = gather_doubling(pair[:, half:], "node", bits_b[1:-1])
+    rows_a = [rows_a, swap(rows_a, "node", bits_a[-1])]
+    rows_b = [rows_b, swap(rows_b, "node", bits_b[-1])]
+    sent12 = jnp.concatenate([sent1, sent2])
+    (sent12,) = fence([sent12], near0 + [rows_a[1], rows_b[1]])
+    chain = chain_step([sent12, sent12], "local", 1)
+    outbound0, mixing0 = pick(
+        [sent0] + near0, 0, near_lane, bits, near_group, turn, same_order, features
+    )
+
+    outbound0, *last_rows = fence([outbound0, rows_a[1], rows_b[1]], chain)
     arrived0 = to_experts(outbound0)
-    near1 += gather(sent1, peers - 1, peers)
+    parts12 = [sent12] + chain
+    for step in range(2, peers):
+        chain = chain_step(chain, "local", step)
+        parts12 += chain
     outbound3, mixing3a, mixing3b = pick_cross(
-        rows_a, rows_b, order_b, cross_lane, *cross_own, turn, features, cuts
+        [rows_a[0], last_rows[0]],
+        [rows_b[0], last_rows[1]],
+        order_b,
+        cross_lane,
+        by_token(order_a),
+        by_token(order_b),
+        cross_group,
+        turn,
+        features,
+        cuts,
     )
     arrived3 = outbound3[:1] + swaps(outbound3, "local", 1, peers - 1)
-    outbound1, mixing1 = pick_near(sent1, near1)
-
-    outbound1, sent2, first3, last3 = fence(
-        [outbound1, sent2] + outbound3[-2:], [arrived0] + arrived3[1:]
+    outbound1, mixing1 = pick(
+        parts12, 0, near_lane, chain_bits, near_group, turn, chain_order, features
     )
+
+    outbound1, *later3 = fence([outbound1] + outbound3[-3:], arrived3[1:])
     arrived1 = to_experts(outbound1)
-    near2 = gather(sent2, 1, peers)
-    arrived3.append(swap(first3, "local", peers - 1))
+    outbound2, mixing2 = pick(
+        parts12, 1, near_lane, chain_bits, near_group, turn, chain_order, features
+    )
+    arrived3.append(swap(later3[0], "local", peers - 2))
+    arrived3 += [swap(part, "local", peers - 1) for part in later3[1:]]
     (out0,) = expert([arrived0], *weights)
-    outbound2, mixing2 = pick_near(sent2, near2)
-
-    outbound2, last3 = fence([outbound2, last3], [arrived1, out0, arrived3[-1]])
+
+    (outbound2,) = fence([outbound2], [out0])
     arrived2 = to_experts(outbound2)
-    arrived3.append(swap(last3, "local", peers - 1))
+    out3 = list(expert(arrived3, *weights))
     (out1,) = expert([arrived1], *weights)
-    arrived3[-1], = fence([arrived3[-1]], [out1])
-    out3 = list(expert(arrived3, *weights))
-
-    out0, *out3 = fence([out0] + out3, [arrived2, out1])
+
+    out0, *out3 = fence([out0] + out3, [out1])
     landed0 = to_experts(out0)
     landed3 = out3[:1] + swaps(out3, "local", 1, peers - 1)
+    landed3.append(swap(out3[-3], "local", peers - 2))
     (out2,) = expert([arrived2], *weights)
 
-    out1, first3, last3 = fence([out1] + out3[-2:], [landed0, out2] + landed3[1:])
+    out1, *later3 = fence([out1] + out3[-2:], [out2] + landed3[1:])
     landed1 = to_experts(out1)
-    landed3.append(swap(first3, "local", peers - 1))
+    landed3.append(swap(later3[0], "local", peers - 1))
     sum0, parts0 = mix(mixing0, landed0)
     parts0 = swaps(parts0, "local", 1, peers)
 
-    out2, last3 = fence([out2, last3], [landed1, landed3[-1]] + parts0)
+    out2, last3 = fence([out2, later3[1]], [landed3[-1]] + parts0)
     landed2 = to_experts(out2)
     landed3.append(swap(last3, "local", peers - 1))
     sum1, parts1 = mix(mixing1, landed1)
@@ -429,7 +484,7 @@
     piece0 = total(sum0, parts0)
     cross = mix_cross(mixing3a, mixing3b, landed3)
 
-    landed2, *cross = fence([landed2] + list(cross), parts1)
+    (mixing2,) = fence([mixing2], [cross[1], cross[3]])
     sum2, parts2 = mix(mixing2, landed2)
     cross = fence(list(cross), parts2[1:])
     parts2 = swaps(parts2, "local", 1, peers)

time: 405 us -> 452 us (1.12)
  starting transfers between devices: 72.3 us -> 92.9 us
  waiting for transfers between devices: 192 us -> 210 us
  local copies, waits for them, and re-layouts: 6.78 us -> 22.2 us
  other arithmetic: 26.6 us -> 16 us
    ppermute x37 -> x33, waiting for transfers between devices: 192 us -> 170 us  [swap(): return lax.ppermute(array, axis, [(i, i ^ bits) for i in range(size)])]
    all_to_all x6, waiting for transfers between devices: 0.02 us -> 20.5 us  [to_experts(): return lax.all_to_all(rows, 'node', 0, 0, tiled=True)]
    ppermute x0 -> x6, waiting for transfers between devices: none -> 19.3 us  [chain_step(): lax.ppermute(a, axis, way)]
    ppermute x0 -> x6, starting transfers between devices: none -> 14.4 us  [chain_step(): lax.ppermute(a, axis, way)]
    unnamed x74 -> x85, local copies, waits for them, and re-layouts: 5.65 us -> 16.2 us
    add x9 -> x7, other arithmetic: 11 us -> 6.4 us  [fence(): token = sum((a[:16, :LANES].astype(F32) for a in after))]
    ppermute x37 -> x33, starting transfers between devices: 41.5 us -> 45.4 us  [swap(): return lax.ppermute(array, axis, [(i, i ^ bits) for i in range(size)])]
  transfers between devices with their start and end apart: 43 -> 45, of which waited for: 23 -> 27; matrix products, arithmetic and copies ran while one was open for 3% -> 4% of each run, Pallas kernels for 25% -> 23%
where the time goes in v4:
time: 452 us; the launch traced here: 450 us
  waiting for transfers between devices  210 us (46%)
  Pallas kernels  108 us (24%)
  starting transfers between devices  92.9 us (21%)
  local copies, waits for them, and re-layouts  22.2 us (5%)
  other arithmetic  16 us (4%)
    ppermute x33, waiting for transfers between devices, swap(): return lax.ppermute(array, axis, [(i, i ^ bits) for i in range(size)])  170 us
    pallas_call x4, Pallas kernels, expert(): pl.pallas_call(functools.partial(expert_kernel, len(parts)), grid=(hidden...  64.6 us
    ppermute x33, starting transfers between devices, swap(): return lax.ppermute(array, axis, [(i, i ^ bits) for i in range(size)])  45.4 us
    all_to_all x6, starting transfers between devices, to_experts(): return lax.all_to_all(rows, 'node', 0, 0, tiled=True)  33.1 us
    all_to_all x6, waiting for transfers between devices, to_experts(): return lax.all_to_all(rows, 'node', 0, 0, tiled=True)  20.5 us
    ppermute x6, waiting for transfers between devices, chain_step(): lax.ppermute(a, axis, way)  19.3 us
    pallas_call x3, Pallas kernels, pick(): pl.pallas_call(functools.partial(pick_kernel, len(parts)), grid=(TILES,),...  16.3 us
    unnamed x85, local copies, waits for them, and re-layouts  16.2 us
  transfers between devices with their start and end apart: 45, of which 27 were waited for; matrix products, arithmetic and copies ran while one was open for 4% of the time, Pallas kernels for 23%

profile of v4, /device:TPU:9, one launch (start us, length us, event | category | flops | bytes accessed | tf_op | source)
XLA Modules:
  0.0 450.0 jit_solution(8418102565373105344)
XLA Ops:
  2.5 1.4 copy.53.routes
  3.9 1.4 copy.54.gates
  5.3 2.9 shard_map.217
  11.6 1.3 collective-permute-start.6
  16.4 1.5 collective-permute-done.4
  18.0 1.3 collective-permute-start.5
  21.5 10.8 %collective-permute-done.2.refs_3_.refs_7_ = bf16[32,4224]{1,0:T(8,128)(2,1)S(1)} collective-permute-done((bf16[32,4224]{1,0:T(8,128)(2,1)}, bf16[32,4224]{1,0:T(8,128)(2,1)S(1)}, u32[]{:S(2)}, u32[]{:S(2)}) %collective-permute-start.2) | collective-permute-done | bytes 270368 | tf_op jit(solution)/shard_map/ppermute | solution.py:38
  32.3 4.5 %collective-permute-done.1.refs_2_.refs_6_ = bf16[32,4224]{1,0:T(8,128)(2,1)S(1)} collective-permute-done((bf16[32,4224]{1,0:T(8,128)(2,1)}, bf16[32,4224]{1,0:T(8,128)(2,1)S(1)}, u32[]{:S(2)}, u32[]{:S(2)}) %collective-permute-start.1) | collective-permute-done | bytes 270368 | tf_op jit(solution)/shard_map/ppermute | solution.py:38
  38.3 4.3 collective-permute-start.9
  42.6 1.9 collective-permute-start.8
  45.9 5.2 %shard_map.218 = (bf16[384,4096]{1,0:T(8,128)(2,1)}, bf16[128,384]{1,0:T(8,128)(2,1)}) custom-call(bf16[32,4224]{1,0:T(8,128)(2,1)} %get-tuple-element.68.refs_0_.refs_4_, bf16[32,4224]{1,0:T(8,128)(2,1)} %copy-done.18, bf16[32,4224]{1,0:T(8,128)(2,1)} %copy-done.17, bf16[32,4224]{1,0:T(8,128)(2,1)} %copy-done.16, ...), custom_call_target="tpu_custom_call" | custom-call | flops 402653184 | bytes 4194304 | tf_op jit(solution)/shard_map/pallas_call | solution.py:124
  51.1 2.0 collective-permute-done.9.refs_2_.refs_9_
  53.1 3.7 collective-permute-done.8.refs_1_.refs_8_
  57.5 6.9 %all-to-all-start = ((bf16[8,48,4096]{2,1,0:T(8,128)(2,1)}), bf16[8,48,4096]{2,1,0:T(8,128)(2,1)}, u32[]{:S(2)}, u32[]{:S(2)}) async-start(bf16[8,48,4096]{2,1,0:T(8,128)(2,1)} %bitcast.22), calls=%async_computation | async-start | bytes 6291456 | tf_op jit(solution)/shard_map/all_to_all | solution.py:372
  66.1 1.9 collective-permute-start.13
  68.0 3.4 collective-permute-start.12
  72.0 5.8 %shard_map.222 = (bf16[96,4096]{1,0:T(8,128)(2,1)}, bf16[96,4096]{1,0:T(8,128)(2,1)}, bf16[64,4096]{1,0:T(8,128)(2,1)}, bf16[32,4096]{1,0:T(8,128)(2,1)}, bf16[6...) custom-call(bf16[128,2048]{1,0:T(8,128)(2,1)} %copy-done.15, ...), custom_call_target="tpu_custom_call" | custom-call | flops 805306368 | bytes 5242880 | tf_op jit(solution)/shard_map/pallas_call | solution.py:191
  79.1 2.7 collective-permute-done.13.refs_4_.refs_11_
  81.8 2.2 collective-permute-start.15
  86.4 21.3 %collective-permute-done.11.refs_2_ = bf16[64,4096]{1,0:T(8,128)(2,1)S(1)} collective-permute-done((bf16[64,4096]{1,0:T(8,128)(2,1)}, bf16[64,4096]{1,0:T(8,128)(2,1)S(1)}, u32[]{:S(2)}, u32[]{:S(2)}) %collective-permute-start.11) | collective-permute-done | bytes 524320 | tf_op jit(solution)/shard_map/ppermute | solution.py:38
  108.6 10.8 %collective-permute-done.15.refs_6_.refs_13_ = bf16[64,4224]{1,0:T(8,128)(2,1)S(1)} collective-permute-done((bf16[64,4224]{1,0:T(8,128)(2,1)S(1)}, bf16[64,4224]{1,0:T(8,128)(2,1)S(1)}, u32[]{:S(2)}, u32[]{:S(2)}) %collective-permute-start.15) | collective-permute-done | bytes 540704 | tf_op jit(solution)/shard_map/ppermute | solution.py:54
  121.0 5.5 %shard_map.223 = (bf16[384,4096]{1,0:T(8,128)(2,1)}, bf16[128,384]{1,0:T(8,128)(2,1)}) custom-call(bf16[64,4224]{1,0:T(8,128)(2,1)} %shard_map.219.refs_0_.refs_7_, bf16[64,4224]{1,0:T(8,128)(2,1)} %copy-done.3, bf16[64,4224]{1,0:T(8,128)(2,1)} %copy-done.2, bf16[64,4224]{1,0:T(8,128)(2,1)} %copy-done.5, bf16[64,4224]{1,0:T(8,128)(2,1)} %copy-done.4, ...), custom_call_target="tpu_custom_call" | custom-call | flops 704643072 | bytes 4980736 | tf_op jit(solution)/shard_map/pallas_call | solution.py:124
  126.6 4.6 %all-to-all-start.1 = ((bf16[8,48,4096]{2,1,0:T(8,128)(2,1)}), bf16[8,48,4096]{2,1,0:T(8,128)(2,1)S(1)}, u32[]{:S(2)}, u32[]{:S(2)}) async-start(bf16[8,48,4096]{2,1,0:T(8,128)(2,1)} %bitcast.24), calls=%async_computation.1 | async-start | bytes 6291456 | tf_op jit(solution)/shard_map/all_to_all | solution.py:372
  131.2 5.6 %shard_map.229 = (bf16[384,4096]{1,0:T(8,128)(2,1)}, bf16[128,384]{1,0:T(8,128)(2,1)}) custom-call(bf16[64,4224]{1,0:T(8,128)(2,1)} %shard_map.219.refs_0_.refs_7_, bf16[64,4224]{1,0:T(8,128)(2,1)} %copy-done.3, bf16[64,4224]{1,0:T(8,128)(2,1)} %copy-done.2, bf16[64,4224]{1,0:T(8,128)(2,1)} %copy-done.5, bf16[64,4224]{1,0:T(8,128)(2,1)} %copy-done.4, ...), custom_call_target="tpu_custom_call" | custom-call | flops 704643072 | bytes 4980736 | tf_op jit(solution)/shard_map/pallas_call | solution.py:124
  136.8 16.1 %shard_map.221.refs_0_ = bf16[384,4096]{1,0:T(8,128)(2,1)} custom-call(bf16[384,4096]{1,0:T(8,128)(2,1)} %bitcast.2.refs_0_, bf16[4096,768]{1,0:T(8,128)(2,1)} %bitcast.27, bf16[4096,768]{1,0:T(8,128)(2,1)} %bitcast.31, bf16[768,4096]{1,0:T(8,128)(2,1)} %bitcast.35), custom_call_target="tpu_custom_call" | custom-call | flops 7247757312 | bytes 25165824 | tf_op jit(solution)/shard_map/pallas_call | solution.py:321
  154.1 11.5 %all-to-all-done.1 = bf16[8,48,4096]{2,1,0:T(8,128)(2,1)S(1)} async-done(((bf16[8,48,4096]{2,1,0:T(8,128)(2,1)}), bf16[8,48,4096]{2,1,0:T(8,128)(2,1)S(1)}, u32[]{:S(2)}, u32[]{:S(2)}) %all-to-all-start.1) | async-done | bytes 3145760 | tf_op jit(solution)/shard_map/all_to_all | solution.py:372
  165.7 1.8 copy-done.12
  167.4 7.0 %all-to-all-start.3 = ((bf16[8,48,4096]{2,1,0:T(8,128)(2,1)}), bf16[8,48,4096]{2,1,0:T(8,128)(2,1)S(1)}, u32[]{:S(2)}, u32[]{:S(2)}) async-start(bf16[8,48,4096]{2,1,0:T(8,128)(2,1)} %bitcast.23), calls=%async_computation.3 | async-start | bytes 6291456 | tf_op jit(solution)/shard_map/all_to_all | solution.py:372
  174.4 2.6 collective-permute-start.17
  177.0 2.0 collective-permute-start.16
  179.0 2.3 collective-permute-start.18
  181.3 35.0 %collective-permute-done.16.refs_3_ = bf16[32,4096]{1,0:T(8,128)(2,1)S(1)} collective-permute-done((bf16[32,4096]{1,0:T(8,128)(2,1)S(1)}, bf16[32,4096]{1,0:T(8,128)(2,1)S(1)}, u32[]{:S(2)}, u32[]{:S(2)}) %collective-permute-start.16) | collective-permute-done | bytes 262176 | tf_op jit(solution)/shard_map/ppermute | solution.py:38
  216.3 6.7 %collective-permute-done.18.refs_5_ = bf16[32,4096]{1,0:T(8,128)(2,1)S(1)} collective-permute-done((bf16[32,4096]{1,0:T(8,128)(2,1)}, bf16[32,4096]{1,0:T(8,128)(2,1)S(1)}, u32[]{:S(2)}, u32[]{:S(2)}) %collective-permute-start.18) | collective-permute-done | bytes 262176 | tf_op jit(solution)/shard_map/ppermute | solution.py:38
  224.5 16.2 %shard_map.225 = (bf16[96,4096]{1,0:T(8,128)(2,1)}, bf16[96,4096]{1,0:T(8,128)(2,1)}, bf16[64,4096]{1,0:T(8,128)(2,1)}, bf16[32,4096]{1,0:T(8,128)(2,1)}, bf16[6...) custom-call(bf16[96,4096]{1,0:T(8,128)(2,1)} %get-tuple-element.77.refs_0_, bf16[96,4096]{1,0:T(8,128)(2,1)} %copy-done.36, ...), custom_call_target="tpu_custom_call" | custom-call | flops 7247757312 | bytes 25165824 | tf_op jit(solution)/shard_map/pallas_call | solution.py:321
  240.7 16.1 %shard_map.226.refs_0_ = bf16[384,4096]{1,0:T(8,128)(2,1)} custom-call(bf16[384,4096]{1,0:T(8,128)(2,1)} %bitcast.26, bf16[4096,768]{1,0:T(8,128)(2,1)} %bitcast.29, bf16[4096,768]{1,0:T(8,128)(2,1)} %bitcast.33, bf16[768,4096]{1,0:T(8,128)(2,1)} %bitcast.37), custom_call_target="tpu_custom_call" | custom-call | flops 7247757312 | bytes 25165824 | tf_op jit(solution)/shard_map/pallas_call | solution.py:321
  258.0 1.7 copy-done.11
  259.8 4.7 %all-to-all-start.2 = ((bf16[8,48,4096]{2,1,0:T(8,128)(2,1)}), bf16[8,48,4096]{2,1,0:T(8,128)(2,1)S(1)}, u32[]{:S(2)}, u32[]{:S(2)}) async-start(bf16[8,48,4096]{2,1,0:T(8,128)(2,1)} %bitcast.18), calls=%async_computation.2 | async-start | bytes 6291456 | tf_op jit(solution)/shard_map/all_to_all | solution.py:372
  264.5 2.6 collective-permute-start.24
  267.2 16.2 %shard_map.231.refs_0_ = bf16[384,4096]{1,0:T(8,128)(2,1)} custom-call(bf16[384,4096]{1,0:T(8,128)(2,1)} %bitcast.25, bf16[4096,768]{1,0:T(8,128)(2,1)} %bitcast.30, bf16[4096,768]{1,0:T(8,128)(2,1)} %bitcast.34, bf16[768,4096]{1,0:T(8,128)(2,1)} %bitcast.38), custom_call_target="tpu_custom_call" | custom-call | flops 7247757312 | bytes 25165824 | tf_op jit(solution)/shard_map/pallas_call | solution.py:321
  283.4 7.3 %collective-permute-done.24.refs_3_ = bf16[32,4096]{1,0:T(8,128)(2,1)S(1)} collective-permute-done((bf16[32,4096]{1,0:T(8,128)(2,1)}, bf16[32,4096]{1,0:T(8,128)(2,1)S(1)}, u32[]{:S(2)}, u32[]{:S(2)}) %collective-permute-start.24) | collective-permute-done | bytes 262176 | tf_op jit(solution)/shard_map/ppermute | solution.py:38
  290.7 11.2 %collective-permute-done.23.refs_2_ = bf16[64,4096]{1,0:T(8,128)(2,1)S(1)} collective-permute-done((bf16[64,4096]{1,0:T(8,128)(2,1)}, bf16[64,4096]{1,0:T(8,128)(2,1)S(1)}, u32[]{:S(2)}, u32[]{:S(2)}) %collective-permute-start.23) | collective-permute-done | bytes 524320 | tf_op jit(solution)/shard_map/ppermute | solution.py:38
  304.0 1.6 copy-done.1
  305.7 4.7 %all-to-all-start.4 = ((bf16[8,48,4096]{2,1,0:T(8,128)(2,1)}), bf16[8,48,4096]{2,1,0:T(8,128)(2,1)S(1)}, u32[]{:S(2)}, u32[]{:S(2)}) async-start(bf16[8,48,4096]{2,1,0:T(8,128)(2,1)} %bitcast.19), calls=%async_computation.4 | async-start | bytes 6291456 | tf_op jit(solution)/shard_map/all_to_all | solution.py:372
  310.4 4.4 shard_map.228
  314.8 3.5 collective-permute-start.19
  319.5 27.1 %collective-permute-done.28.refs_4_ = bf16[64,4096]{1,0:T(8,128)(2,1)S(1)} collective-permute-done((bf16[64,4096]{1,0:T(8,128)(2,1)}, bf16[64,4096]{1,0:T(8,128)(2,1)S(1)}, u32[]{:S(2)}, u32[]{:S(2)}) %collective-permute-start.28) | collective-permute-done | bytes 524320 | tf_op jit(solution)/shard_map/ppermute | solution.py:38
  346.6 3.6 collective-permute-done.20
  350.2 7.7 %collective-permute-done.21 = bf16[32,4096]{1,0:T(8,128)(2,1)S(1)} collective-permute-done((bf16[32,4096]{1,0:T(8,128)(2,1)}, bf16[32,4096]{1,0:T(8,128)(2,1)S(1)}, u32[]{:S(2)}, u32[]{:S(2)}) %collective-permute-start.21) | collective-permute-done | bytes 262176 | tf_op jit(solution)/shard_map/ppermute | solution.py:38
  358.5 1.6 copy-done
  360.2 5.1 %all-to-all-start.5 = ((bf16[8,48,4096]{2,1,0:T(8,128)(2,1)}), bf16[8,48,4096]{2,1,0:T(8,128)(2,1)}, u32[]{:S(2)}, u32[]{:S(2)}) async-start(bf16[8,48,4096]{2,1,0:T(8,128)(2,1)} %bitcast.17), calls=%async_computation.5 | async-start | bytes 6291456 | tf_op jit(solution)/shard_map/all_to_all | solution.py:372
  365.3 1.4 add_convert_fusion.2
  366.7 9.2 %collective-permute-done.29.refs_5_ = bf16[32,4096]{1,0:T(8,128)(2,1)S(1)} collective-permute-done((bf16[32,4096]{1,0:T(8,128)(2,1)S(1)}, bf16[32,4096]{1,0:T(8,128)(2,1)S(1)}, u32[]{:S(2)}, u32[]{:S(2)}) %collective-permute-start.29) | collective-permute-done | bytes 262176 | tf_op jit(solution)/shard_map/ppermute | solution.py:38
  376.6 5.6 %shard_map.235 = (f32[128,2048]{1,0:T(8,128)}, bf16[128,2048]{1,0:T(8,128)(2,1)}, f32[128,2048]{1,0:T(8,128)}, bf16[128,2048]{1,0:T(8,128)(2,1)}) custom-call(bf16[256,384]{1,0:T(8,128)(2,1)} %get-tuple-element.112.mixing_a, bf16[256,384]{1,0:T(8,128)(2,1)} %get-tuple-element.113.mixing_b, bf16[96,4096]{1,0:T(8,128)(2,1)} %get-tuple-element.114.refs_0_, ...), custom_call_target="tpu_custom_call" | custom-call | flops 805306368 | bytes 5242880 | tf_op jit(solution)/shard_map/pallas_call | solution.py:267
  382.2 4.4 shard_map.233
  387.9 1.4 collective-permute-start.27
  390.6 9.0 %all-to-all-done.5 = bf16[8,48,4096]{2,1,0:T(8,128)(2,1)} async-done(((bf16[8,48,4096]{2,1,0:T(8,128)(2,1)}), bf16[8,48,4096]{2,1,0:T(8,128)(2,1)}, u32[]{:S(2)}, u32[]{:S(2)}) %all-to-all-start.5) | async-done | bytes 3145760 | tf_op jit(solution)/shard_map/all_to_all | solution.py:372
  399.5 4.3 shard_map.237
  405.1 1.4 collective-permute-start.32
  406.5 9.8 %collective-permute-done.27 = bf16[32,4096]{1,0:T(8,128)(2,1)S(1)} collective-permute-done((bf16[32,4096]{1,0:T(8,128)(2,1)}, bf16[32,4096]{1,0:T(8,128)(2,1)S(1)}, u32[]{:S(2)}, u32[]{:S(2)}) %collective-permute-start.27) | collective-permute-done | bytes 262176 | tf_op jit(solution)/shard_map/ppermute | solution.py:38
  417.8 8.5 %collective-permute-start.33 = (bf16[128,2048]{1,0:T(8,128)(2,1)}, bf16[128,2048]{1,0:T(8,128)(2,1)S(1)}, u32[]{:S(2)}, u32[]{:S(2)}) collective-permute-start(bf16[128,2048]{1,0:T(8,128)(2,1)} %get-tuple-element.128), channel_id=1, source_target_pairs={{0,16},{4,20},{8,24},{12,28},{16,0},{20,4},{24,8},{28,12},{1,17},{... | collective-permute-start | bytes 1572872 | tf_op jit(solution)/shard_map/ppermute | solution.py:38
  427.0 7.6 %collective-permute-done.32 = bf16[32,4096]{1,0:T(8,128)(2,1)S(1)} collective-permute-done((bf16[32,4096]{1,0:T(8,128)(2,1)}, bf16[32,4096]{1,0:T(8,128)(2,1)S(1)}, u32[]{:S(2)}, u32[]{:S(2)}) %collective-permute-start.32) | collective-permute-done | bytes 262176 | tf_op jit(solution)/shard_map/ppermute | solution.py:38
  435.8 1.3 convert_add_fusion.1
  439.1 3.8 collective-permute-done.34
  443.0 4.3 collective-permute-start.35
  (178 shorter events, 44.1 us)
Async XLA Ops:
  8.2 12.4 %copy-start.28 = (bf16[32,4224]{1,0:T(8,128)(2,1)S(1)}, bf16[32,4224]{1,0:T(8,128)(2,1)}, u32[]{:S(2)}) copy-start(bf16[32,4224]{1,0:T(8,128)(2,1)} %get-tuple-element.73) | copy-start | bytes 811012
  8.2 2.1 collective-permute-start.3
  9.9 35.4 %copy-start.32 = (s32[1,384]{1,0:T(1,128)S(1)}, s32[1,384]{1,0:T(1,128)}, u32[]{:S(2)}) copy-start(s32[1,384]{1,0:T(1,128)} %constant.46.clone) | copy-start | bytes 4612
  10.3 7.6 %collective-permute-start.4 = (bf16[64,2048]{1,0:T(8,128)(2,1)S(1)}, bf16[64,2048]{1,0:T(8,128)(2,1)S(1)}, u32[]{:S(2)}, u32[]{:S(2)}) collective-permute-start(bf16[64,2048]{1,0:T(8,128)(2,1)S(1)} %slice.104), channel_id=1, source_target_pairs={{0,8},{4,12},{8,0},{12,4},{16,24},{20,28},{24,16},{28,20},{1,9},{5... | collective-permute-start | bytes 786440 | tf_op jit(solution)/shard_map/ppermute | solution.py:38
  11.6 7.6 %collective-permute-start.6 = (bf16[64,2176]{1,0:T(8,128)(2,1)S(1)}, bf16[64,2176]{1,0:T(8,128)(2,1)S(1)}, u32[]{:S(2)}, u32[]{:S(2)}) collective-permute-start(bf16[64,2176]{1,0:T(8,128)(2,1)S(1)} %slice.105), channel_id=1, source_target_pairs={{0,16},{4,20},{8,24},{12,28},{16,0},{20,4},{24,8},{28,12},{1,17},{... | collective-permute-start | bytes 835592 | tf_op jit(solution)/shard_map/ppermute | solution.py:38
  13.0 19.3 %collective-permute-start.2 = (bf16[32,4224]{1,0:T(8,128)(2,1)}, bf16[32,4224]{1,0:T(8,128)(2,1)S(1)}, u32[]{:S(2)}, u32[]{:S(2)}) collective-permute-start(bf16[32,4224]{1,0:T(8,128)(2,1)} %get-tuple-element.68.refs_0_.refs_4_), channel_id=1, source_target_pairs={{0,3},{1,2},{2,1},{3,0},{4,7},{5,6},{6,5},{7,4},{8,11},{9,10},{10,... | collective-permute-start | bytes 811016 | tf_op jit(solution)/shard_map/ppermute | solution.py:38
  14.3 22.5 %collective-permute-start.1 = (bf16[32,4224]{1,0:T(8,128)(2,1)}, bf16[32,4224]{1,0:T(8,128)(2,1)S(1)}, u32[]{:S(2)}, u32[]{:S(2)}) collective-permute-start(bf16[32,4224]{1,0:T(8,128)(2,1)} %get-tuple-element.68.refs_0_.refs_4_), channel_id=1, source_target_pairs={{0,2},{1,3},{2,0},{3,1},{4,6},{5,7},{6,4},{7,5},{8,10},{9,11},{10,... | collective-permute-start | bytes 811016 | tf_op jit(solution)/shard_map/ppermute | solution.py:38
  15.3 21.5 %collective-permute-start = (bf16[32,4224]{1,0:T(8,128)(2,1)}, bf16[32,4224]{1,0:T(8,128)(2,1)S(1)}, u32[]{:S(2)}, u32[]{:S(2)}) collective-permute-start(bf16[32,4224]{1,0:T(8,128)(2,1)} %get-tuple-element.68.refs_0_.refs_4_), channel_id=1, source_target_pairs={{0,1},{1,0},{2,3},{3,2},{4,5},{5,4},{6,7},{7,6},{8,9},{9,8},{10,11... | collective-permute-start | bytes 811016 | tf_op jit(solution)/shard_map/ppermute | solution.py:38
  18.0 39.5 %copy-start.15 = (bf16[128,2048]{1,0:T(8,128)(2,1)}, bf16[128,2048]{1,0:T(8,128)(2,1)S(1)}, u32[]{:S(2)}) copy-start(bf16[128,2048]{1,0:T(8,128)(2,1)S(1)} %pad_maximum_fusion.2.a0) | copy-start | bytes 1572868
  18.0 18.8 %collective-permute-start.5 = (bf16[128,2048]{1,0:T(8,128)(2,1)S(1)}, bf16[128,2048]{1,0:T(8,128)(2,1)S(1)}, u32[]{:S(2)}, u32[]{:S(2)}) collective-permute-start(bf16[128,2048]{1,0:T(8,128)(2,1)S(1)} %pad_maximum_fusion.2.a0), channel_id=1, source_target_pairs={{0,16},{4,20},{8,24},{12,28},{16,0},{20,4},{24,8},{28,12},{1,17},{... | collective-permute-start | bytes 1572872 | tf_op jit(solution)/shard_map/ppermute | solution.py:38
  19.3 38.1 %copy-start.9 = (bf16[128,2176]{1,0:T(8,128)(2,1)}, bf16[128,2176]{1,0:T(8,128)(2,1)S(1)}, u32[]{:S(2)}) copy-start(bf16[128,2176]{1,0:T(8,128)(2,1)S(1)} %pad_maximum_fusion.b0.t0) | copy-start | bytes 1671172
  19.3 17.5 %collective-permute-start.7 = (bf16[128,2176]{1,0:T(8,128)(2,1)S(1)}, bf16[128,2176]{1,0:T(8,128)(2,1)S(1)}, u32[]{:S(2)}, u32[]{:S(2)}) collective-permute-start(bf16[128,2176]{1,0:T(8,128)(2,1)S(1)} %pad_maximum_fusion.b0.t0), channel_id=1, source_target_pairs={{0,8},{4,12},{8,0},{12,4},{16,24},{20,28},{24,16},{28,20},{1,9},{5... | collective-permute-start | bytes 1671176 | tf_op jit(solution)/shard_map/ppermute | solution.py:38
  32.3 13.6 %copy-start.16 = (bf16[32,4224]{1,0:T(8,128)(2,1)}, bf16[32,4224]{1,0:T(8,128)(2,1)S(1)}, u32[]{:S(2)}) copy-start(bf16[32,4224]{1,0:T(8,128)(2,1)S(1)} %collective-permute-done.2.refs_3_.refs_7_) | copy-start | bytes 811012
  36.8 20.7 %copy-start.14 = (bf16[128,2048]{1,0:T(8,128)(2,1)}, bf16[128,2048]{1,0:T(8,128)(2,1)S(1)}, u32[]{:S(2)}) copy-start(bf16[128,2048]{1,0:T(8,128)(2,1)S(1)} %collective-permute-done.5.refs_1_) | copy-start | bytes 1572868
  37.6 19.8 %copy-start.8 = (bf16[128,2176]{1,0:T(8,128)(2,1)}, bf16[128,2176]{1,0:T(8,128)(2,1)S(1)}, u32[]{:S(2)}) copy-start(bf16[128,2176]{1,0:T(8,128)(2,1)S(1)} %collective-permute-done.7.refs_2_) | copy-start | bytes 1671172
  38.3 14.8 %collective-permute-start.9 = (bf16[64,4224]{1,0:T(8,128)(2,1)}, bf16[64,4224]{1,0:T(8,128)(2,1)S(1)}, u32[]{:S(2)}, u32[]{:S(2)}) collective-permute-start(bf16[64,4224]{1,0:T(8,128)(2,1)} %shard_map.219.refs_0_.refs_7_), channel_id=1, source_target_pairs={{3,2},{2,1},{1,0},{7,6},{6,5},{5,4},{11,10},{10,9},{9,8},{15,14},{... | collective-permute-start | bytes 1622024 | tf_op jit(solution)/shard_map/ppermute | solution.py:54
  42.6 14.2 %collective-permute-start.8 = (bf16[64,4224]{1,0:T(8,128)(2,1)}, bf16[64,4224]{1,0:T(8,128)(2,1)S(1)}, u32[]{:S(2)}, u32[]{:S(2)}) collective-permute-start(bf16[64,4224]{1,0:T(8,128)(2,1)} %shard_map.219.refs_0_.refs_7_), channel_id=1, source_target_pairs={{0,1},{1,2},{2,3},{4,5},{5,6},{6,7},{8,9},{9,10},{10,11},{12,13},{... | collective-permute-start | bytes 1622024 | tf_op jit(solution)/shard_map/ppermute | solution.py:54
  53.1 13.0 %copy-start.2 = (bf16[64,4224]{1,0:T(8,128)(2,1)}, bf16[64,4224]{1,0:T(8,128)(2,1)S(1)}, u32[]{:S(2)}) copy-start(bf16[64,4224]{1,0:T(8,128)(2,1)S(1)} %collective-permute-done.9.refs_2_.refs_9_) | copy-start | bytes 1622020
  57.5 14.0 %copy-start.33 = (s32[1,384]{1,0:T(1,128)S(1)}, s32[1,384]{1,0:T(1,128)}, u32[]{:S(2)}) copy-start(s32[1,384]{1,0:T(1,128)} %constant.48.clone) | copy-start | bytes 4612
  57.5 69.1 %all-to-all-start = ((bf16[8,48,4096]{2,1,0:T(8,128)(2,1)}), bf16[8,48,4096]{2,1,0:T(8,128)(2,1)}, u32[]{:S(2)}, u32[]{:S(2)}) async-start(bf16[8,48,4096]{2,1,0:T(8,128)(2,1)} %bitcast.22), calls=%async_computation | async-start | bytes 6291456 | tf_op jit(solution)/shard_map/all_to_all | solution.py:372
  64.4 20.3 %copy-start.40 = (s32[7]{0:T(128)S(1)}, s32[7]{0:T(128)}, u32[]{:S(2)}) copy-start(s32[7]{0:T(128)} %constant.49.clone) | copy-start | bytes 88
  64.4 21.3 %copy-start.31 = (pred[128,224]{1,0:T(32,128)(4,1)S(1)}, pred[128,224]{1,0:T(32,128)(4,1)}, u32[]{:S(2)}) copy-start(pred[128,224]{1,0:T(32,128)(4,1)} %constant.50.clone) | copy-start | bytes 86020
  66.1 15.7 %collective-permute-start.13 = (bf16[64,4224]{1,0:T(8,128)(2,1)S(1)}, bf16[64,4224]{1,0:T(8,128)(2,1)S(1)}, u32[]{:S(2)}, u32[]{:S(2)}) collective-permute-start(bf16[64,4224]{1,0:T(8,128)(2,1)S(1)} %collective-permute-done.9.refs_2_.refs_9_), channel_id=1, source_target_pairs={{2,1},{1,0},{6,5},{5,4},{10,9},{9,8},{14,13},{13,12},{18,17},{17,1... | collective-permute-start | bytes 1622024 | tf_op jit(solution)/shard_map/ppermute | solution.py:54
  68.0 16.0 %collective-permute-start.12 = (bf16[64,4224]{1,0:T(8,128)(2,1)S(1)}, bf16[64,4224]{1,0:T(8,128)(2,1)S(1)}, u32[]{:S(2)}, u32[]{:S(2)}) collective-permute-start(bf16[64,4224]{1,0:T(8,128)(2,1)S(1)} %collective-permute-done.8.refs_1_.refs_8_), channel_id=1, source_target_pairs={{1,2},{2,3},{5,6},{6,7},{9,10},{10,11},{13,14},{14,15},{17,18},{18... | collective-permute-start | bytes 1622024 | tf_op jit(solution)/shard_map/ppermute | solution.py:54
  77.9 30.1 %collective-permute-start.10 = (bf16[96,4096]{1,0:T(8,128)(2,1)}, bf16[96,4096]{1,0:T(8,128)(2,1)S(1)}, u32[]{:S(2)}, u32[]{:S(2)}) collective-permute-start(bf16[96,4096]{1,0:T(8,128)(2,1)} %get-tuple-element.78), channel_id=1, source_target_pairs={{0,1},{1,0},{2,3},{3,2},{4,5},{5,4},{6,7},{7,6},{8,9},{9,8},{10,11... | collective-permute-start | bytes 2359304 | tf_op jit(solution)/shard_map/ppermute | solution.py:38
  77.9 29.8 %collective-permute-start.11 = (bf16[64,4096]{1,0:T(8,128)(2,1)}, bf16[64,4096]{1,0:T(8,128)(2,1)S(1)}, u32[]{:S(2)}, u32[]{:S(2)}) collective-permute-start(bf16[64,4096]{1,0:T(8,128)(2,1)} %get-tuple-element.79), channel_id=1, source_target_pairs={{0,2},{1,3},{2,0},{3,1},{4,6},{5,7},{6,4},{7,5},{8,10},{9,11},{10,... | collective-permute-start | bytes 1572872 | tf_op jit(solution)/shard_map/ppermute | solution.py:38
  81.8 37.6 %copy-start.4 = (bf16[64,4224]{1,0:T(8,128)(2,1)}, bf16[64,4224]{1,0:T(8,128)(2,1)S(1)}, u32[]{:S(2)}) copy-start(bf16[64,4224]{1,0:T(8,128)(2,1)S(1)} %collective-permute-done.13.refs_4_.refs_11_) | copy-start | bytes 1622020
  81.8 37.6 %collective-permute-start.15 = (bf16[64,4224]{1,0:T(8,128)(2,1)S(1)}, bf16[64,4224]{1,0:T(8,128)(2,1)S(1)}, u32[]{:S(2)}, u32[]{:S(2)}) collective-permute-start(bf16[64,4224]{1,0:T(8,128)(2,1)S(1)} %collective-permute-done.13.refs_4_.refs_11_), channel_id=1, source_target_pairs={{1,0},{5,4},{9,8},{13,12},{17,16},{21,20},{25,24},{29,28}} | collective-permute-start | bytes 1622024 | tf_op jit(solution)/shard_map/ppermute | solution.py:54
  84.0 35.4 %copy-start.5 = (bf16[64,4224]{1,0:T(8,128)(2,1)}, bf16[64,4224]{1,0:T(8,128)(2,1)S(1)}, u32[]{:S(2)}) copy-start(bf16[64,4224]{1,0:T(8,128)(2,1)S(1)} %collective-permute-done.12.refs_3_.refs_10_) | copy-start | bytes 1622020
  84.0 35.4 %collective-permute-start.14 = (bf16[64,4224]{1,0:T(8,128)(2,1)S(1)}, bf16[64,4224]{1,0:T(8,128)(2,1)S(1)}, u32[]{:S(2)}, u32[]{:S(2)}) collective-permute-start(bf16[64,4224]{1,0:T(8,128)(2,1)S(1)} %collective-permute-done.12.refs_3_.refs_10_), channel_id=1, source_target_pairs={{2,3},{6,7},{10,11},{14,15},{18,19},{22,23},{26,27},{30,31}} | collective-permute-start | bytes 1622024 | tf_op jit(solution)/shard_map/ppermute | solution.py:54
  107.7 18.9 %copy-start.35 = (bf16[64,4096]{1,0:T(8,128)(2,1)}, bf16[64,4096]{1,0:T(8,128)(2,1)S(1)}, u32[]{:S(2)}) copy-start(bf16[64,4096]{1,0:T(8,128)(2,1)S(1)} %collective-permute-done.11.refs_2_) | copy-start | bytes 1572868
  107.9 18.7 %copy-start.36 = (bf16[96,4096]{1,0:T(8,128)(2,1)}, bf16[96,4096]{1,0:T(8,128)(2,1)S(1)}, u32[]{:S(2)}) copy-start(bf16[96,4096]{1,0:T(8,128)(2,1)S(1)} %collective-permute-done.10.refs_1_) | copy-start | bytes 2359300
  126.6 39.0 %all-to-all-start.1 = ((bf16[8,48,4096]{2,1,0:T(8,128)(2,1)}), bf16[8,48,4096]{2,1,0:T(8,128)(2,1)S(1)}, u32[]{:S(2)}, u32[]{:S(2)}) async-start(bf16[8,48,4096]{2,1,0:T(8,128)(2,1)} %bitcast.24), calls=%async_computation.1 | async-start | bytes 6291456 | tf_op jit(solution)/shard_map/all_to_all | solution.py:372
  167.4 90.6 %all-to-all-start.3 = ((bf16[8,48,4096]{2,1,0:T(8,128)(2,1)}), bf16[8,48,4096]{2,1,0:T(8,128)(2,1)S(1)}, u32[]{:S(2)}, u32[]{:S(2)}) async-start(bf16[8,48,4096]{2,1,0:T(8,128)(2,1)} %bitcast.23), calls=%async_computation.3 | async-start | bytes 6291456 | tf_op jit(solution)/shard_map/all_to_all | solution.py:372
  174.4 48.5 %collective-permute-start.17 = (bf16[64,4096]{1,0:T(8,128)(2,1)}, bf16[64,4096]{1,0:T(8,128)(2,1)S(1)}, u32[]{:S(2)}, u32[]{:S(2)}) collective-permute-start(bf16[64,4096]{1,0:T(8,128)(2,1)} %get-tuple-element.85), channel_id=1, source_target_pairs={{0,3},{1,2},{2,1},{3,0},{4,7},{5,6},{6,5},{7,4},{8,11},{9,10},{10,... | collective-permute-start | bytes 1572872 | tf_op jit(solution)/shard_map/ppermute | solution.py:38
  177.0 39.3 %collective-permute-start.16 = (bf16[32,4096]{1,0:T(8,128)(2,1)S(1)}, bf16[32,4096]{1,0:T(8,128)(2,1)S(1)}, u32[]{:S(2)}, u32[]{:S(2)}) collective-permute-start(bf16[32,4096]{1,0:T(8,128)(2,1)S(1)} %copy-done.29), channel_id=1, source_target_pairs={{0,2},{1,3},{2,0},{3,1},{4,6},{5,7},{6,4},{7,5},{8,10},{9,11},{10,... | collective-permute-start | bytes 786440 | tf_op jit(solution)/shard_map/ppermute | solution.py:38
  179.0 43.9 %collective-permute-start.18 = (bf16[32,4096]{1,0:T(8,128)(2,1)}, bf16[32,4096]{1,0:T(8,128)(2,1)S(1)}, u32[]{:S(2)}, u32[]{:S(2)}) collective-permute-start(bf16[32,4096]{1,0:T(8,128)(2,1)} %get-tuple-element.86), channel_id=1, source_target_pairs={{0,3},{1,2},{2,1},{3,0},{4,7},{5,6},{6,5},{7,4},{8,11},{9,10},{10,... | collective-permute-start | bytes 786440 | tf_op jit(solution)/shard_map/ppermute | solution.py:38
  259.8 44.3 %all-to-all-start.2 = ((bf16[8,48,4096]{2,1,0:T(8,128)(2,1)}), bf16[8,48,4096]{2,1,0:T(8,128)(2,1)S(1)}, u32[]{:S(2)}, u32[]{:S(2)}) async-start(bf16[8,48,4096]{2,1,0:T(8,128)(2,1)} %bitcast.18), calls=%async_computation.2 | async-start | bytes 6291456 | tf_op jit(solution)/shard_map/all_to_all | solution.py:372
  264.5 37.4 %collective-permute-start.22 = (bf16[96,4096]{1,0:T(8,128)(2,1)}, bf16[96,4096]{1,0:T(8,128)(2,1)}, u32[]{:S(2)}, u32[]{:S(2)}) collective-permute-start(bf16[96,4096]{1,0:T(8,128)(2,1)} %get-tuple-element.103), channel_id=1, source_target_pairs={{0,1},{1,0},{2,3},{3,2},{4,5},{5,4},{6,7},{7,6},{8,9},{9,8},{10,11... | collective-permute-start | bytes 2359304 | tf_op jit(solution)/shard_map/ppermute | solution.py:38
  264.5 26.2 %collective-permute-start.24 = (bf16[32,4096]{1,0:T(8,128)(2,1)}, bf16[32,4096]{1,0:T(8,128)(2,1)S(1)}, u32[]{:S(2)}, u32[]{:S(2)}) collective-permute-start(bf16[32,4096]{1,0:T(8,128)(2,1)} %get-tuple-element.105), channel_id=1, source_target_pairs={{0,2},{1,3},{2,0},{3,1},{4,6},{5,7},{6,4},{7,5},{8,10},{9,11},{10,... | collective-permute-start | bytes 786440 | tf_op jit(solution)/shard_map/ppermute | solution.py:38
  267.2 34.8 %collective-permute-start.23 = (bf16[64,4096]{1,0:T(8,128)(2,1)}, bf16[64,4096]{1,0:T(8,128)(2,1)S(1)}, u32[]{:S(2)}, u32[]{:S(2)}) collective-permute-start(bf16[64,4096]{1,0:T(8,128)(2,1)} %get-tuple-element.104), channel_id=1, source_target_pairs={{0,2},{1,3},{2,0},{3,1},{4,6},{5,7},{6,4},{7,5},{8,10},{9,11},{10,... | collective-permute-start | bytes 1572872 | tf_op jit(solution)/shard_map/ppermute | solution.py:38
  290.7 67.8 %copy-start.23 = (bf16[32,4096]{1,0:T(8,128)(2,1)}, bf16[32,4096]{1,0:T(8,128)(2,1)S(1)}, u32[]{:S(2)}) copy-start(bf16[32,4096]{1,0:T(8,128)(2,1)S(1)} %collective-permute-done.24.refs_3_) | copy-start | bytes 786436
  305.7 52.9 %all-to-all-start.4 = ((bf16[8,48,4096]{2,1,0:T(8,128)(2,1)}), bf16[8,48,4096]{2,1,0:T(8,128)(2,1)S(1)}, u32[]{:S(2)}, u32[]{:S(2)}) async-start(bf16[8,48,4096]{2,1,0:T(8,128)(2,1)} %bitcast.19), calls=%async_computation.4 | async-start | bytes 6291456 | tf_op jit(solution)/shard_map/all_to_all | solution.py:372
  310.3 36.2 %collective-permute-start.28 = (bf16[64,4096]{1,0:T(8,128)(2,1)}, bf16[64,4096]{1,0:T(8,128)(2,1)S(1)}, u32[]{:S(2)}, u32[]{:S(2)}) collective-permute-start(bf16[64,4096]{1,0:T(8,128)(2,1)} %get-tuple-element.115), channel_id=1, source_target_pairs={{0,3},{1,2},{2,1},{3,0},{4,7},{5,6},{6,5},{7,4},{8,11},{9,10},{10,... | collective-permute-start | bytes 1572872 | tf_op jit(solution)/shard_map/ppermute | solution.py:38
  314.8 31.8 %collective-permute-start.19 = (bf16[32,4096]{1,0:T(8,128)(2,1)}, bf16[32,4096]{1,0:T(8,128)(2,1)S(1)}, u32[]{:S(2)}, u32[]{:S(2)}) collective-permute-start(bf16[32,4096]{1,0:T(8,128)(2,1)} %get-tuple-element.96), channel_id=1, source_target_pairs={{0,1},{1,0},{2,3},{3,2},{4,5},{5,4},{6,7},{7,6},{8,9},{9,8},{10,11... | collective-permute-start | bytes 786440 | tf_op jit(solution)/shard_map/ppermute | solution.py:38
  318.2 31.9 %collective-permute-start.20 = (bf16[32,4096]{1,0:T(8,128)(2,1)}, bf16[32,4096]{1,0:T(8,128)(2,1)S(1)}, u32[]{:S(2)}, u32[]{:S(2)}) collective-permute-start(bf16[32,4096]{1,0:T(8,128)(2,1)} %get-tuple-element.97), channel_id=1, source_target_pairs={{0,2},{1,3},{2,0},{3,1},{4,6},{5,7},{6,4},{7,5},{8,10},{9,11},{10,... | collective-permute-start | bytes 786440 | tf_op jit(solution)/shard_map/ppermute | solution.py:38
  318.2 39.6 %collective-permute-start.21 = (bf16[32,4096]{1,0:T(8,128)(2,1)}, bf16[32,4096]{1,0:T(8,128)(2,1)S(1)}, u32[]{:S(2)}, u32[]{:S(2)}) collective-permute-start(bf16[32,4096]{1,0:T(8,128)(2,1)} %get-tuple-element.98), channel_id=1, source_target_pairs={{0,3},{1,2},{2,1},{3,0},{4,7},{5,6},{6,5},{7,4},{8,11},{9,10},{10,... | collective-permute-start | bytes 786440 | tf_op jit(solution)/shard_map/ppermute | solution.py:38
  360.2 39.3 %all-to-all-start.5 = ((bf16[8,48,4096]{2,1,0:T(8,128)(2,1)}), bf16[8,48,4096]{2,1,0:T(8,128)(2,1)}, u32[]{:S(2)}, u32[]{:S(2)}) async-start(bf16[8,48,4096]{2,1,0:T(8,128)(2,1)} %bitcast.17), calls=%async_computation.5 | async-start | bytes 6291456 | tf_op jit(solution)/shard_map/all_to_all | solution.py:372
  365.3 10.6 %collective-permute-start.29 = (bf16[32,4096]{1,0:T(8,128)(2,1)S(1)}, bf16[32,4096]{1,0:T(8,128)(2,1)S(1)}, u32[]{:S(2)}, u32[]{:S(2)}) collective-permute-start(bf16[32,4096]{1,0:T(8,128)(2,1)S(1)} %copy-done.13), channel_id=1, source_target_pairs={{0,3},{1,2},{2,1},{3,0},{4,7},{5,6},{6,5},{7,4},{8,11},{9,10},{10,... | collective-permute-start | bytes 786440 | tf_op jit(solution)/shard_map/ppermute | solution.py:38
  386.6 29.8 %copy-start.22 = (f32[32,4096]{1,0:T(8,128)S(1)}, f32[32,4096]{1,0:T(8,128)}, u32[]{:S(2)}) copy-start(f32[32,4096]{1,0:T(8,128)} %get-tuple-element.107) | copy-start | bytes 1572868
  386.6 18.5 %collective-permute-start.25 = (bf16[32,4096]{1,0:T(8,128)(2,1)}, bf16[32,4096]{1,0:T(8,128)(2,1)S(1)}, u32[]{:S(2)}, u32[]{:S(2)}) collective-permute-start(bf16[32,4096]{1,0:T(8,128)(2,1)} %get-tuple-element.108), channel_id=1, source_target_pairs={{0,1},{1,0},{2,3},{3,2},{4,5},{5,4},{6,7},{7,6},{8,9},{9,8},{10,11... | collective-permute-start | bytes 786440 | tf_op jit(solution)/shard_map/ppermute | solution.py:38
  386.6 19.9 %collective-permute-start.26 = (bf16[32,4096]{1,0:T(8,128)(2,1)}, bf16[32,4096]{1,0:T(8,128)(2,1)S(1)}, u32[]{:S(2)}, u32[]{:S(2)}) collective-permute-start(bf16[32,4096]{1,0:T(8,128)(2,1)} %get-tuple-element.109), channel_id=1, source_target_pairs={{0,2},{1,3},{2,0},{3,1},{4,6},{5,7},{6,4},{7,5},{8,10},{9,11},{10,... | collective-permute-start | bytes 786440 | tf_op jit(solution)/shard_map/ppermute | solution.py:38
  387.9 28.5 %collective-permute-start.27 = (bf16[32,4096]{1,0:T(8,128)(2,1)}, bf16[32,4096]{1,0:T(8,128)(2,1)S(1)}, u32[]{:S(2)}, u32[]{:S(2)}) collective-permute-start(bf16[32,4096]{1,0:T(8,128)(2,1)} %get-tuple-element.110), channel_id=1, source_target_pairs={{0,3},{1,2},{2,1},{3,0},{4,7},{5,6},{6,5},{7,4},{8,11},{9,10},{10,... | collective-permute-start | bytes 786440 | tf_op jit(solution)/shard_map/ppermute | solution.py:38
  403.9 30.8 %copy-start.21 = (f32[32,4096]{1,0:T(8,128)S(1)}, f32[32,4096]{1,0:T(8,128)}, u32[]{:S(2)}) copy-start(f32[32,4096]{1,0:T(8,128)} %get-tuple-element.121) | copy-start | bytes 1572868
  403.9 22.4 %collective-permute-start.30 = (bf16[32,4096]{1,0:T(8,128)(2,1)}, bf16[32,4096]{1,0:T(8,128)(2,1)S(1)}, u32[]{:S(2)}, u32[]{:S(2)}) collective-permute-start(bf16[32,4096]{1,0:T(8,128)(2,1)} %get-tuple-element.122), channel_id=1, source_target_pairs={{0,1},{1,0},{2,3},{3,2},{4,5},{5,4},{6,7},{7,6},{8,9},{9,8},{10,11... | collective-permute-start | bytes 786440 | tf_op jit(solution)/shard_map/ppermute | solution.py:38
  403.9 23.1 %collective-permute-start.31 = (bf16[32,4096]{1,0:T(8,128)(2,1)}, bf16[32,4096]{1,0:T(8,128)(2,1)S(1)}, u32[]{:S(2)}, u32[]{:S(2)}) collective-permute-start(bf16[32,4096]{1,0:T(8,128)(2,1)} %get-tuple-element.123), channel_id=1, source_target_pairs={{0,2},{1,3},{2,0},{3,1},{4,6},{5,7},{6,4},{7,5},{8,10},{9,11},{10,... | collective-permute-start | bytes 786440 | tf_op jit(solution)/shard_map/ppermute | solution.py:38
  405.1 29.5 %collective-permute-start.32 = (bf16[32,4096]{1,0:T(8,128)(2,1)}, bf16[32,4096]{1,0:T(8,128)(2,1)S(1)}, u32[]{:S(2)}, u32[]{:S(2)}) collective-permute-start(bf16[32,4096]{1,0:T(8,128)(2,1)} %get-tuple-element.124), channel_id=1, source_target_pairs={{0,3},{1,2},{2,1},{3,0},{4,7},{5,6},{6,5},{7,4},{8,11},{9,10},{10,... | collective-permute-start | bytes 786440 | tf_op jit(solution)/shard_map/ppermute | solution.py:38
  417.8 19.9 %copy-start.10 = (f32[128,2048]{1,0:T(8,128)S(1)}, f32[128,2048]{1,0:T(8,128)}, u32[]{:S(2)}) copy-start(f32[128,2048]{1,0:T(8,128)} %get-tuple-element.129) | copy-start | bytes 3145732
  417.8 18.0 %collective-permute-start.33 = (bf16[128,2048]{1,0:T(8,128)(2,1)}, bf16[128,2048]{1,0:T(8,128)(2,1)S(1)}, u32[]{:S(2)}, u32[]{:S(2)}) collective-permute-start(bf16[128,2048]{1,0:T(8,128)(2,1)} %get-tuple-element.128), channel_id=1, source_target_pairs={{0,16},{4,20},{8,24},{12,28},{16,0},{20,4},{24,8},{28,12},{1,17},{... | collective-permute-start | bytes 1572872 | tf_op jit(solution)/shard_map/ppermute | solution.py:38
  426.2 11.4 %collective-permute-start.36 = (bf16[128,2048]{1,0:T(8,128)(2,1)}, bf16[128,2048]{1,0:T(8,128)(2,1)S(1)}, u32[]{:S(2)}, u32[]{:S(2)}) collective-permute-start(bf16[128,2048]{1,0:T(8,128)(2,1)} %get-tuple-element.130), channel_id=1, source_target_pairs={{0,8},{4,12},{8,0},{12,4},{16,24},{20,28},{24,16},{28,20},{1,9},{5... | collective-permute-start | bytes 1572872 | tf_op jit(solution)/shard_map/ppermute | solution.py:38
  437.2 5.7 %collective-permute-start.34 = (bf16[64,2048]{1,0:T(8,128)(2,1)S(1)}, bf16[64,2048]{1,0:T(8,128)(2,1)S(1)}, u32[]{:S(2)}, u32[]{:S(2)}) collective-permute-start(bf16[64,2048]{1,0:T(8,128)(2,1)S(1)} %split.57), channel_id=1, source_target_pairs={{0,8},{4,12},{8,0},{12,4},{16,24},{20,28},{24,16},{28,20},{1,9},{5... | collective-permute-start | bytes 786440 | tf_op jit(solution)/shard_map/ppermute | solution.py:38
  437.8 9.5 %collective-permute-start.37 = (bf16[64,2048]{1,0:T(8,128)(2,1)S(1)}, bf16[64,2048]{1,0:T(8,128)(2,1)S(1)}, u32[]{:S(2)}, u32[]{:S(2)}) collective-permute-start(bf16[64,2048]{1,0:T(8,128)(2,1)S(1)} %split.56), channel_id=1, source_target_pairs={{0,16},{4,20},{8,24},{12,28},{16,0},{20,4},{24,8},{28,12},{1,17},{... | collective-permute-start | bytes 786440 | tf_op jit(solution)/shard_map/ppermute | solution.py:38
  443.0 5.3 %collective-permute-start.35 = (bf16[32,2048]{1,0:T(8,128)(2,1)S(1)}, bf16[32,2048]{1,0:T(8,128)(2,1)S(1)}, u32[]{:S(2)}, u32[]{:S(2)}) collective-permute-start(bf16[32,2048]{1,0:T(8,128)(2,1)S(1)} %split.59), channel_id=1, source_target_pairs={{0,4},{4,0},{8,12},{12,8},{16,20},{20,16},{24,28},{28,24},{1,5},{5... | collective-permute-start | bytes 393224 | tf_op jit(solution)/shard_map/ppermute | solution.py:38
  447.4 1.5 collective-permute-start.38
  (22 other events, 101.3 us)

commit v5 on v4

v5 whole, which is shorter than its diff:
```python
import functools

import jax
import jax.numpy as jnp
import numpy as np
from jax import lax
from jax.experimental import pallas as pl
from jax.experimental.pallas import tpu as pltpu
from jax.sharding import PartitionSpec as P

BLOCK_TOK = 32
EPSILON = 1e-06
AXES = ("node", "local")
LANES = 128
TILES = 4
BF16, F32, I32 = jnp.bfloat16, jnp.float32, jnp.int32
ANYWHERE = pl.BlockSpec(memory_space=pl.ANY)
PARAMS = pltpu.CompilerParams(vmem_limit_bytes=60 * 2**20)


def fence(arrays, after):
    token = sum(a[:16, :LANES].astype(F32) for a in after)

    def kernel(*refs):
        pass

    return list(pl.pallas_call(
        kernel,
        out_shape=[jax.ShapeDtypeStruct(a.shape, a.dtype) for a in arrays],
        in_specs=[ANYWHERE] * (len(arrays) + 1),
        out_specs=[ANYWHERE] * len(arrays),
        input_output_aliases={i: i for i in range(len(arrays))},
    )(*arrays, token))


def swap(array, axis, bits):
    size = lax.axis_size(axis)
    return lax.ppermute(array, axis, [(i, i ^ bits) for i in range(size)])


def swaps(parts, axis, first, last):
    return [swap(parts[k], axis, k) for k in range(first, last)]


def bit_order(size, last_first):
    bits = [1 << i for i in range(size.bit_length() - 1)]
    return bits[:1] + bits[:0:-1] if last_first else bits


def chain_step(arrays, axis, step):
    size = lax.axis_size(axis)
    rightward = [(i, i + 1) for i in range(step - 1, size - 1)]
    leftward = [(size - 1 - i, size - 2 - i) for i in range(step - 1, size - 1)]
    return [lax.ppermute(a, axis, way) for a, way in zip(arrays, (rightward, leftward))]


def chain_offsets(size):
    return [0] + [offset for d in range(1, size) for offset in (-d, d)]


def chain_sum(own, parts, axis):
    size = lax.axis_size(axis)
    left, right = parts[0::2], parts[1::2]
    for step in range(1, size):
        ways = [(i, i + 1) for i in range(step)], [(size - 1 - i, size - 2 - i) for i in range(step)]
        moved = [
            lax.ppermute(side[size - 1 - step].astype(BF16), axis, way)
            for side, way in zip((right, left), ways)
        ]
        if step < size - 1:
            at = size - 2 - step
            right[at], left[at] = (
                side[at].astype(F32) + came.astype(F32) for side, came in zip((right, left), moved)
            )
    return own, moved


def gather_doubling(array, axis, bits):
    for bit in bits:
        array = jnp.concatenate([array, swap(array, axis, bit)])
    return array


def gathered_from(bits):
    found = [0]
    for bit in bits:
        found += [k ^ bit for k in found]
    return found


def sum_halving(keep, give, axis, bits):
    for step, bit in enumerate(bits[::-1]):
        if step:
            keep, give = jnp.split(keep, 2)
        keep = keep + swap(give.astype(BF16), axis, bit).astype(F32)
    return keep.astype(BF16)


def below(rows):
    at = np.arange(rows)
    same = at[:, None] // BLOCK_TOK == at[None, :] // BLOCK_TOK
    return (same & (at[None, :] < at[:, None])).astype(BF16)


def choose(table, lane, row_group, slot_group, turn, before):
    select = lax.broadcasted_iota(I32, (table.shape[1], lane.shape[1]), 0) == lane
    weight = jnp.dot(table, select.astype(BF16), preferred_element_type=F32)
    mask = jnp.where((weight > 0) & (row_group == slot_group), 1.0, 0.0)
    rank = jnp.dot(before, mask.astype(BF16), preferred_element_type=F32)
    place = jnp.where(rank == turn, mask, 0.0)
    return place.astype(BF16), (place * weight).astype(BF16)


def gather_rows(place, rows):
    return lax.dot_general(
        place, rows, (((0,), (0,)), ((), ())), preferred_element_type=F32
    ).astype(BF16)


def bits_of(labels, local, peers, chained):
    if not chained:
        return labels
    source = labels + local
    return jnp.where((source >= 0) & (source < peers), source ^ local, -1)


def pick_kernel(count, peers, chain_in, chain_out, ids, *refs):
    parts, refs = refs[:count], refs[count:]
    tables, refs = refs[:count], refs[count:]
    lane, slot_group, turn, before, in_column, in_row, out_column, out, mixing, place = refs

    @pl.when(pl.program_id(0) == 0)
    def _():
        local = ids[1]
        table = jnp.concatenate([t[...] for t in tables])
        row_group = bits_of(in_column[...], local, peers, chain_in)
        place[...], weights = choose(
            table, lane[...] + local, row_group, slot_group[...], turn[...], before[...]
        )
        if chain_in != chain_out:
            shape = mixing.shape[0], weights.shape[0]
            same = bits_of(out_column[...], local, peers, chain_out) == bits_of(
                in_row[...], local, peers, chain_in
            )
            row = lax.broadcasted_iota(I32, shape, 0) & (BLOCK_TOK - 1)
            column = lax.broadcasted_iota(I32, shape, 1) & (BLOCK_TOK - 1)
            order = jnp.where(same & (row == column), 1.0, 0.0).astype(BF16)
            weights = jnp.dot(order, weights, preferred_element_type=F32).astype(BF16)
        mixing[...] = weights

    out[...] = gather_rows(place[...], jnp.concatenate([p[...] for p in parts]))


def whole_block(array):
    return pl.BlockSpec(array.shape, lambda j: (0,) * array.ndim)


def by_token(labels):
    return np.repeat(np.array(labels, np.int32), BLOCK_TOK)


def pick(parts, block, ids, peers, capacity, features, chain_in, chain_out):
    nodes = lax.axis_size("node")
    slots = nodes * peers * capacity
    slot = np.arange(slots, dtype=np.int32)[None, :]
    labels = chain_offsets(peers), list(range(peers))
    in_labels, out_labels = by_token(labels[not chain_in]), by_token(labels[not chain_out])
    rows, tile = len(in_labels), features // TILES
    small = (
        slot // (capacity * peers) * peers,
        slot // capacity % peers,
        (slot % capacity).astype(np.float32),
        below(rows),
        in_labels[:, None],
        in_labels[None, :],
        out_labels[:, None],
    )
    return pl.pallas_call(
        functools.partial(pick_kernel, len(parts), peers, chain_in, chain_out),
        grid=(TILES,),
        out_shape=[
            jax.ShapeDtypeStruct((slots, features), BF16),
            jax.ShapeDtypeStruct((len(out_labels), slots), BF16),
        ],
        in_specs=[pl.BlockSpec(memory_space=pltpu.SMEM)]
        + [pl.BlockSpec((BLOCK_TOK, tile), lambda j: (block, j))] * len(parts)
        + [pl.BlockSpec((BLOCK_TOK, LANES), lambda j: (block, features // LANES))] * len(parts)
        + [whole_block(a) for a in small],
        out_specs=[
            pl.BlockSpec((slots, tile), lambda j: (0, j)),
            pl.BlockSpec((len(out_labels), slots), lambda j: (0, 0)),
        ],
        scratch_shapes=[pltpu.VMEM((rows, slots), BF16)],
        compiler_params=PARAMS,
        cost_estimate=pl.CostEstimate(
            flops=2 * rows * slots * features,
            bytes_accessed=2 * (rows + slots) * features,
            transcendentals=0,
        ),
    )(ids, *parts, *parts, *small)


def pick_cross_kernel(order, cuts, peers, ids, a0, a1, b0, b1, t0, t1, *refs):
    peer, group_a, group_b, slot_group, turn, before = refs[:6]
    outs, (mixing_a, mixing_b, place_a, place_b) = refs[6:-4], refs[-4:]
    step = pl.program_id(0)

    @pl.when(step == 0)
    def _():
        known = jnp.concatenate([t0[...], t1[...]])
        lane = (peer[...] ^ ids[1]) + ids[0] * peers
        common = slot_group[...], turn[...], before[...]
        place_b[...], mixing_b[...] = choose(known, lane, group_b[...], *common)
        back = [order.index(k) * BLOCK_TOK for k in range(len(order))]
        known = jnp.concatenate([known[at : at + BLOCK_TOK] for at in back])
        place_a[...], mixing_a[...] = choose(known, lane, group_a[...], *common)

    def store(place, first_rows, last_rows):
        result = gather_rows(place[...], jnp.concatenate([first_rows[...], last_rows[...]]))
        for out, first, last in zip(outs, cuts[:-1], cuts[1:]):
            out[...] = result[first:last]

    @pl.when(step < TILES // 2)
    def _():
        store(place_a, a0, a1)

    @pl.when(step >= TILES // 2)
    def _():
        store(place_b, b0, b1)


def in_first_half(shape):
    return pl.BlockSpec(shape, lambda j: (0, jnp.minimum(j, TILES // 2 - 1)))


def in_second_half(shape):
    return pl.BlockSpec(shape, lambda j: (0, jnp.maximum(j - TILES // 2, 0)))


def pick_cross(rows_a, rows_b, order_a, order_b, ids, peers, capacity, features, cuts):
    part = rows_a[0].shape[0]
    rows = 2 * part
    nodes = rows // BLOCK_TOK
    slots = cuts[-1]
    slot = np.arange(slots, dtype=np.int32)[None, :]
    tile = features // TILES
    small = (
        slot // (capacity * nodes),
        by_token(order_a)[:, None],
        by_token(order_b)[:, None],
        slot // capacity % nodes,
        (slot % capacity).astype(np.float32),
        below(rows),
    )
    sizes = [last - first for first, last in zip(cuts[:-1], cuts[1:])]
    results = pl.pallas_call(
        functools.partial(pick_cross_kernel, order_b, cuts, peers),
        grid=(TILES,),
        out_shape=[jax.ShapeDtypeStruct((size, features), BF16) for size in sizes]
        + [jax.ShapeDtypeStruct((rows, slots), BF16)] * 2,
        in_specs=[pl.BlockSpec(memory_space=pltpu.SMEM)]
        + [in_first_half((part, tile))] * 2
        + [in_second_half((part, tile))] * 2
        + [pl.BlockSpec((part, LANES), lambda j: (0, features // 2 // LANES))] * 2
        + [whole_block(a) for a in small],
        out_specs=[pl.BlockSpec((size, tile), lambda j: (0, j)) for size in sizes]
        + [pl.BlockSpec((rows, slots), lambda j: (0, 0))] * 2,
        scratch_shapes=[pltpu.VMEM((rows, slots), BF16)] * 2,
        compiler_params=PARAMS,
        cost_estimate=pl.CostEstimate(
            flops=2 * rows * slots * features,
            bytes_accessed=2 * (rows + slots) * features,
            transcendentals=0,
        ),
    )(ids, *rows_a, *rows_b, *rows_b, *small)
    return list(results[:-2]), results[-2], results[-1]


def mix_kernel(mixing, landed, own, *outs):
    result = jnp.dot(mixing[...], landed[...], preferred_element_type=F32)
    own[...] = result[:BLOCK_TOK]
    for k, out in enumerate(outs):
        out[...] = result[(k + 1) * BLOCK_TOK : (k + 2) * BLOCK_TOK].astype(BF16)


def mix(mixing, landed):
    rows, slots = mixing.shape
    features = landed.shape[1]
    tile = features // TILES
    count = rows // BLOCK_TOK
    own, *parts = pl.pallas_call(
        mix_kernel,
        grid=(TILES,),
        out_shape=[jax.ShapeDtypeStruct((BLOCK_TOK, features), F32)]
        + [jax.ShapeDtypeStruct((BLOCK_TOK, features), BF16)] * (count - 1),
        in_specs=[whole_block(mixing), pl.BlockSpec((slots, tile), lambda j: (0, j))],
        out_specs=[pl.BlockSpec((BLOCK_TOK, tile), lambda j: (0, j))] * count,
        compiler_params=PARAMS,
        cost_estimate=pl.CostEstimate(
            flops=2 * rows * slots * features,
            bytes_accessed=2 * (rows + slots) * features,
            transcendentals=0,
        ),
    )(mixing, landed)
    return own, parts


def mix_cross_kernel(mixing_a, mixing_b, *refs):
    landed, (keep_a, give_a, keep_b, give_b) = refs[:-4], refs[-4:]
    step = pl.program_id(0)
    half = keep_a.shape[0]
    rows = jnp.concatenate([part[...] for part in landed])

    def store(mixing, keep, give):
        result = jnp.dot(mixing[...], rows, preferred_element_type=F32)
        keep[...] = result[:half]
        give[...] = result[half:].astype(BF16)

    @pl.when(step < TILES // 2)
    def _():
        store(mixing_a, keep_a, give_a)

    @pl.when(step >= TILES // 2)
    def _():
        store(mixing_b, keep_b, give_b)


def mix_cross(mixing_a, mixing_b, landed):
    rows, slots = mixing_a.shape
    features = landed[0].shape[1]
    tile = features // TILES
    shape = (rows // 2, features // 2)
    return pl.pallas_call(
        mix_cross_kernel,
        grid=(TILES,),
        out_shape=[jax.ShapeDtypeStruct(shape, F32), jax.ShapeDtypeStruct(shape, BF16)] * 2,
        in_specs=[whole_block(mixing_a), whole_block(mixing_b)]
        + [pl.BlockSpec((part.shape[0], tile), lambda j: (0, j)) for part in landed],
        out_specs=[in_first_half((rows // 2, tile))] * 2 + [in_second_half((rows // 2, tile))] * 2,
        compiler_params=PARAMS,
        cost_estimate=pl.CostEstimate(
            flops=2 * rows * slots * features,
            bytes_accessed=2 * (rows + slots) * features,
            transcendentals=0,
        ),
    )(mixing_a, mixing_b, *landed)


def expert_kernel(count, first_tiles, *refs):
    parts, (gate_ref, up_ref, down_ref) = refs[:count], refs[count : count + 3]
    outs, (joined, hidden) = refs[count + 3 : -2], refs[-2:]
    step = pl.program_id(0)
    x_ref = parts[0] if count == 1 else joined

    if count > 1:

        @pl.when(step == 0)
        def _():
            joined[...] = jnp.concatenate([part[...] for part in parts])

    @pl.when(step < first_tiles)
    def _():
        x = x_ref[...]
        gate_pre = jnp.dot(x, gate_ref[...], preferred_element_type=F32)
        up_pre = jnp.dot(x, up_ref[...], preferred_element_type=F32)
        hidden[step] = (gate_pre / (1 + jnp.exp(-gate_pre)) * up_pre).astype(BF16)

    @pl.when(step >= first_tiles)
    def _():
        rows = jnp.concatenate([hidden[i] for i in range(first_tiles)], axis=1)
        result = jnp.dot(rows, down_ref[...], preferred_element_type=F32).astype(BF16)
        at = 0
        for out in outs:
            out[...] = result[at : at + out.shape[0]]
            at += out.shape[0]


def expert(parts, gate_weight, up_weight, down_weight):
    rows = sum(part.shape[0] for part in parts)
    features, hidden = gate_weight.shape
    tile = 256
    first_tiles = hidden // tile
    out_tile = features // TILES

    def first(i):
        return jnp.minimum(i, first_tiles - 1)

    def second(i):
        return jnp.maximum(i - first_tiles, 0)

    return pl.pallas_call(
        functools.partial(expert_kernel, len(parts), first_tiles),
        grid=(first_tiles + TILES,),
        out_shape=[jax.ShapeDtypeStruct(part.shape, BF16) for part in parts],
        in_specs=[whole_block(part) for part in parts]
        + [
            pl.BlockSpec((features, tile), lambda i: (0, first(i))),
            pl.BlockSpec((features, tile), lambda i: (0, first(i))),
            pl.BlockSpec((hidden, out_tile), lambda i: (0, second(i))),
        ],
        out_specs=[
            pl.BlockSpec((part.shape[0], out_tile), lambda i: (0, second(i))) for part in parts
        ],
        scratch_shapes=[
            pltpu.VMEM((rows if len(parts) > 1 else 16, features), BF16),
            pltpu.VMEM((first_tiles, rows, tile), BF16),
        ],
        compiler_params=PARAMS,
        cost_estimate=pl.CostEstimate(
            flops=6 * rows * features * hidden,
            bytes_accessed=6 * features * hidden + 4 * rows * features,
            transcendentals=rows * hidden,
        ),
    )(*parts, gate_weight, up_weight, down_weight)


def prepare_kernel(tokens, gain, routes, gates, placement, *outs):
    experts = placement.shape[0]
    features = tokens.shape[1]
    chosen = gates[...] / jnp.sum(gates[...], axis=0, keepdims=True)
    columns = jnp.concatenate([routes[...].astype(F32), chosen]).T
    count = routes.shape[0]
    lanes = outs[0].shape[1] - features
    lane = lax.broadcasted_iota(I32, (1, lanes), 1)
    named = jnp.full((1, lanes), -1.0, F32)
    for e in range(experts):
        named = jnp.where(lane == e, placement[e].astype(F32), named)
    start = 0
    for out in outs:
        rows = out.shape[0]
        at = slice(start, start + rows)
        start += rows
        values = tokens[at].astype(F32)
        rescale = lax.rsqrt(jnp.mean(values * values, axis=-1, keepdims=True) + EPSILON)
        for c in range(features // LANES):
            to = slice(c * LANES, (c + 1) * LANES)
            out[:, to] = (values[:, to] * rescale * gain[c : c + 1].astype(F32)).astype(BF16)
        table = jnp.zeros((rows, lanes), F32)
        for k in range(count):
            held = columns[at, k : k + 1] == named
            table = jnp.where(held, columns[at, count + k : count + k + 1], table)
        out[:, features:] = table.astype(BF16)


def prepare(tokens, norm_gain, routes, route_gates, placement, sizes):
    features = tokens.shape[1]
    width = features + -(-placement.shape[0] // LANES) * LANES
    vmem = pl.BlockSpec(memory_space=pltpu.VMEM)
    return pl.pallas_call(
        prepare_kernel,
        out_shape=[jax.ShapeDtypeStruct((size, width), BF16) for size in sizes],
        in_specs=[vmem] * 4 + [pl.BlockSpec(memory_space=pltpu.SMEM)],
        compiler_params=PARAMS,
    )(tokens, norm_gain.reshape(-1, LANES), routes.T, route_gates.T, placement)


def to_experts(rows):
    return lax.all_to_all(rows, "node", 0, 0, tiled=True)


def total(own, parts):
    for part in parts:
        own = own + part.astype(F32)
    return own.astype(BF16)


def body(tokens, norm_gain, routes, route_gates, placement, gate_weight, up_weight, down_weight):
    nodes, peers = lax.axis_size("node"), lax.axis_size("local")
    node, local = lax.axis_index("node"), lax.axis_index("local")
    experts = placement.shape[0]
    features = tokens.shape[1]
    capacity = BLOCK_TOK * routes.shape[1] // experts * 3 // 2
    slots = experts * capacity
    half = features // 2
    weights = (gate_weight[0], up_weight[0], down_weight[0])
    sizes = [BLOCK_TOK, 2 * BLOCK_TOK, BLOCK_TOK]
    sent0, sent12, sent3 = prepare(tokens, norm_gain, routes, route_gates, placement, sizes)

    bits_a, bits_b = bit_order(nodes, False), bit_order(nodes, True)
    ids = jnp.stack([node, local]).astype(I32)
    near = ids, peers, capacity, features
    size = slots // peers
    cuts = [size * k for k in range(peers - 1)]
    cuts += [cuts[-1] + size // 3, cuts[-1] + size // 3 * 2, size * (peers - 1)]
    cuts += [slots - size // 3, slots]

    near0 = swaps([sent0] * peers, "local", 1, peers)
    pair = jnp.concatenate([sent3, swap(sent3, "node", bits_a[0])])
    rows_a = gather_doubling(pair[:, :half], "node", bits_a[1:-1])
    rows_b = gather_doubling(pair[:, half:], "node", bits_b[1:-1])
    sent12, rows_a, rows_b = fence([sent12, rows_a, rows_b], near0)
    rows_a = [rows_a, swap(rows_a, "node", bits_a[-1])]
    rows_b = [rows_b, swap(rows_b, "node", bits_b[-1])]
    chain = chain_step([sent12, sent12], "local", 1)
    outbound0, mixing0 = pick([sent0] + near0, 0, *near, chain_in=False, chain_out=True)
    outbound3, mixing3a, mixing3b = pick_cross(
        rows_a,
        rows_b,
        gathered_from(bits_a),
        gathered_from(bits_b),
        *near,
        cuts,
    )

    outbound0, *outbound3 = fence([outbound0] + outbound3, chain)
    arrived0 = to_experts(outbound0)
    parts12 = [sent12] + chain
    for step in range(2, peers):
        chain = chain_step(chain, "local", step)
        parts12 += chain
    own3, *outbound3 = outbound3
    last2, last1 = peers - 2, peers - 1
    third = [swap(outbound3[-5], "local", last2)]
    (late_ids,) = fence([ids], third)
    third.append(swap(outbound3[-4], "local", last2))
    outbound1, mixing1 = pick(parts12, 0, late_ids, *near[1:], chain_in=True, chain_out=False)
    (third[1],) = fence([third[1]], [outbound1])

    outbound1, ids, *later3 = fence(
        [outbound1, ids] + outbound3[:-5] + outbound3[-3:], [arrived0, third[1]]
    )
    arrived1 = to_experts(outbound1)
    early = [swap(part, "local", k + 1) for k, part in enumerate(later3[:-3])]
    third.append(swap(later3[-3], "local", last2))
    third.append(swap(later3[-2], "local", last1))
    outbound2, mixing2 = pick(parts12, 1, ids, *near[1:], chain_in=True, chain_out=False)
    (out0,) = expert([arrived0], *weights)

    outbound2, last3 = fence([outbound2, later3[-1]], [arrived1, out0] + early + third[2:])
    arrived2 = to_experts(outbound2)
    last3 = swap(last3, "local", last1)
    (out1,) = expert([arrived1], *weights)
    (last3,) = fence([last3], [out1])
    out3 = list(expert([own3] + early + third + [last3], *weights))

    out0, *out3 = fence([out0] + out3, [arrived2, out1])
    landed0 = to_experts(out0)
    landed3 = out3[:1] + swaps(out3, "local", 1, last1)
    landed3 += [swap(part, "local", last2) for part in out3[-4:-2]]
    (out2,) = expert([arrived2], *weights)

    out1, later3, mixing0 = fence([out1, out3[-2], mixing0], [landed0, out2] + landed3[1:])
    landed1 = to_experts(out1)
    landed3.append(swap(later3, "local", last1))
    own0, parts0 = chain_sum(*mix(mixing0, landed0), "local")

    out2, last3, mixing1 = fence([out2, out3[-1], mixing1], [landed1, landed3[-1]] + parts0)
    landed2 = to_experts(out2)
    landed3.append(swap(last3, "local", last1))
    own1, parts1 = mix(mixing1, landed1)
    parts1 = swaps([None] + parts1, "local", 1, peers)
    cross = mix_cross(mixing3a, mixing3b, landed3)
    piece0 = total(own0, parts0)

    own2, parts2 = mix(mixing2, landed2)
    parts2 = swaps([None] + parts2, "local", 1, peers)
    piece1 = total(own1, parts1)
    piece3 = jnp.concatenate(
        [sum_halving(*cross[:2], "node", bits_a), sum_halving(*cross[2:], "node", bits_b)], axis=1
    )
    piece2 = total(own2, parts2)
    return jnp.concatenate([piece0, piece1, piece2, piece3], axis=0)


def solution(mesh):
    rows = P(AXES, None)
    stacked = P(AXES, None, None)
    in_specs = (rows, P(), rows, rows, P(), stacked, stacked, stacked)
    return jax.shard_map(body, mesh=mesh, in_specs=in_specs, out_specs=rows, check_vma=False)
```

time: 452 us -> 416 us (0.920)
  waiting for transfers between devices: 210 us -> 166 us
  local copies, waits for them, and re-layouts: 22.2 us -> 10.4 us
  other arithmetic: 16 us -> 26.4 us
  starting transfers between devices: 92.9 us -> 101 us
    ppermute x33 -> x32, waiting for transfers between devices: 170 us -> 115 us  [swap(): return lax.ppermute(array, axis, [(i, i ^ bits) for i in range(size)])]
    ppermute x0 -> x6, waiting for transfers between devices: none -> 29.9 us  [chain_sum(): lax.ppermute(side[size - 1 - step].astype(BF16), axis, way)]
    all_to_all x6, waiting for transfers between devices: 20.5 us -> 6.85 us  [to_experts(): return lax.all_to_all(rows, 'node', 0, 0, tiled=True)]
    ppermute x33 -> x32, starting transfers between devices: 45.4 us -> 33 us  [swap(): return lax.ppermute(array, axis, [(i, i ^ bits) for i in range(size)])]
    ppermute x0 -> x6, starting transfers between devices: none -> 11.2 us  [chain_sum(): lax.ppermute(side[size - 1 - step].astype(BF16), axis, way)]
    all_to_all x6, starting transfers between devices: 33.1 us -> 41.2 us  [to_experts(): return lax.all_to_all(rows, 'node', 0, 0, tiled=True)]
    unnamed x85 -> x72, local copies, waits for them, and re-layouts: 16.2 us -> 9.5 us
    ppermute x6, waiting for transfers between devices: 19.3 us -> 14.2 us  [chain_step(): lax.ppermute(a, axis, way)]
  transfers between devices with their start and end apart: 45 -> 50, of which waited for: 27 -> 22; matrix products, arithmetic and copies ran while one was open for 4% -> 4% of each run, Pallas kernels for 23% -> 22%
where the time goes in v5:
time: 416 us; the launch traced here: 414 us
  waiting for transfers between devices  166 us (40%)
  Pallas kernels  110 us (26%)
  starting transfers between devices  101 us (24%)
  other arithmetic  26.4 us (6%)
  local copies, waits for them, and re-layouts  10.4 us (2%)
    ppermute x32, waiting for transfers between devices, swap(): return lax.ppermute(array, axis, [(i, i ^ bits) for i in range(size)])  115 us
    pallas_call x4, Pallas kernels, expert(): pl.pallas_call(functools.partial(expert_kernel, len(parts), first_tiles),...  65.6 us
    all_to_all x6, starting transfers between devices, to_experts(): return lax.all_to_all(rows, 'node', 0, 0, tiled=True)  41.2 us
    ppermute x32, starting transfers between devices, swap(): return lax.ppermute(array, axis, [(i, i ^ bits) for i in range(size)])  33 us
    ppermute x6, waiting for transfers between devices, chain_sum(): lax.ppermute(side[size - 1 - step].astype(BF16), axis, way)  29.9 us
    pallas_call x3, Pallas kernels, pick(): pl.pallas_call(functools.partial(pick_kernel, len(parts), peers, chain_in...  16.5 us
    ppermute x6, starting transfers between devices, chain_step(): lax.ppermute(a, axis, way)  15.4 us
    ppermute x6, waiting for transfers between devices, chain_step(): lax.ppermute(a, axis, way)  14.2 us
  transfers between devices with their start and end apart: 50, of which 22 were waited for; matrix products, arithmetic and copies ran while one was open for 4% of the time, Pallas kernels for 22%

profile of v5, /device:TPU:9, one launch (start us, length us, event | category | flops | bytes accessed | tf_op | source)
XLA Modules:
  0.0 413.5 jit_solution(8949189231568995443)
XLA Ops:
  0.0 2.9 shard_map.325
  2.9 1.3 collective-permute-start.2
  10.4 1.3 collective-permute-start.5
  11.7 10.6 %collective-permute-done.2.refs_3_.refs_7_ = bf16[32,4224]{1,0:T(8,128)(2,1)S(1)} collective-permute-done((bf16[32,4224]{1,0:T(8,128)(2,1)}, bf16[32,4224]{1,0:T(8,128)(2,1)S(1)}, u32[]{:S(2)}, u32[]{:S(2)}) %collective-permute-start.2) | collective-permute-done | bytes 270368 | tf_op jit(solution)/shard_map/ppermute | solution.py:38
  22.2 4.8 %collective-permute-done.1.refs_2_.refs_6_ = bf16[32,4224]{1,0:T(8,128)(2,1)S(1)} collective-permute-done((bf16[32,4224]{1,0:T(8,128)(2,1)}, bf16[32,4224]{1,0:T(8,128)(2,1)S(1)}, u32[]{:S(2)}, u32[]{:S(2)}) %collective-permute-start.1) | collective-permute-done | bytes 270368 | tf_op jit(solution)/shard_map/ppermute | solution.py:38
  29.5 4.1 collective-permute-start.9
  33.5 1.9 collective-permute-start.8
  38.6 5.4 %shard_map.326 = (bf16[384,4096]{1,0:T(8,128)(2,1)}, bf16[224,384]{1,0:T(8,128)(2,1)}) custom-call(s32[2]{0:T(128)} %pad_add_fusion.ids.refs_0_, bf16[32,4224]{1,0:T(8,128)(2,1)} %get-tuple-element.82.refs_0_.refs_4_, bf16[32,4224]{1,0:T(8,128)(2,1)} %copy-done.17, bf16[32,4224]{1,0:T(8,128)(2,1)} %copy-done.16, bf16[32,4224]{1,0:T(8,128)(2,1)} %copy-done.15, ...), custom_call_target="tpu_custom_call" | custom-call | flops 402653184 | bytes 4194304 | tf_op jit(solution)/shard_map/pallas_call | solution.py:178
  44.0 3.7 collective-permute-done.8.refs_1_.refs_8_
  50.0 5.9 %shard_map.328 = (bf16[96,4096]{1,0:T(8,128)(2,1)}, bf16[96,4096]{1,0:T(8,128)(2,1)}, bf16[32,4096]{1,0:T(8,128)(2,1)}, bf16[32,4096]{1,0:T(8,128)(2,1)}, bf16[3...) custom-call(s32[2]{0:T(128)} %pad_add_fusion.ids.refs_0_, ...), custom_call_target="tpu_custom_call" | custom-call | flops 805306368 | bytes 5242880 | tf_op jit(solution)/shard_map/pallas_call | solution.py:256
  56.0 7.3 %all-to-all-start = ((bf16[8,48,4096]{2,1,0:T(8,128)(2,1)}), bf16[8,48,4096]{2,1,0:T(8,128)(2,1)}, u32[]{:S(2)}, u32[]{:S(2)}) async-start(bf16[8,48,4096]{2,1,0:T(8,128)(2,1)} %bitcast.27), calls=%async_computation | async-start | bytes 6291456 | tf_op jit(solution)/shard_map/all_to_all | solution.py:458
  63.3 3.4 collective-permute-start.12
  66.7 1.9 collective-permute-start.11
  68.6 10.4 %collective-permute-done.12.refs_4_.refs_11_ = bf16[64,4224]{1,0:T(8,128)(2,1)S(1)} collective-permute-done((bf16[64,4224]{1,0:T(8,128)(2,1)S(1)}, bf16[64,4224]{1,0:T(8,128)(2,1)S(1)}, u32[]{:S(2)}, u32[]{:S(2)}) %collective-permute-start.12) | collective-permute-done | bytes 540704 | tf_op jit(solution)/shard_map/ppermute | solution.py:54
  79.0 3.4 collective-permute-start.14
  84.1 2.1 collective-permute-start.15
  86.1 13.5 %collective-permute-done.10.refs_2_ = bf16[32,4096]{1,0:T(8,128)(2,1)S(1)} collective-permute-done((bf16[32,4096]{1,0:T(8,128)(2,1)S(1)}, bf16[32,4096]{1,0:T(8,128)(2,1)S(1)}, u32[]{:S(2)}, u32[]{:S(2)}) %collective-permute-start.10) | collective-permute-done | bytes 262176 | tf_op jit(solution)/shard_map/ppermute | solution.py:38
  102.6 5.6 %shard_map.331 = (bf16[384,4096]{1,0:T(8,128)(2,1)}, bf16[128,384]{1,0:T(8,128)(2,1)}) custom-call(s32[2]{0:T(128)} %shard_map.330.ids, bf16[64,4224]{1,0:T(8,128)(2,1)} %get-tuple-element.95.refs_0_.refs_7_, bf16[64,4224]{1,0:T(8,128)(2,1)} %copy-done.4, bf16[64,4224]{1,0:T(8,128)(2,1)} %copy-done.3, bf16[64,4224]{1,0:T(8,128)(2,1)} %copy-done.6, ...), custom_call_target="tpu_custom_call" | custom-call | flops 704643072 | bytes 4980736 | tf_op jit(solution)/shard_map/pallas_call | solution.py:178
  108.1 1.3 slice_convert_fusion.6.refs_1_
  110.1 1.3 convert_add_fusion.6.refs_6_
  111.4 7.1 %all-to-all-start.1 = ((bf16[8,48,4096]{2,1,0:T(8,128)(2,1)}), bf16[8,48,4096]{2,1,0:T(8,128)(2,1)S(1)}, u32[]{:S(2)}, u32[]{:S(2)}) async-start(bf16[8,48,4096]{2,1,0:T(8,128)(2,1)} %bitcast.25), calls=%async_computation.1 | async-start | bytes 6291456 | tf_op jit(solution)/shard_map/all_to_all | solution.py:458
  118.5 2.5 collective-permute-start.16
  122.3 16.5 %shard_map.335.refs_0_ = bf16[384,4096]{1,0:T(8,128)(2,1)} custom-call(bf16[384,4096]{1,0:T(8,128)(2,1)} %bitcast.6.refs_0_, bf16[4096,768]{1,0:T(8,128)(2,1)} %bitcast.36, bf16[4096,768]{1,0:T(8,128)(2,1)} %bitcast.40, bf16[768,4096]{1,0:T(8,128)(2,1)} %bitcast.44), custom_call_target="tpu_custom_call" | custom-call | flops 7247757312 | bytes 25165824 | tf_op jit(solution)/shard_map/pallas_call | solution.py:391
  138.8 5.6 %shard_map.336 = (bf16[384,4096]{1,0:T(8,128)(2,1)}, bf16[128,384]{1,0:T(8,128)(2,1)}) custom-call(s32[2]{0:T(128)} %get-tuple-element.109.ids, bf16[64,4224]{1,0:T(8,128)(2,1)} %get-tuple-element.95.refs_0_.refs_7_, bf16[64,4224]{1,0:T(8,128)(2,1)} %copy-done.4, bf16[64,4224]{1,0:T(8,128)(2,1)} %copy-done.3, bf16[64,4224]{1,0:T(8,128)(2,1)} %copy-done.6, ...), custom_call_target="tpu_custom_call" | custom-call | flops 704643072 | bytes 4980736 | tf_op jit(solution)/shard_map/pallas_call | solution.py:178
  146.1 6.8 %all-to-all-done.1 = bf16[8,48,4096]{2,1,0:T(8,128)(2,1)S(1)} async-done(((bf16[8,48,4096]{2,1,0:T(8,128)(2,1)}), bf16[8,48,4096]{2,1,0:T(8,128)(2,1)S(1)}, u32[]{:S(2)}, u32[]{:S(2)}) %all-to-all-start.1) | async-done | bytes 3145760 | tf_op jit(solution)/shard_map/all_to_all | solution.py:458
  152.9 1.6 convert_add_fusion.5.refs_2_
  154.7 8.7 %all-to-all-start.2 = ((bf16[8,48,4096]{2,1,0:T(8,128)(2,1)}), bf16[8,48,4096]{2,1,0:T(8,128)(2,1)S(1)}, u32[]{:S(2)}, u32[]{:S(2)}) async-start(bf16[8,48,4096]{2,1,0:T(8,128)(2,1)} %bitcast.28), calls=%async_computation.2 | async-start | bytes 6291456 | tf_op jit(solution)/shard_map/all_to_all | solution.py:458
  164.2 16.5 %shard_map.334.refs_0_ = bf16[384,4096]{1,0:T(8,128)(2,1)} custom-call(bf16[384,4096]{1,0:T(8,128)(2,1)} %bitcast.32, bf16[4096,768]{1,0:T(8,128)(2,1)} %bitcast.37, bf16[4096,768]{1,0:T(8,128)(2,1)} %bitcast.41, bf16[768,4096]{1,0:T(8,128)(2,1)} %bitcast.45), custom_call_target="tpu_custom_call" | custom-call | flops 7247757312 | bytes 25165824 | tf_op jit(solution)/shard_map/pallas_call | solution.py:391
  182.0 16.1 %shard_map.339 = (bf16[96,4096]{1,0:T(8,128)(2,1)}, bf16[96,4096]{1,0:T(8,128)(2,1)}, bf16[32,4096]{1,0:T(8,128)(2,1)}, bf16[32,4096]{1,0:T(8,128)(2,1)}, bf16[3...) custom-call(bf16[96,4096]{1,0:T(8,128)(2,1)} %get-tuple-element.105.refs_0_, ...), custom_call_target="tpu_custom_call" | custom-call | flops 7247757312 | bytes 25165824 | tf_op jit(solution)/shard_map/pallas_call | solution.py:391
  198.1 1.6 convert_add_fusion.4.refs_8_
  199.8 6.7 %all-to-all-start.3 = ((bf16[8,48,4096]{2,1,0:T(8,128)(2,1)}), bf16[8,48,4096]{2,1,0:T(8,128)(2,1)S(1)}, u32[]{:S(2)}, u32[]{:S(2)}) async-start(bf16[8,48,4096]{2,1,0:T(8,128)(2,1)} %bitcast.20), calls=%async_computation.3 | async-start | bytes 6291456 | tf_op jit(solution)/shard_map/all_to_all | solution.py:458
  210.9 16.5 %shard_map.341.refs_0_ = bf16[384,4096]{1,0:T(8,128)(2,1)} custom-call(bf16[384,4096]{1,0:T(8,128)(2,1)} %bitcast.30, bf16[4096,768]{1,0:T(8,128)(2,1)} %bitcast.39, bf16[4096,768]{1,0:T(8,128)(2,1)} %bitcast.43, bf16[768,4096]{1,0:T(8,128)(2,1)} %bitcast.47), custom_call_target="tpu_custom_call" | custom-call | flops 7247757312 | bytes 25165824 | tf_op jit(solution)/shard_map/pallas_call | solution.py:391
  227.4 4.5 %collective-permute-done.21.refs_2_ = bf16[32,4096]{1,0:T(8,128)(2,1)S(1)} collective-permute-done((bf16[32,4096]{1,0:T(8,128)(2,1)}, bf16[32,4096]{1,0:T(8,128)(2,1)S(1)}, u32[]{:S(2)}, u32[]{:S(2)}) %collective-permute-start.21) | collective-permute-done | bytes 262176 | tf_op jit(solution)/shard_map/ppermute | solution.py:38
  232.0 5.6 %collective-permute-done.22.refs_3_ = bf16[32,4096]{1,0:T(8,128)(2,1)S(1)} collective-permute-done((bf16[32,4096]{1,0:T(8,128)(2,1)}, bf16[32,4096]{1,0:T(8,128)(2,1)S(1)}, u32[]{:S(2)}, u32[]{:S(2)}) %collective-permute-start.22) | collective-permute-done | bytes 262176 | tf_op jit(solution)/shard_map/ppermute | solution.py:38
  237.6 5.6 %collective-permute-done.23.refs_4_ = bf16[32,4096]{1,0:T(8,128)(2,1)S(1)} collective-permute-done((bf16[32,4096]{1,0:T(8,128)(2,1)}, bf16[32,4096]{1,0:T(8,128)(2,1)S(1)}, u32[]{:S(2)}, u32[]{:S(2)}) %collective-permute-start.23) | collective-permute-done | bytes 262176 | tf_op jit(solution)/shard_map/ppermute | solution.py:38
  243.9 1.6 convert_add_fusion.3.refs_3_
  245.5 4.6 %shard_map.343 = (f32[32,4096]{1,0:T(8,128)}, bf16[32,4096]{1,0:T(8,128)(2,1)}, bf16[32,4096]{1,0:T(8,128)(2,1)}, bf16[32,4096]{1,0:T(8,128)(2,1)}, bf16[32,4096...) custom-call(bf16[224,384]{1,0:T(8,128)(2,1)} %get-tuple-element.128.mixing, ...), custom_call_target="tpu_custom_call" | custom-call | flops 704643072 | bytes 4980736 | tf_op jit(solution)/shard_map/pallas_call | solution.py:291
  250.1 1.3 collective-permute-start.24
  251.5 5.0 %all-to-all-start.4 = ((bf16[8,48,4096]{2,1,0:T(8,128)(2,1)}), bf16[8,48,4096]{2,1,0:T(8,128)(2,1)S(1)}, u32[]{:S(2)}, u32[]{:S(2)}) async-start(bf16[8,48,4096]{2,1,0:T(8,128)(2,1)} %bitcast.16), calls=%async_computation.4 | async-start | bytes 6291456 | tf_op jit(solution)/shard_map/all_to_all | solution.py:458
  257.2 1.4 collective-permute-start.30
  260.2 1.9 collective-permute-start.25
  263.2 1.3 collective-permute-start.28
  264.5 22.5 %collective-permute-done.25 = bf16[32,4096]{1,0:T(8,128)(2,1)S(1)} collective-permute-done((bf16[32,4096]{1,0:T(8,128)(2,1)S(1)}, bf16[32,4096]{1,0:T(8,128)(2,1)S(1)}, u32[]{:S(2)}, u32[]{:S(2)}) %collective-permute-start.25) | collective-permute-done | bytes 262176 | tf_op jit(solution)/shard_map/ppermute | solution.py:67
  287.0 4.1 collective-permute-start.26
  292.2 1.9 collective-permute-start.29
  294.1 1.8 collective-permute-done.26
  296.0 4.9 %collective-permute-done.29 = bf16[32,4096]{1,0:T(8,128)(2,1)} collective-permute-done((bf16[32,4096]{1,0:T(8,128)(2,1)S(1)}, bf16[32,4096]{1,0:T(8,128)(2,1)}, u32[]{:S(2)}, u32[]{:S(2)}) %collective-permute-start.29) | collective-permute-done | bytes 262176 | tf_op jit(solution)/shard_map/ppermute | solution.py:67
  300.9 1.6 convert_add_fusion.2.refs_3_
  302.5 4.4 %shard_map.345 = (f32[32,4096]{1,0:T(8,128)}, bf16[32,4096]{1,0:T(8,128)(2,1)}, bf16[32,4096]{1,0:T(8,128)(2,1)}, bf16[32,4096]{1,0:T(8,128)(2,1)}) custom-call(bf16[128,384]{1,0:T(8,128)(2,1)} %get-tuple-element.140.mixing, bf16[384,4096]{1,0:T(8,128)(2,1)} %bitcast.22), custom_call_target="tpu_custom_call" | custom-call | flops 402653184 | bytes 4194304 | tf_op jit(solution)/shard_map/pallas_call | solution.py:291
  311.1 6.3 %all-to-all-start.5 = ((bf16[8,48,4096]{2,1,0:T(8,128)(2,1)}), bf16[8,48,4096]{2,1,0:T(8,128)(2,1)S(1)}, u32[]{:S(2)}, u32[]{:S(2)}) async-start(bf16[8,48,4096]{2,1,0:T(8,128)(2,1)} %bitcast.18), calls=%async_computation.5 | async-start | bytes 6291456 | tf_op jit(solution)/shard_map/all_to_all | solution.py:458
  317.4 25.0 %collective-permute-done.37.refs_6_ = bf16[32,4096]{1,0:T(8,128)(2,1)} collective-permute-done((bf16[32,4096]{1,0:T(8,128)(2,1)}, bf16[32,4096]{1,0:T(8,128)(2,1)}, u32[]{:S(2)}, u32[]{:S(2)}) %collective-permute-start.37) | collective-permute-done | bytes 262176 | tf_op jit(solution)/shard_map/ppermute | solution.py:38
  342.4 5.7 %shard_map.347 = (f32[128,2048]{1,0:T(8,128)}, bf16[128,2048]{1,0:T(8,128)(2,1)}, f32[128,2048]{1,0:T(8,128)}, bf16[128,2048]{1,0:T(8,128)(2,1)}) custom-call(bf16[256,384]{1,0:T(8,128)(2,1)} %get-tuple-element.151.mixing_a, bf16[256,384]{1,0:T(8,128)(2,1)} %get-tuple-element.152.mixing_b, bf16[96,4096]{1,0:T(8,128)(2,1)} %get-tuple-element.153.refs_0_, ...), custom_call_target="tpu_custom_call" | custom-call | flops 805306368 | bytes 5242880 | tf_op jit(solution)/shard_map/pallas_call | solution.py:333
  350.0 1.9 add_convert_fusion.1
  351.9 14.2 %collective-permute-done.38 = bf16[128,2048]{1,0:T(8,128)(2,1)S(1)} collective-permute-done((bf16[128,2048]{1,0:T(8,128)(2,1)}, bf16[128,2048]{1,0:T(8,128)(2,1)S(1)}, u32[]{:S(2)}, u32[]{:S(2)}) %collective-permute-start.38) | collective-permute-done | bytes 524320 | tf_op jit(solution)/shard_map/ppermute | solution.py:38
  366.1 1.3 convert_add_fusion.1
  368.1 6.9 %collective-permute-done.39 = bf16[64,2048]{1,0:T(8,128)(2,1)S(1)} collective-permute-done((bf16[64,2048]{1,0:T(8,128)(2,1)S(1)}, bf16[64,2048]{1,0:T(8,128)(2,1)S(1)}, u32[]{:S(2)}, u32[]{:S(2)}) %collective-permute-start.39) | collective-permute-done | bytes 262176 | tf_op jit(solution)/shard_map/ppermute | solution.py:38
  375.0 1.4 collective-permute-start.40
  377.6 1.6 copy-done.2
  379.2 4.4 %shard_map.346 = (f32[32,4096]{1,0:T(8,128)}, bf16[32,4096]{1,0:T(8,128)(2,1)}, bf16[32,4096]{1,0:T(8,128)(2,1)}, bf16[32,4096]{1,0:T(8,128)(2,1)}) custom-call(bf16[128,384]{1,0:T(8,128)(2,1)} %get-tuple-element.145.mixing, bf16[384,4096]{1,0:T(8,128)(2,1)} %bitcast.26), custom_call_target="tpu_custom_call" | custom-call | flops 402653184 | bytes 4194304 | tf_op jit(solution)/shard_map/pallas_call | solution.py:291
  383.6 1.8 collective-permute-start.34
  387.8 8.8 %collective-permute-done.34 = bf16[32,4096]{1,0:T(8,128)(2,1)S(1)} collective-permute-done((bf16[32,4096]{1,0:T(8,128)(2,1)}, bf16[32,4096]{1,0:T(8,128)(2,1)S(1)}, u32[]{:S(2)}, u32[]{:S(2)}) %collective-permute-start.34) | collective-permute-done | bytes 262176 | tf_op jit(solution)/shard_map/ppermute | solution.py:38
  396.6 7.1 %collective-permute-done.35 = bf16[32,4096]{1,0:T(8,128)(2,1)S(1)} collective-permute-done((bf16[32,4096]{1,0:T(8,128)(2,1)}, bf16[32,4096]{1,0:T(8,128)(2,1)S(1)}, u32[]{:S(2)}, u32[]{:S(2)}) %collective-permute-start.35) | collective-permute-done | bytes 262176 | tf_op jit(solution)/shard_map/ppermute | solution.py:38
  403.8 6.6 %collective-permute-done.36 = bf16[32,4096]{1,0:T(8,128)(2,1)S(1)} collective-permute-done((bf16[32,4096]{1,0:T(8,128)(2,1)}, bf16[32,4096]{1,0:T(8,128)(2,1)S(1)}, u32[]{:S(2)}, u32[]{:S(2)}) %collective-permute-start.36) | collective-permute-done | bytes 262176 | tf_op jit(solution)/shard_map/ppermute | solution.py:38
  411.5 2.0 maximum_maximum_fusion
  (165 shorter events, 45.6 us)
Async XLA Ops:
  2.9 19.3 %collective-permute-start.2 = (bf16[32,4224]{1,0:T(8,128)(2,1)}, bf16[32,4224]{1,0:T(8,128)(2,1)S(1)}, u32[]{:S(2)}, u32[]{:S(2)}) collective-permute-start(bf16[32,4224]{1,0:T(8,128)(2,1)} %get-tuple-element.82.refs_0_.refs_4_), channel_id=1, source_target_pairs={{0,3},{1,2},{2,1},{3,0},{4,7},{5,6},{6,5},{7,4},{8,11},{9,10},{10,... | collective-permute-start | bytes 811016 | tf_op jit(solution)/shard_map/ppermute | solution.py:38
  4.2 22.8 %collective-permute-start.1 = (bf16[32,4224]{1,0:T(8,128)(2,1)}, bf16[32,4224]{1,0:T(8,128)(2,1)S(1)}, u32[]{:S(2)}, u32[]{:S(2)}) collective-permute-start(bf16[32,4224]{1,0:T(8,128)(2,1)} %get-tuple-element.82.refs_0_.refs_4_), channel_id=1, source_target_pairs={{0,2},{1,3},{2,0},{3,1},{4,6},{5,7},{6,4},{7,5},{8,10},{9,11},{10,... | collective-permute-start | bytes 811016 | tf_op jit(solution)/shard_map/ppermute | solution.py:38
  5.2 21.8 %collective-permute-start = (bf16[32,4224]{1,0:T(8,128)(2,1)}, bf16[32,4224]{1,0:T(8,128)(2,1)S(1)}, u32[]{:S(2)}, u32[]{:S(2)}) collective-permute-start(bf16[32,4224]{1,0:T(8,128)(2,1)} %get-tuple-element.82.refs_0_.refs_4_), channel_id=1, source_target_pairs={{0,1},{1,0},{2,3},{3,2},{4,5},{5,4},{6,7},{7,6},{8,9},{9,8},{10,11... | collective-permute-start | bytes 811016 | tf_op jit(solution)/shard_map/ppermute | solution.py:38
  6.4 2.6 collective-permute-start.3
  9.1 18.6 %collective-permute-start.4 = (bf16[64,2048]{1,0:T(8,128)(2,1)S(1)}, bf16[64,2048]{1,0:T(8,128)(2,1)S(1)}, u32[]{:S(2)}, u32[]{:S(2)}) collective-permute-start(bf16[64,2048]{1,0:T(8,128)(2,1)S(1)} %slice.113), channel_id=1, source_target_pairs={{0,8},{4,12},{8,0},{12,4},{16,24},{20,28},{24,16},{28,20},{1,9},{5... | collective-permute-start | bytes 786440 | tf_op jit(solution)/shard_map/ppermute | solution.py:38
  10.4 18.2 %collective-permute-start.5 = (bf16[64,2176]{1,0:T(8,128)(2,1)S(1)}, bf16[64,2176]{1,0:T(8,128)(2,1)S(1)}, u32[]{:S(2)}, u32[]{:S(2)}) collective-permute-start(bf16[64,2176]{1,0:T(8,128)(2,1)S(1)} %slice.114), channel_id=1, source_target_pairs={{0,16},{4,20},{8,24},{12,28},{16,0},{20,4},{24,8},{28,12},{1,17},{... | collective-permute-start | bytes 835592 | tf_op jit(solution)/shard_map/ppermute | solution.py:38
  22.2 16.4 %copy-start.15 = (bf16[32,4224]{1,0:T(8,128)(2,1)}, bf16[32,4224]{1,0:T(8,128)(2,1)S(1)}, u32[]{:S(2)}) copy-start(bf16[32,4224]{1,0:T(8,128)(2,1)S(1)} %collective-permute-done.2.refs_3_.refs_7_) | copy-start | bytes 811012
  27.1 11.5 %copy-start.16 = (bf16[32,4224]{1,0:T(8,128)(2,1)}, bf16[32,4224]{1,0:T(8,128)(2,1)S(1)}, u32[]{:S(2)}) copy-start(bf16[32,4224]{1,0:T(8,128)(2,1)S(1)} %collective-permute-done.1.refs_2_.refs_6_) | copy-start | bytes 811012
  27.1 11.5 %copy-start.17 = (bf16[32,4224]{1,0:T(8,128)(2,1)}, bf16[32,4224]{1,0:T(8,128)(2,1)S(1)}, u32[]{:S(2)}) copy-start(bf16[32,4224]{1,0:T(8,128)(2,1)S(1)} %collective-permute-done.refs_1_.refs_5_) | copy-start | bytes 811012
  29.5 14.6 %collective-permute-start.9 = (bf16[64,4224]{1,0:T(8,128)(2,1)}, bf16[64,4224]{1,0:T(8,128)(2,1)S(1)}, u32[]{:S(2)}, u32[]{:S(2)}) collective-permute-start(bf16[64,4224]{1,0:T(8,128)(2,1)} %get-tuple-element.95.refs_0_.refs_7_), channel_id=1, source_target_pairs={{3,2},{2,1},{1,0},{7,6},{6,5},{5,4},{11,10},{10,9},{9,8},{15,14},{... | collective-permute-start | bytes 1622024 | tf_op jit(solution)/shard_map/ppermute | solution.py:54
  33.5 14.2 %collective-permute-start.8 = (bf16[64,4224]{1,0:T(8,128)(2,1)}, bf16[64,4224]{1,0:T(8,128)(2,1)S(1)}, u32[]{:S(2)}, u32[]{:S(2)}) collective-permute-start(bf16[64,4224]{1,0:T(8,128)(2,1)} %get-tuple-element.95.refs_0_.refs_7_), channel_id=1, source_target_pairs={{0,1},{1,2},{2,3},{4,5},{5,6},{6,7},{8,9},{9,10},{10,11},{12,13},{... | collective-permute-start | bytes 1622024 | tf_op jit(solution)/shard_map/ppermute | solution.py:54
  35.5 13.0 %collective-permute-start.7 = (bf16[128,2176]{1,0:T(8,128)(2,1)}, bf16[128,2176]{1,0:T(8,128)(2,1)S(1)}, u32[]{:S(2)}, u32[]{:S(2)}) collective-permute-start(bf16[128,2176]{1,0:T(8,128)(2,1)} %get-tuple-element.87.b0.t0), channel_id=1, source_target_pairs={{0,8},{4,12},{8,0},{12,4},{16,24},{20,28},{24,16},{28,20},{1,9},{5... | collective-permute-start | bytes 1671176 | tf_op jit(solution)/shard_map/ppermute | solution.py:38
  36.7 11.7 %collective-permute-start.6 = (bf16[128,2048]{1,0:T(8,128)(2,1)}, bf16[128,2048]{1,0:T(8,128)(2,1)S(1)}, u32[]{:S(2)}, u32[]{:S(2)}) collective-permute-start(bf16[128,2048]{1,0:T(8,128)(2,1)} %get-tuple-element.86.a0), channel_id=1, source_target_pairs={{0,16},{4,20},{8,24},{12,28},{16,0},{20,4},{24,8},{28,12},{1,17},{... | collective-permute-start | bytes 1572872 | tf_op jit(solution)/shard_map/ppermute | solution.py:38
  44.0 19.2 %copy-start.3 = (bf16[64,4224]{1,0:T(8,128)(2,1)}, bf16[64,4224]{1,0:T(8,128)(2,1)S(1)}, u32[]{:S(2)}) copy-start(bf16[64,4224]{1,0:T(8,128)(2,1)S(1)} %collective-permute-done.9.refs_2_.refs_9_) | copy-start | bytes 1622020
  47.8 18.9 %copy-start.4 = (bf16[64,4224]{1,0:T(8,128)(2,1)}, bf16[64,4224]{1,0:T(8,128)(2,1)S(1)}, u32[]{:S(2)}) copy-start(bf16[64,4224]{1,0:T(8,128)(2,1)S(1)} %collective-permute-done.8.refs_1_.refs_8_) | copy-start | bytes 1622020
  55.9 27.2 %copy-start.30 = (bf16[32,4096]{1,0:T(8,128)(2,1)S(1)}, bf16[32,4096]{1,0:T(8,128)(2,1)}, u32[]{:S(2)}) copy-start(bf16[32,4096]{1,0:T(8,128)(2,1)} %get-tuple-element.96) | copy-start | bytes 786436
  55.9 27.6 %copy-start.32 = (s32[2]{0:T(128)S(1)}, s32[2]{0:T(128)}, u32[]{:S(2)}) copy-start(s32[2]{0:T(128)} %pad_add_fusion.ids.refs_0_) | copy-start | bytes 28
  56.0 28.1 %copy-start.31 = (bf16[32,4096]{1,0:T(8,128)(2,1)S(1)}, bf16[32,4096]{1,0:T(8,128)(2,1)}, u32[]{:S(2)}) copy-start(bf16[32,4096]{1,0:T(8,128)(2,1)} %get-tuple-element.103) | copy-start | bytes 786436
  56.0 54.2 %all-to-all-start = ((bf16[8,48,4096]{2,1,0:T(8,128)(2,1)}), bf16[8,48,4096]{2,1,0:T(8,128)(2,1)}, u32[]{:S(2)}, u32[]{:S(2)}) async-start(bf16[8,48,4096]{2,1,0:T(8,128)(2,1)} %bitcast.27), calls=%async_computation | async-start | bytes 6291456 | tf_op jit(solution)/shard_map/all_to_all | solution.py:458
  63.3 15.7 %collective-permute-start.12 = (bf16[64,4224]{1,0:T(8,128)(2,1)S(1)}, bf16[64,4224]{1,0:T(8,128)(2,1)S(1)}, u32[]{:S(2)}, u32[]{:S(2)}) collective-permute-start(bf16[64,4224]{1,0:T(8,128)(2,1)S(1)} %collective-permute-done.9.refs_2_.refs_9_), channel_id=1, source_target_pairs={{2,1},{1,0},{6,5},{5,4},{10,9},{9,8},{14,13},{13,12},{18,17},{17,1... | collective-permute-start | bytes 1622024 | tf_op jit(solution)/shard_map/ppermute | solution.py:54
  66.7 15.7 %collective-permute-start.11 = (bf16[64,4224]{1,0:T(8,128)(2,1)S(1)}, bf16[64,4224]{1,0:T(8,128)(2,1)S(1)}, u32[]{:S(2)}, u32[]{:S(2)}) collective-permute-start(bf16[64,4224]{1,0:T(8,128)(2,1)S(1)} %collective-permute-done.8.refs_1_.refs_8_), channel_id=1, source_target_pairs={{1,2},{2,3},{5,6},{6,7},{9,10},{10,11},{13,14},{14,15},{17,18},{18... | collective-permute-start | bytes 1622024 | tf_op jit(solution)/shard_map/ppermute | solution.py:54
  79.0 21.9 %copy-start.5 = (bf16[64,4224]{1,0:T(8,128)(2,1)}, bf16[64,4224]{1,0:T(8,128)(2,1)S(1)}, u32[]{:S(2)}) copy-start(bf16[64,4224]{1,0:T(8,128)(2,1)S(1)} %collective-permute-done.12.refs_4_.refs_11_) | copy-start | bytes 1622020
  79.0 21.9 %collective-permute-start.14 = (bf16[64,4224]{1,0:T(8,128)(2,1)S(1)}, bf16[64,4224]{1,0:T(8,128)(2,1)S(1)}, u32[]{:S(2)}, u32[]{:S(2)}) collective-permute-start(bf16[64,4224]{1,0:T(8,128)(2,1)S(1)} %collective-permute-done.12.refs_4_.refs_11_), channel_id=1, source_target_pairs={{1,0},{5,4},{9,8},{13,12},{17,16},{21,20},{25,24},{29,28}} | collective-permute-start | bytes 1622024 | tf_op jit(solution)/shard_map/ppermute | solution.py:54
  82.4 18.5 %copy-start.6 = (bf16[64,4224]{1,0:T(8,128)(2,1)}, bf16[64,4224]{1,0:T(8,128)(2,1)S(1)}, u32[]{:S(2)}) copy-start(bf16[64,4224]{1,0:T(8,128)(2,1)S(1)} %collective-permute-done.11.refs_3_.refs_10_) | copy-start | bytes 1622020
  82.4 18.5 %collective-permute-start.13 = (bf16[64,4224]{1,0:T(8,128)(2,1)S(1)}, bf16[64,4224]{1,0:T(8,128)(2,1)S(1)}, u32[]{:S(2)}, u32[]{:S(2)}) collective-permute-start(bf16[64,4224]{1,0:T(8,128)(2,1)S(1)} %collective-permute-done.11.refs_3_.refs_10_), channel_id=1, source_target_pairs={{2,3},{6,7},{10,11},{14,15},{18,19},{22,23},{26,27},{30,31}} | collective-permute-start | bytes 1622024 | tf_op jit(solution)/shard_map/ppermute | solution.py:54
  83.1 16.4 %collective-permute-start.10 = (bf16[32,4096]{1,0:T(8,128)(2,1)S(1)}, bf16[32,4096]{1,0:T(8,128)(2,1)S(1)}, u32[]{:S(2)}, u32[]{:S(2)}) collective-permute-start(bf16[32,4096]{1,0:T(8,128)(2,1)S(1)} %copy-done.30), channel_id=1, source_target_pairs={{0,2},{1,3},{2,0},{3,1},{4,6},{5,7},{6,4},{7,5},{8,10},{9,11},{10,... | collective-permute-start | bytes 786440 | tf_op jit(solution)/shard_map/ppermute | solution.py:38
  84.1 25.3 %collective-permute-start.15 = (bf16[32,4096]{1,0:T(8,128)(2,1)S(1)}, bf16[32,4096]{1,0:T(8,128)(2,1)S(1)}, u32[]{:S(2)}, u32[]{:S(2)}) collective-permute-start(bf16[32,4096]{1,0:T(8,128)(2,1)S(1)} %copy-done.31), channel_id=1, source_target_pairs={{0,2},{1,3},{2,0},{3,1},{4,6},{5,7},{6,4},{7,5},{8,10},{9,11},{10,... | collective-permute-start | bytes 786440 | tf_op jit(solution)/shard_map/ppermute | solution.py:38
  111.4 41.5 %all-to-all-start.1 = ((bf16[8,48,4096]{2,1,0:T(8,128)(2,1)}), bf16[8,48,4096]{2,1,0:T(8,128)(2,1)S(1)}, u32[]{:S(2)}, u32[]{:S(2)}) async-start(bf16[8,48,4096]{2,1,0:T(8,128)(2,1)} %bitcast.25), calls=%async_computation.1 | async-start | bytes 6291456 | tf_op jit(solution)/shard_map/all_to_all | solution.py:458
  118.5 27.6 %collective-permute-start.16 = (bf16[96,4096]{1,0:T(8,128)(2,1)}, bf16[96,4096]{1,0:T(8,128)(2,1)}, u32[]{:S(2)}, u32[]{:S(2)}) collective-permute-start(bf16[96,4096]{1,0:T(8,128)(2,1)} %get-tuple-element.106), channel_id=1, source_target_pairs={{0,1},{1,0},{2,3},{3,2},{4,5},{5,4},{6,7},{7,6},{8,9},{9,8},{10,11... | collective-permute-start | bytes 2359304 | tf_op jit(solution)/shard_map/ppermute | solution.py:38
  121.0 24.3 %collective-permute-start.17 = (bf16[32,4096]{1,0:T(8,128)(2,1)S(1)}, bf16[32,4096]{1,0:T(8,128)(2,1)S(1)}, u32[]{:S(2)}, u32[]{:S(2)}) collective-permute-start(bf16[32,4096]{1,0:T(8,128)(2,1)S(1)} %copy-done.18), channel_id=1, source_target_pairs={{0,2},{1,3},{2,0},{3,1},{4,6},{5,7},{6,4},{7,5},{8,10},{9,11},{10,... | collective-permute-start | bytes 786440 | tf_op jit(solution)/shard_map/ppermute | solution.py:38
  121.6 23.7 %collective-permute-start.18 = (bf16[64,4096]{1,0:T(8,128)(2,1)}, bf16[64,4096]{1,0:T(8,128)(2,1)}, u32[]{:S(2)}, u32[]{:S(2)}) collective-permute-start(bf16[64,4096]{1,0:T(8,128)(2,1)} %get-tuple-element.108), channel_id=1, source_target_pairs={{0,3},{1,2},{2,1},{3,0},{4,7},{5,6},{6,5},{7,4},{8,11},{9,10},{10,... | collective-permute-start | bytes 1572872 | tf_op jit(solution)/shard_map/ppermute | solution.py:38
  154.7 43.4 %all-to-all-start.2 = ((bf16[8,48,4096]{2,1,0:T(8,128)(2,1)}), bf16[8,48,4096]{2,1,0:T(8,128)(2,1)S(1)}, u32[]{:S(2)}, u32[]{:S(2)}) async-start(bf16[8,48,4096]{2,1,0:T(8,128)(2,1)} %bitcast.28), calls=%async_computation.2 | async-start | bytes 6291456 | tf_op jit(solution)/shard_map/all_to_all | solution.py:458
  163.4 18.7 %collective-permute-start.19 = (bf16[32,4096]{1,0:T(8,128)(2,1)S(1)}, bf16[32,4096]{1,0:T(8,128)(2,1)}, u32[]{:S(2)}, u32[]{:S(2)}) collective-permute-start(bf16[32,4096]{1,0:T(8,128)(2,1)S(1)} %copy-done.11), channel_id=1, source_target_pairs={{0,3},{1,2},{2,1},{3,0},{4,7},{5,6},{6,5},{7,4},{8,11},{9,10},{10,... | collective-permute-start | bytes 786440 | tf_op jit(solution)/shard_map/ppermute | solution.py:38
  199.8 44.1 %all-to-all-start.3 = ((bf16[8,48,4096]{2,1,0:T(8,128)(2,1)}), bf16[8,48,4096]{2,1,0:T(8,128)(2,1)S(1)}, u32[]{:S(2)}, u32[]{:S(2)}) async-start(bf16[8,48,4096]{2,1,0:T(8,128)(2,1)} %bitcast.20), calls=%async_computation.3 | async-start | bytes 6291456 | tf_op jit(solution)/shard_map/all_to_all | solution.py:458
  206.5 37.4 %collective-permute-start.20 = (bf16[96,4096]{1,0:T(8,128)(2,1)}, bf16[96,4096]{1,0:T(8,128)(2,1)}, u32[]{:S(2)}, u32[]{:S(2)}) collective-permute-start(bf16[96,4096]{1,0:T(8,128)(2,1)} %get-tuple-element.124), channel_id=1, source_target_pairs={{0,1},{1,0},{2,3},{3,2},{4,5},{5,4},{6,7},{7,6},{8,9},{9,8},{10,11... | collective-permute-start | bytes 2359304 | tf_op jit(solution)/shard_map/ppermute | solution.py:38
  207.4 24.6 %collective-permute-start.21 = (bf16[32,4096]{1,0:T(8,128)(2,1)}, bf16[32,4096]{1,0:T(8,128)(2,1)S(1)}, u32[]{:S(2)}, u32[]{:S(2)}) collective-permute-start(bf16[32,4096]{1,0:T(8,128)(2,1)} %get-tuple-element.125), channel_id=1, source_target_pairs={{0,2},{1,3},{2,0},{3,1},{4,6},{5,7},{6,4},{7,5},{8,10},{9,11},{10,... | collective-permute-start | bytes 786440 | tf_op jit(solution)/shard_map/ppermute | solution.py:38
  208.6 29.0 %collective-permute-start.22 = (bf16[32,4096]{1,0:T(8,128)(2,1)}, bf16[32,4096]{1,0:T(8,128)(2,1)S(1)}, u32[]{:S(2)}, u32[]{:S(2)}) collective-permute-start(bf16[32,4096]{1,0:T(8,128)(2,1)} %get-tuple-element.126), channel_id=1, source_target_pairs={{0,2},{1,3},{2,0},{3,1},{4,6},{5,7},{6,4},{7,5},{8,10},{9,11},{10,... | collective-permute-start | bytes 786440 | tf_op jit(solution)/shard_map/ppermute | solution.py:38
  209.8 33.4 %collective-permute-start.23 = (bf16[32,4096]{1,0:T(8,128)(2,1)}, bf16[32,4096]{1,0:T(8,128)(2,1)S(1)}, u32[]{:S(2)}, u32[]{:S(2)}) collective-permute-start(bf16[32,4096]{1,0:T(8,128)(2,1)} %get-tuple-element.127), channel_id=1, source_target_pairs={{0,2},{1,3},{2,0},{3,1},{4,6},{5,7},{6,4},{7,5},{8,10},{9,11},{10,... | collective-permute-start | bytes 786440 | tf_op jit(solution)/shard_map/ppermute | solution.py:38
  232.0 18.2 %copy-start.24 = (bf16[32,4096]{1,0:T(8,128)(2,1)}, bf16[32,4096]{1,0:T(8,128)(2,1)S(1)}, u32[]{:S(2)}) copy-start(bf16[32,4096]{1,0:T(8,128)(2,1)S(1)} %collective-permute-done.21.refs_2_) | copy-start | bytes 786436
  250.1 9.0 %collective-permute-start.24 = (bf16[32,4096]{1,0:T(8,128)(2,1)}, bf16[32,4096]{1,0:T(8,128)(2,1)}, u32[]{:S(2)}, u32[]{:S(2)}) collective-permute-start(bf16[32,4096]{1,0:T(8,128)(2,1)} %get-tuple-element.132), channel_id=1, source_target_pairs={{0,1},{4,5},{8,9},{12,13},{16,17},{20,21},{24,25},{28,29}} | collective-permute-start | bytes 786440 | tf_op jit(solution)/shard_map/ppermute | solution.py:67
  251.4 35.5 %copy-start.29 = (bf16[32,4096]{1,0:T(8,128)(2,1)S(1)}, bf16[32,4096]{1,0:T(8,128)(2,1)}, u32[]{:S(2)}) copy-start(bf16[32,4096]{1,0:T(8,128)(2,1)} %get-tuple-element.130) | copy-start | bytes 786436
  251.5 49.4 %all-to-all-start.4 = ((bf16[8,48,4096]{2,1,0:T(8,128)(2,1)}), bf16[8,48,4096]{2,1,0:T(8,128)(2,1)S(1)}, u32[]{:S(2)}, u32[]{:S(2)}) async-start(bf16[8,48,4096]{2,1,0:T(8,128)(2,1)} %bitcast.16), calls=%async_computation.4 | async-start | bytes 6291456 | tf_op jit(solution)/shard_map/all_to_all | solution.py:458
  256.5 5.6 %collective-permute-start.27 = (bf16[32,4096]{1,0:T(8,128)(2,1)}, bf16[32,4096]{1,0:T(8,128)(2,1)S(1)}, u32[]{:S(2)}, u32[]{:S(2)}) collective-permute-start(bf16[32,4096]{1,0:T(8,128)(2,1)} %get-tuple-element.135), channel_id=1, source_target_pairs={{3,2},{7,6},{11,10},{15,14},{19,18},{23,22},{27,26},{31,30}} | collective-permute-start | bytes 786440 | tf_op jit(solution)/shard_map/ppermute | solution.py:67
  257.2 36.9 %collective-permute-start.30 = (bf16[64,4096]{1,0:T(8,128)(2,1)}, bf16[64,4096]{1,0:T(8,128)(2,1)S(1)}, u32[]{:S(2)}, u32[]{:S(2)}) collective-permute-start(bf16[64,4096]{1,0:T(8,128)(2,1)} %get-tuple-element.139), channel_id=1, source_target_pairs={{0,3},{1,2},{2,1},{3,0},{4,7},{5,6},{6,5},{7,4},{8,11},{9,10},{10,... | collective-permute-start | bytes 1572872 | tf_op jit(solution)/shard_map/ppermute | solution.py:38
  260.2 26.7 %collective-permute-start.25 = (bf16[32,4096]{1,0:T(8,128)(2,1)S(1)}, bf16[32,4096]{1,0:T(8,128)(2,1)S(1)}, u32[]{:S(2)}, u32[]{:S(2)}) collective-permute-start(bf16[32,4096]{1,0:T(8,128)(2,1)S(1)} %add_convert_fusion.6), channel_id=1, source_target_pairs={{0,1},{1,2},{4,5},{5,6},{8,9},{9,10},{12,13},{13,14},{16,17},{17,1... | collective-permute-start | bytes 786440 | tf_op jit(solution)/shard_map/ppermute | solution.py:67
  263.2 28.0 %collective-permute-start.28 = (bf16[32,4096]{1,0:T(8,128)(2,1)S(1)}, bf16[32,4096]{1,0:T(8,128)(2,1)S(1)}, u32[]{:S(2)}, u32[]{:S(2)}) collective-permute-start(bf16[32,4096]{1,0:T(8,128)(2,1)S(1)} %add_convert_fusion.4), channel_id=1, source_target_pairs={{3,2},{2,1},{7,6},{6,5},{11,10},{10,9},{15,14},{14,13},{19,18},{18... | collective-permute-start | bytes 786440 | tf_op jit(solution)/shard_map/ppermute | solution.py:67
  287.0 8.9 %collective-permute-start.26 = (bf16[32,4096]{1,0:T(8,128)(2,1)S(1)}, bf16[32,4096]{1,0:T(8,128)(2,1)S(1)}, u32[]{:S(2)}, u32[]{:S(2)}) collective-permute-start(bf16[32,4096]{1,0:T(8,128)(2,1)S(1)} %add_convert_fusion.5), channel_id=1, source_target_pairs={{0,1},{1,2},{2,3},{4,5},{5,6},{6,7},{8,9},{9,10},{10,11},{12,13},{... | collective-permute-start | bytes 786440 | tf_op jit(solution)/shard_map/ppermute | solution.py:67
  292.2 8.7 %collective-permute-start.29 = (bf16[32,4096]{1,0:T(8,128)(2,1)S(1)}, bf16[32,4096]{1,0:T(8,128)(2,1)}, u32[]{:S(2)}, u32[]{:S(2)}) collective-permute-start(bf16[32,4096]{1,0:T(8,128)(2,1)S(1)} %add_convert_fusion.3), channel_id=1, source_target_pairs={{3,2},{2,1},{1,0},{7,6},{6,5},{5,4},{11,10},{10,9},{9,8},{15,14},{... | collective-permute-start | bytes 786440 | tf_op jit(solution)/shard_map/ppermute | solution.py:67
  307.0 43.0 %collective-permute-start.31 = (bf16[32,4096]{1,0:T(8,128)(2,1)}, bf16[32,4096]{1,0:T(8,128)(2,1)}, u32[]{:S(2)}, u32[]{:S(2)}) collective-permute-start(bf16[32,4096]{1,0:T(8,128)(2,1)} %get-tuple-element.142), channel_id=1, source_target_pairs={{0,1},{1,0},{2,3},{3,2},{4,5},{5,4},{6,7},{7,6},{8,9},{9,8},{10,11... | collective-permute-start | bytes 786440 | tf_op jit(solution)/shard_map/ppermute | solution.py:38
  307.3 42.6 %collective-permute-start.32 = (bf16[32,4096]{1,0:T(8,128)(2,1)}, bf16[32,4096]{1,0:T(8,128)(2,1)}, u32[]{:S(2)}, u32[]{:S(2)}) collective-permute-start(bf16[32,4096]{1,0:T(8,128)(2,1)} %get-tuple-element.143), channel_id=1, source_target_pairs={{0,2},{1,3},{2,0},{3,1},{4,6},{5,7},{6,4},{7,5},{8,10},{9,11},{10,... | collective-permute-start | bytes 786440 | tf_op jit(solution)/shard_map/ppermute | solution.py:38
  308.5 41.5 %collective-permute-start.33 = (bf16[32,4096]{1,0:T(8,128)(2,1)}, bf16[32,4096]{1,0:T(8,128)(2,1)}, u32[]{:S(2)}, u32[]{:S(2)}) collective-permute-start(bf16[32,4096]{1,0:T(8,128)(2,1)} %get-tuple-element.144), channel_id=1, source_target_pairs={{0,3},{1,2},{2,1},{3,0},{4,7},{5,6},{6,5},{7,4},{8,11},{9,10},{10,... | collective-permute-start | bytes 786440 | tf_op jit(solution)/shard_map/ppermute | solution.py:38
  309.7 32.8 %collective-permute-start.37 = (bf16[32,4096]{1,0:T(8,128)(2,1)}, bf16[32,4096]{1,0:T(8,128)(2,1)}, u32[]{:S(2)}, u32[]{:S(2)}) collective-permute-start(bf16[32,4096]{1,0:T(8,128)(2,1)} %get-tuple-element.154), channel_id=1, source_target_pairs={{0,3},{1,2},{2,1},{3,0},{4,7},{5,6},{6,5},{7,4},{8,11},{9,10},{10,... | collective-permute-start | bytes 786440 | tf_op jit(solution)/shard_map/ppermute | solution.py:38
  311.1 66.5 %all-to-all-start.5 = ((bf16[8,48,4096]{2,1,0:T(8,128)(2,1)}), bf16[8,48,4096]{2,1,0:T(8,128)(2,1)S(1)}, u32[]{:S(2)}, u32[]{:S(2)}) async-start(bf16[8,48,4096]{2,1,0:T(8,128)(2,1)} %bitcast.18), calls=%async_computation.5 | async-start | bytes 6291456 | tf_op jit(solution)/shard_map/all_to_all | solution.py:458
  317.4 32.5 %copy-start.21 = (f32[32,4096]{1,0:T(8,128)S(1)}, f32[32,4096]{1,0:T(8,128)}, u32[]{:S(2)}) copy-start(f32[32,4096]{1,0:T(8,128)} %get-tuple-element.141) | copy-start | bytes 1572868
  348.1 19.7 %copy-start.19 = (f32[128,2048]{1,0:T(8,128)S(1)}, f32[128,2048]{1,0:T(8,128)}, u32[]{:S(2)}) copy-start(f32[128,2048]{1,0:T(8,128)} %get-tuple-element.157) | copy-start | bytes 3145732
  348.1 18.0 %collective-permute-start.38 = (bf16[128,2048]{1,0:T(8,128)(2,1)}, bf16[128,2048]{1,0:T(8,128)(2,1)S(1)}, u32[]{:S(2)}, u32[]{:S(2)}) collective-permute-start(bf16[128,2048]{1,0:T(8,128)(2,1)} %get-tuple-element.156), channel_id=1, source_target_pairs={{0,16},{4,20},{8,24},{12,28},{16,0},{20,4},{24,8},{28,12},{1,17},{... | collective-permute-start | bytes 1572872 | tf_op jit(solution)/shard_map/ppermute | solution.py:38
  348.8 19.0 %collective-permute-start.41 = (bf16[128,2048]{1,0:T(8,128)(2,1)}, bf16[128,2048]{1,0:T(8,128)(2,1)S(1)}, u32[]{:S(2)}, u32[]{:S(2)}) collective-permute-start(bf16[128,2048]{1,0:T(8,128)(2,1)} %get-tuple-element.158), channel_id=1, source_target_pairs={{0,8},{4,12},{8,0},{12,4},{16,24},{20,28},{24,16},{28,20},{1,9},{5... | collective-permute-start | bytes 1572872 | tf_op jit(solution)/shard_map/ppermute | solution.py:38
  367.5 7.4 %collective-permute-start.39 = (bf16[64,2048]{1,0:T(8,128)(2,1)S(1)}, bf16[64,2048]{1,0:T(8,128)(2,1)S(1)}, u32[]{:S(2)}, u32[]{:S(2)}) collective-permute-start(bf16[64,2048]{1,0:T(8,128)(2,1)S(1)} %split.57), channel_id=1, source_target_pairs={{0,8},{4,12},{8,0},{12,4},{16,24},{20,28},{24,16},{28,20},{1,9},{5... | collective-permute-start | bytes 786440 | tf_op jit(solution)/shard_map/ppermute | solution.py:38
  368.0 8.4 %collective-permute-start.42 = (bf16[64,2048]{1,0:T(8,128)(2,1)S(1)}, bf16[64,2048]{1,0:T(8,128)(2,1)S(1)}, u32[]{:S(2)}, u32[]{:S(2)}) collective-permute-start(bf16[64,2048]{1,0:T(8,128)(2,1)S(1)} %split.56), channel_id=1, source_target_pairs={{0,16},{4,20},{8,24},{12,28},{16,0},{20,4},{24,8},{28,12},{1,17},{... | collective-permute-start | bytes 786440 | tf_op jit(solution)/shard_map/ppermute | solution.py:38
  375.0 2.5 collective-permute-start.40
  377.2 9.7 %collective-permute-start.43 = (bf16[32,2048]{1,0:T(8,128)(2,1)}, bf16[32,2048]{1,0:T(8,128)(2,1)}, u32[]{:S(2)}, u32[]{:S(2)}) collective-permute-start(bf16[32,2048]{1,0:T(8,128)(2,1)} %split.58), channel_id=1, source_target_pairs={{0,4},{4,0},{8,12},{12,8},{16,20},{20,16},{24,28},{28,24},{1,5},{5... | collective-permute-start | bytes 393224 | tf_op jit(solution)/shard_map/ppermute | solution.py:38
  383.6 13.0 %collective-permute-start.34 = (bf16[32,4096]{1,0:T(8,128)(2,1)}, bf16[32,4096]{1,0:T(8,128)(2,1)S(1)}, u32[]{:S(2)}, u32[]{:S(2)}) collective-permute-start(bf16[32,4096]{1,0:T(8,128)(2,1)} %get-tuple-element.148), channel_id=1, source_target_pairs={{0,1},{1,0},{2,3},{3,2},{4,5},{5,4},{6,7},{7,6},{8,9},{9,8},{10,11... | collective-permute-start | bytes 786440 | tf_op jit(solution)/shard_map/ppermute | solution.py:38
  385.4 18.4 %collective-permute-start.35 = (bf16[32,4096]{1,0:T(8,128)(2,1)}, bf16[32,4096]{1,0:T(8,128)(2,1)S(1)}, u32[]{:S(2)}, u32[]{:S(2)}) collective-permute-start(bf16[32,4096]{1,0:T(8,128)(2,1)} %get-tuple-element.149), channel_id=1, source_target_pairs={{0,2},{1,3},{2,0},{3,1},{4,6},{5,7},{6,4},{7,5},{8,10},{9,11},{10,... | collective-permute-start | bytes 786440 | tf_op jit(solution)/shard_map/ppermute | solution.py:38
  386.6 23.7 %collective-permute-start.36 = (bf16[32,4096]{1,0:T(8,128)(2,1)}, bf16[32,4096]{1,0:T(8,128)(2,1)S(1)}, u32[]{:S(2)}, u32[]{:S(2)}) collective-permute-start(bf16[32,4096]{1,0:T(8,128)(2,1)} %get-tuple-element.150), channel_id=1, source_target_pairs={{0,3},{1,2},{2,1},{3,0},{4,7},{5,6},{6,5},{7,4},{8,11},{9,10},{10,... | collective-permute-start | bytes 786440 | tf_op jit(solution)/shard_map/ppermute | solution.py:38
  (21 other events, 69.2 us)

commit v6 on v5

--- a/solution.py
+++ b/solution.py
@@ -19,7 +19,7 @@
 
 
 def fence(arrays, after):
-    token = sum(a[:16, :LANES].astype(F32) for a in after)
+    token = sum(a.reshape(-1, a.shape[-1])[:16, :LANES].astype(F32) for a in after)
 
     def kernel(*refs):
         pass
@@ -124,31 +124,48 @@
     return jnp.where((source >= 0) & (source < peers), source ^ local, -1)
 
 
-def pick_kernel(count, peers, chain_in, chain_out, ids, *refs):
+def pick_kernel(count, blocks, peers, chain_in, chain_out, ids, *refs):
     parts, refs = refs[:count], refs[count:]
     tables, refs = refs[:count], refs[count:]
-    lane, slot_group, turn, before, in_column, in_row, out_column, out, mixing, place = refs
+    lane, slot_group, turn, before, in_column, in_row, out_column, out = refs[:8]
+    mixings, places = refs[8 : 8 + blocks], refs[8 + blocks :]
+
+    def rows_of(refs, block):
+        return jnp.concatenate([r[block * BLOCK_TOK : (block + 1) * BLOCK_TOK] for r in refs])
 
     @pl.when(pl.program_id(0) == 0)
     def _():
         local = ids[1]
-        table = jnp.concatenate([t[...] for t in tables])
         row_group = bits_of(in_column[...], local, peers, chain_in)
-        place[...], weights = choose(
-            table, lane[...] + local, row_group, slot_group[...], turn[...], before[...]
+        for block, (mixing, place) in enumerate(zip(mixings, places)):
+            place[...], weights = choose(
+                rows_of(tables, block),
+                lane[...] + local,
+                row_group,
+                slot_group[...],
+                turn[...],
+                before[...],
+            )
+            if chain_in != chain_out:
+                shape = mixing.shape[0], weights.shape[0]
+                same = bits_of(out_column[...], local, peers, chain_out) == bits_of(
+                    in_row[...], local, peers, chain_in
+                )
+                row = lax.broadcasted_iota(I32, shape, 0) & (BLOCK_TOK - 1)
+                column = lax.broadcasted_iota(I32, shape, 1) & (BLOCK_TOK - 1)
+                order = jnp.where(same & (row == column), 1.0, 0.0).astype(BF16)
+                weights = jnp.dot(order, weights, preferred_element_type=F32).astype(BF16)
+            mixing[...] = weights
+
+    for block, place in enumerate(places):
+        rows = lax.dot_general(
+            place[...],
+            rows_of(parts, block),
+            (((0,), (0,)), ((), ())),
+            preferred_element_type=F32,
         )
-        if chain_in != chain_out:
-            shape = mixing.shape[0], weights.shape[0]
-            same = bits_of(out_column[...], local, peers, chain_out) == bits_of(
-                in_row[...], local, peers, chain_in
-            )
-            row = lax.broadcasted_iota(I32, shape, 0) & (BLOCK_TOK - 1)
-            column = lax.broadcasted_iota(I32, shape, 1) & (BLOCK_TOK - 1)
-            order = jnp.where(same & (row == column), 1.0, 0.0).astype(BF16)
-            weights = jnp.dot(order, weights, preferred_element_type=F32).astype(BF16)
-        mixing[...] = weights
-
-    out[...] = gather_rows(place[...], jnp.concatenate([p[...] for p in parts]))
+        nodes, _, size, tile = out.shape
+        out[:, block] = rows.reshape(nodes, size, tile).astype(BF16)
 
 
 def whole_block(array):
@@ -159,8 +176,10 @@
     return np.repeat(np.array(labels, np.int32), BLOCK_TOK)
 
 
-def pick(parts, block, ids, peers, capacity, features, chain_in, chain_out):
+def pick(parts, ids, peers, capacity, features, chain_in, chain_out):
     nodes = lax.axis_size("node")
+    held = parts[0].shape[0]
+    blocks = held // BLOCK_TOK
     slots = nodes * peers * capacity
     slot = np.arange(slots, dtype=np.int32)[None, :]
     labels = chain_offsets(peers), list(range(peers))
@@ -176,25 +195,25 @@
         out_labels[:, None],
     )
     return pl.pallas_call(
-        functools.partial(pick_kernel, len(parts), peers, chain_in, chain_out),
+        functools.partial(pick_kernel, len(parts), blocks, peers, chain_in, chain_out),
         grid=(TILES,),
         out_shape=[
-            jax.ShapeDtypeStruct((slots, features), BF16),
-            jax.ShapeDtypeStruct((len(out_labels), slots), BF16),
-        ],
+            jax.ShapeDtypeStruct((nodes, blocks, peers * capacity, features), BF16),
+        ]
+        + [jax.ShapeDtypeStruct((len(out_labels), slots), BF16)] * blocks,
         in_specs=[pl.BlockSpec(memory_space=pltpu.SMEM)]
-        + [pl.BlockSpec((BLOCK_TOK, tile), lambda j: (block, j))] * len(parts)
-        + [pl.BlockSpec((BLOCK_TOK, LANES), lambda j: (block, features // LANES))] * len(parts)
+        + [pl.BlockSpec((held, tile), lambda j: (0, j))] * len(parts)
+        + [pl.BlockSpec((held, LANES), lambda j: (0, features // LANES))] * len(parts)
         + [whole_block(a) for a in small],
         out_specs=[
-            pl.BlockSpec((slots, tile), lambda j: (0, j)),
-            pl.BlockSpec((len(out_labels), slots), lambda j: (0, 0)),
-        ],
-        scratch_shapes=[pltpu.VMEM((rows, slots), BF16)],
+            pl.BlockSpec((nodes, blocks, peers * capacity, tile), lambda j: (0, 0, 0, j)),
+        ]
+        + [pl.BlockSpec((len(out_labels), slots), lambda j: (0, 0))] * blocks,
+        scratch_shapes=[pltpu.VMEM((rows, slots), BF16)] * blocks,
         compiler_params=PARAMS,
         cost_estimate=pl.CostEstimate(
-            flops=2 * rows * slots * features,
-            bytes_accessed=2 * (rows + slots) * features,
+            flops=2 * blocks * rows * slots * features,
+            bytes_accessed=2 * blocks * (rows + slots) * features,
             transcendentals=0,
         ),
     )(ids, *parts, *parts, *small)
@@ -346,7 +365,7 @@
     )(mixing_a, mixing_b, *landed)
 
 
-def expert_kernel(count, first_tiles, *refs):
+def expert_kernel(count, first_tiles, split, tie, *refs):
     parts, (gate_ref, up_ref, down_ref) = refs[:count], refs[count : count + 3]
     outs, (joined, hidden) = refs[count + 3 : -2], refs[-2:]
     step = pl.program_id(0)
@@ -368,14 +387,27 @@
     @pl.when(step >= first_tiles)
     def _():
         rows = jnp.concatenate([hidden[i] for i in range(first_tiles)], axis=1)
-        result = jnp.dot(rows, down_ref[...], preferred_element_type=F32).astype(BF16)
+        result = jnp.dot(rows, down_ref[...], preferred_element_type=F32)
+        if split is not None:
+            result = result.reshape(*split, result.shape[1])
+            for block, out in enumerate(outs):
+                out[...] = result[:, block].reshape(out.shape).astype(BF16)
+            return
+        result = result.astype(BF16)
         at = 0
         for out in outs:
             out[...] = result[at : at + out.shape[0]]
             at += out.shape[0]
 
 
-def expert(parts, gate_weight, up_weight, down_weight):
+def expert(parts, tie, gate_weight, up_weight, down_weight):
+    split = None
+    sizes = [part.shape[0] for part in parts]
+    if parts[0].ndim == 4:
+        (part,) = parts
+        split = part.shape[:3]
+        parts = [part.reshape(-1, part.shape[3])]
+        sizes = [split[0] * split[2]] * split[1]
     rows = sum(part.shape[0] for part in parts)
     features, hidden = gate_weight.shape
     tile = 256
@@ -389,17 +421,18 @@
         return jnp.maximum(i - first_tiles, 0)
 
     return pl.pallas_call(
-        functools.partial(expert_kernel, len(parts), first_tiles),
+        functools.partial(expert_kernel, len(parts), first_tiles, split),
         grid=(first_tiles + TILES,),
-        out_shape=[jax.ShapeDtypeStruct(part.shape, BF16) for part in parts],
-        in_specs=[whole_block(part) for part in parts]
+        out_shape=[jax.ShapeDtypeStruct((size, features), BF16) for size in sizes],
+        in_specs=[pl.BlockSpec(memory_space=pltpu.SMEM)]
+        + [whole_block(part) for part in parts]
         + [
             pl.BlockSpec((features, tile), lambda i: (0, first(i))),
             pl.BlockSpec((features, tile), lambda i: (0, first(i))),
             pl.BlockSpec((hidden, out_tile), lambda i: (0, second(i))),
         ],
         out_specs=[
-            pl.BlockSpec((part.shape[0], out_tile), lambda i: (0, second(i))) for part in parts
+            pl.BlockSpec((size, out_tile), lambda i: (0, second(i))) for size in sizes
         ],
         scratch_shapes=[
             pltpu.VMEM((rows if len(parts) > 1 else 16, features), BF16),
@@ -411,7 +444,7 @@
             bytes_accessed=6 * features * hidden + 4 * rows * features,
             transcendentals=rows * hidden,
         ),
-    )(*parts, gate_weight, up_weight, down_weight)
+    )(tie, *parts, gate_weight, up_weight, down_weight)
 
 
 def prepare_kernel(tokens, gain, routes, gates, placement, *outs):
@@ -479,10 +512,7 @@
     bits_a, bits_b = bit_order(nodes, False), bit_order(nodes, True)
     ids = jnp.stack([node, local]).astype(I32)
     near = ids, peers, capacity, features
-    size = slots // peers
-    cuts = [size * k for k in range(peers - 1)]
-    cuts += [cuts[-1] + size // 3, cuts[-1] + size // 3 * 2, size * (peers - 1)]
-    cuts += [slots - size // 3, slots]
+    cuts = [slots // peers * k for k in range(peers + 1)]
 
     near0 = swaps([sent0] * peers, "local", 1, peers)
     pair = jnp.concatenate([sent3, swap(sent3, "node", bits_a[0])])
@@ -492,66 +522,51 @@
     rows_a = [rows_a, swap(rows_a, "node", bits_a[-1])]
     rows_b = [rows_b, swap(rows_b, "node", bits_b[-1])]
     chain = chain_step([sent12, sent12], "local", 1)
-    outbound0, mixing0 = pick([sent0] + near0, 0, *near, chain_in=False, chain_out=True)
+    outbound0, mixing0 = pick([sent0] + near0, *near, chain_in=False, chain_out=True)
+
+    outbound0, *last_rows = fence([outbound0, rows_a[1], rows_b[1]], chain)
+    arrived0 = to_experts(outbound0)
+    parts12 = [sent12] + chain
+    for step in range(2, peers):
+        chain = chain_step(chain, "local", step)
+        parts12 += chain
     outbound3, mixing3a, mixing3b = pick_cross(
-        rows_a,
-        rows_b,
+        [rows_a[0], last_rows[0]],
+        [rows_b[0], last_rows[1]],
         gathered_from(bits_a),
         gathered_from(bits_b),
         *near,
         cuts,
     )
-
-    outbound0, *outbound3 = fence([outbound0] + outbound3, chain)
-    arrived0 = to_experts(outbound0)
-    parts12 = [sent12] + chain
-    for step in range(2, peers):
-        chain = chain_step(chain, "local", step)
-        parts12 += chain
+    outbound12, mixing1, mixing2 = pick(parts12, *near, chain_in=True, chain_out=False)
+
     own3, *outbound3 = outbound3
-    last2, last1 = peers - 2, peers - 1
-    third = [swap(outbound3[-5], "local", last2)]
-    (late_ids,) = fence([ids], third)
-    third.append(swap(outbound3[-4], "local", last2))
-    outbound1, mixing1 = pick(parts12, 0, late_ids, *near[1:], chain_in=True, chain_out=False)
-    (third[1],) = fence([third[1]], [outbound1])
-
-    outbound1, ids, *later3 = fence(
-        [outbound1, ids] + outbound3[:-5] + outbound3[-3:], [arrived0, third[1]]
-    )
-    arrived1 = to_experts(outbound1)
-    early = [swap(part, "local", k + 1) for k, part in enumerate(later3[:-3])]
-    third.append(swap(later3[-3], "local", last2))
-    third.append(swap(later3[-2], "local", last1))
-    outbound2, mixing2 = pick(parts12, 1, ids, *near[1:], chain_in=True, chain_out=False)
-    (out0,) = expert([arrived0], *weights)
-
-    outbound2, last3 = fence([outbound2, later3[-1]], [arrived1, out0] + early + third[2:])
-    arrived2 = to_experts(outbound2)
-    last3 = swap(last3, "local", last1)
-    (out1,) = expert([arrived1], *weights)
-    (last3,) = fence([last3], [out1])
-    out3 = list(expert([own3] + early + third + [last3], *weights))
-
-    out0, *out3 = fence([out0] + out3, [arrived2, out1])
+    outbound12, *outbound3 = fence([outbound12] + outbound3, [arrived0])
+    arrived12 = to_experts(outbound12)
+    arrived3 = swaps([None] + outbound3, "local", 1, peers)
+    (out0,) = expert([arrived0.reshape(slots, features)], ids, *weights)
+
+    out0, tie = fence([out0, ids], [arrived12] + arrived3)
     landed0 = to_experts(out0)
-    landed3 = out3[:1] + swaps(out3, "local", 1, last1)
-    landed3 += [swap(part, "local", last2) for part in out3[-4:-2]]
-    (out2,) = expert([arrived2], *weights)
-
-    out1, later3, mixing0 = fence([out1, out3[-2], mixing0], [landed0, out2] + landed3[1:])
+    out3 = list(expert([own3] + arrived3, tie, *weights))
+    landed3 = out3[:1] + swaps(out3, "local", 1, peers - 1)
+    out1, out2 = expert([arrived12], tie, *weights)
+
+    (mixing0,) = fence([mixing0], [out1])
+    out1, last3 = fence([out1, out3[-1]], [landed0, out2] + landed3[1:])
     landed1 = to_experts(out1)
-    landed3.append(swap(later3, "local", last1))
+    landed3.append(swap(last3, "local", peers - 1))
     own0, parts0 = chain_sum(*mix(mixing0, landed0), "local")
 
-    out2, last3, mixing1 = fence([out2, out3[-1], mixing1], [landed1, landed3[-1]] + parts0)
+    (out2,) = fence([out2], [landed1, landed3[-1]] + parts0)
     landed2 = to_experts(out2)
-    landed3.append(swap(last3, "local", last1))
     own1, parts1 = mix(mixing1, landed1)
     parts1 = swaps([None] + parts1, "local", 1, peers)
     cross = mix_cross(mixing3a, mixing3b, landed3)
     piece0 = total(own0, parts0)
 
+    cross = fence(list(cross), [landed2])
+    (mixing2,) = fence([mixing2], [cross[1]])
     own2, parts2 = mix(mixing2, landed2)
     parts2 = swaps([None] + parts2, "local", 1, peers)
     piece1 = total(own1, parts1)

time: 416 us -> 387 us (0.930)
  Pallas kernels: 110 us -> 96.2 us
  other arithmetic: 26.4 us -> 20 us
  starting transfers between devices: 101 us -> 95.6 us
  local copies, waits for them, and re-layouts: 10.4 us -> 5.47 us
    ppermute x32 -> x26, waiting for transfers between devices: 115 us -> 89.5 us  [swap(): return lax.ppermute(array, axis, [(i, i ^ bits) for i in range(size)])]
    pallas_call x7 -> x5, Pallas kernels: 82.1 us -> 68.2 us  [the longest x3 55.2 us: expert(): pl.pallas_call(functools.partial(expert_kernel, len(parts), first_tiles,...]
    all_to_all x6 -> x5, waiting for transfers between devices: 6.85 us -> 20.6 us  [to_experts(): return lax.all_to_all(rows, 'node', 0, 0, tiled=True)]
    all_to_all x6 -> x5, starting transfers between devices: 41.2 us -> 28.3 us  [to_experts(): return lax.all_to_all(rows, 'node', 0, 0, tiled=True)]
    ppermute x6, waiting for transfers between devices: 29.9 us -> 40.4 us  [chain_sum(): lax.ppermute(side[size - 1 - step].astype(BF16), axis, way)]
    ppermute x32 -> x26, starting transfers between devices: 33 us -> 37.8 us  [swap(): return lax.ppermute(array, axis, [(i, i ^ bits) for i in range(size)])]
    unnamed x72 -> x47, local copies, waits for them, and re-layouts: 9.5 us -> 5.32 us
    add x7 -> x5, other arithmetic: 9.06 us -> 5.54 us  [fence(): sum((a.reshape(-1, a.shape[-1])[:16, :LANES].astype(F32) for a in after))]
  transfers between devices with their start and end apart: 50 -> 43, of which waited for: 22 -> 20; matrix products, arithmetic and copies ran while one was open for 4% -> 4% of each run, Pallas kernels for 22% -> 24%
where the time goes in v6:
time: 387 us; the launch traced here: 384 us
  waiting for transfers between devices  166 us (43%)
  Pallas kernels  96.2 us (25%)
  starting transfers between devices  95.6 us (25%)
  other arithmetic  20 us (5%)
  local copies, waits for them, and re-layouts  5.47 us (1%)
    ppermute x26, waiting for transfers between devices, swap(): return lax.ppermute(array, axis, [(i, i ^ bits) for i in range(size)])  89.5 us
    pallas_call x3, Pallas kernels, expert(): pl.pallas_call(functools.partial(expert_kernel, len(parts), first_tiles,...  55.2 us
    ppermute x6, waiting for transfers between devices, chain_sum(): lax.ppermute(side[size - 1 - step].astype(BF16), axis, way)  40.4 us
    ppermute x26, starting transfers between devices, swap(): return lax.ppermute(array, axis, [(i, i ^ bits) for i in range(size)])  37.8 us
    all_to_all x5, starting transfers between devices, to_experts(): return lax.all_to_all(rows, 'node', 0, 0, tiled=True)  28.3 us
    all_to_all x5, waiting for transfers between devices, to_experts(): return lax.all_to_all(rows, 'node', 0, 0, tiled=True)  20.6 us
    ppermute x6, starting transfers between devices, chain_step(): lax.ppermute(a, axis, way)  17.8 us
    ppermute x6, waiting for transfers between devices, chain_step(): lax.ppermute(a, axis, way)  16 us
  transfers between devices with their start and end apart: 43, of which 20 were waited for; matrix products, arithmetic and copies ran while one was open for 4% of the time, Pallas kernels for 24%

profile of v6, /device:TPU:9, one launch (start us, length us, event | category | flops | bytes accessed | tf_op | source)
XLA Modules:
  0.0 384.1 jit_solution(4212798181843484161)
XLA Ops:
  0.0 2.9 shard_map.262
  2.9 1.3 collective-permute-start.2
  9.1 1.3 collective-permute-start.4
  10.4 1.3 collective-permute-start.5
  11.7 10.6 %collective-permute-done.2.refs_3_.refs_7_ = bf16[32,4224]{1,0:T(8,128)(2,1)S(1)} collective-permute-done((bf16[32,4224]{1,0:T(8,128)(2,1)}, bf16[32,4224]{1,0:T(8,128)(2,1)S(1)}, u32[]{:S(2)}, u32[]{:S(2)}) %collective-permute-start.2) | collective-permute-done | bytes 270368 | tf_op jit(solution)/shard_map/ppermute | solution.py:38
  22.2 4.8 %collective-permute-done.1.refs_2_.refs_6_ = bf16[32,4224]{1,0:T(8,128)(2,1)S(1)} collective-permute-done((bf16[32,4224]{1,0:T(8,128)(2,1)}, bf16[32,4224]{1,0:T(8,128)(2,1)S(1)}, u32[]{:S(2)}, u32[]{:S(2)}) %collective-permute-start.1) | collective-permute-done | bytes 270368 | tf_op jit(solution)/shard_map/ppermute | solution.py:38
  29.4 4.1 %collective-permute-start.9 = (bf16[64,4224]{1,0:T(8,128)(2,1)}, bf16[64,4224]{1,0:T(8,128)(2,1)S(1)}, u32[]{:S(2)}, u32[]{:S(2)}) collective-permute-start(bf16[64,4224]{1,0:T(8,128)(2,1)} %get-tuple-element.69.refs_0_.refs_7_), channel_id=1, source_target_pairs={{3,2},{2,1},{1,0},{7,6},{6,5},{5,4},{11,10},{10,9},{9,8},{15,14},{... | collective-permute-start | bytes 1622024 | tf_op jit(solution)/shard_map/ppermute | solution.py:54
  33.5 1.9 collective-permute-start.8
  35.4 1.3 collective-permute-start.7
  36.7 1.2 collective-permute-start.6
  38.6 5.3 %shard_map.263 = (bf16[8,1,48,4096]{3,2,1,0:T(8,128)(2,1)}, bf16[224,384]{1,0:T(8,128)(2,1)}) custom-call(s32[2]{0:T(128)} %pad_add_fusion.ids.tie.refs_1_, bf16[32,4224]{1,0:T(8,128)(2,1)} %get-tuple-element.62.refs_0_.refs_4_, bf16[32,4224]{1,0:T(8,128)(2,1)} %copy-done.13, bf16[32,4224]{1,0:T(8,128)(2,1)} %copy-done.12, bf16[32,4224]{1,0:T(8,128)(2,1)} %copy-done.11, ...), custom_call_target="tpu_custom_call" | custom-call | flops 402653184 | bytes 4194304 | tf_op jit(solution)/shard_map/pallas_call | solution.py:197
  44.0 3.7 collective-permute-done.8.refs_1_.refs_8_
  49.4 6.4 %all-to-all-start = ((bf16[8,1,48,4096]{3,2,1,0:T(8,128)(2,1)}), bf16[8,1,48,4096]{3,2,1,0:T(8,128)(2,1)S(1)}, u32[]{:S(2)}, u32[]{:S(2)}) async-start(bf16[8,1,48,4096]{3,2,1,0:T(8,128)(2,1)} %get-tuple-element.70), calls=%async_computation | async-start | bytes 6291456 | tf_op jit(solution)/shard_map/all_to_all | solution.py:491
  55.8 3.4 collective-permute-start.11
  59.2 2.7 collective-permute-start.10
  61.9 9.7 %collective-permute-done.11.refs_4_.refs_11_ = bf16[64,4224]{1,0:T(8,128)(2,1)S(1)} collective-permute-done((bf16[64,4224]{1,0:T(8,128)(2,1)}, bf16[64,4224]{1,0:T(8,128)(2,1)S(1)}, u32[]{:S(2)}, u32[]{:S(2)}) %collective-permute-start.11) | collective-permute-done | bytes 540704 | tf_op jit(solution)/shard_map/ppermute | solution.py:54
  71.6 4.2 %collective-permute-start.13 = (bf16[64,4224]{1,0:T(8,128)(2,1)S(1)}, bf16[64,4224]{1,0:T(8,128)(2,1)}, u32[]{:S(2)}, u32[]{:S(2)}) collective-permute-start(bf16[64,4224]{1,0:T(8,128)(2,1)S(1)} %collective-permute-done.11.refs_4_.refs_11_), channel_id=1, source_target_pairs={{1,0},{5,4},{9,8},{13,12},{17,16},{21,20},{25,24},{29,28}} | collective-permute-start | bytes 1622024 | tf_op jit(solution)/shard_map/ppermute | solution.py:54
  75.8 1.5 collective-permute-start.12
  77.3 5.8 %shard_map.268 = (bf16[96,4096]{1,0:T(8,128)(2,1)}, bf16[96,4096]{1,0:T(8,128)(2,1)}, bf16[96,4096]{1,0:T(8,128)(2,1)}, bf16[96,4096]{1,0:T(8,128)(2,1)}, bf16[2...) custom-call(s32[2]{0:T(128)} %pad_add_fusion.ids.tie.refs_1_, bf16[128,2048]{1,0:T(8,128)(2,1)} %get-tuple-element.67.a0, ...), custom_call_target="tpu_custom_call" | custom-call | flops 805306368 | bytes 5242880 | tf_op jit(solution)/shard_map/pallas_call | solution.py:275
  83.1 2.5 collective-permute-done.13.refs_6_.refs_13_
  85.6 7.7 %shard_map.267 = (bf16[8,2,48,4096]{3,2,1,0:T(8,128)(2,1)}, bf16[128,384]{1,0:T(8,128)(2,1)}, bf16[128,384]{1,0:T(8,128)(2,1)}) custom-call(s32[2]{0:T(128)} %pad_add_fusion.ids.tie.refs_1_, bf16[64,4224]{1,0:T(8,128)(2,1)} %get-tuple-element.69.refs_0_.refs_7_, bf16[64,4224]{1,0:T(8,128)(2,1)} %copy-done.8, bf16[64,4224]{1,0:T(8,128)(2,1)} %copy-done.7, ...), custom_call_target="tpu_custom_call" | custom-call | flops 1409286144 | bytes 9961472 | tf_op jit(solution)/shard_map/pallas_call | solution.py:197
  95.0 6.6 %all-to-all-start.1 = ((bf16[8,2,48,4096]{3,2,1,0:T(8,128)(2,1)}), bf16[8,2,48,4096]{3,2,1,0:T(8,128)(2,1)}, u32[]{:S(2)}, u32[]{:S(2)}) async-start(bf16[8,2,48,4096]{3,2,1,0:T(8,128)(2,1)} %get-tuple-element.77), calls=%async_computation.1 | async-start | bytes 12582912 | tf_op jit(solution)/shard_map/all_to_all | solution.py:491
  101.6 2.3 collective-permute-start.14
  103.9 2.0 collective-permute-start.15
  106.3 15.9 %shard_map.266.refs_0_ = bf16[384,4096]{1,0:T(8,128)(2,1)} custom-call(s32[2]{0:T(128)} %pad_add_fusion.ids.tie.refs_1_, bf16[384,4096]{1,0:T(8,128)(2,1)} %bitcast.26, bf16[4096,768]{1,0:T(8,128)(2,1)} %bitcast.30, bf16[4096,768]{1,0:T(8,128)(2,1)} %bitcast.33, bf16[768,4096]{1,0:T(8,128)(2,1)} %bitcast.36), custom_call_target="tpu_custom_call" | custom-call | flops 7247757312 | bytes 25165824 | tf_op jit(solution)/shard_map/pallas_call | solution.py:423
  122.2 14.9 %collective-permute-done.14.refs_1_ = bf16[96,4096]{1,0:T(8,128)(2,1)S(1)} collective-permute-done((bf16[96,4096]{1,0:T(8,128)(2,1)S(1)}, bf16[96,4096]{1,0:T(8,128)(2,1)S(1)}, u32[]{:S(2)}, u32[]{:S(2)}) %collective-permute-start.14) | collective-permute-done | bytes 786464 | tf_op jit(solution)/shard_map/ppermute | solution.py:38
  137.1 19.4 %collective-permute-done.15.refs_2_ = bf16[96,4096]{1,0:T(8,128)(2,1)} collective-permute-done((bf16[96,4096]{1,0:T(8,128)(2,1)S(1)}, bf16[96,4096]{1,0:T(8,128)(2,1)}, u32[]{:S(2)}, u32[]{:S(2)}) %collective-permute-start.15) | collective-permute-done | bytes 786464 | tf_op jit(solution)/shard_map/ppermute | solution.py:38
  156.5 17.9 %collective-permute-done.16.refs_3_ = bf16[96,4096]{1,0:T(8,128)(2,1)} collective-permute-done((bf16[96,4096]{1,0:T(8,128)(2,1)S(1)}, bf16[96,4096]{1,0:T(8,128)(2,1)}, u32[]{:S(2)}, u32[]{:S(2)}) %collective-permute-start.16) | collective-permute-done | bytes 786464 | tf_op jit(solution)/shard_map/ppermute | solution.py:38
  174.4 1.3 convert_add_fusion.4.refs_2_
  175.7 4.9 %all-to-all-start.2 = ((bf16[8,48,4096]{2,1,0:T(8,128)(2,1)}), bf16[8,48,4096]{2,1,0:T(8,128)(2,1)S(1)}, u32[]{:S(2)}, u32[]{:S(2)}) async-start(bf16[8,48,4096]{2,1,0:T(8,128)(2,1)} %bitcast.24), calls=%async_computation.2 | async-start | bytes 6291456 | tf_op jit(solution)/shard_map/all_to_all | solution.py:491
  180.6 16.1 %shard_map.274 = (bf16[96,4096]{1,0:T(8,128)(2,1)}, bf16[96,4096]{1,0:T(8,128)(2,1)}, bf16[96,4096]{1,0:T(8,128)(2,1)}, bf16[96,4096]{1,0:T(8,128)(2,1)}) custom-call(s32[2]{0:T(128)} %get-tuple-element.81.tie, bf16[96,4096]{1,0:T(8,128)(2,1)} %get-tuple-element.92.refs_0_, bf16[96,4096]{1,0:T(8,128)(2,1)} %copy-done.22, ...), custom_call_target="tpu_custom_call" | custom-call | flops 7247757312 | bytes 25165824 | tf_op jit(solution)/shard_map/pallas_call | solution.py:423
  196.7 2.4 collective-permute-start.24
  199.1 23.2 %shard_map.271 = (bf16[384,4096]{1,0:T(8,128)(2,1)}, bf16[384,4096]{1,0:T(8,128)(2,1)}) custom-call(s32[2]{0:T(128)} %get-tuple-element.81.tie, bf16[768,4096]{1,0:T(8,128)(2,1)} %bitcast.9.refs_0_, bf16[4096,768]{1,0:T(8,128)(2,1)} %bitcast.32, bf16[4096,768]{1,0:T(8,128)(2,1)} %bitcast.35, bf16[768,4096]{1,0:T(8,128)(2,1)} %bitcast.38), custom_call_target="tpu_custom_call" | custom-call | flops 14495514624 | bytes 31457280 | tf_op jit(solution)/shard_map/pallas_call | solution.py:423
  222.3 1.3 slice_convert_fusion.7.refs_1_
  223.6 1.6 copy-done.2
  225.2 4.6 %shard_map.273 = (f32[32,4096]{1,0:T(8,128)}, bf16[32,4096]{1,0:T(8,128)(2,1)}, bf16[32,4096]{1,0:T(8,128)(2,1)}, bf16[32,4096]{1,0:T(8,128)(2,1)}, bf16[32,4096...) custom-call(bf16[224,384]{1,0:T(8,128)(2,1)} %shard_map.272.mixing, bf16[384,4096]{1,0:T(8,128)(2,1)} %bitcast.21), custom_call_target="tpu_custom_call" | custom-call | flops 704643072 | bytes 4980736 | tf_op jit(solution)/shard_map/pallas_call | solution.py:310
  229.8 1.3 collective-permute-start.17
  231.1 2.9 collective-permute-done.24.refs_2_
  234.1 1.3 convert_add_fusion.3.refs_2_
  235.4 4.8 %all-to-all-start.3 = ((bf16[8,48,4096]{2,1,0:T(8,128)(2,1)}), bf16[8,48,4096]{2,1,0:T(8,128)(2,1)S(1)}, u32[]{:S(2)}, u32[]{:S(2)}) async-start(bf16[8,48,4096]{2,1,0:T(8,128)(2,1)} %bitcast.23), calls=%async_computation.3 | async-start | bytes 6291456 | tf_op jit(solution)/shard_map/all_to_all | solution.py:491
  242.8 2.5 collective-permute-start.18
  246.4 1.3 collective-permute-start.21
  247.7 33.7 %collective-permute-done.18 = bf16[32,4096]{1,0:T(8,128)(2,1)S(1)} collective-permute-done((bf16[32,4096]{1,0:T(8,128)(2,1)S(1)}, bf16[32,4096]{1,0:T(8,128)(2,1)S(1)}, u32[]{:S(2)}, u32[]{:S(2)}) %collective-permute-start.18) | collective-permute-done | bytes 262176 | tf_op jit(solution)/shard_map/ppermute | solution.py:67
  281.5 4.1 %collective-permute-start.19 = (bf16[32,4096]{1,0:T(8,128)(2,1)S(1)}, bf16[32,4096]{1,0:T(8,128)(2,1)S(1)}, u32[]{:S(2)}, u32[]{:S(2)}) collective-permute-start(bf16[32,4096]{1,0:T(8,128)(2,1)S(1)} %add_convert_fusion.5), channel_id=1, source_target_pairs={{0,1},{1,2},{2,3},{4,5},{5,6},{6,7},{8,9},{9,10},{10,11},{12,13},{... | collective-permute-start | bytes 786440 | tf_op jit(solution)/shard_map/ppermute | solution.py:67
  286.6 1.9 collective-permute-start.22
  288.5 1.9 collective-permute-done.19
  290.4 4.8 %collective-permute-done.22 = bf16[32,4096]{1,0:T(8,128)(2,1)S(1)} collective-permute-done((bf16[32,4096]{1,0:T(8,128)(2,1)S(1)}, bf16[32,4096]{1,0:T(8,128)(2,1)S(1)}, u32[]{:S(2)}, u32[]{:S(2)}) %collective-permute-start.22) | collective-permute-done | bytes 262176 | tf_op jit(solution)/shard_map/ppermute | solution.py:67
  295.9 1.6 convert_add_fusion.2.refs_1_
  297.6 5.5 %all-to-all-start.4 = ((bf16[8,48,4096]{2,1,0:T(8,128)(2,1)}), bf16[8,48,4096]{2,1,0:T(8,128)(2,1)S(1)}, u32[]{:S(2)}, u32[]{:S(2)}) async-start(bf16[8,48,4096]{2,1,0:T(8,128)(2,1)} %bitcast.16), calls=%async_computation.4 | async-start | bytes 6291456 | tf_op jit(solution)/shard_map/all_to_all | solution.py:491
  303.1 5.7 %shard_map.277 = (f32[128,2048]{1,0:T(8,128)}, bf16[128,2048]{1,0:T(8,128)(2,1)}, f32[128,2048]{1,0:T(8,128)}, bf16[128,2048]{1,0:T(8,128)(2,1)}) custom-call(bf16[256,384]{1,0:T(8,128)(2,1)} %get-tuple-element.103.mixing_a, bf16[256,384]{1,0:T(8,128)(2,1)} %get-tuple-element.104.mixing_b, bf16[96,4096]{1,0:T(8,128)(2,1)} %get-tuple-element.105.refs_0_, ...), custom_call_target="tpu_custom_call" | custom-call | flops 805306368 | bytes 5242880 | tf_op jit(solution)/shard_map/pallas_call | solution.py:352
  309.9 4.4 %shard_map.276 = (f32[32,4096]{1,0:T(8,128)}, bf16[32,4096]{1,0:T(8,128)(2,1)}, bf16[32,4096]{1,0:T(8,128)(2,1)}, bf16[32,4096]{1,0:T(8,128)(2,1)}) custom-call(bf16[128,384]{1,0:T(8,128)(2,1)} %get-tuple-element.91.mixing, bf16[384,4096]{1,0:T(8,128)(2,1)} %bitcast.18), custom_call_target="tpu_custom_call" | custom-call | flops 402653184 | bytes 4194304 | tf_op jit(solution)/shard_map/pallas_call | solution.py:310
  315.5 1.4 collective-permute-start.27
  316.9 20.6 %all-to-all-done.4 = bf16[8,48,4096]{2,1,0:T(8,128)(2,1)S(1)} async-done(((bf16[8,48,4096]{2,1,0:T(8,128)(2,1)}), bf16[8,48,4096]{2,1,0:T(8,128)(2,1)S(1)}, u32[]{:S(2)}, u32[]{:S(2)}) %all-to-all-start.4) | async-done | bytes 3145760 | tf_op jit(solution)/shard_map/all_to_all | solution.py:491
  338.1 1.3 slice_convert_fusion.6.refs_1_
  339.4 4.5 %shard_map.281 = (f32[32,4096]{1,0:T(8,128)}, bf16[32,4096]{1,0:T(8,128)(2,1)}, bf16[32,4096]{1,0:T(8,128)(2,1)}, bf16[32,4096]{1,0:T(8,128)(2,1)}) custom-call(bf16[128,384]{1,0:T(8,128)(2,1)} %shard_map.280.mixing, bf16[384,4096]{1,0:T(8,128)(2,1)} %bitcast.20), custom_call_target="tpu_custom_call" | custom-call | flops 402653184 | bytes 4194304 | tf_op jit(solution)/shard_map/pallas_call | solution.py:310
  345.2 1.5 collective-permute-start.31
  346.6 1.5 add_convert_fusion.1
  349.3 2.3 collective-permute-start.35
  351.7 1.9 collective-permute-done.30
  353.6 14.8 %collective-permute-done.31 = bf16[32,4096]{1,0:T(8,128)(2,1)S(1)} collective-permute-done((bf16[32,4096]{1,0:T(8,128)(2,1)}, bf16[32,4096]{1,0:T(8,128)(2,1)S(1)}, u32[]{:S(2)}, u32[]{:S(2)}) %collective-permute-start.31) | collective-permute-done | bytes 262176 | tf_op jit(solution)/shard_map/ppermute | solution.py:38
  369.7 1.3 collective-permute-start.36
  371.1 3.5 collective-permute-start.33
  375.1 3.9 %collective-permute-start.37 = (bf16[32,2048]{1,0:T(8,128)(2,1)S(1)}, bf16[32,2048]{1,0:T(8,128)(2,1)S(1)}, u32[]{:S(2)}, u32[]{:S(2)}) collective-permute-start(bf16[32,2048]{1,0:T(8,128)(2,1)S(1)} %split.58), channel_id=1, source_target_pairs={{0,4},{4,0},{8,12},{12,8},{16,20},{20,16},{24,28},{28,24},{1,5},{5... | collective-permute-start | bytes 393224 | tf_op jit(solution)/shard_map/ppermute | solution.py:38
  379.5 2.5 collective-permute-start.34
  (122 shorter events, 27.0 us)
Async XLA Ops:
  2.9 19.3 %collective-permute-start.2 = (bf16[32,4224]{1,0:T(8,128)(2,1)}, bf16[32,4224]{1,0:T(8,128)(2,1)S(1)}, u32[]{:S(2)}, u32[]{:S(2)}) collective-permute-start(bf16[32,4224]{1,0:T(8,128)(2,1)} %get-tuple-element.62.refs_0_.refs_4_), channel_id=1, source_target_pairs={{0,3},{1,2},{2,1},{3,0},{4,7},{5,6},{6,5},{7,4},{8,11},{9,10},{10,... | collective-permute-start | bytes 811016 | tf_op jit(solution)/shard_map/ppermute | solution.py:38
  4.2 22.8 %collective-permute-start.1 = (bf16[32,4224]{1,0:T(8,128)(2,1)}, bf16[32,4224]{1,0:T(8,128)(2,1)S(1)}, u32[]{:S(2)}, u32[]{:S(2)}) collective-permute-start(bf16[32,4224]{1,0:T(8,128)(2,1)} %get-tuple-element.62.refs_0_.refs_4_), channel_id=1, source_target_pairs={{0,2},{1,3},{2,0},{3,1},{4,6},{5,7},{6,4},{7,5},{8,10},{9,11},{10,... | collective-permute-start | bytes 811016 | tf_op jit(solution)/shard_map/ppermute | solution.py:38
  5.2 21.8 %collective-permute-start = (bf16[32,4224]{1,0:T(8,128)(2,1)}, bf16[32,4224]{1,0:T(8,128)(2,1)S(1)}, u32[]{:S(2)}, u32[]{:S(2)}) collective-permute-start(bf16[32,4224]{1,0:T(8,128)(2,1)} %get-tuple-element.62.refs_0_.refs_4_), channel_id=1, source_target_pairs={{0,1},{1,0},{2,3},{3,2},{4,5},{5,4},{6,7},{7,6},{8,9},{9,8},{10,11... | collective-permute-start | bytes 811016 | tf_op jit(solution)/shard_map/ppermute | solution.py:38
  6.4 2.6 collective-permute-start.3
  9.1 18.6 %collective-permute-start.4 = (bf16[64,2048]{1,0:T(8,128)(2,1)S(1)}, bf16[64,2048]{1,0:T(8,128)(2,1)S(1)}, u32[]{:S(2)}, u32[]{:S(2)}) collective-permute-start(bf16[64,2048]{1,0:T(8,128)(2,1)S(1)} %slice.92), channel_id=1, source_target_pairs={{0,8},{4,12},{8,0},{12,4},{16,24},{20,28},{24,16},{28,20},{1,9},{5... | collective-permute-start | bytes 786440 | tf_op jit(solution)/shard_map/ppermute | solution.py:38
  10.4 18.2 %collective-permute-start.5 = (bf16[64,2176]{1,0:T(8,128)(2,1)S(1)}, bf16[64,2176]{1,0:T(8,128)(2,1)S(1)}, u32[]{:S(2)}, u32[]{:S(2)}) collective-permute-start(bf16[64,2176]{1,0:T(8,128)(2,1)S(1)} %slice.93), channel_id=1, source_target_pairs={{0,16},{4,20},{8,24},{12,28},{16,0},{20,4},{24,8},{28,12},{1,17},{... | collective-permute-start | bytes 835592 | tf_op jit(solution)/shard_map/ppermute | solution.py:38
  22.2 16.3 %copy-start.11 = (bf16[32,4224]{1,0:T(8,128)(2,1)}, bf16[32,4224]{1,0:T(8,128)(2,1)S(1)}, u32[]{:S(2)}) copy-start(bf16[32,4224]{1,0:T(8,128)(2,1)S(1)} %collective-permute-done.2.refs_3_.refs_7_) | copy-start | bytes 811012
  27.0 11.5 %copy-start.12 = (bf16[32,4224]{1,0:T(8,128)(2,1)}, bf16[32,4224]{1,0:T(8,128)(2,1)S(1)}, u32[]{:S(2)}) copy-start(bf16[32,4224]{1,0:T(8,128)(2,1)S(1)} %collective-permute-done.1.refs_2_.refs_6_) | copy-start | bytes 811012
  27.0 11.5 %copy-start.13 = (bf16[32,4224]{1,0:T(8,128)(2,1)}, bf16[32,4224]{1,0:T(8,128)(2,1)S(1)}, u32[]{:S(2)}) copy-start(bf16[32,4224]{1,0:T(8,128)(2,1)S(1)} %collective-permute-done.refs_1_.refs_5_) | copy-start | bytes 811012
  29.4 14.6 %collective-permute-start.9 = (bf16[64,4224]{1,0:T(8,128)(2,1)}, bf16[64,4224]{1,0:T(8,128)(2,1)S(1)}, u32[]{:S(2)}, u32[]{:S(2)}) collective-permute-start(bf16[64,4224]{1,0:T(8,128)(2,1)} %get-tuple-element.69.refs_0_.refs_7_), channel_id=1, source_target_pairs={{3,2},{2,1},{1,0},{7,6},{6,5},{5,4},{11,10},{10,9},{9,8},{15,14},{... | collective-permute-start | bytes 1622024 | tf_op jit(solution)/shard_map/ppermute | solution.py:54
  33.5 14.2 %collective-permute-start.8 = (bf16[64,4224]{1,0:T(8,128)(2,1)}, bf16[64,4224]{1,0:T(8,128)(2,1)S(1)}, u32[]{:S(2)}, u32[]{:S(2)}) collective-permute-start(bf16[64,4224]{1,0:T(8,128)(2,1)} %get-tuple-element.69.refs_0_.refs_7_), channel_id=1, source_target_pairs={{0,1},{1,2},{2,3},{4,5},{5,6},{6,7},{8,9},{9,10},{10,11},{12,13},{... | collective-permute-start | bytes 1622024 | tf_op jit(solution)/shard_map/ppermute | solution.py:54
  35.4 13.0 %collective-permute-start.7 = (bf16[128,2176]{1,0:T(8,128)(2,1)}, bf16[128,2176]{1,0:T(8,128)(2,1)S(1)}, u32[]{:S(2)}, u32[]{:S(2)}) collective-permute-start(bf16[128,2176]{1,0:T(8,128)(2,1)} %get-tuple-element.68.b0.t0), channel_id=1, source_target_pairs={{0,8},{4,12},{8,0},{12,4},{16,24},{20,28},{24,16},{28,20},{1,9},{5... | collective-permute-start | bytes 1671176 | tf_op jit(solution)/shard_map/ppermute | solution.py:38
  36.7 11.7 %collective-permute-start.6 = (bf16[128,2048]{1,0:T(8,128)(2,1)}, bf16[128,2048]{1,0:T(8,128)(2,1)S(1)}, u32[]{:S(2)}, u32[]{:S(2)}) collective-permute-start(bf16[128,2048]{1,0:T(8,128)(2,1)} %get-tuple-element.67.a0), channel_id=1, source_target_pairs={{0,16},{4,20},{8,24},{12,28},{16,0},{20,4},{24,8},{28,12},{1,17},{... | collective-permute-start | bytes 1572872 | tf_op jit(solution)/shard_map/ppermute | solution.py:38
  44.0 5.4 %copy-start.7 = (bf16[64,4224]{1,0:T(8,128)(2,1)}, bf16[64,4224]{1,0:T(8,128)(2,1)S(1)}, u32[]{:S(2)}) copy-start(bf16[64,4224]{1,0:T(8,128)(2,1)S(1)} %collective-permute-done.9.refs_2_.refs_9_) | copy-start | bytes 1622020
  47.7 1.7 copy-start.8
  48.4 1.0 copy-start.3
  49.4 43.9 %all-to-all-start = ((bf16[8,1,48,4096]{3,2,1,0:T(8,128)(2,1)}), bf16[8,1,48,4096]{3,2,1,0:T(8,128)(2,1)S(1)}, u32[]{:S(2)}, u32[]{:S(2)}) async-start(bf16[8,1,48,4096]{3,2,1,0:T(8,128)(2,1)} %get-tuple-element.70), calls=%async_computation | async-start | bytes 6291456 | tf_op jit(solution)/shard_map/all_to_all | solution.py:491
  55.8 15.8 %collective-permute-start.11 = (bf16[64,4224]{1,0:T(8,128)(2,1)}, bf16[64,4224]{1,0:T(8,128)(2,1)S(1)}, u32[]{:S(2)}, u32[]{:S(2)}) collective-permute-start(bf16[64,4224]{1,0:T(8,128)(2,1)} %copy-done.7), channel_id=1, source_target_pairs={{2,1},{1,0},{6,5},{5,4},{10,9},{9,8},{14,13},{13,12},{18,17},{17,1... | collective-permute-start | bytes 1622024 | tf_op jit(solution)/shard_map/ppermute | solution.py:54
  59.2 16.6 %collective-permute-start.10 = (bf16[64,4224]{1,0:T(8,128)(2,1)}, bf16[64,4224]{1,0:T(8,128)(2,1)}, u32[]{:S(2)}, u32[]{:S(2)}) collective-permute-start(bf16[64,4224]{1,0:T(8,128)(2,1)} %copy-done.8), channel_id=1, source_target_pairs={{1,2},{2,3},{5,6},{6,7},{9,10},{10,11},{13,14},{14,15},{17,18},{18... | collective-permute-start | bytes 1622024 | tf_op jit(solution)/shard_map/ppermute | solution.py:54
  71.6 14.0 %copy-start.9 = (bf16[64,4224]{1,0:T(8,128)(2,1)}, bf16[64,4224]{1,0:T(8,128)(2,1)S(1)}, u32[]{:S(2)}) copy-start(bf16[64,4224]{1,0:T(8,128)(2,1)S(1)} %collective-permute-done.11.refs_4_.refs_11_) | copy-start | bytes 1622020
  71.6 14.0 %collective-permute-start.13 = (bf16[64,4224]{1,0:T(8,128)(2,1)S(1)}, bf16[64,4224]{1,0:T(8,128)(2,1)}, u32[]{:S(2)}, u32[]{:S(2)}) collective-permute-start(bf16[64,4224]{1,0:T(8,128)(2,1)S(1)} %collective-permute-done.11.refs_4_.refs_11_), channel_id=1, source_target_pairs={{1,0},{5,4},{9,8},{13,12},{17,16},{21,20},{25,24},{29,28}} | collective-permute-start | bytes 1622024 | tf_op jit(solution)/shard_map/ppermute | solution.py:54
  75.8 9.8 %collective-permute-start.12 = (bf16[64,4224]{1,0:T(8,128)(2,1)}, bf16[64,4224]{1,0:T(8,128)(2,1)}, u32[]{:S(2)}, u32[]{:S(2)}) collective-permute-start(bf16[64,4224]{1,0:T(8,128)(2,1)} %collective-permute-done.10.refs_3_.refs_10_), channel_id=1, source_target_pairs={{2,3},{6,7},{10,11},{14,15},{18,19},{22,23},{26,27},{30,31}} | collective-permute-start | bytes 1622024 | tf_op jit(solution)/shard_map/ppermute | solution.py:54
  93.4 1.6 copy-start.6
  95.0 6.6 %copy-start.14 = (bf16[96,4096]{1,0:T(8,128)(2,1)S(1)}, bf16[96,4096]{1,0:T(8,128)(2,1)}, u32[]{:S(2)}) copy-start(bf16[96,4096]{1,0:T(8,128)(2,1)} %get-tuple-element.78) | copy-start | bytes 2359300
  95.0 9.0 %copy-start.15 = (bf16[96,4096]{1,0:T(8,128)(2,1)S(1)}, bf16[96,4096]{1,0:T(8,128)(2,1)}, u32[]{:S(2)}) copy-start(bf16[96,4096]{1,0:T(8,128)(2,1)} %get-tuple-element.79) | copy-start | bytes 2359300
  95.0 11.0 %copy-start.16 = (bf16[96,4096]{1,0:T(8,128)(2,1)S(1)}, bf16[96,4096]{1,0:T(8,128)(2,1)}, u32[]{:S(2)}) copy-start(bf16[96,4096]{1,0:T(8,128)(2,1)} %get-tuple-element.80) | copy-start | bytes 2359300
  95.0 79.4 %all-to-all-start.1 = ((bf16[8,2,48,4096]{3,2,1,0:T(8,128)(2,1)}), bf16[8,2,48,4096]{3,2,1,0:T(8,128)(2,1)}, u32[]{:S(2)}, u32[]{:S(2)}) async-start(bf16[8,2,48,4096]{3,2,1,0:T(8,128)(2,1)} %get-tuple-element.77), calls=%async_computation.1 | async-start | bytes 12582912 | tf_op jit(solution)/shard_map/all_to_all | solution.py:491
  101.6 35.5 %collective-permute-start.14 = (bf16[96,4096]{1,0:T(8,128)(2,1)S(1)}, bf16[96,4096]{1,0:T(8,128)(2,1)S(1)}, u32[]{:S(2)}, u32[]{:S(2)}) collective-permute-start(bf16[96,4096]{1,0:T(8,128)(2,1)S(1)} %copy-done.14), channel_id=1, source_target_pairs={{0,1},{1,0},{2,3},{3,2},{4,5},{5,4},{6,7},{7,6},{8,9},{9,8},{10,11... | collective-permute-start | bytes 2359304 | tf_op jit(solution)/shard_map/ppermute | solution.py:38
  103.9 52.5 %collective-permute-start.15 = (bf16[96,4096]{1,0:T(8,128)(2,1)S(1)}, bf16[96,4096]{1,0:T(8,128)(2,1)}, u32[]{:S(2)}, u32[]{:S(2)}) collective-permute-start(bf16[96,4096]{1,0:T(8,128)(2,1)S(1)} %copy-done.15), channel_id=1, source_target_pairs={{0,2},{1,3},{2,0},{3,1},{4,6},{5,7},{6,4},{7,5},{8,10},{9,11},{10,... | collective-permute-start | bytes 2359304 | tf_op jit(solution)/shard_map/ppermute | solution.py:38
  106.0 68.4 %collective-permute-start.16 = (bf16[96,4096]{1,0:T(8,128)(2,1)S(1)}, bf16[96,4096]{1,0:T(8,128)(2,1)}, u32[]{:S(2)}, u32[]{:S(2)}) collective-permute-start(bf16[96,4096]{1,0:T(8,128)(2,1)S(1)} %copy-done.16), channel_id=1, source_target_pairs={{0,3},{1,2},{2,1},{3,0},{4,7},{5,6},{6,5},{7,4},{8,11},{9,10},{10,... | collective-permute-start | bytes 2359304 | tf_op jit(solution)/shard_map/ppermute | solution.py:38
  137.1 38.6 %copy-start.22 = (bf16[96,4096]{1,0:T(8,128)(2,1)}, bf16[96,4096]{1,0:T(8,128)(2,1)S(1)}, u32[]{:S(2)}) copy-start(bf16[96,4096]{1,0:T(8,128)(2,1)S(1)} %collective-permute-done.14.refs_1_) | copy-start | bytes 2359300
  175.7 47.9 %all-to-all-start.2 = ((bf16[8,48,4096]{2,1,0:T(8,128)(2,1)}), bf16[8,48,4096]{2,1,0:T(8,128)(2,1)S(1)}, u32[]{:S(2)}, u32[]{:S(2)}) async-start(bf16[8,48,4096]{2,1,0:T(8,128)(2,1)} %bitcast.24), calls=%async_computation.2 | async-start | bytes 6291456 | tf_op jit(solution)/shard_map/all_to_all | solution.py:491
  196.7 34.5 %collective-permute-start.23 = (bf16[96,4096]{1,0:T(8,128)(2,1)}, bf16[96,4096]{1,0:T(8,128)(2,1)}, u32[]{:S(2)}, u32[]{:S(2)}) collective-permute-start(bf16[96,4096]{1,0:T(8,128)(2,1)} %get-tuple-element.95), channel_id=1, source_target_pairs={{0,1},{1,0},{2,3},{3,2},{4,5},{5,4},{6,7},{7,6},{8,9},{9,8},{10,11... | collective-permute-start | bytes 2359304 | tf_op jit(solution)/shard_map/ppermute | solution.py:38
  196.7 37.3 %collective-permute-start.24 = (bf16[96,4096]{1,0:T(8,128)(2,1)}, bf16[96,4096]{1,0:T(8,128)(2,1)}, u32[]{:S(2)}, u32[]{:S(2)}) collective-permute-start(bf16[96,4096]{1,0:T(8,128)(2,1)} %get-tuple-element.96), channel_id=1, source_target_pairs={{0,2},{1,3},{2,0},{3,1},{4,6},{5,7},{6,4},{7,5},{8,10},{9,11},{10,... | collective-permute-start | bytes 2359304 | tf_op jit(solution)/shard_map/ppermute | solution.py:38
  223.6 1.6 copy-start.2
  229.8 11.9 %collective-permute-start.17 = (bf16[32,4096]{1,0:T(8,128)(2,1)}, bf16[32,4096]{1,0:T(8,128)(2,1)}, u32[]{:S(2)}, u32[]{:S(2)}) collective-permute-start(bf16[32,4096]{1,0:T(8,128)(2,1)} %get-tuple-element.87), channel_id=1, source_target_pairs={{0,1},{4,5},{8,9},{12,13},{16,17},{20,21},{24,25},{28,29}} | collective-permute-start | bytes 786440 | tf_op jit(solution)/shard_map/ppermute | solution.py:67
  235.3 46.0 %copy-start.21 = (bf16[32,4096]{1,0:T(8,128)(2,1)S(1)}, bf16[32,4096]{1,0:T(8,128)(2,1)}, u32[]{:S(2)}) copy-start(bf16[32,4096]{1,0:T(8,128)(2,1)} %get-tuple-element.85) | copy-start | bytes 786436
  235.4 60.6 %all-to-all-start.3 = ((bf16[8,48,4096]{2,1,0:T(8,128)(2,1)}), bf16[8,48,4096]{2,1,0:T(8,128)(2,1)S(1)}, u32[]{:S(2)}, u32[]{:S(2)}) async-start(bf16[8,48,4096]{2,1,0:T(8,128)(2,1)} %bitcast.23), calls=%async_computation.3 | async-start | bytes 6291456 | tf_op jit(solution)/shard_map/all_to_all | solution.py:491
  240.2 5.2 %collective-permute-start.20 = (bf16[32,4096]{1,0:T(8,128)(2,1)}, bf16[32,4096]{1,0:T(8,128)(2,1)S(1)}, u32[]{:S(2)}, u32[]{:S(2)}) collective-permute-start(bf16[32,4096]{1,0:T(8,128)(2,1)} %get-tuple-element.90), channel_id=1, source_target_pairs={{3,2},{7,6},{11,10},{15,14},{19,18},{23,22},{27,26},{31,30}} | collective-permute-start | bytes 786440 | tf_op jit(solution)/shard_map/ppermute | solution.py:67
  240.8 55.1 %collective-permute-start.28 = (bf16[96,4096]{1,0:T(8,128)(2,1)}, bf16[96,4096]{1,0:T(8,128)(2,1)}, u32[]{:S(2)}, u32[]{:S(2)}) collective-permute-start(bf16[96,4096]{1,0:T(8,128)(2,1)} %get-tuple-element.106), channel_id=1, source_target_pairs={{0,3},{1,2},{2,1},{3,0},{4,7},{5,6},{6,5},{7,4},{8,11},{9,10},{10,... | collective-permute-start | bytes 2359304 | tf_op jit(solution)/shard_map/ppermute | solution.py:38
  242.8 38.6 %collective-permute-start.18 = (bf16[32,4096]{1,0:T(8,128)(2,1)S(1)}, bf16[32,4096]{1,0:T(8,128)(2,1)S(1)}, u32[]{:S(2)}, u32[]{:S(2)}) collective-permute-start(bf16[32,4096]{1,0:T(8,128)(2,1)S(1)} %add_convert_fusion.6), channel_id=1, source_target_pairs={{0,1},{1,2},{4,5},{5,6},{8,9},{9,10},{12,13},{13,14},{16,17},{17,1... | collective-permute-start | bytes 786440 | tf_op jit(solution)/shard_map/ppermute | solution.py:67
  246.4 39.2 %collective-permute-start.21 = (bf16[32,4096]{1,0:T(8,128)(2,1)S(1)}, bf16[32,4096]{1,0:T(8,128)(2,1)S(1)}, u32[]{:S(2)}, u32[]{:S(2)}) collective-permute-start(bf16[32,4096]{1,0:T(8,128)(2,1)S(1)} %add_convert_fusion.4), channel_id=1, source_target_pairs={{3,2},{2,1},{7,6},{6,5},{11,10},{10,9},{15,14},{14,13},{19,18},{18... | collective-permute-start | bytes 786440 | tf_op jit(solution)/shard_map/ppermute | solution.py:67
  281.5 8.9 %collective-permute-start.19 = (bf16[32,4096]{1,0:T(8,128)(2,1)S(1)}, bf16[32,4096]{1,0:T(8,128)(2,1)S(1)}, u32[]{:S(2)}, u32[]{:S(2)}) collective-permute-start(bf16[32,4096]{1,0:T(8,128)(2,1)S(1)} %add_convert_fusion.5), channel_id=1, source_target_pairs={{0,1},{1,2},{2,3},{4,5},{5,6},{6,7},{8,9},{9,10},{10,11},{12,13},{... | collective-permute-start | bytes 786440 | tf_op jit(solution)/shard_map/ppermute | solution.py:67
  286.6 8.6 %collective-permute-start.22 = (bf16[32,4096]{1,0:T(8,128)(2,1)S(1)}, bf16[32,4096]{1,0:T(8,128)(2,1)S(1)}, u32[]{:S(2)}, u32[]{:S(2)}) collective-permute-start(bf16[32,4096]{1,0:T(8,128)(2,1)S(1)} %add_convert_fusion.3), channel_id=1, source_target_pairs={{3,2},{2,1},{1,0},{7,6},{6,5},{5,4},{11,10},{10,9},{9,8},{15,14},{... | collective-permute-start | bytes 786440 | tf_op jit(solution)/shard_map/ppermute | solution.py:67
  290.4 7.2 %copy-start.19 = (bf16[32,4096]{1,0:T(8,128)(2,1)}, bf16[32,4096]{1,0:T(8,128)(2,1)S(1)}, u32[]{:S(2)}) copy-start(bf16[32,4096]{1,0:T(8,128)(2,1)S(1)} %collective-permute-done.19) | copy-start | bytes 786436
  295.9 1.6 copy-start
  297.6 39.9 %all-to-all-start.4 = ((bf16[8,48,4096]{2,1,0:T(8,128)(2,1)}), bf16[8,48,4096]{2,1,0:T(8,128)(2,1)S(1)}, u32[]{:S(2)}, u32[]{:S(2)}) async-start(bf16[8,48,4096]{2,1,0:T(8,128)(2,1)} %bitcast.16), calls=%async_computation.4 | async-start | bytes 6291456 | tf_op jit(solution)/shard_map/all_to_all | solution.py:491
  303.1 5.7 %copy-start.18 = (f32[32,4096]{1,0:T(8,128)S(1)}, f32[32,4096]{1,0:T(8,128)}, u32[]{:S(2)}) copy-start(f32[32,4096]{1,0:T(8,128)} %get-tuple-element.84) | copy-start | bytes 1572868
  314.3 30.9 %collective-permute-start.25 = (bf16[32,4096]{1,0:T(8,128)(2,1)}, bf16[32,4096]{1,0:T(8,128)(2,1)}, u32[]{:S(2)}, u32[]{:S(2)}) collective-permute-start(bf16[32,4096]{1,0:T(8,128)(2,1)} %get-tuple-element.99), channel_id=1, source_target_pairs={{0,1},{1,0},{2,3},{3,2},{4,5},{5,4},{6,7},{7,6},{8,9},{9,8},{10,11... | collective-permute-start | bytes 786440 | tf_op jit(solution)/shard_map/ppermute | solution.py:38
  314.3 32.3 %collective-permute-start.26 = (bf16[32,4096]{1,0:T(8,128)(2,1)}, bf16[32,4096]{1,0:T(8,128)(2,1)}, u32[]{:S(2)}, u32[]{:S(2)}) collective-permute-start(bf16[32,4096]{1,0:T(8,128)(2,1)} %get-tuple-element.100), channel_id=1, source_target_pairs={{0,2},{1,3},{2,0},{3,1},{4,6},{5,7},{6,4},{7,5},{8,10},{9,11},{10,... | collective-permute-start | bytes 786440 | tf_op jit(solution)/shard_map/ppermute | solution.py:38
  315.5 31.1 %collective-permute-start.27 = (bf16[32,4096]{1,0:T(8,128)(2,1)}, bf16[32,4096]{1,0:T(8,128)(2,1)}, u32[]{:S(2)}, u32[]{:S(2)}) collective-permute-start(bf16[32,4096]{1,0:T(8,128)(2,1)} %get-tuple-element.101), channel_id=1, source_target_pairs={{0,3},{1,2},{2,1},{3,0},{4,7},{5,6},{6,5},{7,4},{8,11},{9,10},{10,... | collective-permute-start | bytes 786440 | tf_op jit(solution)/shard_map/ppermute | solution.py:38
  337.5 1.9 copy-start.1
  339.4 8.7 %copy-start.17 = (bf16[128,2048]{1,0:T(8,128)(2,1)S(1)}, bf16[128,2048]{1,0:T(8,128)(2,1)}, u32[]{:S(2)}) copy-start(bf16[128,2048]{1,0:T(8,128)(2,1)} %get-tuple-element.111) | copy-start | bytes 1572868
  343.9 25.6 %copy-start.5 = (f32[128,2048]{1,0:T(8,128)S(1)}, f32[128,2048]{1,0:T(8,128)}, u32[]{:S(2)}) copy-start(f32[128,2048]{1,0:T(8,128)} %get-tuple-element.117) | copy-start | bytes 3145732
  343.9 7.8 %collective-permute-start.29 = (bf16[32,4096]{1,0:T(8,128)(2,1)}, bf16[32,4096]{1,0:T(8,128)(2,1)S(1)}, u32[]{:S(2)}, u32[]{:S(2)}) collective-permute-start(bf16[32,4096]{1,0:T(8,128)(2,1)} %get-tuple-element.113), channel_id=1, source_target_pairs={{0,1},{1,0},{2,3},{3,2},{4,5},{5,4},{6,7},{7,6},{8,9},{9,8},{10,11... | collective-permute-start | bytes 786440 | tf_op jit(solution)/shard_map/ppermute | solution.py:38
  344.0 9.6 %collective-permute-start.30 = (bf16[32,4096]{1,0:T(8,128)(2,1)}, bf16[32,4096]{1,0:T(8,128)(2,1)S(1)}, u32[]{:S(2)}, u32[]{:S(2)}) collective-permute-start(bf16[32,4096]{1,0:T(8,128)(2,1)} %get-tuple-element.114), channel_id=1, source_target_pairs={{0,2},{1,3},{2,0},{3,1},{4,6},{5,7},{6,4},{7,5},{8,10},{9,11},{10,... | collective-permute-start | bytes 786440 | tf_op jit(solution)/shard_map/ppermute | solution.py:38
  345.2 23.2 %collective-permute-start.31 = (bf16[32,4096]{1,0:T(8,128)(2,1)}, bf16[32,4096]{1,0:T(8,128)(2,1)S(1)}, u32[]{:S(2)}, u32[]{:S(2)}) collective-permute-start(bf16[32,4096]{1,0:T(8,128)(2,1)} %get-tuple-element.115), channel_id=1, source_target_pairs={{0,3},{1,2},{2,1},{3,0},{4,7},{5,6},{6,5},{7,4},{8,11},{9,10},{10,... | collective-permute-start | bytes 786440 | tf_op jit(solution)/shard_map/ppermute | solution.py:38
  346.6 24.3 %copy-start.4 = (f32[128,2048]{1,0:T(8,128)S(1)}, f32[128,2048]{1,0:T(8,128)}, u32[]{:S(2)}) copy-start(f32[128,2048]{1,0:T(8,128)} %get-tuple-element.116) | copy-start | bytes 3145732
  348.1 22.8 %collective-permute-start.32 = (bf16[128,2048]{1,0:T(8,128)(2,1)S(1)}, bf16[128,2048]{1,0:T(8,128)(2,1)S(1)}, u32[]{:S(2)}, u32[]{:S(2)}) collective-permute-start(bf16[128,2048]{1,0:T(8,128)(2,1)S(1)} %copy-done.17), channel_id=1, source_target_pairs={{0,16},{4,20},{8,24},{12,28},{16,0},{20,4},{24,8},{28,12},{1,17},{... | collective-permute-start | bytes 1572872 | tf_op jit(solution)/shard_map/ppermute | solution.py:38
  349.3 20.2 %collective-permute-start.35 = (bf16[128,2048]{1,0:T(8,128)(2,1)}, bf16[128,2048]{1,0:T(8,128)(2,1)S(1)}, u32[]{:S(2)}, u32[]{:S(2)}) collective-permute-start(bf16[128,2048]{1,0:T(8,128)(2,1)} %get-tuple-element.118), channel_id=1, source_target_pairs={{0,8},{4,12},{8,0},{12,4},{16,24},{20,28},{24,16},{28,20},{1,9},{5... | collective-permute-start | bytes 1572872 | tf_op jit(solution)/shard_map/ppermute | solution.py:38
  369.7 5.3 %collective-permute-start.36 = (bf16[64,2048]{1,0:T(8,128)(2,1)S(1)}, bf16[64,2048]{1,0:T(8,128)(2,1)S(1)}, u32[]{:S(2)}, u32[]{:S(2)}) collective-permute-start(bf16[64,2048]{1,0:T(8,128)(2,1)S(1)} %split.56), channel_id=1, source_target_pairs={{0,16},{4,20},{8,24},{12,28},{16,0},{20,4},{24,8},{28,12},{1,17},{... | collective-permute-start | bytes 786440 | tf_op jit(solution)/shard_map/ppermute | solution.py:38
  371.1 8.3 %collective-permute-start.33 = (bf16[64,2048]{1,0:T(8,128)(2,1)S(1)}, bf16[64,2048]{1,0:T(8,128)(2,1)S(1)}, u32[]{:S(2)}, u32[]{:S(2)}) collective-permute-start(bf16[64,2048]{1,0:T(8,128)(2,1)S(1)} %split.57), channel_id=1, source_target_pairs={{0,8},{4,12},{8,0},{12,4},{16,24},{20,28},{24,16},{28,20},{1,9},{5... | collective-permute-start | bytes 786440 | tf_op jit(solution)/shard_map/ppermute | solution.py:38
  375.1 7.0 %collective-permute-start.37 = (bf16[32,2048]{1,0:T(8,128)(2,1)S(1)}, bf16[32,2048]{1,0:T(8,128)(2,1)S(1)}, u32[]{:S(2)}, u32[]{:S(2)}) collective-permute-start(bf16[32,2048]{1,0:T(8,128)(2,1)S(1)} %split.58), channel_id=1, source_target_pairs={{0,4},{4,0},{8,12},{12,8},{16,20},{20,16},{24,28},{28,24},{1,5},{5... | collective-permute-start | bytes 393224 | tf_op jit(solution)/shard_map/ppermute | solution.py:38
  379.5 3.5 collective-permute-start.34
  (2 other events, 1.5 us)

commit v7 on v6

--- a/solution.py
+++ b/solution.py
@@ -58,21 +58,14 @@
     return [0] + [offset for d in range(1, size) for offset in (-d, d)]
 
 
-def chain_sum(own, parts, axis):
+def chain_sum_step(parts, axis, step, moved=None):
     size = lax.axis_size(axis)
-    left, right = parts[0::2], parts[1::2]
-    for step in range(1, size):
-        ways = [(i, i + 1) for i in range(step)], [(size - 1 - i, size - 2 - i) for i in range(step)]
-        moved = [
-            lax.ppermute(side[size - 1 - step].astype(BF16), axis, way)
-            for side, way in zip((right, left), ways)
-        ]
-        if step < size - 1:
-            at = size - 2 - step
-            right[at], left[at] = (
-                side[at].astype(F32) + came.astype(F32) for side, came in zip((right, left), moved)
-            )
-    return own, moved
+    at = size - 1 - step
+    sides = parts[1::2][at], parts[0::2][at]
+    if moved is not None:
+        sides = [side.astype(F32) + came.astype(F32) for side, came in zip(sides, moved)]
+    ways = [(i, i + 1) for i in range(step)], [(size - 1 - i, size - 2 - i) for i in range(step)]
+    return [lax.ppermute(side.astype(BF16), axis, way) for side, way in zip(sides, ways)]
 
 
 def gather_doubling(array, axis, bits):
@@ -88,12 +81,14 @@
     return found
 
 
-def sum_halving(keep, give, axis, bits):
-    for step, bit in enumerate(bits[::-1]):
-        if step:
-            keep, give = jnp.split(keep, 2)
-        keep = keep + swap(give.astype(BF16), axis, bit).astype(F32)
-    return keep.astype(BF16)
+def halve(keep, give, axis, bit):
+    return keep + swap(give.astype(BF16), axis, bit).astype(F32)
+
+
+def sum_halving(array, axis, bits):
+    for bit in bits[::-1]:
+        array = halve(*jnp.split(array, 2), axis, bit)
+    return array.astype(BF16)
 
 
 def below(rows):
@@ -365,17 +360,18 @@
     )(mixing_a, mixing_b, *landed)
 
 
-def expert_kernel(count, first_tiles, split, tie, *refs):
+def expert_kernel(count, first_tiles, nodes, tie, *refs):
     parts, (gate_ref, up_ref, down_ref) = refs[:count], refs[count : count + 3]
     outs, (joined, hidden) = refs[count + 3 : -2], refs[-2:]
     step = pl.program_id(0)
-    x_ref = parts[0] if count == 1 else joined
-
-    if count > 1:
+    x_ref = parts[0] if count == 1 and not nodes else joined
+
+    if x_ref is joined:
 
         @pl.when(step == 0)
         def _():
-            joined[...] = jnp.concatenate([part[...] for part in parts])
+            pieces = [parts[0][n, 0] for n in range(nodes)] or [part[...] for part in parts]
+            joined[...] = jnp.concatenate(pieces)
 
     @pl.when(step < first_tiles)
     def _():
@@ -388,11 +384,6 @@
     def _():
         rows = jnp.concatenate([hidden[i] for i in range(first_tiles)], axis=1)
         result = jnp.dot(rows, down_ref[...], preferred_element_type=F32)
-        if split is not None:
-            result = result.reshape(*split, result.shape[1])
-            for block, out in enumerate(outs):
-                out[...] = result[:, block].reshape(out.shape).astype(BF16)
-            return
         result = result.astype(BF16)
         at = 0
         for out in outs:
@@ -400,15 +391,15 @@
             at += out.shape[0]
 
 
-def expert(parts, tie, gate_weight, up_weight, down_weight):
-    split = None
+def expert(parts, tie, gate_weight, up_weight, down_weight, block=None):
     sizes = [part.shape[0] for part in parts]
-    if parts[0].ndim == 4:
-        (part,) = parts
-        split = part.shape[:3]
-        parts = [part.reshape(-1, part.shape[3])]
-        sizes = [split[0] * split[2]] * split[1]
-    rows = sum(part.shape[0] for part in parts)
+    specs = [whole_block(part) for part in parts]
+    nodes = 0
+    if block is not None:
+        nodes, _, size, features = parts[0].shape
+        sizes = [nodes * size]
+        specs = [pl.BlockSpec((nodes, 1, size, features), lambda i: (0, block, 0, 0))]
+    rows = sum(sizes)
     features, hidden = gate_weight.shape
     tile = 256
     first_tiles = hidden // tile
@@ -421,11 +412,11 @@
         return jnp.maximum(i - first_tiles, 0)
 
     return pl.pallas_call(
-        functools.partial(expert_kernel, len(parts), first_tiles, split),
+        functools.partial(expert_kernel, len(parts), first_tiles, nodes),
         grid=(first_tiles + TILES,),
         out_shape=[jax.ShapeDtypeStruct((size, features), BF16) for size in sizes],
         in_specs=[pl.BlockSpec(memory_space=pltpu.SMEM)]
-        + [whole_block(part) for part in parts]
+        + specs
         + [
             pl.BlockSpec((features, tile), lambda i: (0, first(i))),
             pl.BlockSpec((features, tile), lambda i: (0, first(i))),
@@ -435,7 +426,7 @@
             pl.BlockSpec((size, out_tile), lambda i: (0, second(i))) for size in sizes
         ],
         scratch_shapes=[
-            pltpu.VMEM((rows if len(parts) > 1 else 16, features), BF16),
+            pltpu.VMEM((rows if nodes or len(parts) > 1 else 16, features), BF16),
             pltpu.VMEM((first_tiles, rows, tile), BF16),
         ],
         compiler_params=PARAMS,
@@ -550,29 +541,33 @@
     landed0 = to_experts(out0)
     out3 = list(expert([own3] + arrived3, tie, *weights))
     landed3 = out3[:1] + swaps(out3, "local", 1, peers - 1)
-    out1, out2 = expert([arrived12], tie, *weights)
+    (out1,) = expert([arrived12], tie, *weights, block=0)
 
     (mixing0,) = fence([mixing0], [out1])
-    out1, last3 = fence([out1, out3[-1]], [landed0, out2] + landed3[1:])
+    out1, last3, tie = fence([out1, out3[-1], tie], [landed0] + landed3[1:])
     landed1 = to_experts(out1)
     landed3.append(swap(last3, "local", peers - 1))
-    own0, parts0 = chain_sum(*mix(mixing0, landed0), "local")
-
-    (out2,) = fence([out2], [landed1, landed3[-1]] + parts0)
+    own0, sends0 = mix(mixing0, landed0)
+    parts0 = chain_sum_step(sends0, "local", 1)
+    (out2,) = expert([arrived12], tie, *weights, block=1)
+
+    out2, *parts0 = fence([out2] + parts0, [landed1, landed3[-1]])
     landed2 = to_experts(out2)
+    for step in range(2, peers):
+        parts0 = chain_sum_step(sends0, "local", step, parts0)
     own1, parts1 = mix(mixing1, landed1)
     parts1 = swaps([None] + parts1, "local", 1, peers)
     cross = mix_cross(mixing3a, mixing3b, landed3)
-    piece0 = total(own0, parts0)
-
-    cross = fence(list(cross), [landed2])
-    (mixing2,) = fence([mixing2], [cross[1]])
+
+    cross = fence(list(cross), parts0 + parts1)
+    sums3 = halve(*cross[:2], "node", bits_a[-1]), halve(*cross[2:], "node", bits_b[-1])
+    sums3 = fence(sums3, [landed2])
+    (mixing2,) = fence([mixing2], sums3[:1])
     own2, parts2 = mix(mixing2, landed2)
     parts2 = swaps([None] + parts2, "local", 1, peers)
-    piece1 = total(own1, parts1)
-    piece3 = jnp.concatenate(
-        [sum_halving(*cross[:2], "node", bits_a), sum_halving(*cross[2:], "node", bits_b)], axis=1
-    )
+    piece0, piece1 = total(own0, parts0), total(own1, parts1)
+    piece3 = [sum_halving(s, "node", bits[:-1]) for s, bits in zip(sums3, (bits_a, bits_b))]
+    piece3 = jnp.concatenate(piece3, axis=1)
     piece2 = total(own2, parts2)
     return jnp.concatenate([piece0, piece1, piece2, piece3], axis=0)
 

time: 387 us -> 396 us (1.023)
  waiting for transfers between devices: 166 us -> 154 us
  local copies, waits for them, and re-layouts: 5.47 us -> 14.5 us
  Pallas kernels: 96.2 us -> 104 us
  other arithmetic: 20 us -> 26.8 us
    ppermute x6, waiting for transfers between devices: 40.4 us -> 21.3 us  [chain_sum_step(): lax.ppermute(side.astype(BF16), axis, way)]
    ppermute x26, waiting for transfers between devices: 89.5 us -> 106 us  [swap(): return lax.ppermute(array, axis, [(i, i ^ bits) for i in range(size)])]
    all_to_all x5, waiting for transfers between devices: 20.6 us -> 10.7 us  [to_experts(): return lax.all_to_all(rows, 'node', 0, 0, tiled=True)]
    pallas_call x3 -> x4, Pallas kernels: 55.2 us -> 63.4 us  [expert(): pl.pallas_call(functools.partial(expert_kernel, len(parts), first_tiles,...]
    ppermute x26, starting transfers between devices: 37.8 us -> 31.7 us  [swap(): return lax.ppermute(array, axis, [(i, i ^ bits) for i in range(size)])]
    add x4, other arithmetic: 0.31 us -> 5.73 us  [halve(): return keep + swap(give.astype(BF16), axis, bit).astype(F32)]
    unnamed x47 -> x50, local copies, waits for them, and re-layouts: 5.32 us -> 9.13 us
  transfers between devices with their start and end apart: 43 -> 43, of which waited for: 20 -> 15; matrix products, arithmetic and copies ran while one was open for 4% -> 7% of each run, Pallas kernels for 24% -> 26%
where the time goes in v7:
time: 396 us; the launch traced here: 392 us
  waiting for transfers between devices  154 us (39%)
  Pallas kernels  104 us (26%)
  starting transfers between devices  92.4 us (23%)
  other arithmetic  26.8 us (7%)
  local copies, waits for them, and re-layouts  14.5 us (4%)
    ppermute x26, waiting for transfers between devices, swap(): return lax.ppermute(array, axis, [(i, i ^ bits) for i in range(size)])  106 us
    pallas_call x4, Pallas kernels, expert(): pl.pallas_call(functools.partial(expert_kernel, len(parts), first_tiles,...  63.4 us
    ppermute x26, starting transfers between devices, swap(): return lax.ppermute(array, axis, [(i, i ^ bits) for i in range(size)])  31.7 us
    all_to_all x5, starting transfers between devices, to_experts(): return lax.all_to_all(rows, 'node', 0, 0, tiled=True)  30.5 us
    ppermute x6, waiting for transfers between devices, chain_sum_step(): lax.ppermute(side.astype(BF16), axis, way)  21.3 us
    ppermute x6, starting transfers between devices, chain_step(): lax.ppermute(a, axis, way)  17.8 us
    ppermute x6, waiting for transfers between devices, chain_step(): lax.ppermute(a, axis, way)  15.9 us
    pallas_call x3, Pallas kernels, mix(): pl.pallas_call(mix_kernel, grid=(TILES,), out_shape=[jax.ShapeDtypeStruct...  13.4 us
  transfers between devices with their start and end apart: 43, of which 15 were waited for; matrix products, arithmetic and copies ran while one was open for 7% of the time, Pallas kernels for 26%

profile of v7, /device:TPU:9, one launch (start us, length us, event | category | flops | bytes accessed | tf_op | source)
XLA Modules:
  0.0 392.2 jit_solution(1175172878482442552)
XLA Ops:
  0.0 2.9 shard_map.262
  2.9 1.3 collective-permute-start.2
  9.1 1.3 collective-permute-start.4
  10.4 1.3 collective-permute-start.5
  11.7 10.6 %collective-permute-done.2.refs_3_.refs_7_ = bf16[32,4224]{1,0:T(8,128)(2,1)S(1)} collective-permute-done((bf16[32,4224]{1,0:T(8,128)(2,1)}, bf16[32,4224]{1,0:T(8,128)(2,1)S(1)}, u32[]{:S(2)}, u32[]{:S(2)}) %collective-permute-start.2) | collective-permute-done | bytes 270368 | tf_op jit(solution)/shard_map/ppermute | solution.py:38
  22.2 4.8 %collective-permute-done.1.refs_2_.refs_6_ = bf16[32,4224]{1,0:T(8,128)(2,1)S(1)} collective-permute-done((bf16[32,4224]{1,0:T(8,128)(2,1)}, bf16[32,4224]{1,0:T(8,128)(2,1)S(1)}, u32[]{:S(2)}, u32[]{:S(2)}) %collective-permute-start.1) | collective-permute-done | bytes 270368 | tf_op jit(solution)/shard_map/ppermute | solution.py:38
  29.4 4.1 %collective-permute-start.9 = (bf16[64,4224]{1,0:T(8,128)(2,1)}, bf16[64,4224]{1,0:T(8,128)(2,1)S(1)}, u32[]{:S(2)}, u32[]{:S(2)}) collective-permute-start(bf16[64,4224]{1,0:T(8,128)(2,1)} %get-tuple-element.73.refs_0_.refs_7_), channel_id=1, source_target_pairs={{3,2},{2,1},{1,0},{7,6},{6,5},{5,4},{11,10},{10,9},{9,8},{15,14},{... | collective-permute-start | bytes 1622024 | tf_op jit(solution)/shard_map/ppermute | solution.py:54
  33.5 1.9 collective-permute-start.8
  35.4 1.3 collective-permute-start.7
  38.6 5.4 %shard_map.263 = (bf16[8,1,48,4096]{3,2,1,0:T(8,128)(2,1)}, bf16[224,384]{1,0:T(8,128)(2,1)}) custom-call(s32[2]{0:T(128)} %pad_add_fusion.ids.tie.refs_1_, bf16[32,4224]{1,0:T(8,128)(2,1)} %get-tuple-element.66.refs_0_.refs_4_, bf16[32,4224]{1,0:T(8,128)(2,1)} %copy-done.11, bf16[32,4224]{1,0:T(8,128)(2,1)} %copy-done.10, bf16[32,4224]{1,0:T(8,128)(2,1)} %copy-done.9, ...), custom_call_target="tpu_custom_call" | custom-call | flops 402653184 | bytes 4194304 | tf_op jit(solution)/shard_map/pallas_call | solution.py:192
  44.0 3.7 collective-permute-done.8.refs_1_.refs_8_
  49.4 6.4 %all-to-all-start = ((bf16[8,1,48,4096]{3,2,1,0:T(8,128)(2,1)}), bf16[8,1,48,4096]{3,2,1,0:T(8,128)(2,1)S(1)}, u32[]{:S(2)}, u32[]{:S(2)}) async-start(bf16[8,1,48,4096]{3,2,1,0:T(8,128)(2,1)} %get-tuple-element.74), calls=%async_computation | async-start | bytes 6291456 | tf_op jit(solution)/shard_map/all_to_all | solution.py:482
  55.8 3.4 collective-permute-start.11
  59.2 2.7 collective-permute-start.10
  62.0 9.7 %collective-permute-done.11.refs_4_.refs_11_ = bf16[64,4224]{1,0:T(8,128)(2,1)S(1)} collective-permute-done((bf16[64,4224]{1,0:T(8,128)(2,1)}, bf16[64,4224]{1,0:T(8,128)(2,1)S(1)}, u32[]{:S(2)}, u32[]{:S(2)}) %collective-permute-start.11) | collective-permute-done | bytes 540704 | tf_op jit(solution)/shard_map/ppermute | solution.py:54
  71.7 4.2 %collective-permute-start.13 = (bf16[64,4224]{1,0:T(8,128)(2,1)S(1)}, bf16[64,4224]{1,0:T(8,128)(2,1)}, u32[]{:S(2)}, u32[]{:S(2)}) collective-permute-start(bf16[64,4224]{1,0:T(8,128)(2,1)S(1)} %collective-permute-done.11.refs_4_.refs_11_), channel_id=1, source_target_pairs={{1,0},{5,4},{9,8},{13,12},{17,16},{21,20},{25,24},{29,28}} | collective-permute-start | bytes 1622024 | tf_op jit(solution)/shard_map/ppermute | solution.py:54
  75.9 1.5 collective-permute-start.12
  77.3 5.8 %shard_map.268 = (bf16[96,4096]{1,0:T(8,128)(2,1)}, bf16[96,4096]{1,0:T(8,128)(2,1)}, bf16[96,4096]{1,0:T(8,128)(2,1)}, bf16[96,4096]{1,0:T(8,128)(2,1)}, bf16[2...) custom-call(s32[2]{0:T(128)} %pad_add_fusion.ids.tie.refs_1_, bf16[128,2048]{1,0:T(8,128)(2,1)} %get-tuple-element.71.a0, ...), custom_call_target="tpu_custom_call" | custom-call | flops 805306368 | bytes 5242880 | tf_op jit(solution)/shard_map/pallas_call | solution.py:270
  83.2 2.5 collective-permute-done.13.refs_6_.refs_13_
  85.7 7.8 %shard_map.267 = (bf16[8,2,48,4096]{3,2,1,0:T(8,128)(2,1)}, bf16[128,384]{1,0:T(8,128)(2,1)}, bf16[128,384]{1,0:T(8,128)(2,1)}) custom-call(s32[2]{0:T(128)} %pad_add_fusion.ids.tie.refs_1_, bf16[64,4224]{1,0:T(8,128)(2,1)} %get-tuple-element.73.refs_0_.refs_7_, bf16[64,4224]{1,0:T(8,128)(2,1)} %copy-done.6, bf16[64,4224]{1,0:T(8,128)(2,1)} %copy-done.5, ...), custom_call_target="tpu_custom_call" | custom-call | flops 1409286144 | bytes 9961472 | tf_op jit(solution)/shard_map/pallas_call | solution.py:192
  95.1 6.7 %all-to-all-start.1 = ((bf16[8,2,48,4096]{3,2,1,0:T(8,128)(2,1)}), bf16[8,2,48,4096]{3,2,1,0:T(8,128)(2,1)}, u32[]{:S(2)}, u32[]{:S(2)}) async-start(bf16[8,2,48,4096]{3,2,1,0:T(8,128)(2,1)} %get-tuple-element.81), calls=%async_computation.1 | async-start | bytes 12582912 | tf_op jit(solution)/shard_map/all_to_all | solution.py:482
  101.8 2.3 collective-permute-start.14
  104.1 2.0 collective-permute-start.15
  106.5 16.0 %shard_map.266.refs_0_ = bf16[384,4096]{1,0:T(8,128)(2,1)} custom-call(s32[2]{0:T(128)} %pad_add_fusion.ids.tie.refs_1_, bf16[384,4096]{1,0:T(8,128)(2,1)} %bitcast.36, bf16[4096,768]{1,0:T(8,128)(2,1)} %bitcast.18, bf16[4096,768]{1,0:T(8,128)(2,1)} %bitcast.22, bf16[768,4096]{1,0:T(8,128)(2,1)} %bitcast.26), custom_call_target="tpu_custom_call" | custom-call | flops 7247757312 | bytes 25165824 | tf_op jit(solution)/shard_map/pallas_call | solution.py:414
  122.4 14.9 %collective-permute-done.14.refs_1_ = bf16[96,4096]{1,0:T(8,128)(2,1)S(1)} collective-permute-done((bf16[96,4096]{1,0:T(8,128)(2,1)S(1)}, bf16[96,4096]{1,0:T(8,128)(2,1)S(1)}, u32[]{:S(2)}, u32[]{:S(2)}) %collective-permute-start.14) | collective-permute-done | bytes 786464 | tf_op jit(solution)/shard_map/ppermute | solution.py:38
  137.3 19.4 %collective-permute-done.15.refs_2_ = bf16[96,4096]{1,0:T(8,128)(2,1)} collective-permute-done((bf16[96,4096]{1,0:T(8,128)(2,1)S(1)}, bf16[96,4096]{1,0:T(8,128)(2,1)}, u32[]{:S(2)}, u32[]{:S(2)}) %collective-permute-start.15) | collective-permute-done | bytes 786464 | tf_op jit(solution)/shard_map/ppermute | solution.py:38
  156.7 17.9 %collective-permute-done.16.refs_3_ = bf16[96,4096]{1,0:T(8,128)(2,1)} collective-permute-done((bf16[96,4096]{1,0:T(8,128)(2,1)S(1)}, bf16[96,4096]{1,0:T(8,128)(2,1)}, u32[]{:S(2)}, u32[]{:S(2)}) %collective-permute-start.16) | collective-permute-done | bytes 786464 | tf_op jit(solution)/shard_map/ppermute | solution.py:38
  174.6 1.3 convert_add_fusion.7.refs_2_
  175.9 4.9 %all-to-all-start.2 = ((bf16[8,48,4096]{2,1,0:T(8,128)(2,1)}), bf16[8,48,4096]{2,1,0:T(8,128)(2,1)S(1)}, u32[]{:S(2)}, u32[]{:S(2)}) async-start(bf16[8,48,4096]{2,1,0:T(8,128)(2,1)} %bitcast.34), calls=%async_computation.2 | async-start | bytes 6291456 | tf_op jit(solution)/shard_map/all_to_all | solution.py:482
  180.8 16.1 %shard_map.274 = (bf16[96,4096]{1,0:T(8,128)(2,1)}, bf16[96,4096]{1,0:T(8,128)(2,1)}, bf16[96,4096]{1,0:T(8,128)(2,1)}, bf16[96,4096]{1,0:T(8,128)(2,1)}) custom-call(s32[2]{0:T(128)} %get-tuple-element.85.tie.refs_2_, bf16[96,4096]{1,0:T(8,128)(2,1)} %get-tuple-element.90.refs_0_, bf16[96,4096]{1,0:T(8,128)(2,1)} %copy-done.23, ...), custom_call_target="tpu_custom_call" | custom-call | flops 7247757312 | bytes 25165824 | tf_op jit(solution)/shard_map/pallas_call | solution.py:414
  196.9 2.4 collective-permute-start.18
  199.4 15.7 %shard_map.271 = bf16[384,4096]{1,0:T(8,128)(2,1)} custom-call(s32[2]{0:T(128)} %get-tuple-element.85.tie.refs_2_, bf16[8,2,48,4096]{3,2,1,0:T(8,128)(2,1)} %all-to-all-done.1.refs_0_, bf16[4096,768]{1,0:T(8,128)(2,1)} %bitcast.20, bf16[4096,768]{1,0:T(8,128)(2,1)} %bitcast.24, bf16[768,4096]{1,0:T(8,128)(2,1)} %bitcast.28), custom_call_target="tpu_custom_call" | custom-call | flops 7247757312 | bytes 25165824 | tf_op jit(solution)/shard_map/pallas_call | solution.py:414
  215.0 3.9 copy.68.refs_0_
  218.9 11.7 %collective-permute-done.17.refs_1_ = bf16[96,4096]{1,0:T(8,128)(2,1)} collective-permute-done((bf16[96,4096]{1,0:T(8,128)(2,1)}, bf16[96,4096]{1,0:T(8,128)(2,1)}, u32[]{:S(2)}, u32[]{:S(2)}) %collective-permute-start.17) | collective-permute-done | bytes 786464 | tf_op jit(solution)/shard_map/ppermute | solution.py:38
  230.7 3.6 collective-permute-done.18.refs_2_
  234.3 1.6 convert_add_fusion.6.refs_3_
  236.0 5.2 %all-to-all-start.3 = ((bf16[8,48,4096]{2,1,0:T(8,128)(2,1)}), bf16[8,48,4096]{2,1,0:T(8,128)(2,1)}, u32[]{:S(2)}, u32[]{:S(2)}) async-start(bf16[8,48,4096]{2,1,0:T(8,128)(2,1)} %bitcast.16), calls=%async_computation.3 | async-start | bytes 6291456 | tf_op jit(solution)/shard_map/all_to_all | solution.py:482
  241.4 1.3 slice_convert_fusion.5.refs_1_
  242.6 4.6 %shard_map.273 = (f32[32,4096]{1,0:T(8,128)}, bf16[32,4096]{1,0:T(8,128)(2,1)}, bf16[32,4096]{1,0:T(8,128)(2,1)}, bf16[32,4096]{1,0:T(8,128)(2,1)}, bf16[32,4096...) custom-call(bf16[224,384]{1,0:T(8,128)(2,1)} %shard_map.272.mixing, bf16[384,4096]{1,0:T(8,128)(2,1)} %bitcast.33), custom_call_target="tpu_custom_call" | custom-call | flops 704643072 | bytes 4980736 | tf_op jit(solution)/shard_map/pallas_call | solution.py:305
  247.2 1.3 collective-permute-start.19
  249.2 15.6 %shard_map.276.refs_0_ = bf16[384,4096]{1,0:T(8,128)(2,1)} custom-call(s32[2]{0:T(128)} %get-tuple-element.94.tie, bf16[8,2,48,4096]{3,2,1,0:T(8,128)(2,1)} %all-to-all-done.1.refs_0_, bf16[4096,768]{1,0:T(8,128)(2,1)} %bitcast.21, bf16[4096,768]{1,0:T(8,128)(2,1)} %bitcast.25, bf16[768,4096]{1,0:T(8,128)(2,1)} %bitcast.29), custom_call_target="tpu_custom_call" | custom-call | flops 7247757312 | bytes 25165824 | tf_op jit(solution)/shard_map/pallas_call | solution.py:414
  264.9 10.7 %all-to-all-done.3 = bf16[8,48,4096]{2,1,0:T(8,128)(2,1)} async-done(((bf16[8,48,4096]{2,1,0:T(8,128)(2,1)}), bf16[8,48,4096]{2,1,0:T(8,128)(2,1)}, u32[]{:S(2)}, u32[]{:S(2)}) %all-to-all-start.3) | async-done | bytes 3145760 | tf_op jit(solution)/shard_map/all_to_all | solution.py:482
  275.5 4.4 %shard_map.278 = (f32[32,4096]{1,0:T(8,128)}, bf16[32,4096]{1,0:T(8,128)(2,1)}, bf16[32,4096]{1,0:T(8,128)(2,1)}, bf16[32,4096]{1,0:T(8,128)(2,1)}) custom-call(bf16[128,384]{1,0:T(8,128)(2,1)} %get-tuple-element.103.mixing, bf16[384,4096]{1,0:T(8,128)(2,1)} %bitcast.13.landed), custom_call_target="tpu_custom_call" | custom-call | flops 402653184 | bytes 4194304 | tf_op jit(solution)/shard_map/pallas_call | solution.py:305
  279.9 1.3 convert_add_fusion.5.refs_3_
  282.6 7.3 %all-to-all-start.4 = ((bf16[8,48,4096]{2,1,0:T(8,128)(2,1)}), bf16[8,48,4096]{2,1,0:T(8,128)(2,1)S(1)}, u32[]{:S(2)}, u32[]{:S(2)}) async-start(bf16[8,48,4096]{2,1,0:T(8,128)(2,1)} %bitcast.17), calls=%async_computation.4 | async-start | bytes 6291456 | tf_op jit(solution)/shard_map/all_to_all | solution.py:482
  290.0 1.3 collective-permute-start.26
  293.7 1.3 collective-permute-start.24
  296.0 4.0 %collective-permute-start.22 = (bf16[32,4096]{1,0:T(8,128)(2,1)S(1)}, bf16[32,4096]{1,0:T(8,128)(2,1)S(1)}, u32[]{:S(2)}, u32[]{:S(2)}) collective-permute-start(bf16[32,4096]{1,0:T(8,128)(2,1)S(1)} %add_convert_fusion.6), channel_id=1, source_target_pairs={{0,1},{1,2},{4,5},{5,6},{8,9},{9,10},{12,13},{13,14},{16,17},{17,1... | collective-permute-start | bytes 786440 | tf_op jit(solution)/shard_map/ppermute | solution.py:68
  300.0 21.3 %collective-permute-done.24 = bf16[32,4096]{1,0:T(8,128)(2,1)S(1)} collective-permute-done((bf16[32,4096]{1,0:T(8,128)(2,1)S(1)}, bf16[32,4096]{1,0:T(8,128)(2,1)S(1)}, u32[]{:S(2)}, u32[]{:S(2)}) %collective-permute-start.24) | collective-permute-done | bytes 262176 | tf_op jit(solution)/shard_map/ppermute | solution.py:68
  322.3 1.9 collective-permute-start.25
  324.3 1.7 add_convert_fusion.5
  326.0 3.3 collective-permute-start.23
  329.4 5.7 %shard_map.279 = (f32[128,2048]{1,0:T(8,128)}, bf16[128,2048]{1,0:T(8,128)(2,1)}, f32[128,2048]{1,0:T(8,128)}, bf16[128,2048]{1,0:T(8,128)(2,1)}) custom-call(bf16[256,384]{1,0:T(8,128)(2,1)} %get-tuple-element.109.mixing_a, bf16[256,384]{1,0:T(8,128)(2,1)} %get-tuple-element.110.mixing_b, bf16[96,4096]{1,0:T(8,128)(2,1)} %get-tuple-element.111.refs_0_, ...), custom_call_target="tpu_custom_call" | custom-call | flops 805306368 | bytes 5242880 | tf_op jit(solution)/shard_map/pallas_call | solution.py:347
  335.8 1.3 convert_add_fusion.4.refs_4_
  339.5 2.1 add_convert_fusion.1
  341.6 7.3 %collective-permute-done.29 = bf16[128,2048]{1,0:T(8,128)(2,1)S(1)} collective-permute-done((bf16[128,2048]{1,0:T(8,128)(2,1)}, bf16[128,2048]{1,0:T(8,128)(2,1)S(1)}, u32[]{:S(2)}, u32[]{:S(2)}) %collective-permute-start.29) | collective-permute-done | bytes 524320 | tf_op jit(solution)/shard_map/ppermute | solution.py:38
  348.8 2.3 convert_add_fusion.1.refs_0_
  352.9 2.2 split.55
  357.3 1.3 slice.99.refs_1_
  358.6 1.8 split.54
  361.6 4.4 %shard_map.283 = (f32[32,4096]{1,0:T(8,128)}, bf16[32,4096]{1,0:T(8,128)(2,1)}, bf16[32,4096]{1,0:T(8,128)(2,1)}, bf16[32,4096]{1,0:T(8,128)(2,1)}) custom-call(bf16[128,384]{1,0:T(8,128)(2,1)} %shard_map.282.mixing, bf16[384,4096]{1,0:T(8,128)(2,1)} %bitcast.31), custom_call_target="tpu_custom_call" | custom-call | flops 402653184 | bytes 4194304 | tf_op jit(solution)/shard_map/pallas_call | solution.py:305
  366.8 2.0 collective-permute-start.33
  370.0 4.4 %collective-permute-start.35 = (bf16[32,2048]{1,0:T(8,128)(2,1)S(1)}, bf16[32,2048]{1,0:T(8,128)(2,1)S(1)}, u32[]{:S(2)}, u32[]{:S(2)}) collective-permute-start(bf16[32,2048]{1,0:T(8,128)(2,1)S(1)} %split.57), channel_id=1, source_target_pairs={{0,4},{4,0},{8,12},{12,8},{16,20},{20,16},{24,28},{28,24},{1,5},{5... | collective-permute-start | bytes 393224 | tf_op jit(solution)/shard_map/ppermute | solution.py:38
  375.7 15.2 %collective-permute-done.33 = bf16[32,4096]{1,0:T(8,128)(2,1)S(1)} collective-permute-done((bf16[32,4096]{1,0:T(8,128)(2,1)}, bf16[32,4096]{1,0:T(8,128)(2,1)S(1)}, u32[]{:S(2)}, u32[]{:S(2)}) %collective-permute-start.33) | collective-permute-done | bytes 262176 | tf_op jit(solution)/shard_map/ppermute | solution.py:38
  (128 shorter events, 32.5 us)
Async XLA Ops:
  2.9 19.3 %collective-permute-start.2 = (bf16[32,4224]{1,0:T(8,128)(2,1)}, bf16[32,4224]{1,0:T(8,128)(2,1)S(1)}, u32[]{:S(2)}, u32[]{:S(2)}) collective-permute-start(bf16[32,4224]{1,0:T(8,128)(2,1)} %get-tuple-element.66.refs_0_.refs_4_), channel_id=1, source_target_pairs={{0,3},{1,2},{2,1},{3,0},{4,7},{5,6},{6,5},{7,4},{8,11},{9,10},{10,... | collective-permute-start | bytes 811016 | tf_op jit(solution)/shard_map/ppermute | solution.py:38
  4.2 22.8 %collective-permute-start.1 = (bf16[32,4224]{1,0:T(8,128)(2,1)}, bf16[32,4224]{1,0:T(8,128)(2,1)S(1)}, u32[]{:S(2)}, u32[]{:S(2)}) collective-permute-start(bf16[32,4224]{1,0:T(8,128)(2,1)} %get-tuple-element.66.refs_0_.refs_4_), channel_id=1, source_target_pairs={{0,2},{1,3},{2,0},{3,1},{4,6},{5,7},{6,4},{7,5},{8,10},{9,11},{10,... | collective-permute-start | bytes 811016 | tf_op jit(solution)/shard_map/ppermute | solution.py:38
  5.2 21.8 %collective-permute-start = (bf16[32,4224]{1,0:T(8,128)(2,1)}, bf16[32,4224]{1,0:T(8,128)(2,1)S(1)}, u32[]{:S(2)}, u32[]{:S(2)}) collective-permute-start(bf16[32,4224]{1,0:T(8,128)(2,1)} %get-tuple-element.66.refs_0_.refs_4_), channel_id=1, source_target_pairs={{0,1},{1,0},{2,3},{3,2},{4,5},{5,4},{6,7},{7,6},{8,9},{9,8},{10,11... | collective-permute-start | bytes 811016 | tf_op jit(solution)/shard_map/ppermute | solution.py:38
  6.4 2.6 collective-permute-start.3
  9.1 18.6 %collective-permute-start.4 = (bf16[64,2048]{1,0:T(8,128)(2,1)S(1)}, bf16[64,2048]{1,0:T(8,128)(2,1)S(1)}, u32[]{:S(2)}, u32[]{:S(2)}) collective-permute-start(bf16[64,2048]{1,0:T(8,128)(2,1)S(1)} %slice.100), channel_id=1, source_target_pairs={{0,8},{4,12},{8,0},{12,4},{16,24},{20,28},{24,16},{28,20},{1,9},{5... | collective-permute-start | bytes 786440 | tf_op jit(solution)/shard_map/ppermute | solution.py:38
  10.4 18.2 %collective-permute-start.5 = (bf16[64,2176]{1,0:T(8,128)(2,1)S(1)}, bf16[64,2176]{1,0:T(8,128)(2,1)S(1)}, u32[]{:S(2)}, u32[]{:S(2)}) collective-permute-start(bf16[64,2176]{1,0:T(8,128)(2,1)S(1)} %slice.101), channel_id=1, source_target_pairs={{0,16},{4,20},{8,24},{12,28},{16,0},{20,4},{24,8},{28,12},{1,17},{... | collective-permute-start | bytes 835592 | tf_op jit(solution)/shard_map/ppermute | solution.py:38
  22.2 16.3 %copy-start.9 = (bf16[32,4224]{1,0:T(8,128)(2,1)}, bf16[32,4224]{1,0:T(8,128)(2,1)S(1)}, u32[]{:S(2)}) copy-start(bf16[32,4224]{1,0:T(8,128)(2,1)S(1)} %collective-permute-done.2.refs_3_.refs_7_) | copy-start | bytes 811012
  27.0 11.5 %copy-start.10 = (bf16[32,4224]{1,0:T(8,128)(2,1)}, bf16[32,4224]{1,0:T(8,128)(2,1)S(1)}, u32[]{:S(2)}) copy-start(bf16[32,4224]{1,0:T(8,128)(2,1)S(1)} %collective-permute-done.1.refs_2_.refs_6_) | copy-start | bytes 811012
  27.1 11.5 %copy-start.11 = (bf16[32,4224]{1,0:T(8,128)(2,1)}, bf16[32,4224]{1,0:T(8,128)(2,1)S(1)}, u32[]{:S(2)}) copy-start(bf16[32,4224]{1,0:T(8,128)(2,1)S(1)} %collective-permute-done.refs_1_.refs_5_) | copy-start | bytes 811012
  29.4 14.6 %collective-permute-start.9 = (bf16[64,4224]{1,0:T(8,128)(2,1)}, bf16[64,4224]{1,0:T(8,128)(2,1)S(1)}, u32[]{:S(2)}, u32[]{:S(2)}) collective-permute-start(bf16[64,4224]{1,0:T(8,128)(2,1)} %get-tuple-element.73.refs_0_.refs_7_), channel_id=1, source_target_pairs={{3,2},{2,1},{1,0},{7,6},{6,5},{5,4},{11,10},{10,9},{9,8},{15,14},{... | collective-permute-start | bytes 1622024 | tf_op jit(solution)/shard_map/ppermute | solution.py:54
  33.5 14.2 %collective-permute-start.8 = (bf16[64,4224]{1,0:T(8,128)(2,1)}, bf16[64,4224]{1,0:T(8,128)(2,1)S(1)}, u32[]{:S(2)}, u32[]{:S(2)}) collective-permute-start(bf16[64,4224]{1,0:T(8,128)(2,1)} %get-tuple-element.73.refs_0_.refs_7_), channel_id=1, source_target_pairs={{0,1},{1,2},{2,3},{4,5},{5,6},{6,7},{8,9},{9,10},{10,11},{12,13},{... | collective-permute-start | bytes 1622024 | tf_op jit(solution)/shard_map/ppermute | solution.py:54
  35.4 13.0 %collective-permute-start.7 = (bf16[128,2176]{1,0:T(8,128)(2,1)}, bf16[128,2176]{1,0:T(8,128)(2,1)S(1)}, u32[]{:S(2)}, u32[]{:S(2)}) collective-permute-start(bf16[128,2176]{1,0:T(8,128)(2,1)} %get-tuple-element.72.b0.t0), channel_id=1, source_target_pairs={{0,8},{4,12},{8,0},{12,4},{16,24},{20,28},{24,16},{28,20},{1,9},{5... | collective-permute-start | bytes 1671176 | tf_op jit(solution)/shard_map/ppermute | solution.py:38
  36.7 11.7 %collective-permute-start.6 = (bf16[128,2048]{1,0:T(8,128)(2,1)}, bf16[128,2048]{1,0:T(8,128)(2,1)S(1)}, u32[]{:S(2)}, u32[]{:S(2)}) collective-permute-start(bf16[128,2048]{1,0:T(8,128)(2,1)} %get-tuple-element.71.a0), channel_id=1, source_target_pairs={{0,16},{4,20},{8,24},{12,28},{16,0},{20,4},{24,8},{28,12},{1,17},{... | collective-permute-start | bytes 1572872 | tf_op jit(solution)/shard_map/ppermute | solution.py:38
  44.0 5.5 %copy-start.5 = (bf16[64,4224]{1,0:T(8,128)(2,1)}, bf16[64,4224]{1,0:T(8,128)(2,1)S(1)}, u32[]{:S(2)}) copy-start(bf16[64,4224]{1,0:T(8,128)(2,1)S(1)} %collective-permute-done.9.refs_2_.refs_9_) | copy-start | bytes 1622020
  47.7 1.7 copy-start.6
  48.4 0.8 copy-start.8
  48.4 1.0 copy-start.2
  49.4 44.0 %all-to-all-start = ((bf16[8,1,48,4096]{3,2,1,0:T(8,128)(2,1)}), bf16[8,1,48,4096]{3,2,1,0:T(8,128)(2,1)S(1)}, u32[]{:S(2)}, u32[]{:S(2)}) async-start(bf16[8,1,48,4096]{3,2,1,0:T(8,128)(2,1)} %get-tuple-element.74), calls=%async_computation | async-start | bytes 6291456 | tf_op jit(solution)/shard_map/all_to_all | solution.py:482
  55.8 15.8 %collective-permute-start.11 = (bf16[64,4224]{1,0:T(8,128)(2,1)}, bf16[64,4224]{1,0:T(8,128)(2,1)S(1)}, u32[]{:S(2)}, u32[]{:S(2)}) collective-permute-start(bf16[64,4224]{1,0:T(8,128)(2,1)} %copy-done.5), channel_id=1, source_target_pairs={{2,1},{1,0},{6,5},{5,4},{10,9},{9,8},{14,13},{13,12},{18,17},{17,1... | collective-permute-start | bytes 1622024 | tf_op jit(solution)/shard_map/ppermute | solution.py:54
  59.2 16.6 %collective-permute-start.10 = (bf16[64,4224]{1,0:T(8,128)(2,1)}, bf16[64,4224]{1,0:T(8,128)(2,1)}, u32[]{:S(2)}, u32[]{:S(2)}) collective-permute-start(bf16[64,4224]{1,0:T(8,128)(2,1)} %copy-done.6), channel_id=1, source_target_pairs={{1,2},{2,3},{5,6},{6,7},{9,10},{10,11},{13,14},{14,15},{17,18},{18... | collective-permute-start | bytes 1622024 | tf_op jit(solution)/shard_map/ppermute | solution.py:54
  71.7 14.0 %copy-start.7 = (bf16[64,4224]{1,0:T(8,128)(2,1)}, bf16[64,4224]{1,0:T(8,128)(2,1)S(1)}, u32[]{:S(2)}) copy-start(bf16[64,4224]{1,0:T(8,128)(2,1)S(1)} %collective-permute-done.11.refs_4_.refs_11_) | copy-start | bytes 1622020
  71.7 14.0 %collective-permute-start.13 = (bf16[64,4224]{1,0:T(8,128)(2,1)S(1)}, bf16[64,4224]{1,0:T(8,128)(2,1)}, u32[]{:S(2)}, u32[]{:S(2)}) collective-permute-start(bf16[64,4224]{1,0:T(8,128)(2,1)S(1)} %collective-permute-done.11.refs_4_.refs_11_), channel_id=1, source_target_pairs={{1,0},{5,4},{9,8},{13,12},{17,16},{21,20},{25,24},{29,28}} | collective-permute-start | bytes 1622024 | tf_op jit(solution)/shard_map/ppermute | solution.py:54
  75.9 9.8 %collective-permute-start.12 = (bf16[64,4224]{1,0:T(8,128)(2,1)}, bf16[64,4224]{1,0:T(8,128)(2,1)}, u32[]{:S(2)}, u32[]{:S(2)}) collective-permute-start(bf16[64,4224]{1,0:T(8,128)(2,1)} %collective-permute-done.10.refs_3_.refs_10_), channel_id=1, source_target_pairs={{2,3},{6,7},{10,11},{14,15},{18,19},{22,23},{26,27},{30,31}} | collective-permute-start | bytes 1622024 | tf_op jit(solution)/shard_map/ppermute | solution.py:54
  93.5 1.7 copy-start.4
  95.1 6.7 %copy-start.17 = (bf16[96,4096]{1,0:T(8,128)(2,1)S(1)}, bf16[96,4096]{1,0:T(8,128)(2,1)}, u32[]{:S(2)}) copy-start(bf16[96,4096]{1,0:T(8,128)(2,1)} %get-tuple-element.82) | copy-start | bytes 2359300
  95.1 9.0 %copy-start.18 = (bf16[96,4096]{1,0:T(8,128)(2,1)S(1)}, bf16[96,4096]{1,0:T(8,128)(2,1)}, u32[]{:S(2)}) copy-start(bf16[96,4096]{1,0:T(8,128)(2,1)} %get-tuple-element.83) | copy-start | bytes 2359300
  95.1 11.0 %copy-start.19 = (bf16[96,4096]{1,0:T(8,128)(2,1)S(1)}, bf16[96,4096]{1,0:T(8,128)(2,1)}, u32[]{:S(2)}) copy-start(bf16[96,4096]{1,0:T(8,128)(2,1)} %get-tuple-element.84) | copy-start | bytes 2359300
  95.1 79.4 %all-to-all-start.1 = ((bf16[8,2,48,4096]{3,2,1,0:T(8,128)(2,1)}), bf16[8,2,48,4096]{3,2,1,0:T(8,128)(2,1)}, u32[]{:S(2)}, u32[]{:S(2)}) async-start(bf16[8,2,48,4096]{3,2,1,0:T(8,128)(2,1)} %get-tuple-element.81), calls=%async_computation.1 | async-start | bytes 12582912 | tf_op jit(solution)/shard_map/all_to_all | solution.py:482
  101.8 35.5 %collective-permute-start.14 = (bf16[96,4096]{1,0:T(8,128)(2,1)S(1)}, bf16[96,4096]{1,0:T(8,128)(2,1)S(1)}, u32[]{:S(2)}, u32[]{:S(2)}) collective-permute-start(bf16[96,4096]{1,0:T(8,128)(2,1)S(1)} %copy-done.17), channel_id=1, source_target_pairs={{0,1},{1,0},{2,3},{3,2},{4,5},{5,4},{6,7},{7,6},{8,9},{9,8},{10,11... | collective-permute-start | bytes 2359304 | tf_op jit(solution)/shard_map/ppermute | solution.py:38
  104.1 52.5 %collective-permute-start.15 = (bf16[96,4096]{1,0:T(8,128)(2,1)S(1)}, bf16[96,4096]{1,0:T(8,128)(2,1)}, u32[]{:S(2)}, u32[]{:S(2)}) collective-permute-start(bf16[96,4096]{1,0:T(8,128)(2,1)S(1)} %copy-done.18), channel_id=1, source_target_pairs={{0,2},{1,3},{2,0},{3,1},{4,6},{5,7},{6,4},{7,5},{8,10},{9,11},{10,... | collective-permute-start | bytes 2359304 | tf_op jit(solution)/shard_map/ppermute | solution.py:38
  106.2 68.4 %collective-permute-start.16 = (bf16[96,4096]{1,0:T(8,128)(2,1)S(1)}, bf16[96,4096]{1,0:T(8,128)(2,1)}, u32[]{:S(2)}, u32[]{:S(2)}) collective-permute-start(bf16[96,4096]{1,0:T(8,128)(2,1)S(1)} %copy-done.19), channel_id=1, source_target_pairs={{0,3},{1,2},{2,1},{3,0},{4,7},{5,6},{6,5},{7,4},{8,11},{9,10},{10,... | collective-permute-start | bytes 2359304 | tf_op jit(solution)/shard_map/ppermute | solution.py:38
  137.3 38.6 %copy-start.23 = (bf16[96,4096]{1,0:T(8,128)(2,1)}, bf16[96,4096]{1,0:T(8,128)(2,1)S(1)}, u32[]{:S(2)}) copy-start(bf16[96,4096]{1,0:T(8,128)(2,1)S(1)} %collective-permute-done.14.refs_1_) | copy-start | bytes 2359300
  175.9 58.4 %all-to-all-start.2 = ((bf16[8,48,4096]{2,1,0:T(8,128)(2,1)}), bf16[8,48,4096]{2,1,0:T(8,128)(2,1)S(1)}, u32[]{:S(2)}, u32[]{:S(2)}) async-start(bf16[8,48,4096]{2,1,0:T(8,128)(2,1)} %bitcast.34), calls=%async_computation.2 | async-start | bytes 6291456 | tf_op jit(solution)/shard_map/all_to_all | solution.py:482
  196.9 33.8 %collective-permute-start.17 = (bf16[96,4096]{1,0:T(8,128)(2,1)}, bf16[96,4096]{1,0:T(8,128)(2,1)}, u32[]{:S(2)}, u32[]{:S(2)}) collective-permute-start(bf16[96,4096]{1,0:T(8,128)(2,1)} %get-tuple-element.92), channel_id=1, source_target_pairs={{0,1},{1,0},{2,3},{3,2},{4,5},{5,4},{6,7},{7,6},{8,9},{9,8},{10,11... | collective-permute-start | bytes 2359304 | tf_op jit(solution)/shard_map/ppermute | solution.py:38
  196.9 37.3 %collective-permute-start.18 = (bf16[96,4096]{1,0:T(8,128)(2,1)}, bf16[96,4096]{1,0:T(8,128)(2,1)}, u32[]{:S(2)}, u32[]{:S(2)}) collective-permute-start(bf16[96,4096]{1,0:T(8,128)(2,1)} %get-tuple-element.93), channel_id=1, source_target_pairs={{0,2},{1,3},{2,0},{3,1},{4,6},{5,7},{6,4},{7,5},{8,10},{9,11},{10,... | collective-permute-start | bytes 2359304 | tf_op jit(solution)/shard_map/ppermute | solution.py:38
  234.3 1.7 copy-start.1
  236.0 39.6 %all-to-all-start.3 = ((bf16[8,48,4096]{2,1,0:T(8,128)(2,1)}), bf16[8,48,4096]{2,1,0:T(8,128)(2,1)}, u32[]{:S(2)}, u32[]{:S(2)}) async-start(bf16[8,48,4096]{2,1,0:T(8,128)(2,1)} %bitcast.16), calls=%async_computation.3 | async-start | bytes 6291456 | tf_op jit(solution)/shard_map/all_to_all | solution.py:482
  241.1 38.8 %collective-permute-start.21 = (bf16[96,4096]{1,0:T(8,128)(2,1)}, bf16[96,4096]{1,0:T(8,128)(2,1)S(1)}, u32[]{:S(2)}, u32[]{:S(2)}) collective-permute-start(bf16[96,4096]{1,0:T(8,128)(2,1)} %get-tuple-element.98), channel_id=1, source_target_pairs={{0,3},{1,2},{2,1},{3,0},{4,7},{5,6},{6,5},{7,4},{8,11},{9,10},{10,... | collective-permute-start | bytes 2359304 | tf_op jit(solution)/shard_map/ppermute | solution.py:38
  247.2 34.0 %collective-permute-start.19 = (bf16[32,4096]{1,0:T(8,128)(2,1)}, bf16[32,4096]{1,0:T(8,128)(2,1)S(1)}, u32[]{:S(2)}, u32[]{:S(2)}) collective-permute-start(bf16[32,4096]{1,0:T(8,128)(2,1)} %get-tuple-element.95), channel_id=1, source_target_pairs={{0,1},{4,5},{8,9},{12,13},{16,17},{20,21},{24,25},{28,29}} | collective-permute-start | bytes 786440 | tf_op jit(solution)/shard_map/ppermute | solution.py:68
  248.5 32.7 %collective-permute-start.20 = (bf16[32,4096]{1,0:T(8,128)(2,1)}, bf16[32,4096]{1,0:T(8,128)(2,1)S(1)}, u32[]{:S(2)}, u32[]{:S(2)}) collective-permute-start(bf16[32,4096]{1,0:T(8,128)(2,1)} %get-tuple-element.96), channel_id=1, source_target_pairs={{3,2},{7,6},{11,10},{15,14},{19,18},{23,22},{27,26},{31,30}} | collective-permute-start | bytes 786440 | tf_op jit(solution)/shard_map/ppermute | solution.py:68
  279.9 2.7 copy-start.16
  282.6 12.4 %copy-start.13 = (bf16[32,4096]{1,0:T(8,128)(2,1)S(1)}, bf16[32,4096]{1,0:T(8,128)(2,1)}, u32[]{:S(2)}) copy-start(bf16[32,4096]{1,0:T(8,128)(2,1)} %get-tuple-element.99) | copy-start | bytes 786436
  282.6 69.6 %all-to-all-start.4 = ((bf16[8,48,4096]{2,1,0:T(8,128)(2,1)}), bf16[8,48,4096]{2,1,0:T(8,128)(2,1)S(1)}, u32[]{:S(2)}, u32[]{:S(2)}) async-start(bf16[8,48,4096]{2,1,0:T(8,128)(2,1)} %bitcast.17), calls=%async_computation.4 | async-start | bytes 6291456 | tf_op jit(solution)/shard_map/all_to_all | solution.py:482
  290.0 45.0 %collective-permute-start.26 = (bf16[32,4096]{1,0:T(8,128)(2,1)}, bf16[32,4096]{1,0:T(8,128)(2,1)}, u32[]{:S(2)}, u32[]{:S(2)}) collective-permute-start(bf16[32,4096]{1,0:T(8,128)(2,1)} %get-tuple-element.105), channel_id=1, source_target_pairs={{0,1},{1,0},{2,3},{3,2},{4,5},{5,4},{6,7},{7,6},{8,9},{9,8},{10,11... | collective-permute-start | bytes 786440 | tf_op jit(solution)/shard_map/ppermute | solution.py:38
  291.3 43.7 %collective-permute-start.27 = (bf16[32,4096]{1,0:T(8,128)(2,1)}, bf16[32,4096]{1,0:T(8,128)(2,1)}, u32[]{:S(2)}, u32[]{:S(2)}) collective-permute-start(bf16[32,4096]{1,0:T(8,128)(2,1)} %get-tuple-element.106), channel_id=1, source_target_pairs={{0,2},{1,3},{2,0},{3,1},{4,6},{5,7},{6,4},{7,5},{8,10},{9,11},{10,... | collective-permute-start | bytes 786440 | tf_op jit(solution)/shard_map/ppermute | solution.py:38
  292.3 42.8 %collective-permute-start.28 = (bf16[32,4096]{1,0:T(8,128)(2,1)}, bf16[32,4096]{1,0:T(8,128)(2,1)}, u32[]{:S(2)}, u32[]{:S(2)}) collective-permute-start(bf16[32,4096]{1,0:T(8,128)(2,1)} %get-tuple-element.107), channel_id=1, source_target_pairs={{0,3},{1,2},{2,1},{3,0},{4,7},{5,6},{6,5},{7,4},{8,11},{9,10},{10,... | collective-permute-start | bytes 786440 | tf_op jit(solution)/shard_map/ppermute | solution.py:38
  293.7 27.6 %collective-permute-start.24 = (bf16[32,4096]{1,0:T(8,128)(2,1)S(1)}, bf16[32,4096]{1,0:T(8,128)(2,1)S(1)}, u32[]{:S(2)}, u32[]{:S(2)}) collective-permute-start(bf16[32,4096]{1,0:T(8,128)(2,1)S(1)} %add_convert_fusion.4), channel_id=1, source_target_pairs={{3,2},{2,1},{7,6},{6,5},{11,10},{10,9},{15,14},{14,13},{19,18},{18... | collective-permute-start | bytes 786440 | tf_op jit(solution)/shard_map/ppermute | solution.py:68
  296.0 28.2 %collective-permute-start.22 = (bf16[32,4096]{1,0:T(8,128)(2,1)S(1)}, bf16[32,4096]{1,0:T(8,128)(2,1)S(1)}, u32[]{:S(2)}, u32[]{:S(2)}) collective-permute-start(bf16[32,4096]{1,0:T(8,128)(2,1)S(1)} %add_convert_fusion.6), channel_id=1, source_target_pairs={{0,1},{1,2},{4,5},{5,6},{8,9},{9,10},{12,13},{13,14},{16,17},{17,1... | collective-permute-start | bytes 786440 | tf_op jit(solution)/shard_map/ppermute | solution.py:68
  322.3 12.7 %collective-permute-start.25 = (bf16[32,4096]{1,0:T(8,128)(2,1)S(1)}, bf16[32,4096]{1,0:T(8,128)(2,1)S(1)}, u32[]{:S(2)}, u32[]{:S(2)}) collective-permute-start(bf16[32,4096]{1,0:T(8,128)(2,1)S(1)} %add_convert_fusion.3), channel_id=1, source_target_pairs={{3,2},{2,1},{1,0},{7,6},{6,5},{5,4},{11,10},{10,9},{9,8},{15,14},{... | collective-permute-start | bytes 786440 | tf_op jit(solution)/shard_map/ppermute | solution.py:68
  326.0 9.1 %collective-permute-start.23 = (bf16[32,4096]{1,0:T(8,128)(2,1)}, bf16[32,4096]{1,0:T(8,128)(2,1)S(1)}, u32[]{:S(2)}, u32[]{:S(2)}) collective-permute-start(bf16[32,4096]{1,0:T(8,128)(2,1)} %add_convert_fusion.5), channel_id=1, source_target_pairs={{0,1},{1,2},{2,3},{4,5},{5,6},{6,7},{8,9},{9,10},{10,11},{12,13},{... | collective-permute-start | bytes 786440 | tf_op jit(solution)/shard_map/ppermute | solution.py:68
  335.8 1.3 copy-start.22
  337.1 14.1 %copy-start.3 = (f32[128,2048]{1,0:T(8,128)S(1)}, f32[128,2048]{1,0:T(8,128)}, u32[]{:S(2)}) copy-start(f32[128,2048]{1,0:T(8,128)} %get-tuple-element.118) | copy-start | bytes 3145732
  337.1 11.8 %collective-permute-start.29 = (bf16[128,2048]{1,0:T(8,128)(2,1)}, bf16[128,2048]{1,0:T(8,128)(2,1)S(1)}, u32[]{:S(2)}, u32[]{:S(2)}) collective-permute-start(bf16[128,2048]{1,0:T(8,128)(2,1)} %get-tuple-element.117), channel_id=1, source_target_pairs={{0,16},{4,20},{8,24},{12,28},{16,0},{20,4},{24,8},{28,12},{1,17},{... | collective-permute-start | bytes 1572872 | tf_op jit(solution)/shard_map/ppermute | solution.py:38
  338.3 12.8 %collective-permute-start.30 = (bf16[128,2048]{1,0:T(8,128)(2,1)}, bf16[128,2048]{1,0:T(8,128)(2,1)S(1)}, u32[]{:S(2)}, u32[]{:S(2)}) collective-permute-start(bf16[128,2048]{1,0:T(8,128)(2,1)} %get-tuple-element.119), channel_id=1, source_target_pairs={{0,8},{4,12},{8,0},{12,4},{16,24},{20,28},{24,16},{28,20},{1,9},{5... | collective-permute-start | bytes 1572872 | tf_op jit(solution)/shard_map/ppermute | solution.py:38
  352.2 9.4 %copy-start = (bf16[8,48,4096]{2,1,0:T(8,128)(2,1)}, bf16[8,48,4096]{2,1,0:T(8,128)(2,1)S(1)}, u32[]{:S(2)}) copy-start(bf16[8,48,4096]{2,1,0:T(8,128)(2,1)S(1)} %all-to-all-done.4) | copy-start | bytes 9437188
  355.0 13.8 %collective-permute-start.34 = (bf16[64,2048]{1,0:T(8,128)(2,1)}, bf16[64,2048]{1,0:T(8,128)(2,1)}, u32[]{:S(2)}, u32[]{:S(2)}) collective-permute-start(bf16[64,2048]{1,0:T(8,128)(2,1)} %split.55), channel_id=1, source_target_pairs={{0,8},{4,12},{8,0},{12,4},{16,24},{20,28},{24,16},{28,20},{1,9},{5... | collective-permute-start | bytes 786440 | tf_op jit(solution)/shard_map/ppermute | solution.py:38
  360.4 14.0 %collective-permute-start.36 = (bf16[64,2048]{1,0:T(8,128)(2,1)}, bf16[64,2048]{1,0:T(8,128)(2,1)}, u32[]{:S(2)}, u32[]{:S(2)}) collective-permute-start(bf16[64,2048]{1,0:T(8,128)(2,1)} %split.54), channel_id=1, source_target_pairs={{0,16},{4,20},{8,24},{12,28},{16,0},{20,4},{24,8},{28,12},{1,17},{... | collective-permute-start | bytes 786440 | tf_op jit(solution)/shard_map/ppermute | solution.py:38
  366.1 24.9 %copy-start.20 = (f32[32,4096]{1,0:T(8,128)S(1)}, f32[32,4096]{1,0:T(8,128)}, u32[]{:S(2)}) copy-start(f32[32,4096]{1,0:T(8,128)} %get-tuple-element.122) | copy-start | bytes 1572868
  366.1 25.1 %copy-start.15 = (bf16[32,4096]{1,0:T(8,128)(2,1)S(1)}, bf16[32,4096]{1,0:T(8,128)(2,1)}, u32[]{:S(2)}) copy-start(bf16[32,4096]{1,0:T(8,128)(2,1)} %add_convert_fusion.1) | copy-start | bytes 786436
  366.1 9.6 %collective-permute-start.31 = (bf16[32,4096]{1,0:T(8,128)(2,1)}, bf16[32,4096]{1,0:T(8,128)(2,1)S(1)}, u32[]{:S(2)}, u32[]{:S(2)}) collective-permute-start(bf16[32,4096]{1,0:T(8,128)(2,1)} %get-tuple-element.123), channel_id=1, source_target_pairs={{0,1},{1,0},{2,3},{3,2},{4,5},{5,4},{6,7},{7,6},{8,9},{9,8},{10,11... | collective-permute-start | bytes 786440 | tf_op jit(solution)/shard_map/ppermute | solution.py:38
  366.4 9.3 %collective-permute-start.32 = (bf16[32,4096]{1,0:T(8,128)(2,1)}, bf16[32,4096]{1,0:T(8,128)(2,1)S(1)}, u32[]{:S(2)}, u32[]{:S(2)}) collective-permute-start(bf16[32,4096]{1,0:T(8,128)(2,1)} %get-tuple-element.124), channel_id=1, source_target_pairs={{0,2},{1,3},{2,0},{3,1},{4,6},{5,7},{6,4},{7,5},{8,10},{9,11},{10,... | collective-permute-start | bytes 786440 | tf_op jit(solution)/shard_map/ppermute | solution.py:38
  366.8 24.1 %collective-permute-start.33 = (bf16[32,4096]{1,0:T(8,128)(2,1)}, bf16[32,4096]{1,0:T(8,128)(2,1)S(1)}, u32[]{:S(2)}, u32[]{:S(2)}) collective-permute-start(bf16[32,4096]{1,0:T(8,128)(2,1)} %get-tuple-element.125), channel_id=1, source_target_pairs={{0,3},{1,2},{2,1},{3,0},{4,7},{5,6},{6,5},{7,4},{8,11},{9,10},{10,... | collective-permute-start | bytes 786440 | tf_op jit(solution)/shard_map/ppermute | solution.py:38
  370.0 21.1 %collective-permute-start.35 = (bf16[32,2048]{1,0:T(8,128)(2,1)S(1)}, bf16[32,2048]{1,0:T(8,128)(2,1)S(1)}, u32[]{:S(2)}, u32[]{:S(2)}) collective-permute-start(bf16[32,2048]{1,0:T(8,128)(2,1)S(1)} %split.57), channel_id=1, source_target_pairs={{0,4},{4,0},{8,12},{12,8},{16,20},{20,16},{24,28},{28,24},{1,5},{5... | collective-permute-start | bytes 393224 | tf_op jit(solution)/shard_map/ppermute | solution.py:38
  375.6 15.5 %collective-permute-start.37 = (bf16[32,2048]{1,0:T(8,128)(2,1)S(1)}, bf16[32,2048]{1,0:T(8,128)(2,1)S(1)}, u32[]{:S(2)}, u32[]{:S(2)}) collective-permute-start(bf16[32,2048]{1,0:T(8,128)(2,1)S(1)} %split.56), channel_id=1, source_target_pairs={{0,4},{4,0},{8,12},{12,8},{16,20},{20,16},{24,28},{28,24},{1,5},{5... | collective-permute-start | bytes 393224 | tf_op jit(solution)/shard_map/ppermute | solution.py:38
  (3 other events, 2.1 us)

commit v8 on v7

--- a/solution.py
+++ b/solution.py
@@ -56,16 +56,6 @@
 
 def chain_offsets(size):
     return [0] + [offset for d in range(1, size) for offset in (-d, d)]
-
-
-def chain_sum_step(parts, axis, step, moved=None):
-    size = lax.axis_size(axis)
-    at = size - 1 - step
-    sides = parts[1::2][at], parts[0::2][at]
-    if moved is not None:
-        sides = [side.astype(F32) + came.astype(F32) for side, came in zip(sides, moved)]
-    ways = [(i, i + 1) for i in range(step)], [(size - 1 - i, size - 2 - i) for i in range(step)]
-    return [lax.ppermute(side.astype(BF16), axis, way) for side, way in zip(sides, ways)]
 
 
 def gather_doubling(array, axis, bits):
@@ -391,8 +381,8 @@
             at += out.shape[0]
 
 
-def expert(parts, tie, gate_weight, up_weight, down_weight, block=None):
-    sizes = [part.shape[0] for part in parts]
+def expert(parts, tie, gate_weight, up_weight, down_weight, block=None, sizes=None):
+    sizes = sizes or [part.shape[0] for part in parts]
     specs = [whole_block(part) for part in parts]
     nodes = 0
     if block is not None:
@@ -513,7 +503,7 @@
     rows_a = [rows_a, swap(rows_a, "node", bits_a[-1])]
     rows_b = [rows_b, swap(rows_b, "node", bits_b[-1])]
     chain = chain_step([sent12, sent12], "local", 1)
-    outbound0, mixing0 = pick([sent0] + near0, *near, chain_in=False, chain_out=True)
+    outbound0, mixing0 = pick([sent0] + near0, *near, chain_in=False, chain_out=False)
 
     outbound0, *last_rows = fence([outbound0, rows_a[1], rows_b[1]], chain)
     arrived0 = to_experts(outbound0)
@@ -539,32 +529,33 @@
 
     out0, tie = fence([out0, ids], [arrived12] + arrived3)
     landed0 = to_experts(out0)
-    out3 = list(expert([own3] + arrived3, tie, *weights))
-    landed3 = out3[:1] + swaps(out3, "local", 1, peers - 1)
+    size = slots // peers
+    sizes = [size] * (peers - 2) + [size * 2 // 3, size // 3] * 2
+    last2, last1 = peers - 2, peers - 1
+    out3 = list(expert([own3] + arrived3, tie, *weights, sizes=sizes))
+    landed3 = out3[:1] + swaps(out3, "local", 1, last1)
+    (tie,) = fence([tie], out3[:1])
     (out1,) = expert([arrived12], tie, *weights, block=0)
 
-    (mixing0,) = fence([mixing0], [out1])
-    out1, last3, tie = fence([out1, out3[-1], tie], [landed0] + landed3[1:])
+    (mixing0,) = fence([mixing0], [out1] + landed3[1:])
+    out1, part2, part3, tie = fence([out1] + out3[-3:-1] + [tie], [landed0] + landed3[1:])
     landed1 = to_experts(out1)
-    landed3.append(swap(last3, "local", peers - 1))
-    own0, sends0 = mix(mixing0, landed0)
-    parts0 = chain_sum_step(sends0, "local", 1)
+    landed3 += [swap(part2, "local", last2), swap(part3, "local", last1)]
+    own0, parts0 = mix(mixing0, landed0)
+    parts0 = swaps([None] + parts0, "local", 1, peers)
     (out2,) = expert([arrived12], tie, *weights, block=1)
 
-    out2, *parts0 = fence([out2] + parts0, [landed1, landed3[-1]])
+    out2, part3 = fence([out2, out3[-1]], [landed1] + landed3[-2:])
     landed2 = to_experts(out2)
-    for step in range(2, peers):
-        parts0 = chain_sum_step(sends0, "local", step, parts0)
+    landed3.append(swap(part3, "local", last1))
     own1, parts1 = mix(mixing1, landed1)
     parts1 = swaps([None] + parts1, "local", 1, peers)
     cross = mix_cross(mixing3a, mixing3b, landed3)
 
-    cross = fence(list(cross), parts0 + parts1)
+    own2, parts2 = mix(mixing2, landed2)
+    cross = fence(list(cross), parts2[:1])
+    parts2 = swaps([None] + parts2, "local", 1, peers)
     sums3 = halve(*cross[:2], "node", bits_a[-1]), halve(*cross[2:], "node", bits_b[-1])
-    sums3 = fence(sums3, [landed2])
-    (mixing2,) = fence([mixing2], sums3[:1])
-    own2, parts2 = mix(mixing2, landed2)
-    parts2 = swaps([None] + parts2, "local", 1, peers)
     piece0, piece1 = total(own0, parts0), total(own1, parts1)
     piece3 = [sum_halving(s, "node", bits[:-1]) for s, bits in zip(sums3, (bits_a, bits_b))]
     piece3 = jnp.concatenate(piece3, axis=1)

time: 396 us -> 385 us (0.972)
  waiting for transfers between devices: 154 us -> 172 us
  other arithmetic: 26.8 us -> 16.8 us
  local copies, waits for them, and re-layouts: 14.5 us -> 5.69 us
  starting transfers between devices: 92.4 us -> 84.1 us
    ppermute x26 -> x31, waiting for transfers between devices: 106 us -> 155 us  [swap(): return lax.ppermute(array, axis, [(i, i ^ bits) for i in range(size)])]
    ppermute x6 -> x0, waiting for transfers between devices: 21.3 us -> none  [chain_sum_step(): lax.ppermute(side.astype(BF16), axis, way)]
    ppermute x6 -> x0, starting transfers between devices: 12.5 us -> none  [chain_sum_step(): lax.ppermute(side.astype(BF16), axis, way)]
    all_to_all x5, waiting for transfers between devices: 10.7 us -> 0.01 us  [to_experts(): return lax.all_to_all(rows, 'node', 0, 0, tiled=True)]
    convert_element_type x4 -> x0, other arithmetic: 4.85 us -> none  [chain_sum_step(): side.astype(BF16)]
    ppermute x26 -> x31, starting transfers between devices: 31.7 us -> 36.5 us  [swap(): return lax.ppermute(array, axis, [(i, i ^ bits) for i in range(size)])]
    add x4, other arithmetic: 5.73 us -> 1.53 us  [halve(): return keep + swap(give.astype(BF16), axis, bit).astype(F32)]
    unnamed x50 -> x49, local copies, waits for them, and re-layouts: 9.13 us -> 5.53 us
  transfers between devices with their start and end apart: 43 -> 42, of which waited for: 15 -> 22; matrix products, arithmetic and copies ran while one was open for 7% -> 3% of each run, Pallas kernels for 26% -> 26%
where the time goes in v8:
time: 385 us; the launch traced here: 382 us
  waiting for transfers between devices  172 us (45%)
  Pallas kernels  104 us (27%)
  starting transfers between devices  84.1 us (22%)
  other arithmetic  16.8 us (4%)
  local copies, waits for them, and re-layouts  5.69 us (1%)
    ppermute x31, waiting for transfers between devices, swap(): return lax.ppermute(array, axis, [(i, i ^ bits) for i in range(size)])  155 us
    pallas_call x4, Pallas kernels, expert(): pl.pallas_call(functools.partial(expert_kernel, len(parts), first_tiles,...  63.2 us
    ppermute x31, starting transfers between devices, swap(): return lax.ppermute(array, axis, [(i, i ^ bits) for i in range(size)])  36.5 us
    all_to_all x5, starting transfers between devices, to_experts(): return lax.all_to_all(rows, 'node', 0, 0, tiled=True)  29.8 us
    ppermute x6, starting transfers between devices, chain_step(): lax.ppermute(a, axis, way)  17.8 us
    ppermute x6, waiting for transfers between devices, chain_step(): lax.ppermute(a, axis, way)  16.3 us
    pallas_call x3, Pallas kernels, mix(): pl.pallas_call(mix_kernel, grid=(TILES,), out_shape=[jax.ShapeDtypeStruct...  13.2 us
    pallas_call x2, Pallas kernels, pick(): pl.pallas_call(functools.partial(pick_kernel, len(parts), blocks, peers,...  12.8 us
  transfers between devices with their start and end apart: 42, of which 22 were waited for; matrix products, arithmetic and copies ran while one was open for 3% of the time, Pallas kernels for 26%

profile of v8, /device:TPU:9, one launch (start us, length us, event | category | flops | bytes accessed | tf_op | source)
XLA Modules:
  0.0 382.1 jit_solution(3276595926485980692)
XLA Ops:
  0.0 2.9 shard_map.262
  2.9 1.3 collective-permute-start.2
  9.1 1.3 collective-permute-start.4
  10.4 1.3 collective-permute-start.5
  11.7 10.6 %collective-permute-done.2.refs_3_.refs_7_ = bf16[32,4224]{1,0:T(8,128)(2,1)S(1)} collective-permute-done((bf16[32,4224]{1,0:T(8,128)(2,1)}, bf16[32,4224]{1,0:T(8,128)(2,1)S(1)}, u32[]{:S(2)}, u32[]{:S(2)}) %collective-permute-start.2) | collective-permute-done | bytes 270368 | tf_op jit(solution)/shard_map/ppermute | solution.py:38
  22.2 4.8 %collective-permute-done.1.refs_2_.refs_6_ = bf16[32,4224]{1,0:T(8,128)(2,1)S(1)} collective-permute-done((bf16[32,4224]{1,0:T(8,128)(2,1)}, bf16[32,4224]{1,0:T(8,128)(2,1)S(1)}, u32[]{:S(2)}, u32[]{:S(2)}) %collective-permute-start.1) | collective-permute-done | bytes 270368 | tf_op jit(solution)/shard_map/ppermute | solution.py:38
  29.4 4.1 %collective-permute-start.9 = (bf16[64,4224]{1,0:T(8,128)(2,1)}, bf16[64,4224]{1,0:T(8,128)(2,1)S(1)}, u32[]{:S(2)}, u32[]{:S(2)}) collective-permute-start(bf16[64,4224]{1,0:T(8,128)(2,1)} %get-tuple-element.70.refs_0_.refs_7_), channel_id=1, source_target_pairs={{3,2},{2,1},{1,0},{7,6},{6,5},{5,4},{11,10},{10,9},{9,8},{15,14},{... | collective-permute-start | bytes 1622024 | tf_op jit(solution)/shard_map/ppermute | solution.py:54
  33.5 1.9 collective-permute-start.8
  35.4 1.3 collective-permute-start.7
  36.7 1.2 collective-permute-start.6
  38.5 5.1 %shard_map.263 = (bf16[8,1,48,4096]{3,2,1,0:T(8,128)(2,1)}, bf16[128,384]{1,0:T(8,128)(2,1)}) custom-call(s32[2]{0:T(128)} %pad_add_fusion.ids.tie.refs_1_, bf16[32,4224]{1,0:T(8,128)(2,1)} %get-tuple-element.63.refs_0_.refs_4_, bf16[32,4224]{1,0:T(8,128)(2,1)} %copy-done.11, bf16[32,4224]{1,0:T(8,128)(2,1)} %copy-done.10, bf16[32,4224]{1,0:T(8,128)(2,1)} %copy-done.9, ...), custom_call_target="tpu_custom_call" | custom-call | flops 402653184 | bytes 4194304 | tf_op jit(solution)/shard_map/pallas_call | solution.py:182
  44.0 3.7 collective-permute-done.8.refs_1_.refs_8_
  49.4 6.4 %all-to-all-start = ((bf16[8,1,48,4096]{3,2,1,0:T(8,128)(2,1)}), bf16[8,1,48,4096]{3,2,1,0:T(8,128)(2,1)S(1)}, u32[]{:S(2)}, u32[]{:S(2)}) async-start(bf16[8,1,48,4096]{3,2,1,0:T(8,128)(2,1)} %get-tuple-element.71), calls=%async_computation | async-start | bytes 6291456 | tf_op jit(solution)/shard_map/all_to_all | solution.py:472
  55.8 3.4 collective-permute-start.11
  59.2 2.7 collective-permute-start.10
  61.9 9.7 %collective-permute-done.11.refs_4_.refs_11_ = bf16[64,4224]{1,0:T(8,128)(2,1)S(1)} collective-permute-done((bf16[64,4224]{1,0:T(8,128)(2,1)}, bf16[64,4224]{1,0:T(8,128)(2,1)S(1)}, u32[]{:S(2)}, u32[]{:S(2)}) %collective-permute-start.11) | collective-permute-done | bytes 540704 | tf_op jit(solution)/shard_map/ppermute | solution.py:54
  71.6 4.2 %collective-permute-start.13 = (bf16[64,4224]{1,0:T(8,128)(2,1)S(1)}, bf16[64,4224]{1,0:T(8,128)(2,1)}, u32[]{:S(2)}, u32[]{:S(2)}) collective-permute-start(bf16[64,4224]{1,0:T(8,128)(2,1)S(1)} %collective-permute-done.11.refs_4_.refs_11_), channel_id=1, source_target_pairs={{1,0},{5,4},{9,8},{13,12},{17,16},{21,20},{25,24},{29,28}} | collective-permute-start | bytes 1622024 | tf_op jit(solution)/shard_map/ppermute | solution.py:54
  75.8 1.5 collective-permute-start.12
  77.3 5.8 %shard_map.268 = (bf16[96,4096]{1,0:T(8,128)(2,1)}, bf16[96,4096]{1,0:T(8,128)(2,1)}, bf16[96,4096]{1,0:T(8,128)(2,1)}, bf16[96,4096]{1,0:T(8,128)(2,1)}, bf16[2...) custom-call(s32[2]{0:T(128)} %pad_add_fusion.ids.tie.refs_1_, bf16[128,2048]{1,0:T(8,128)(2,1)} %get-tuple-element.68.a0, ...), custom_call_target="tpu_custom_call" | custom-call | flops 805306368 | bytes 5242880 | tf_op jit(solution)/shard_map/pallas_call | solution.py:260
  83.1 2.5 collective-permute-done.13.refs_6_.refs_13_
  85.6 7.7 %shard_map.267 = (bf16[8,2,48,4096]{3,2,1,0:T(8,128)(2,1)}, bf16[128,384]{1,0:T(8,128)(2,1)}, bf16[128,384]{1,0:T(8,128)(2,1)}) custom-call(s32[2]{0:T(128)} %pad_add_fusion.ids.tie.refs_1_, bf16[64,4224]{1,0:T(8,128)(2,1)} %get-tuple-element.70.refs_0_.refs_7_, bf16[64,4224]{1,0:T(8,128)(2,1)} %copy-done.6, bf16[64,4224]{1,0:T(8,128)(2,1)} %copy-done.5, ...), custom_call_target="tpu_custom_call" | custom-call | flops 1409286144 | bytes 9961472 | tf_op jit(solution)/shard_map/pallas_call | solution.py:182
  95.0 6.6 %all-to-all-start.1 = ((bf16[8,2,48,4096]{3,2,1,0:T(8,128)(2,1)}), bf16[8,2,48,4096]{3,2,1,0:T(8,128)(2,1)}, u32[]{:S(2)}, u32[]{:S(2)}) async-start(bf16[8,2,48,4096]{3,2,1,0:T(8,128)(2,1)} %get-tuple-element.78), calls=%async_computation.1 | async-start | bytes 12582912 | tf_op jit(solution)/shard_map/all_to_all | solution.py:472
  101.7 2.3 collective-permute-start.14
  104.0 2.0 collective-permute-start.15
  106.3 15.9 %shard_map.266.refs_0_ = bf16[384,4096]{1,0:T(8,128)(2,1)} custom-call(s32[2]{0:T(128)} %pad_add_fusion.ids.tie.refs_1_, bf16[384,4096]{1,0:T(8,128)(2,1)} %bitcast.35, bf16[4096,768]{1,0:T(8,128)(2,1)} %bitcast.18, bf16[4096,768]{1,0:T(8,128)(2,1)} %bitcast.22, bf16[768,4096]{1,0:T(8,128)(2,1)} %bitcast.26), custom_call_target="tpu_custom_call" | custom-call | flops 7247757312 | bytes 25165824 | tf_op jit(solution)/shard_map/pallas_call | solution.py:404
  122.2 14.9 %collective-permute-done.14.refs_1_ = bf16[96,4096]{1,0:T(8,128)(2,1)S(1)} collective-permute-done((bf16[96,4096]{1,0:T(8,128)(2,1)S(1)}, bf16[96,4096]{1,0:T(8,128)(2,1)S(1)}, u32[]{:S(2)}, u32[]{:S(2)}) %collective-permute-start.14) | collective-permute-done | bytes 786464 | tf_op jit(solution)/shard_map/ppermute | solution.py:38
  137.1 19.4 %collective-permute-done.15.refs_2_ = bf16[96,4096]{1,0:T(8,128)(2,1)} collective-permute-done((bf16[96,4096]{1,0:T(8,128)(2,1)S(1)}, bf16[96,4096]{1,0:T(8,128)(2,1)}, u32[]{:S(2)}, u32[]{:S(2)}) %collective-permute-start.15) | collective-permute-done | bytes 786464 | tf_op jit(solution)/shard_map/ppermute | solution.py:38
  156.5 17.9 %collective-permute-done.16.refs_3_ = bf16[96,4096]{1,0:T(8,128)(2,1)} collective-permute-done((bf16[96,4096]{1,0:T(8,128)(2,1)S(1)}, bf16[96,4096]{1,0:T(8,128)(2,1)}, u32[]{:S(2)}, u32[]{:S(2)}) %collective-permute-start.16) | collective-permute-done | bytes 786464 | tf_op jit(solution)/shard_map/ppermute | solution.py:38
  174.4 1.3 convert_add_fusion.7.refs_2_
  175.7 4.9 %all-to-all-start.2 = ((bf16[8,48,4096]{2,1,0:T(8,128)(2,1)}), bf16[8,48,4096]{2,1,0:T(8,128)(2,1)S(1)}, u32[]{:S(2)}, u32[]{:S(2)}) async-start(bf16[8,48,4096]{2,1,0:T(8,128)(2,1)} %bitcast.33), calls=%async_computation.2 | async-start | bytes 6291456 | tf_op jit(solution)/shard_map/all_to_all | solution.py:472
  180.6 16.1 %shard_map.271 = (bf16[96,4096]{1,0:T(8,128)(2,1)}, bf16[96,4096]{1,0:T(8,128)(2,1)}, bf16[64,4096]{1,0:T(8,128)(2,1)}, bf16[32,4096]{1,0:T(8,128)(2,1)}, bf16[6...) custom-call(s32[2]{0:T(128)} %get-tuple-element.82.tie.refs_0_, bf16[96,4096]{1,0:T(8,128)(2,1)} %get-tuple-element.83.refs_0_, ...), custom_call_target="tpu_custom_call" | custom-call | flops 7247757312 | bytes 25165824 | tf_op jit(solution)/shard_map/pallas_call | solution.py:404
  196.8 1.3 slice_convert_fusion.6.refs_1_
  198.1 2.4 collective-permute-start.18
  200.5 15.6 %shard_map.273.refs_0_ = bf16[384,4096]{1,0:T(8,128)(2,1)} custom-call(s32[2]{0:T(128)} %shard_map.272.tie.refs_3_, bf16[8,2,48,4096]{3,2,1,0:T(8,128)(2,1)} %all-to-all-done.1.refs_0_, bf16[4096,768]{1,0:T(8,128)(2,1)} %bitcast.20, bf16[4096,768]{1,0:T(8,128)(2,1)} %bitcast.24, bf16[768,4096]{1,0:T(8,128)(2,1)} %bitcast.28), custom_call_target="tpu_custom_call" | custom-call | flops 7247757312 | bytes 25165824 | tf_op jit(solution)/shard_map/pallas_call | solution.py:404
  216.1 12.3 %collective-permute-done.18.refs_2_ = bf16[64,4096]{1,0:T(8,128)(2,1)S(1)} collective-permute-done((bf16[64,4096]{1,0:T(8,128)(2,1)}, bf16[64,4096]{1,0:T(8,128)(2,1)S(1)}, u32[]{:S(2)}, u32[]{:S(2)}) %collective-permute-start.18) | collective-permute-done | bytes 524320 | tf_op jit(solution)/shard_map/ppermute | solution.py:38
  229.2 1.6 convert_add_fusion.3
  230.9 5.3 %all-to-all-start.3 = ((bf16[8,48,4096]{2,1,0:T(8,128)(2,1)}), bf16[8,48,4096]{2,1,0:T(8,128)(2,1)}, u32[]{:S(2)}, u32[]{:S(2)}) async-start(bf16[8,48,4096]{2,1,0:T(8,128)(2,1)} %bitcast.16), calls=%async_computation.3 | async-start | bytes 6291456 | tf_op jit(solution)/shard_map/all_to_all | solution.py:472
  236.5 15.5 %shard_map.278.refs_0_ = bf16[384,4096]{1,0:T(8,128)(2,1)} custom-call(s32[2]{0:T(128)} %get-tuple-element.101.tie, bf16[8,2,48,4096]{3,2,1,0:T(8,128)(2,1)} %all-to-all-done.1.refs_0_, bf16[4096,768]{1,0:T(8,128)(2,1)} %bitcast.21, bf16[4096,768]{1,0:T(8,128)(2,1)} %bitcast.25, bf16[768,4096]{1,0:T(8,128)(2,1)} %bitcast.29), custom_call_target="tpu_custom_call" | custom-call | flops 7247757312 | bytes 25165824 | tf_op jit(solution)/shard_map/pallas_call | solution.py:404
  252.1 6.8 %collective-permute-done.25.refs_3_ = bf16[32,4096]{1,0:T(8,128)(2,1)S(1)} collective-permute-done((bf16[32,4096]{1,0:T(8,128)(2,1)S(1)}, bf16[32,4096]{1,0:T(8,128)(2,1)S(1)}, u32[]{:S(2)}, u32[]{:S(2)}) %collective-permute-start.25) | collective-permute-done | bytes 262176 | tf_op jit(solution)/shard_map/ppermute | solution.py:38
  258.9 12.3 %collective-permute-done.26.refs_4_ = bf16[64,4096]{1,0:T(8,128)(2,1)S(1)} collective-permute-done((bf16[64,4096]{1,0:T(8,128)(2,1)}, bf16[64,4096]{1,0:T(8,128)(2,1)S(1)}, u32[]{:S(2)}, u32[]{:S(2)}) %collective-permute-start.26) | collective-permute-done | bytes 524320 | tf_op jit(solution)/shard_map/ppermute | solution.py:38
  271.2 1.3 convert_add_fusion.6.refs_2_
  272.5 6.6 %all-to-all-start.4 = ((bf16[8,48,4096]{2,1,0:T(8,128)(2,1)}), bf16[8,48,4096]{2,1,0:T(8,128)(2,1)S(1)}, u32[]{:S(2)}, u32[]{:S(2)}) async-start(bf16[8,48,4096]{2,1,0:T(8,128)(2,1)} %bitcast.17), calls=%async_computation.4 | async-start | bytes 6291456 | tf_op jit(solution)/shard_map/all_to_all | solution.py:472
  279.1 4.5 %shard_map.275 = (f32[32,4096]{1,0:T(8,128)}, bf16[32,4096]{1,0:T(8,128)(2,1)}, bf16[32,4096]{1,0:T(8,128)(2,1)}, bf16[32,4096]{1,0:T(8,128)(2,1)}) custom-call(bf16[128,384]{1,0:T(8,128)(2,1)} %shard_map.274.mixing, bf16[384,4096]{1,0:T(8,128)(2,1)} %bitcast.31), custom_call_target="tpu_custom_call" | custom-call | flops 402653184 | bytes 4194304 | tf_op jit(solution)/shard_map/pallas_call | solution.py:295
  283.6 1.4 collective-permute-start.20
  285.0 1.3 collective-permute-start.21
  286.2 4.3 %shard_map.277 = (f32[32,4096]{1,0:T(8,128)}, bf16[32,4096]{1,0:T(8,128)(2,1)}, bf16[32,4096]{1,0:T(8,128)(2,1)}, bf16[32,4096]{1,0:T(8,128)(2,1)}) custom-call(bf16[128,384]{1,0:T(8,128)(2,1)} %get-tuple-element.92.mixing, bf16[384,4096]{1,0:T(8,128)(2,1)} %bitcast.13.landed), custom_call_target="tpu_custom_call" | custom-call | flops 402653184 | bytes 4194304 | tf_op jit(solution)/shard_map/pallas_call | solution.py:295
  291.9 2.2 collective-permute-done.19
  295.2 2.0 collective-permute-done.20
  297.2 29.1 %collective-permute-done.21 = bf16[32,4096]{1,0:T(8,128)(2,1)} collective-permute-done((bf16[32,4096]{1,0:T(8,128)(2,1)}, bf16[32,4096]{1,0:T(8,128)(2,1)}, u32[]{:S(2)}, u32[]{:S(2)}) %collective-permute-start.21) | collective-permute-done | bytes 262176 | tf_op jit(solution)/shard_map/ppermute | solution.py:38
  327.6 2.3 collective-permute-done.23
  329.9 7.5 %collective-permute-done.24 = bf16[32,4096]{1,0:T(8,128)(2,1)S(1)} collective-permute-done((bf16[32,4096]{1,0:T(8,128)(2,1)}, bf16[32,4096]{1,0:T(8,128)(2,1)S(1)}, u32[]{:S(2)}, u32[]{:S(2)}) %collective-permute-start.24) | collective-permute-done | bytes 262176 | tf_op jit(solution)/shard_map/ppermute | solution.py:38
  337.5 1.8 add_convert_fusion.1
  339.3 1.6 copy-done.1
  340.9 4.4 %shard_map.280 = (f32[32,4096]{1,0:T(8,128)}, bf16[32,4096]{1,0:T(8,128)(2,1)}, bf16[32,4096]{1,0:T(8,128)(2,1)}, bf16[32,4096]{1,0:T(8,128)(2,1)}) custom-call(bf16[128,384]{1,0:T(8,128)(2,1)} %get-tuple-element.100.mixing, bf16[384,4096]{1,0:T(8,128)(2,1)} %bitcast.32), custom_call_target="tpu_custom_call" | custom-call | flops 402653184 | bytes 4194304 | tf_op jit(solution)/shard_map/pallas_call | solution.py:295
  345.5 3.3 collective-permute-start.27
  348.8 5.7 %shard_map.281 = (f32[128,2048]{1,0:T(8,128)}, bf16[128,2048]{1,0:T(8,128)(2,1)}, f32[128,2048]{1,0:T(8,128)}, bf16[128,2048]{1,0:T(8,128)(2,1)}) custom-call(bf16[256,384]{1,0:T(8,128)(2,1)} %get-tuple-element.110.mixing_a, bf16[256,384]{1,0:T(8,128)(2,1)} %get-tuple-element.111.mixing_b, bf16[96,4096]{1,0:T(8,128)(2,1)} %get-tuple-element.84.refs_0_, ...), custom_call_target="tpu_custom_call" | custom-call | flops 805306368 | bytes 5242880 | tf_op jit(solution)/shard_map/pallas_call | solution.py:337
  354.5 1.3 slice_convert_fusion.5.refs_4_
  358.2 3.4 collective-permute-done.28
  361.6 5.8 %collective-permute-done.29 = bf16[32,4096]{1,0:T(8,128)(2,1)S(1)} collective-permute-done((bf16[32,4096]{1,0:T(8,128)(2,1)}, bf16[32,4096]{1,0:T(8,128)(2,1)S(1)}, u32[]{:S(2)}, u32[]{:S(2)}) %collective-permute-start.29) | collective-permute-done | bytes 262176 | tf_op jit(solution)/shard_map/ppermute | solution.py:38
  367.5 1.3 convert_add_fusion.1
  370.3 1.3 collective-permute-start.35
  371.6 2.6 collective-permute-done.32
  374.3 4.0 %collective-permute-start.33 = (bf16[32,2048]{1,0:T(8,128)(2,1)S(1)}, bf16[32,2048]{1,0:T(8,128)(2,1)S(1)}, u32[]{:S(2)}, u32[]{:S(2)}) collective-permute-start(bf16[32,2048]{1,0:T(8,128)(2,1)S(1)} %split.59), channel_id=1, source_target_pairs={{0,4},{4,0},{8,12},{12,8},{16,20},{20,16},{24,28},{28,24},{1,5},{5... | collective-permute-start | bytes 393224 | tf_op jit(solution)/shard_map/ppermute | solution.py:38
  378.4 1.6 collective-permute-start.36
  (118 shorter events, 23.2 us)
Async XLA Ops:
  2.9 19.3 %collective-permute-start.2 = (bf16[32,4224]{1,0:T(8,128)(2,1)}, bf16[32,4224]{1,0:T(8,128)(2,1)S(1)}, u32[]{:S(2)}, u32[]{:S(2)}) collective-permute-start(bf16[32,4224]{1,0:T(8,128)(2,1)} %get-tuple-element.63.refs_0_.refs_4_), channel_id=1, source_target_pairs={{0,3},{1,2},{2,1},{3,0},{4,7},{5,6},{6,5},{7,4},{8,11},{9,10},{10,... | collective-permute-start | bytes 811016 | tf_op jit(solution)/shard_map/ppermute | solution.py:38
  4.2 22.8 %collective-permute-start.1 = (bf16[32,4224]{1,0:T(8,128)(2,1)}, bf16[32,4224]{1,0:T(8,128)(2,1)S(1)}, u32[]{:S(2)}, u32[]{:S(2)}) collective-permute-start(bf16[32,4224]{1,0:T(8,128)(2,1)} %get-tuple-element.63.refs_0_.refs_4_), channel_id=1, source_target_pairs={{0,2},{1,3},{2,0},{3,1},{4,6},{5,7},{6,4},{7,5},{8,10},{9,11},{10,... | collective-permute-start | bytes 811016 | tf_op jit(solution)/shard_map/ppermute | solution.py:38
  5.2 21.8 %collective-permute-start = (bf16[32,4224]{1,0:T(8,128)(2,1)}, bf16[32,4224]{1,0:T(8,128)(2,1)S(1)}, u32[]{:S(2)}, u32[]{:S(2)}) collective-permute-start(bf16[32,4224]{1,0:T(8,128)(2,1)} %get-tuple-element.63.refs_0_.refs_4_), channel_id=1, source_target_pairs={{0,1},{1,0},{2,3},{3,2},{4,5},{5,4},{6,7},{7,6},{8,9},{9,8},{10,11... | collective-permute-start | bytes 811016 | tf_op jit(solution)/shard_map/ppermute | solution.py:38
  6.4 2.6 collective-permute-start.3
  9.1 18.6 %collective-permute-start.4 = (bf16[64,2048]{1,0:T(8,128)(2,1)S(1)}, bf16[64,2048]{1,0:T(8,128)(2,1)S(1)}, u32[]{:S(2)}, u32[]{:S(2)}) collective-permute-start(bf16[64,2048]{1,0:T(8,128)(2,1)S(1)} %slice.86), channel_id=1, source_target_pairs={{0,8},{4,12},{8,0},{12,4},{16,24},{20,28},{24,16},{28,20},{1,9},{5... | collective-permute-start | bytes 786440 | tf_op jit(solution)/shard_map/ppermute | solution.py:38
  10.4 18.2 %collective-permute-start.5 = (bf16[64,2176]{1,0:T(8,128)(2,1)S(1)}, bf16[64,2176]{1,0:T(8,128)(2,1)S(1)}, u32[]{:S(2)}, u32[]{:S(2)}) collective-permute-start(bf16[64,2176]{1,0:T(8,128)(2,1)S(1)} %slice.87), channel_id=1, source_target_pairs={{0,16},{4,20},{8,24},{12,28},{16,0},{20,4},{24,8},{28,12},{1,17},{... | collective-permute-start | bytes 835592 | tf_op jit(solution)/shard_map/ppermute | solution.py:38
  22.2 16.3 %copy-start.9 = (bf16[32,4224]{1,0:T(8,128)(2,1)}, bf16[32,4224]{1,0:T(8,128)(2,1)S(1)}, u32[]{:S(2)}) copy-start(bf16[32,4224]{1,0:T(8,128)(2,1)S(1)} %collective-permute-done.2.refs_3_.refs_7_) | copy-start | bytes 811012
  27.0 11.5 %copy-start.10 = (bf16[32,4224]{1,0:T(8,128)(2,1)}, bf16[32,4224]{1,0:T(8,128)(2,1)S(1)}, u32[]{:S(2)}) copy-start(bf16[32,4224]{1,0:T(8,128)(2,1)S(1)} %collective-permute-done.1.refs_2_.refs_6_) | copy-start | bytes 811012
  27.0 11.5 %copy-start.11 = (bf16[32,4224]{1,0:T(8,128)(2,1)}, bf16[32,4224]{1,0:T(8,128)(2,1)S(1)}, u32[]{:S(2)}) copy-start(bf16[32,4224]{1,0:T(8,128)(2,1)S(1)} %collective-permute-done.refs_1_.refs_5_) | copy-start | bytes 811012
  29.4 14.6 %collective-permute-start.9 = (bf16[64,4224]{1,0:T(8,128)(2,1)}, bf16[64,4224]{1,0:T(8,128)(2,1)S(1)}, u32[]{:S(2)}, u32[]{:S(2)}) collective-permute-start(bf16[64,4224]{1,0:T(8,128)(2,1)} %get-tuple-element.70.refs_0_.refs_7_), channel_id=1, source_target_pairs={{3,2},{2,1},{1,0},{7,6},{6,5},{5,4},{11,10},{10,9},{9,8},{15,14},{... | collective-permute-start | bytes 1622024 | tf_op jit(solution)/shard_map/ppermute | solution.py:54
  33.5 14.2 %collective-permute-start.8 = (bf16[64,4224]{1,0:T(8,128)(2,1)}, bf16[64,4224]{1,0:T(8,128)(2,1)S(1)}, u32[]{:S(2)}, u32[]{:S(2)}) collective-permute-start(bf16[64,4224]{1,0:T(8,128)(2,1)} %get-tuple-element.70.refs_0_.refs_7_), channel_id=1, source_target_pairs={{0,1},{1,2},{2,3},{4,5},{5,6},{6,7},{8,9},{9,10},{10,11},{12,13},{... | collective-permute-start | bytes 1622024 | tf_op jit(solution)/shard_map/ppermute | solution.py:54
  35.4 13.0 %collective-permute-start.7 = (bf16[128,2176]{1,0:T(8,128)(2,1)}, bf16[128,2176]{1,0:T(8,128)(2,1)S(1)}, u32[]{:S(2)}, u32[]{:S(2)}) collective-permute-start(bf16[128,2176]{1,0:T(8,128)(2,1)} %get-tuple-element.69.b0.t0), channel_id=1, source_target_pairs={{0,8},{4,12},{8,0},{12,4},{16,24},{20,28},{24,16},{28,20},{1,9},{5... | collective-permute-start | bytes 1671176 | tf_op jit(solution)/shard_map/ppermute | solution.py:38
  36.7 11.7 %collective-permute-start.6 = (bf16[128,2048]{1,0:T(8,128)(2,1)}, bf16[128,2048]{1,0:T(8,128)(2,1)S(1)}, u32[]{:S(2)}, u32[]{:S(2)}) collective-permute-start(bf16[128,2048]{1,0:T(8,128)(2,1)} %get-tuple-element.68.a0), channel_id=1, source_target_pairs={{0,16},{4,20},{8,24},{12,28},{16,0},{20,4},{24,8},{28,12},{1,17},{... | collective-permute-start | bytes 1572872 | tf_op jit(solution)/shard_map/ppermute | solution.py:38
  44.0 5.4 %copy-start.5 = (bf16[64,4224]{1,0:T(8,128)(2,1)}, bf16[64,4224]{1,0:T(8,128)(2,1)S(1)}, u32[]{:S(2)}) copy-start(bf16[64,4224]{1,0:T(8,128)(2,1)S(1)} %collective-permute-done.9.refs_2_.refs_9_) | copy-start | bytes 1622020
  47.7 1.7 copy-start.6
  48.4 1.0 copy-start.2
  49.4 44.0 %all-to-all-start = ((bf16[8,1,48,4096]{3,2,1,0:T(8,128)(2,1)}), bf16[8,1,48,4096]{3,2,1,0:T(8,128)(2,1)S(1)}, u32[]{:S(2)}, u32[]{:S(2)}) async-start(bf16[8,1,48,4096]{3,2,1,0:T(8,128)(2,1)} %get-tuple-element.71), calls=%async_computation | async-start | bytes 6291456 | tf_op jit(solution)/shard_map/all_to_all | solution.py:472
  55.8 15.8 %collective-permute-start.11 = (bf16[64,4224]{1,0:T(8,128)(2,1)}, bf16[64,4224]{1,0:T(8,128)(2,1)S(1)}, u32[]{:S(2)}, u32[]{:S(2)}) collective-permute-start(bf16[64,4224]{1,0:T(8,128)(2,1)} %copy-done.5), channel_id=1, source_target_pairs={{2,1},{1,0},{6,5},{5,4},{10,9},{9,8},{14,13},{13,12},{18,17},{17,1... | collective-permute-start | bytes 1622024 | tf_op jit(solution)/shard_map/ppermute | solution.py:54
  59.2 16.6 %collective-permute-start.10 = (bf16[64,4224]{1,0:T(8,128)(2,1)}, bf16[64,4224]{1,0:T(8,128)(2,1)}, u32[]{:S(2)}, u32[]{:S(2)}) collective-permute-start(bf16[64,4224]{1,0:T(8,128)(2,1)} %copy-done.6), channel_id=1, source_target_pairs={{1,2},{2,3},{5,6},{6,7},{9,10},{10,11},{13,14},{14,15},{17,18},{18... | collective-permute-start | bytes 1622024 | tf_op jit(solution)/shard_map/ppermute | solution.py:54
  71.6 14.0 %copy-start.7 = (bf16[64,4224]{1,0:T(8,128)(2,1)}, bf16[64,4224]{1,0:T(8,128)(2,1)S(1)}, u32[]{:S(2)}) copy-start(bf16[64,4224]{1,0:T(8,128)(2,1)S(1)} %collective-permute-done.11.refs_4_.refs_11_) | copy-start | bytes 1622020
  71.6 14.0 %collective-permute-start.13 = (bf16[64,4224]{1,0:T(8,128)(2,1)S(1)}, bf16[64,4224]{1,0:T(8,128)(2,1)}, u32[]{:S(2)}, u32[]{:S(2)}) collective-permute-start(bf16[64,4224]{1,0:T(8,128)(2,1)S(1)} %collective-permute-done.11.refs_4_.refs_11_), channel_id=1, source_target_pairs={{1,0},{5,4},{9,8},{13,12},{17,16},{21,20},{25,24},{29,28}} | collective-permute-start | bytes 1622024 | tf_op jit(solution)/shard_map/ppermute | solution.py:54
  75.8 9.8 %collective-permute-start.12 = (bf16[64,4224]{1,0:T(8,128)(2,1)}, bf16[64,4224]{1,0:T(8,128)(2,1)}, u32[]{:S(2)}, u32[]{:S(2)}) collective-permute-start(bf16[64,4224]{1,0:T(8,128)(2,1)} %collective-permute-done.10.refs_3_.refs_10_), channel_id=1, source_target_pairs={{2,3},{6,7},{10,11},{14,15},{18,19},{22,23},{26,27},{30,31}} | collective-permute-start | bytes 1622024 | tf_op jit(solution)/shard_map/ppermute | solution.py:54
  93.4 1.6 copy-start.4
  95.0 6.6 %copy-start.13 = (bf16[96,4096]{1,0:T(8,128)(2,1)S(1)}, bf16[96,4096]{1,0:T(8,128)(2,1)}, u32[]{:S(2)}) copy-start(bf16[96,4096]{1,0:T(8,128)(2,1)} %get-tuple-element.79) | copy-start | bytes 2359300
  95.0 9.0 %copy-start.14 = (bf16[96,4096]{1,0:T(8,128)(2,1)S(1)}, bf16[96,4096]{1,0:T(8,128)(2,1)}, u32[]{:S(2)}) copy-start(bf16[96,4096]{1,0:T(8,128)(2,1)} %get-tuple-element.80) | copy-start | bytes 2359300
  95.0 11.0 %copy-start.15 = (bf16[96,4096]{1,0:T(8,128)(2,1)S(1)}, bf16[96,4096]{1,0:T(8,128)(2,1)}, u32[]{:S(2)}) copy-start(bf16[96,4096]{1,0:T(8,128)(2,1)} %get-tuple-element.81) | copy-start | bytes 2359300
  95.0 79.4 %all-to-all-start.1 = ((bf16[8,2,48,4096]{3,2,1,0:T(8,128)(2,1)}), bf16[8,2,48,4096]{3,2,1,0:T(8,128)(2,1)}, u32[]{:S(2)}, u32[]{:S(2)}) async-start(bf16[8,2,48,4096]{3,2,1,0:T(8,128)(2,1)} %get-tuple-element.78), calls=%async_computation.1 | async-start | bytes 12582912 | tf_op jit(solution)/shard_map/all_to_all | solution.py:472
  101.7 35.5 %collective-permute-start.14 = (bf16[96,4096]{1,0:T(8,128)(2,1)S(1)}, bf16[96,4096]{1,0:T(8,128)(2,1)S(1)}, u32[]{:S(2)}, u32[]{:S(2)}) collective-permute-start(bf16[96,4096]{1,0:T(8,128)(2,1)S(1)} %copy-done.13), channel_id=1, source_target_pairs={{0,1},{1,0},{2,3},{3,2},{4,5},{5,4},{6,7},{7,6},{8,9},{9,8},{10,11... | collective-permute-start | bytes 2359304 | tf_op jit(solution)/shard_map/ppermute | solution.py:38
  104.0 52.5 %collective-permute-start.15 = (bf16[96,4096]{1,0:T(8,128)(2,1)S(1)}, bf16[96,4096]{1,0:T(8,128)(2,1)}, u32[]{:S(2)}, u32[]{:S(2)}) collective-permute-start(bf16[96,4096]{1,0:T(8,128)(2,1)S(1)} %copy-done.14), channel_id=1, source_target_pairs={{0,2},{1,3},{2,0},{3,1},{4,6},{5,7},{6,4},{7,5},{8,10},{9,11},{10,... | collective-permute-start | bytes 2359304 | tf_op jit(solution)/shard_map/ppermute | solution.py:38
  106.0 68.4 %collective-permute-start.16 = (bf16[96,4096]{1,0:T(8,128)(2,1)S(1)}, bf16[96,4096]{1,0:T(8,128)(2,1)}, u32[]{:S(2)}, u32[]{:S(2)}) collective-permute-start(bf16[96,4096]{1,0:T(8,128)(2,1)S(1)} %copy-done.15), channel_id=1, source_target_pairs={{0,3},{1,2},{2,1},{3,0},{4,7},{5,6},{6,5},{7,4},{8,11},{9,10},{10,... | collective-permute-start | bytes 2359304 | tf_op jit(solution)/shard_map/ppermute | solution.py:38
  137.1 38.6 %copy-start.23 = (bf16[96,4096]{1,0:T(8,128)(2,1)}, bf16[96,4096]{1,0:T(8,128)(2,1)S(1)}, u32[]{:S(2)}) copy-start(bf16[96,4096]{1,0:T(8,128)(2,1)S(1)} %collective-permute-done.14.refs_1_) | copy-start | bytes 2359300
  175.7 53.5 %all-to-all-start.2 = ((bf16[8,48,4096]{2,1,0:T(8,128)(2,1)}), bf16[8,48,4096]{2,1,0:T(8,128)(2,1)S(1)}, u32[]{:S(2)}, u32[]{:S(2)}) async-start(bf16[8,48,4096]{2,1,0:T(8,128)(2,1)} %bitcast.33), calls=%async_computation.2 | async-start | bytes 6291456 | tf_op jit(solution)/shard_map/all_to_all | solution.py:472
  196.8 32.4 %collective-permute-start.17 = (bf16[96,4096]{1,0:T(8,128)(2,1)}, bf16[96,4096]{1,0:T(8,128)(2,1)}, u32[]{:S(2)}, u32[]{:S(2)}) collective-permute-start(bf16[96,4096]{1,0:T(8,128)(2,1)} %get-tuple-element.85), channel_id=1, source_target_pairs={{0,1},{1,0},{2,3},{3,2},{4,5},{5,4},{6,7},{7,6},{8,9},{9,8},{10,11... | collective-permute-start | bytes 2359304 | tf_op jit(solution)/shard_map/ppermute | solution.py:38
  198.1 30.3 %collective-permute-start.18 = (bf16[64,4096]{1,0:T(8,128)(2,1)}, bf16[64,4096]{1,0:T(8,128)(2,1)S(1)}, u32[]{:S(2)}, u32[]{:S(2)}) collective-permute-start(bf16[64,4096]{1,0:T(8,128)(2,1)} %get-tuple-element.86), channel_id=1, source_target_pairs={{0,2},{1,3},{2,0},{3,1},{4,6},{5,7},{6,4},{7,5},{8,10},{9,11},{10,... | collective-permute-start | bytes 1572872 | tf_op jit(solution)/shard_map/ppermute | solution.py:38
  229.2 1.8 copy-start
  230.8 5.4 %copy-start.21 = (bf16[32,4096]{1,0:T(8,128)(2,1)S(1)}, bf16[32,4096]{1,0:T(8,128)(2,1)}, u32[]{:S(2)}) copy-start(bf16[32,4096]{1,0:T(8,128)(2,1)} %get-tuple-element.103) | copy-start | bytes 786436
  230.9 40.3 %all-to-all-start.3 = ((bf16[8,48,4096]{2,1,0:T(8,128)(2,1)}), bf16[8,48,4096]{2,1,0:T(8,128)(2,1)}, u32[]{:S(2)}, u32[]{:S(2)}) async-start(bf16[8,48,4096]{2,1,0:T(8,128)(2,1)} %bitcast.16), calls=%async_computation.3 | async-start | bytes 6291456 | tf_op jit(solution)/shard_map/all_to_all | solution.py:472
  236.2 22.6 %collective-permute-start.25 = (bf16[32,4096]{1,0:T(8,128)(2,1)S(1)}, bf16[32,4096]{1,0:T(8,128)(2,1)S(1)}, u32[]{:S(2)}, u32[]{:S(2)}) collective-permute-start(bf16[32,4096]{1,0:T(8,128)(2,1)S(1)} %copy-done.21), channel_id=1, source_target_pairs={{0,2},{1,3},{2,0},{3,1},{4,6},{5,7},{6,4},{7,5},{8,10},{9,11},{10,... | collective-permute-start | bytes 786440 | tf_op jit(solution)/shard_map/ppermute | solution.py:38
  236.5 34.7 %collective-permute-start.26 = (bf16[64,4096]{1,0:T(8,128)(2,1)}, bf16[64,4096]{1,0:T(8,128)(2,1)S(1)}, u32[]{:S(2)}, u32[]{:S(2)}) collective-permute-start(bf16[64,4096]{1,0:T(8,128)(2,1)} %get-tuple-element.104), channel_id=1, source_target_pairs={{0,3},{1,2},{2,1},{3,0},{4,7},{5,6},{6,5},{7,4},{8,11},{9,10},{10,... | collective-permute-start | bytes 1572872 | tf_op jit(solution)/shard_map/ppermute | solution.py:38
  258.9 13.6 %copy-start.20 = (bf16[32,4096]{1,0:T(8,128)(2,1)}, bf16[32,4096]{1,0:T(8,128)(2,1)S(1)}, u32[]{:S(2)}) copy-start(bf16[32,4096]{1,0:T(8,128)(2,1)S(1)} %collective-permute-done.25.refs_3_) | copy-start | bytes 786436
  271.2 1.3 copy-start.17
  272.5 66.8 %all-to-all-start.4 = ((bf16[8,48,4096]{2,1,0:T(8,128)(2,1)}), bf16[8,48,4096]{2,1,0:T(8,128)(2,1)S(1)}, u32[]{:S(2)}, u32[]{:S(2)}) async-start(bf16[8,48,4096]{2,1,0:T(8,128)(2,1)} %bitcast.17), calls=%async_computation.4 | async-start | bytes 6291456 | tf_op jit(solution)/shard_map/all_to_all | solution.py:472
  283.6 42.8 %copy-start.19 = (f32[32,4096]{1,0:T(8,128)S(1)}, f32[32,4096]{1,0:T(8,128)}, u32[]{:S(2)}) copy-start(f32[32,4096]{1,0:T(8,128)} %get-tuple-element.88) | copy-start | bytes 1572868
  283.6 10.6 %collective-permute-start.19 = (bf16[32,4096]{1,0:T(8,128)(2,1)}, bf16[32,4096]{1,0:T(8,128)(2,1)S(1)}, u32[]{:S(2)}, u32[]{:S(2)}) collective-permute-start(bf16[32,4096]{1,0:T(8,128)(2,1)} %get-tuple-element.89), channel_id=1, source_target_pairs={{0,1},{1,0},{2,3},{3,2},{4,5},{5,4},{6,7},{7,6},{8,9},{9,8},{10,11... | collective-permute-start | bytes 786440 | tf_op jit(solution)/shard_map/ppermute | solution.py:38
  283.6 13.7 %collective-permute-start.20 = (bf16[32,4096]{1,0:T(8,128)(2,1)}, bf16[32,4096]{1,0:T(8,128)(2,1)}, u32[]{:S(2)}, u32[]{:S(2)}) collective-permute-start(bf16[32,4096]{1,0:T(8,128)(2,1)} %get-tuple-element.90), channel_id=1, source_target_pairs={{0,2},{1,3},{2,0},{3,1},{4,6},{5,7},{6,4},{7,5},{8,10},{9,11},{10,... | collective-permute-start | bytes 786440 | tf_op jit(solution)/shard_map/ppermute | solution.py:38
  285.0 41.4 %collective-permute-start.21 = (bf16[32,4096]{1,0:T(8,128)(2,1)}, bf16[32,4096]{1,0:T(8,128)(2,1)}, u32[]{:S(2)}, u32[]{:S(2)}) collective-permute-start(bf16[32,4096]{1,0:T(8,128)(2,1)} %get-tuple-element.91), channel_id=1, source_target_pairs={{0,3},{1,2},{2,1},{3,0},{4,7},{5,6},{6,5},{7,4},{8,11},{9,10},{10,... | collective-permute-start | bytes 786440 | tf_op jit(solution)/shard_map/ppermute | solution.py:38
  290.6 37.1 %collective-permute-start.22 = (bf16[32,4096]{1,0:T(8,128)(2,1)}, bf16[32,4096]{1,0:T(8,128)(2,1)S(1)}, u32[]{:S(2)}, u32[]{:S(2)}) collective-permute-start(bf16[32,4096]{1,0:T(8,128)(2,1)} %get-tuple-element.97), channel_id=1, source_target_pairs={{0,1},{1,0},{2,3},{3,2},{4,5},{5,4},{6,7},{7,6},{8,9},{9,8},{10,11... | collective-permute-start | bytes 786440 | tf_op jit(solution)/shard_map/ppermute | solution.py:38
  291.5 38.4 %collective-permute-start.23 = (bf16[32,4096]{1,0:T(8,128)(2,1)}, bf16[32,4096]{1,0:T(8,128)(2,1)S(1)}, u32[]{:S(2)}, u32[]{:S(2)}) collective-permute-start(bf16[32,4096]{1,0:T(8,128)(2,1)} %get-tuple-element.98), channel_id=1, source_target_pairs={{0,2},{1,3},{2,0},{3,1},{4,6},{5,7},{6,4},{7,5},{8,10},{9,11},{10,... | collective-permute-start | bytes 786440 | tf_op jit(solution)/shard_map/ppermute | solution.py:38
  294.1 32.2 %copy-start.22 = (bf16[32,4096]{1,0:T(8,128)(2,1)}, bf16[32,4096]{1,0:T(8,128)(2,1)S(1)}, u32[]{:S(2)}) copy-start(bf16[32,4096]{1,0:T(8,128)(2,1)S(1)} %collective-permute-done.19) | copy-start | bytes 786436
  294.1 43.3 %collective-permute-start.24 = (bf16[32,4096]{1,0:T(8,128)(2,1)}, bf16[32,4096]{1,0:T(8,128)(2,1)S(1)}, u32[]{:S(2)}, u32[]{:S(2)}) collective-permute-start(bf16[32,4096]{1,0:T(8,128)(2,1)} %get-tuple-element.99), channel_id=1, source_target_pairs={{0,3},{1,2},{2,1},{3,0},{4,7},{5,6},{6,5},{7,4},{8,11},{9,10},{10,... | collective-permute-start | bytes 786440 | tf_op jit(solution)/shard_map/ppermute | solution.py:38
  327.6 21.3 %collective-permute-start.30 = (bf16[32,4096]{1,0:T(8,128)(2,1)}, bf16[32,4096]{1,0:T(8,128)(2,1)}, u32[]{:S(2)}, u32[]{:S(2)}) collective-permute-start(bf16[32,4096]{1,0:T(8,128)(2,1)} %get-tuple-element.112), channel_id=1, source_target_pairs={{0,3},{1,2},{2,1},{3,0},{4,7},{5,6},{6,5},{7,4},{8,11},{9,10},{10,... | collective-permute-start | bytes 786440 | tf_op jit(solution)/shard_map/ppermute | solution.py:38
  339.3 1.6 copy-start.1
  345.3 16.3 %collective-permute-start.28 = (bf16[32,4096]{1,0:T(8,128)(2,1)}, bf16[32,4096]{1,0:T(8,128)(2,1)S(1)}, u32[]{:S(2)}, u32[]{:S(2)}) collective-permute-start(bf16[32,4096]{1,0:T(8,128)(2,1)} %get-tuple-element.108), channel_id=1, source_target_pairs={{0,2},{1,3},{2,0},{3,1},{4,6},{5,7},{6,4},{7,5},{8,10},{9,11},{10,... | collective-permute-start | bytes 786440 | tf_op jit(solution)/shard_map/ppermute | solution.py:38
  345.3 22.1 %collective-permute-start.29 = (bf16[32,4096]{1,0:T(8,128)(2,1)}, bf16[32,4096]{1,0:T(8,128)(2,1)S(1)}, u32[]{:S(2)}, u32[]{:S(2)}) collective-permute-start(bf16[32,4096]{1,0:T(8,128)(2,1)} %get-tuple-element.109), channel_id=1, source_target_pairs={{0,3},{1,2},{2,1},{3,0},{4,7},{5,6},{6,5},{7,4},{8,11},{9,10},{10,... | collective-permute-start | bytes 786440 | tf_op jit(solution)/shard_map/ppermute | solution.py:38
  345.5 21.9 %collective-permute-start.27 = (bf16[32,4096]{1,0:T(8,128)(2,1)}, bf16[32,4096]{1,0:T(8,128)(2,1)S(1)}, u32[]{:S(2)}, u32[]{:S(2)}) collective-permute-start(bf16[32,4096]{1,0:T(8,128)(2,1)} %get-tuple-element.107), channel_id=1, source_target_pairs={{0,1},{1,0},{2,3},{3,2},{4,5},{5,4},{6,7},{7,6},{8,9},{9,8},{10,11... | collective-permute-start | bytes 786440 | tf_op jit(solution)/shard_map/ppermute | solution.py:38
  348.8 18.5 %copy-start.18 = (f32[32,4096]{1,0:T(8,128)S(1)}, f32[32,4096]{1,0:T(8,128)}, u32[]{:S(2)}) copy-start(f32[32,4096]{1,0:T(8,128)} %get-tuple-element.106) | copy-start | bytes 1572868
  355.8 14.3 %copy-start.3 = (f32[128,2048]{1,0:T(8,128)S(1)}, f32[128,2048]{1,0:T(8,128)}, u32[]{:S(2)}) copy-start(f32[128,2048]{1,0:T(8,128)} %get-tuple-element.119) | copy-start | bytes 3145732
  355.8 11.7 %collective-permute-start.31 = (bf16[128,2048]{1,0:T(8,128)(2,1)}, bf16[128,2048]{1,0:T(8,128)(2,1)S(1)}, u32[]{:S(2)}, u32[]{:S(2)}) collective-permute-start(bf16[128,2048]{1,0:T(8,128)(2,1)} %get-tuple-element.118), channel_id=1, source_target_pairs={{0,16},{4,20},{8,24},{12,28},{16,0},{20,4},{24,8},{28,12},{1,17},{... | collective-permute-start | bytes 1572872 | tf_op jit(solution)/shard_map/ppermute | solution.py:38
  357.0 13.1 %collective-permute-start.34 = (bf16[128,2048]{1,0:T(8,128)(2,1)}, bf16[128,2048]{1,0:T(8,128)(2,1)S(1)}, u32[]{:S(2)}, u32[]{:S(2)}) collective-permute-start(bf16[128,2048]{1,0:T(8,128)(2,1)} %get-tuple-element.120), channel_id=1, source_target_pairs={{0,8},{4,12},{8,0},{12,4},{16,24},{20,28},{24,16},{28,20},{1,9},{5... | collective-permute-start | bytes 1572872 | tf_op jit(solution)/shard_map/ppermute | solution.py:38
  368.9 5.3 %collective-permute-start.32 = (bf16[64,2048]{1,0:T(8,128)(2,1)S(1)}, bf16[64,2048]{1,0:T(8,128)(2,1)S(1)}, u32[]{:S(2)}, u32[]{:S(2)}) collective-permute-start(bf16[64,2048]{1,0:T(8,128)(2,1)S(1)} %split.57), channel_id=1, source_target_pairs={{0,8},{4,12},{8,0},{12,4},{16,24},{20,28},{24,16},{28,20},{1,9},{5... | collective-permute-start | bytes 786440 | tf_op jit(solution)/shard_map/ppermute | solution.py:38
  370.1 10.9 %copy-start.12 = (bf16[32,4096]{1,0:T(8,128)(2,1)S(1)}, bf16[32,4096]{1,0:T(8,128)(2,1)}, u32[]{:S(2)}) copy-start(bf16[32,4096]{1,0:T(8,128)(2,1)} %add_convert_fusion.1) | copy-start | bytes 786436
  370.3 8.0 %collective-permute-start.35 = (bf16[64,2048]{1,0:T(8,128)(2,1)S(1)}, bf16[64,2048]{1,0:T(8,128)(2,1)S(1)}, u32[]{:S(2)}, u32[]{:S(2)}) collective-permute-start(bf16[64,2048]{1,0:T(8,128)(2,1)S(1)} %split.56), channel_id=1, source_target_pairs={{0,16},{4,20},{8,24},{12,28},{16,0},{20,4},{24,8},{28,12},{1,17},{... | collective-permute-start | bytes 786440 | tf_op jit(solution)/shard_map/ppermute | solution.py:38
  374.3 5.7 %collective-permute-start.33 = (bf16[32,2048]{1,0:T(8,128)(2,1)S(1)}, bf16[32,2048]{1,0:T(8,128)(2,1)S(1)}, u32[]{:S(2)}, u32[]{:S(2)}) collective-permute-start(bf16[32,2048]{1,0:T(8,128)(2,1)S(1)} %split.59), channel_id=1, source_target_pairs={{0,4},{4,0},{8,12},{12,8},{16,20},{20,16},{24,28},{28,24},{1,5},{5... | collective-permute-start | bytes 393224 | tf_op jit(solution)/shard_map/ppermute | solution.py:38
  378.4 2.6 collective-permute-start.36
  (2 other events, 1.6 us)

commit v9 on v8

--- a/solution.py
+++ b/solution.py
@@ -537,15 +537,15 @@
     (tie,) = fence([tie], out3[:1])
     (out1,) = expert([arrived12], tie, *weights, block=0)
 
-    (mixing0,) = fence([mixing0], [out1] + landed3[1:])
     out1, part2, part3, tie = fence([out1] + out3[-3:-1] + [tie], [landed0] + landed3[1:])
     landed1 = to_experts(out1)
     landed3 += [swap(part2, "local", last2), swap(part3, "local", last1)]
+    (out2,) = expert([arrived12], tie, *weights, block=1)
+    (mixing0,) = fence([mixing0], [out2])
     own0, parts0 = mix(mixing0, landed0)
     parts0 = swaps([None] + parts0, "local", 1, peers)
-    (out2,) = expert([arrived12], tie, *weights, block=1)
-
-    out2, part3 = fence([out2, out3[-1]], [landed1] + landed3[-2:])
+
+    out2, part3 = fence([out2, out3[-1]], [landed1, own0] + landed3[-2:])
     landed2 = to_experts(out2)
     landed3.append(swap(part3, "local", last1))
     own1, parts1 = mix(mixing1, landed1)
@@ -553,7 +553,7 @@
     cross = mix_cross(mixing3a, mixing3b, landed3)
 
     own2, parts2 = mix(mixing2, landed2)
-    cross = fence(list(cross), parts2[:1])
+    own0, own1, *cross = fence([own0, own1] + list(cross), parts2[:1])
     parts2 = swaps([None] + parts2, "local", 1, peers)
     sums3 = halve(*cross[:2], "node", bits_a[-1]), halve(*cross[2:], "node", bits_b[-1])
     piece0, piece1 = total(own0, parts0), total(own1, parts1)

time: 385 us -> 375 us (0.974)
  starting transfers between devices: 84.1 us -> 79 us
  waiting for transfers between devices: 172 us -> 167 us
    ppermute x31, waiting for transfers between devices: 155 us -> 136 us  [swap(): return lax.ppermute(array, axis, [(i, i ^ bits) for i in range(size)])]
    all_to_all x5, waiting for transfers between devices: 0.01 us -> 14.4 us  [to_experts(): return lax.all_to_all(rows, 'node', 0, 0, tiled=True)]
    ppermute x31, starting transfers between devices: 36.5 us -> 31.7 us  [swap(): return lax.ppermute(array, axis, [(i, i ^ bits) for i in range(size)])]
  transfers between devices with their start and end apart: 42 -> 42, of which waited for: 22 -> 22; matrix products, arithmetic and copies ran while one was open for 3% -> 3% of each run, Pallas kernels for 26% -> 27%
where the time goes in v9:
time: 375 us; the launch traced here: 373 us
  waiting for transfers between devices  167 us (45%)
  Pallas kernels  104 us (28%)
  starting transfers between devices  79 us (21%)
  other arithmetic  16.6 us (4%)
  local copies, waits for them, and re-layouts  6.35 us (2%)
    ppermute x31, waiting for transfers between devices, swap(): return lax.ppermute(array, axis, [(i, i ^ bits) for i in range(size)])  136 us
    pallas_call x4, Pallas kernels, expert(): pl.pallas_call(functools.partial(expert_kernel, len(parts), first_tiles,...  63.2 us
    ppermute x31, starting transfers between devices, swap(): return lax.ppermute(array, axis, [(i, i ^ bits) for i in range(size)])  31.7 us
    all_to_all x5, starting transfers between devices, to_experts(): return lax.all_to_all(rows, 'node', 0, 0, tiled=True)  29.5 us
    ppermute x6, starting transfers between devices, chain_step(): lax.ppermute(a, axis, way)  17.8 us
    ppermute x6, waiting for transfers between devices, chain_step(): lax.ppermute(a, axis, way)  16.3 us
    all_to_all x5, waiting for transfers between devices, to_experts(): return lax.all_to_all(rows, 'node', 0, 0, tiled=True)  14.4 us
    pallas_call x3, Pallas kernels, mix(): pl.pallas_call(mix_kernel, grid=(TILES,), out_shape=[jax.ShapeDtypeStruct...  13.1 us
  transfers between devices with their start and end apart: 42, of which 22 were waited for; matrix products, arithmetic and copies ran while one was open for 3% of the time, Pallas kernels for 27%

profile of v9, /device:TPU:9, one launch (start us, length us, event | category | flops | bytes accessed | tf_op | source)
XLA Modules:
  0.0 372.8 jit_solution(13387801148790877126)
XLA Ops:
  0.0 2.9 shard_map.262
  2.9 1.3 collective-permute-start.2
  9.1 1.3 collective-permute-start.4
  10.4 1.3 collective-permute-start.5
  11.7 10.6 %collective-permute-done.2.refs_3_.refs_7_ = bf16[32,4224]{1,0:T(8,128)(2,1)S(1)} collective-permute-done((bf16[32,4224]{1,0:T(8,128)(2,1)}, bf16[32,4224]{1,0:T(8,128)(2,1)S(1)}, u32[]{:S(2)}, u32[]{:S(2)}) %collective-permute-start.2) | collective-permute-done | bytes 270368 | tf_op jit(solution)/shard_map/ppermute | solution.py:38
  22.2 4.8 %collective-permute-done.1.refs_2_.refs_6_ = bf16[32,4224]{1,0:T(8,128)(2,1)S(1)} collective-permute-done((bf16[32,4224]{1,0:T(8,128)(2,1)}, bf16[32,4224]{1,0:T(8,128)(2,1)S(1)}, u32[]{:S(2)}, u32[]{:S(2)}) %collective-permute-start.1) | collective-permute-done | bytes 270368 | tf_op jit(solution)/shard_map/ppermute | solution.py:38
  29.4 4.1 %collective-permute-start.9 = (bf16[64,4224]{1,0:T(8,128)(2,1)}, bf16[64,4224]{1,0:T(8,128)(2,1)S(1)}, u32[]{:S(2)}, u32[]{:S(2)}) collective-permute-start(bf16[64,4224]{1,0:T(8,128)(2,1)} %get-tuple-element.72.refs_0_.refs_7_), channel_id=1, source_target_pairs={{3,2},{2,1},{1,0},{7,6},{6,5},{5,4},{11,10},{10,9},{9,8},{15,14},{... | collective-permute-start | bytes 1622024 | tf_op jit(solution)/shard_map/ppermute | solution.py:54
  33.5 1.9 collective-permute-start.8
  35.4 1.3 collective-permute-start.7
  38.5 5.2 %shard_map.263 = (bf16[8,1,48,4096]{3,2,1,0:T(8,128)(2,1)}, bf16[128,384]{1,0:T(8,128)(2,1)}) custom-call(s32[2]{0:T(128)} %pad_add_fusion.ids.tie.refs_1_, bf16[32,4224]{1,0:T(8,128)(2,1)} %get-tuple-element.65.refs_0_.refs_4_, bf16[32,4224]{1,0:T(8,128)(2,1)} %copy-done.12, bf16[32,4224]{1,0:T(8,128)(2,1)} %copy-done.11, bf16[32,4224]{1,0:T(8,128)(2,1)} %copy-done.10, ...), custom_call_target="tpu_custom_call" | custom-call | flops 402653184 | bytes 4194304 | tf_op jit(solution)/shard_map/pallas_call | solution.py:182
  44.0 3.7 %collective-permute-done.8.refs_1_.refs_8_ = bf16[64,4224]{1,0:T(8,128)(2,1)S(1)} collective-permute-done((bf16[64,4224]{1,0:T(8,128)(2,1)}, bf16[64,4224]{1,0:T(8,128)(2,1)S(1)}, u32[]{:S(2)}, u32[]{:S(2)}) %collective-permute-start.8) | collective-permute-done | bytes 540704 | tf_op jit(solution)/shard_map/ppermute | solution.py:54
  49.4 6.4 %all-to-all-start = ((bf16[8,1,48,4096]{3,2,1,0:T(8,128)(2,1)}), bf16[8,1,48,4096]{3,2,1,0:T(8,128)(2,1)S(1)}, u32[]{:S(2)}, u32[]{:S(2)}) async-start(bf16[8,1,48,4096]{3,2,1,0:T(8,128)(2,1)} %get-tuple-element.73), calls=%async_computation | async-start | bytes 6291456 | tf_op jit(solution)/shard_map/all_to_all | solution.py:472
  55.8 3.4 collective-permute-start.11
  59.2 2.8 collective-permute-start.10
  62.0 9.7 %collective-permute-done.11.refs_4_.refs_11_ = bf16[64,4224]{1,0:T(8,128)(2,1)S(1)} collective-permute-done((bf16[64,4224]{1,0:T(8,128)(2,1)}, bf16[64,4224]{1,0:T(8,128)(2,1)S(1)}, u32[]{:S(2)}, u32[]{:S(2)}) %collective-permute-start.11) | collective-permute-done | bytes 540704 | tf_op jit(solution)/shard_map/ppermute | solution.py:54
  71.7 4.2 %collective-permute-start.13 = (bf16[64,4224]{1,0:T(8,128)(2,1)S(1)}, bf16[64,4224]{1,0:T(8,128)(2,1)}, u32[]{:S(2)}, u32[]{:S(2)}) collective-permute-start(bf16[64,4224]{1,0:T(8,128)(2,1)S(1)} %collective-permute-done.11.refs_4_.refs_11_), channel_id=1, source_target_pairs={{1,0},{5,4},{9,8},{13,12},{17,16},{21,20},{25,24},{29,28}} | collective-permute-start | bytes 1622024 | tf_op jit(solution)/shard_map/ppermute | solution.py:54
  75.9 1.5 collective-permute-start.12
  77.3 5.8 %shard_map.268 = (bf16[96,4096]{1,0:T(8,128)(2,1)}, bf16[96,4096]{1,0:T(8,128)(2,1)}, bf16[96,4096]{1,0:T(8,128)(2,1)}, bf16[96,4096]{1,0:T(8,128)(2,1)}, bf16[2...) custom-call(s32[2]{0:T(128)} %pad_add_fusion.ids.tie.refs_1_, bf16[128,2048]{1,0:T(8,128)(2,1)} %get-tuple-element.70.a0, ...), custom_call_target="tpu_custom_call" | custom-call | flops 805306368 | bytes 5242880 | tf_op jit(solution)/shard_map/pallas_call | solution.py:260
  83.2 2.5 collective-permute-done.13.refs_6_.refs_13_
  85.7 7.7 %shard_map.267 = (bf16[8,2,48,4096]{3,2,1,0:T(8,128)(2,1)}, bf16[128,384]{1,0:T(8,128)(2,1)}, bf16[128,384]{1,0:T(8,128)(2,1)}) custom-call(s32[2]{0:T(128)} %pad_add_fusion.ids.tie.refs_1_, bf16[64,4224]{1,0:T(8,128)(2,1)} %get-tuple-element.72.refs_0_.refs_7_, bf16[64,4224]{1,0:T(8,128)(2,1)} %copy-done.7, bf16[64,4224]{1,0:T(8,128)(2,1)} %copy-done.6, ...), custom_call_target="tpu_custom_call" | custom-call | flops 1409286144 | bytes 9961472 | tf_op jit(solution)/shard_map/pallas_call | solution.py:182
  95.1 6.6 %all-to-all-start.1 = ((bf16[8,2,48,4096]{3,2,1,0:T(8,128)(2,1)}), bf16[8,2,48,4096]{3,2,1,0:T(8,128)(2,1)}, u32[]{:S(2)}, u32[]{:S(2)}) async-start(bf16[8,2,48,4096]{3,2,1,0:T(8,128)(2,1)} %get-tuple-element.80), calls=%async_computation.1 | async-start | bytes 12582912 | tf_op jit(solution)/shard_map/all_to_all | solution.py:472
  101.8 2.3 collective-permute-start.14
  104.1 2.0 collective-permute-start.15
  106.4 15.9 %shard_map.266.refs_0_ = bf16[384,4096]{1,0:T(8,128)(2,1)} custom-call(s32[2]{0:T(128)} %pad_add_fusion.ids.tie.refs_1_, bf16[384,4096]{1,0:T(8,128)(2,1)} %bitcast.35, bf16[4096,768]{1,0:T(8,128)(2,1)} %bitcast.18, bf16[4096,768]{1,0:T(8,128)(2,1)} %bitcast.22, bf16[768,4096]{1,0:T(8,128)(2,1)} %bitcast.26), custom_call_target="tpu_custom_call" | custom-call | flops 7247757312 | bytes 25165824 | tf_op jit(solution)/shard_map/pallas_call | solution.py:404
  122.3 14.9 %collective-permute-done.14.refs_1_ = bf16[96,4096]{1,0:T(8,128)(2,1)S(1)} collective-permute-done((bf16[96,4096]{1,0:T(8,128)(2,1)S(1)}, bf16[96,4096]{1,0:T(8,128)(2,1)S(1)}, u32[]{:S(2)}, u32[]{:S(2)}) %collective-permute-start.14) | collective-permute-done | bytes 786464 | tf_op jit(solution)/shard_map/ppermute | solution.py:38
  137.3 19.4 %collective-permute-done.15.refs_2_ = bf16[96,4096]{1,0:T(8,128)(2,1)} collective-permute-done((bf16[96,4096]{1,0:T(8,128)(2,1)S(1)}, bf16[96,4096]{1,0:T(8,128)(2,1)}, u32[]{:S(2)}, u32[]{:S(2)}) %collective-permute-start.15) | collective-permute-done | bytes 786464 | tf_op jit(solution)/shard_map/ppermute | solution.py:38
  156.6 17.9 %collective-permute-done.16.refs_3_ = bf16[96,4096]{1,0:T(8,128)(2,1)} collective-permute-done((bf16[96,4096]{1,0:T(8,128)(2,1)S(1)}, bf16[96,4096]{1,0:T(8,128)(2,1)}, u32[]{:S(2)}, u32[]{:S(2)}) %collective-permute-start.16) | collective-permute-done | bytes 786464 | tf_op jit(solution)/shard_map/ppermute | solution.py:38
  174.5 1.3 convert_add_fusion.4.refs_2_
  175.8 4.9 %all-to-all-start.2 = ((bf16[8,48,4096]{2,1,0:T(8,128)(2,1)}), bf16[8,48,4096]{2,1,0:T(8,128)(2,1)S(1)}, u32[]{:S(2)}, u32[]{:S(2)}) async-start(bf16[8,48,4096]{2,1,0:T(8,128)(2,1)} %bitcast.33), calls=%async_computation.2 | async-start | bytes 6291456 | tf_op jit(solution)/shard_map/all_to_all | solution.py:472
  180.7 16.2 %shard_map.271 = (bf16[96,4096]{1,0:T(8,128)(2,1)}, bf16[96,4096]{1,0:T(8,128)(2,1)}, bf16[64,4096]{1,0:T(8,128)(2,1)}, bf16[32,4096]{1,0:T(8,128)(2,1)}, bf16[6...) custom-call(s32[2]{0:T(128)} %get-tuple-element.84.tie.refs_0_, bf16[96,4096]{1,0:T(8,128)(2,1)} %get-tuple-element.85.refs_0_, ...), custom_call_target="tpu_custom_call" | custom-call | flops 7247757312 | bytes 25165824 | tf_op jit(solution)/shard_map/pallas_call | solution.py:404
  196.9 1.3 slice_convert_fusion.7.refs_1_
  198.2 2.4 collective-permute-start.18
  200.7 15.6 %shard_map.273.refs_0_ = bf16[384,4096]{1,0:T(8,128)(2,1)} custom-call(s32[2]{0:T(128)} %shard_map.272.tie.refs_3_, bf16[8,2,48,4096]{3,2,1,0:T(8,128)(2,1)} %all-to-all-done.1.refs_0_, bf16[4096,768]{1,0:T(8,128)(2,1)} %bitcast.20, bf16[4096,768]{1,0:T(8,128)(2,1)} %bitcast.24, bf16[768,4096]{1,0:T(8,128)(2,1)} %bitcast.28), custom_call_target="tpu_custom_call" | custom-call | flops 7247757312 | bytes 25165824 | tf_op jit(solution)/shard_map/pallas_call | solution.py:404
  216.2 12.3 %collective-permute-done.18.refs_2_ = bf16[64,4096]{1,0:T(8,128)(2,1)S(1)} collective-permute-done((bf16[64,4096]{1,0:T(8,128)(2,1)}, bf16[64,4096]{1,0:T(8,128)(2,1)S(1)}, u32[]{:S(2)}, u32[]{:S(2)}) %collective-permute-start.18) | collective-permute-done | bytes 524320 | tf_op jit(solution)/shard_map/ppermute | solution.py:38
  229.4 1.6 convert_add_fusion.3.refs_4_
  231.0 5.3 %all-to-all-start.3 = ((bf16[8,48,4096]{2,1,0:T(8,128)(2,1)}), bf16[8,48,4096]{2,1,0:T(8,128)(2,1)}, u32[]{:S(2)}, u32[]{:S(2)}) async-start(bf16[8,48,4096]{2,1,0:T(8,128)(2,1)} %bitcast.17), calls=%async_computation.3 | async-start | bytes 6291456 | tf_op jit(solution)/shard_map/all_to_all | solution.py:472
  236.5 15.6 %shard_map.275.refs_0_ = bf16[384,4096]{1,0:T(8,128)(2,1)} custom-call(s32[2]{0:T(128)} %get-tuple-element.92.tie, bf16[8,2,48,4096]{3,2,1,0:T(8,128)(2,1)} %all-to-all-done.1.refs_0_, bf16[4096,768]{1,0:T(8,128)(2,1)} %bitcast.21, bf16[4096,768]{1,0:T(8,128)(2,1)} %bitcast.25, bf16[768,4096]{1,0:T(8,128)(2,1)} %bitcast.29), custom_call_target="tpu_custom_call" | custom-call | flops 7247757312 | bytes 25165824 | tf_op jit(solution)/shard_map/pallas_call | solution.py:404
  252.1 1.3 slice_convert_fusion.4.refs_1_
  253.4 4.4 %shard_map.277 = (f32[32,4096]{1,0:T(8,128)}, bf16[32,4096]{1,0:T(8,128)(2,1)}, bf16[32,4096]{1,0:T(8,128)(2,1)}, bf16[32,4096]{1,0:T(8,128)(2,1)}) custom-call(bf16[128,384]{1,0:T(8,128)(2,1)} %shard_map.276.mixing, bf16[384,4096]{1,0:T(8,128)(2,1)} %bitcast.31), custom_call_target="tpu_custom_call" | custom-call | flops 402653184 | bytes 4194304 | tf_op jit(solution)/shard_map/pallas_call | solution.py:295
  257.8 1.5 collective-permute-done.19.refs_3_
  259.2 12.3 %collective-permute-done.20.refs_4_ = bf16[64,4096]{1,0:T(8,128)(2,1)S(1)} collective-permute-done((bf16[64,4096]{1,0:T(8,128)(2,1)}, bf16[64,4096]{1,0:T(8,128)(2,1)S(1)}, u32[]{:S(2)}, u32[]{:S(2)}) %collective-permute-start.20) | collective-permute-done | bytes 524320 | tf_op jit(solution)/shard_map/ppermute | solution.py:38
  271.5 1.3 convert_add_fusion.2.refs_2_
  272.8 6.4 %all-to-all-start.4 = ((bf16[8,48,4096]{2,1,0:T(8,128)(2,1)}), bf16[8,48,4096]{2,1,0:T(8,128)(2,1)S(1)}, u32[]{:S(2)}, u32[]{:S(2)}) async-start(bf16[8,48,4096]{2,1,0:T(8,128)(2,1)} %bitcast.16), calls=%async_computation.4 | async-start | bytes 6291456 | tf_op jit(solution)/shard_map/all_to_all | solution.py:472
  281.8 4.4 %shard_map.278 = (f32[32,4096]{1,0:T(8,128)}, bf16[32,4096]{1,0:T(8,128)(2,1)}, bf16[32,4096]{1,0:T(8,128)(2,1)}, bf16[32,4096]{1,0:T(8,128)(2,1)}) custom-call(bf16[128,384]{1,0:T(8,128)(2,1)} %get-tuple-element.94.mixing, bf16[384,4096]{1,0:T(8,128)(2,1)} %bitcast.13.landed), custom_call_target="tpu_custom_call" | custom-call | flops 402653184 | bytes 4194304 | tf_op jit(solution)/shard_map/pallas_call | solution.py:295
  286.2 1.4 collective-permute-start.26
  287.6 5.2 %collective-permute-done.21.refs_5_ = bf16[32,4096]{1,0:T(8,128)(2,1)S(1)} collective-permute-done((bf16[32,4096]{1,0:T(8,128)(2,1)}, bf16[32,4096]{1,0:T(8,128)(2,1)S(1)}, u32[]{:S(2)}, u32[]{:S(2)}) %collective-permute-start.21) | collective-permute-done | bytes 262176 | tf_op jit(solution)/shard_map/ppermute | solution.py:38
  293.5 5.7 %shard_map.280 = (f32[128,2048]{1,0:T(8,128)}, bf16[128,2048]{1,0:T(8,128)(2,1)}, f32[128,2048]{1,0:T(8,128)}, bf16[128,2048]{1,0:T(8,128)(2,1)}) custom-call(bf16[256,384]{1,0:T(8,128)(2,1)} %get-tuple-element.97.mixing_a, bf16[256,384]{1,0:T(8,128)(2,1)} %get-tuple-element.98.mixing_b, bf16[96,4096]{1,0:T(8,128)(2,1)} %get-tuple-element.86.refs_0_, ...), custom_call_target="tpu_custom_call" | custom-call | flops 805306368 | bytes 5242880 | tf_op jit(solution)/shard_map/pallas_call | solution.py:337
  299.1 14.4 %all-to-all-done.4 = bf16[8,48,4096]{2,1,0:T(8,128)(2,1)S(1)} async-done(((bf16[8,48,4096]{2,1,0:T(8,128)(2,1)}), bf16[8,48,4096]{2,1,0:T(8,128)(2,1)S(1)}, u32[]{:S(2)}, u32[]{:S(2)}) %all-to-all-start.4) | async-done | bytes 3145760 | tf_op jit(solution)/shard_map/all_to_all | solution.py:472
  313.6 1.7 copy-done.1
  315.3 4.4 %shard_map.281 = (f32[32,4096]{1,0:T(8,128)}, bf16[32,4096]{1,0:T(8,128)(2,1)}, bf16[32,4096]{1,0:T(8,128)(2,1)}, bf16[32,4096]{1,0:T(8,128)(2,1)}) custom-call(bf16[128,384]{1,0:T(8,128)(2,1)} %get-tuple-element.107.mixing, bf16[384,4096]{1,0:T(8,128)(2,1)} %bitcast.32), custom_call_target="tpu_custom_call" | custom-call | flops 402653184 | bytes 4194304 | tf_op jit(solution)/shard_map/pallas_call | solution.py:295
  319.7 1.4 slice_convert_fusion.6.refs_6_
  322.5 9.2 %collective-permute-done.27 = bf16[32,4096]{1,0:T(8,128)(2,1)} collective-permute-done((bf16[32,4096]{1,0:T(8,128)(2,1)}, bf16[32,4096]{1,0:T(8,128)(2,1)}, u32[]{:S(2)}, u32[]{:S(2)}) %collective-permute-start.27) | collective-permute-done | bytes 262176 | tf_op jit(solution)/shard_map/ppermute | solution.py:38
  331.7 1.4 add_convert_fusion.1
  333.2 1.5 collective-permute-start.31
  334.7 13.8 %collective-permute-done.24 = bf16[32,4096]{1,0:T(8,128)(2,1)S(1)} collective-permute-done((bf16[32,4096]{1,0:T(8,128)(2,1)S(1)}, bf16[32,4096]{1,0:T(8,128)(2,1)S(1)}, u32[]{:S(2)}, u32[]{:S(2)}) %collective-permute-start.24) | collective-permute-done | bytes 262176 | tf_op jit(solution)/shard_map/ppermute | solution.py:38
  348.5 1.4 collective-permute-start.34
  349.9 1.3 add_convert_fusion.2
  351.2 1.4 collective-permute-done.29
  352.6 7.1 %collective-permute-done.30 = bf16[32,4096]{1,0:T(8,128)(2,1)S(1)} collective-permute-done((bf16[32,4096]{1,0:T(8,128)(2,1)S(1)}, bf16[32,4096]{1,0:T(8,128)(2,1)S(1)}, u32[]{:S(2)}, u32[]{:S(2)}) %collective-permute-start.30) | collective-permute-done | bytes 262176 | tf_op jit(solution)/shard_map/ppermute | solution.py:38
  360.0 1.4 collective-permute-start.32
  361.8 1.4 collective-permute-start.35
  363.2 4.3 %collective-permute-done.32 = bf16[64,2048]{1,0:T(8,128)(2,1)S(1)} collective-permute-done((bf16[64,2048]{1,0:T(8,128)(2,1)S(1)}, bf16[64,2048]{1,0:T(8,128)(2,1)S(1)}, u32[]{:S(2)}, u32[]{:S(2)}) %collective-permute-start.32) | collective-permute-done | bytes 262176 | tf_op jit(solution)/shard_map/ppermute | solution.py:38
  367.6 1.4 collective-permute-start.33
  369.0 1.7 collective-permute-start.36
  (123 shorter events, 22.0 us)
Async XLA Ops:
  2.9 19.3 %collective-permute-start.2 = (bf16[32,4224]{1,0:T(8,128)(2,1)}, bf16[32,4224]{1,0:T(8,128)(2,1)S(1)}, u32[]{:S(2)}, u32[]{:S(2)}) collective-permute-start(bf16[32,4224]{1,0:T(8,128)(2,1)} %get-tuple-element.65.refs_0_.refs_4_), channel_id=1, source_target_pairs={{0,3},{1,2},{2,1},{3,0},{4,7},{5,6},{6,5},{7,4},{8,11},{9,10},{10,... | collective-permute-start | bytes 811016 | tf_op jit(solution)/shard_map/ppermute | solution.py:38
  4.2 22.8 %collective-permute-start.1 = (bf16[32,4224]{1,0:T(8,128)(2,1)}, bf16[32,4224]{1,0:T(8,128)(2,1)S(1)}, u32[]{:S(2)}, u32[]{:S(2)}) collective-permute-start(bf16[32,4224]{1,0:T(8,128)(2,1)} %get-tuple-element.65.refs_0_.refs_4_), channel_id=1, source_target_pairs={{0,2},{1,3},{2,0},{3,1},{4,6},{5,7},{6,4},{7,5},{8,10},{9,11},{10,... | collective-permute-start | bytes 811016 | tf_op jit(solution)/shard_map/ppermute | solution.py:38
  5.2 21.8 %collective-permute-start = (bf16[32,4224]{1,0:T(8,128)(2,1)}, bf16[32,4224]{1,0:T(8,128)(2,1)S(1)}, u32[]{:S(2)}, u32[]{:S(2)}) collective-permute-start(bf16[32,4224]{1,0:T(8,128)(2,1)} %get-tuple-element.65.refs_0_.refs_4_), channel_id=1, source_target_pairs={{0,1},{1,0},{2,3},{3,2},{4,5},{5,4},{6,7},{7,6},{8,9},{9,8},{10,11... | collective-permute-start | bytes 811016 | tf_op jit(solution)/shard_map/ppermute | solution.py:38
  6.4 2.6 collective-permute-start.3
  9.1 18.6 %collective-permute-start.4 = (bf16[64,2048]{1,0:T(8,128)(2,1)S(1)}, bf16[64,2048]{1,0:T(8,128)(2,1)S(1)}, u32[]{:S(2)}, u32[]{:S(2)}) collective-permute-start(bf16[64,2048]{1,0:T(8,128)(2,1)S(1)} %slice.88), channel_id=1, source_target_pairs={{0,8},{4,12},{8,0},{12,4},{16,24},{20,28},{24,16},{28,20},{1,9},{5... | collective-permute-start | bytes 786440 | tf_op jit(solution)/shard_map/ppermute | solution.py:38
  10.4 18.2 %collective-permute-start.5 = (bf16[64,2176]{1,0:T(8,128)(2,1)S(1)}, bf16[64,2176]{1,0:T(8,128)(2,1)S(1)}, u32[]{:S(2)}, u32[]{:S(2)}) collective-permute-start(bf16[64,2176]{1,0:T(8,128)(2,1)S(1)} %slice.89), channel_id=1, source_target_pairs={{0,16},{4,20},{8,24},{12,28},{16,0},{20,4},{24,8},{28,12},{1,17},{... | collective-permute-start | bytes 835592 | tf_op jit(solution)/shard_map/ppermute | solution.py:38
  22.2 16.3 %copy-start.10 = (bf16[32,4224]{1,0:T(8,128)(2,1)}, bf16[32,4224]{1,0:T(8,128)(2,1)S(1)}, u32[]{:S(2)}) copy-start(bf16[32,4224]{1,0:T(8,128)(2,1)S(1)} %collective-permute-done.2.refs_3_.refs_7_) | copy-start | bytes 811012
  27.0 11.4 %copy-start.11 = (bf16[32,4224]{1,0:T(8,128)(2,1)}, bf16[32,4224]{1,0:T(8,128)(2,1)S(1)}, u32[]{:S(2)}) copy-start(bf16[32,4224]{1,0:T(8,128)(2,1)S(1)} %collective-permute-done.1.refs_2_.refs_6_) | copy-start | bytes 811012
  27.1 11.4 %copy-start.12 = (bf16[32,4224]{1,0:T(8,128)(2,1)}, bf16[32,4224]{1,0:T(8,128)(2,1)S(1)}, u32[]{:S(2)}) copy-start(bf16[32,4224]{1,0:T(8,128)(2,1)S(1)} %collective-permute-done.refs_1_.refs_5_) | copy-start | bytes 811012
  29.4 14.6 %collective-permute-start.9 = (bf16[64,4224]{1,0:T(8,128)(2,1)}, bf16[64,4224]{1,0:T(8,128)(2,1)S(1)}, u32[]{:S(2)}, u32[]{:S(2)}) collective-permute-start(bf16[64,4224]{1,0:T(8,128)(2,1)} %get-tuple-element.72.refs_0_.refs_7_), channel_id=1, source_target_pairs={{3,2},{2,1},{1,0},{7,6},{6,5},{5,4},{11,10},{10,9},{9,8},{15,14},{... | collective-permute-start | bytes 1622024 | tf_op jit(solution)/shard_map/ppermute | solution.py:54
  33.5 14.2 %collective-permute-start.8 = (bf16[64,4224]{1,0:T(8,128)(2,1)}, bf16[64,4224]{1,0:T(8,128)(2,1)S(1)}, u32[]{:S(2)}, u32[]{:S(2)}) collective-permute-start(bf16[64,4224]{1,0:T(8,128)(2,1)} %get-tuple-element.72.refs_0_.refs_7_), channel_id=1, source_target_pairs={{0,1},{1,2},{2,3},{4,5},{5,6},{6,7},{8,9},{9,10},{10,11},{12,13},{... | collective-permute-start | bytes 1622024 | tf_op jit(solution)/shard_map/ppermute | solution.py:54
  35.4 13.0 %collective-permute-start.7 = (bf16[128,2176]{1,0:T(8,128)(2,1)}, bf16[128,2176]{1,0:T(8,128)(2,1)S(1)}, u32[]{:S(2)}, u32[]{:S(2)}) collective-permute-start(bf16[128,2176]{1,0:T(8,128)(2,1)} %get-tuple-element.71.b0.t0), channel_id=1, source_target_pairs={{0,8},{4,12},{8,0},{12,4},{16,24},{20,28},{24,16},{28,20},{1,9},{5... | collective-permute-start | bytes 1671176 | tf_op jit(solution)/shard_map/ppermute | solution.py:38
  36.7 11.7 %collective-permute-start.6 = (bf16[128,2048]{1,0:T(8,128)(2,1)}, bf16[128,2048]{1,0:T(8,128)(2,1)S(1)}, u32[]{:S(2)}, u32[]{:S(2)}) collective-permute-start(bf16[128,2048]{1,0:T(8,128)(2,1)} %get-tuple-element.70.a0), channel_id=1, source_target_pairs={{0,16},{4,20},{8,24},{12,28},{16,0},{20,4},{24,8},{28,12},{1,17},{... | collective-permute-start | bytes 1572872 | tf_op jit(solution)/shard_map/ppermute | solution.py:38
  44.0 5.5 %copy-start.6 = (bf16[64,4224]{1,0:T(8,128)(2,1)}, bf16[64,4224]{1,0:T(8,128)(2,1)S(1)}, u32[]{:S(2)}) copy-start(bf16[64,4224]{1,0:T(8,128)(2,1)S(1)} %collective-permute-done.9.refs_2_.refs_9_) | copy-start | bytes 1622020
  47.7 1.7 copy-start.7
  49.4 44.0 %all-to-all-start = ((bf16[8,1,48,4096]{3,2,1,0:T(8,128)(2,1)}), bf16[8,1,48,4096]{3,2,1,0:T(8,128)(2,1)S(1)}, u32[]{:S(2)}, u32[]{:S(2)}) async-start(bf16[8,1,48,4096]{3,2,1,0:T(8,128)(2,1)} %get-tuple-element.73), calls=%async_computation | async-start | bytes 6291456 | tf_op jit(solution)/shard_map/all_to_all | solution.py:472
  55.8 15.8 %collective-permute-start.11 = (bf16[64,4224]{1,0:T(8,128)(2,1)}, bf16[64,4224]{1,0:T(8,128)(2,1)S(1)}, u32[]{:S(2)}, u32[]{:S(2)}) collective-permute-start(bf16[64,4224]{1,0:T(8,128)(2,1)} %copy-done.6), channel_id=1, source_target_pairs={{2,1},{1,0},{6,5},{5,4},{10,9},{9,8},{14,13},{13,12},{18,17},{17,1... | collective-permute-start | bytes 1622024 | tf_op jit(solution)/shard_map/ppermute | solution.py:54
  59.2 16.6 %collective-permute-start.10 = (bf16[64,4224]{1,0:T(8,128)(2,1)}, bf16[64,4224]{1,0:T(8,128)(2,1)}, u32[]{:S(2)}, u32[]{:S(2)}) collective-permute-start(bf16[64,4224]{1,0:T(8,128)(2,1)} %copy-done.7), channel_id=1, source_target_pairs={{1,2},{2,3},{5,6},{6,7},{9,10},{10,11},{13,14},{14,15},{17,18},{18... | collective-permute-start | bytes 1622024 | tf_op jit(solution)/shard_map/ppermute | solution.py:54
  71.7 14.0 %copy-start.8 = (bf16[64,4224]{1,0:T(8,128)(2,1)}, bf16[64,4224]{1,0:T(8,128)(2,1)S(1)}, u32[]{:S(2)}) copy-start(bf16[64,4224]{1,0:T(8,128)(2,1)S(1)} %collective-permute-done.11.refs_4_.refs_11_) | copy-start | bytes 1622020
  71.7 14.0 %collective-permute-start.13 = (bf16[64,4224]{1,0:T(8,128)(2,1)S(1)}, bf16[64,4224]{1,0:T(8,128)(2,1)}, u32[]{:S(2)}, u32[]{:S(2)}) collective-permute-start(bf16[64,4224]{1,0:T(8,128)(2,1)S(1)} %collective-permute-done.11.refs_4_.refs_11_), channel_id=1, source_target_pairs={{1,0},{5,4},{9,8},{13,12},{17,16},{21,20},{25,24},{29,28}} | collective-permute-start | bytes 1622024 | tf_op jit(solution)/shard_map/ppermute | solution.py:54
  75.9 9.8 %collective-permute-start.12 = (bf16[64,4224]{1,0:T(8,128)(2,1)}, bf16[64,4224]{1,0:T(8,128)(2,1)}, u32[]{:S(2)}, u32[]{:S(2)}) collective-permute-start(bf16[64,4224]{1,0:T(8,128)(2,1)} %collective-permute-done.10.refs_3_.refs_10_), channel_id=1, source_target_pairs={{2,3},{6,7},{10,11},{14,15},{18,19},{22,23},{26,27},{30,31}} | collective-permute-start | bytes 1622024 | tf_op jit(solution)/shard_map/ppermute | solution.py:54
  93.4 1.7 copy-start.5
  95.1 6.6 %copy-start.13 = (bf16[96,4096]{1,0:T(8,128)(2,1)S(1)}, bf16[96,4096]{1,0:T(8,128)(2,1)}, u32[]{:S(2)}) copy-start(bf16[96,4096]{1,0:T(8,128)(2,1)} %get-tuple-element.81) | copy-start | bytes 2359300
  95.1 8.9 %copy-start.14 = (bf16[96,4096]{1,0:T(8,128)(2,1)S(1)}, bf16[96,4096]{1,0:T(8,128)(2,1)}, u32[]{:S(2)}) copy-start(bf16[96,4096]{1,0:T(8,128)(2,1)} %get-tuple-element.82) | copy-start | bytes 2359300
  95.1 11.0 %copy-start.15 = (bf16[96,4096]{1,0:T(8,128)(2,1)S(1)}, bf16[96,4096]{1,0:T(8,128)(2,1)}, u32[]{:S(2)}) copy-start(bf16[96,4096]{1,0:T(8,128)(2,1)} %get-tuple-element.83) | copy-start | bytes 2359300
  95.1 79.4 %all-to-all-start.1 = ((bf16[8,2,48,4096]{3,2,1,0:T(8,128)(2,1)}), bf16[8,2,48,4096]{3,2,1,0:T(8,128)(2,1)}, u32[]{:S(2)}, u32[]{:S(2)}) async-start(bf16[8,2,48,4096]{3,2,1,0:T(8,128)(2,1)} %get-tuple-element.80), calls=%async_computation.1 | async-start | bytes 12582912 | tf_op jit(solution)/shard_map/all_to_all | solution.py:472
  101.8 35.5 %collective-permute-start.14 = (bf16[96,4096]{1,0:T(8,128)(2,1)S(1)}, bf16[96,4096]{1,0:T(8,128)(2,1)S(1)}, u32[]{:S(2)}, u32[]{:S(2)}) collective-permute-start(bf16[96,4096]{1,0:T(8,128)(2,1)S(1)} %copy-done.13), channel_id=1, source_target_pairs={{0,1},{1,0},{2,3},{3,2},{4,5},{5,4},{6,7},{7,6},{8,9},{9,8},{10,11... | collective-permute-start | bytes 2359304 | tf_op jit(solution)/shard_map/ppermute | solution.py:38
  104.1 52.5 %collective-permute-start.15 = (bf16[96,4096]{1,0:T(8,128)(2,1)S(1)}, bf16[96,4096]{1,0:T(8,128)(2,1)}, u32[]{:S(2)}, u32[]{:S(2)}) collective-permute-start(bf16[96,4096]{1,0:T(8,128)(2,1)S(1)} %copy-done.14), channel_id=1, source_target_pairs={{0,2},{1,3},{2,0},{3,1},{4,6},{5,7},{6,4},{7,5},{8,10},{9,11},{10,... | collective-permute-start | bytes 2359304 | tf_op jit(solution)/shard_map/ppermute | solution.py:38
  106.1 68.4 %collective-permute-start.16 = (bf16[96,4096]{1,0:T(8,128)(2,1)S(1)}, bf16[96,4096]{1,0:T(8,128)(2,1)}, u32[]{:S(2)}, u32[]{:S(2)}) collective-permute-start(bf16[96,4096]{1,0:T(8,128)(2,1)S(1)} %copy-done.15), channel_id=1, source_target_pairs={{0,3},{1,2},{2,1},{3,0},{4,7},{5,6},{6,5},{7,4},{8,11},{9,10},{10,... | collective-permute-start | bytes 2359304 | tf_op jit(solution)/shard_map/ppermute | solution.py:38
  137.3 38.6 %copy-start.22 = (bf16[96,4096]{1,0:T(8,128)(2,1)}, bf16[96,4096]{1,0:T(8,128)(2,1)S(1)}, u32[]{:S(2)}) copy-start(bf16[96,4096]{1,0:T(8,128)(2,1)S(1)} %collective-permute-done.14.refs_1_) | copy-start | bytes 2359300
  175.8 53.5 %all-to-all-start.2 = ((bf16[8,48,4096]{2,1,0:T(8,128)(2,1)}), bf16[8,48,4096]{2,1,0:T(8,128)(2,1)S(1)}, u32[]{:S(2)}, u32[]{:S(2)}) async-start(bf16[8,48,4096]{2,1,0:T(8,128)(2,1)} %bitcast.33), calls=%async_computation.2 | async-start | bytes 6291456 | tf_op jit(solution)/shard_map/all_to_all | solution.py:472
  196.9 32.5 %collective-permute-start.17 = (bf16[96,4096]{1,0:T(8,128)(2,1)}, bf16[96,4096]{1,0:T(8,128)(2,1)}, u32[]{:S(2)}, u32[]{:S(2)}) collective-permute-start(bf16[96,4096]{1,0:T(8,128)(2,1)} %get-tuple-element.90), channel_id=1, source_target_pairs={{0,1},{1,0},{2,3},{3,2},{4,5},{5,4},{6,7},{7,6},{8,9},{9,8},{10,11... | collective-permute-start | bytes 2359304 | tf_op jit(solution)/shard_map/ppermute | solution.py:38
  198.2 30.3 %collective-permute-start.18 = (bf16[64,4096]{1,0:T(8,128)(2,1)}, bf16[64,4096]{1,0:T(8,128)(2,1)S(1)}, u32[]{:S(2)}, u32[]{:S(2)}) collective-permute-start(bf16[64,4096]{1,0:T(8,128)(2,1)} %get-tuple-element.91), channel_id=1, source_target_pairs={{0,2},{1,3},{2,0},{3,1},{4,6},{5,7},{6,4},{7,5},{8,10},{9,11},{10,... | collective-permute-start | bytes 1572872 | tf_op jit(solution)/shard_map/ppermute | solution.py:38
  229.3 1.7 copy-start
  231.0 40.5 %all-to-all-start.3 = ((bf16[8,48,4096]{2,1,0:T(8,128)(2,1)}), bf16[8,48,4096]{2,1,0:T(8,128)(2,1)}, u32[]{:S(2)}, u32[]{:S(2)}) async-start(bf16[8,48,4096]{2,1,0:T(8,128)(2,1)} %bitcast.17), calls=%async_computation.3 | async-start | bytes 6291456 | tf_op jit(solution)/shard_map/all_to_all | solution.py:472
  236.3 22.9 %collective-permute-start.19 = (bf16[32,4096]{1,0:T(8,128)(2,1)}, bf16[32,4096]{1,0:T(8,128)(2,1)S(1)}, u32[]{:S(2)}, u32[]{:S(2)}) collective-permute-start(bf16[32,4096]{1,0:T(8,128)(2,1)} %get-tuple-element.99), channel_id=1, source_target_pairs={{0,2},{1,3},{2,0},{3,1},{4,6},{5,7},{6,4},{7,5},{8,10},{9,11},{10,... | collective-permute-start | bytes 786440 | tf_op jit(solution)/shard_map/ppermute | solution.py:38
  236.5 35.0 %collective-permute-start.20 = (bf16[64,4096]{1,0:T(8,128)(2,1)}, bf16[64,4096]{1,0:T(8,128)(2,1)S(1)}, u32[]{:S(2)}, u32[]{:S(2)}) collective-permute-start(bf16[64,4096]{1,0:T(8,128)(2,1)} %get-tuple-element.100), channel_id=1, source_target_pairs={{0,3},{1,2},{2,1},{3,0},{4,7},{5,6},{6,5},{7,4},{8,11},{9,10},{10,... | collective-permute-start | bytes 1572872 | tf_op jit(solution)/shard_map/ppermute | solution.py:38
  259.2 13.6 %copy-start.19 = (bf16[32,4096]{1,0:T(8,128)(2,1)}, bf16[32,4096]{1,0:T(8,128)(2,1)S(1)}, u32[]{:S(2)}) copy-start(bf16[32,4096]{1,0:T(8,128)(2,1)S(1)} %collective-permute-done.19.refs_3_) | copy-start | bytes 786436
  271.5 1.3 copy-start.17
  272.8 40.7 %all-to-all-start.4 = ((bf16[8,48,4096]{2,1,0:T(8,128)(2,1)}), bf16[8,48,4096]{2,1,0:T(8,128)(2,1)S(1)}, u32[]{:S(2)}, u32[]{:S(2)}) async-start(bf16[8,48,4096]{2,1,0:T(8,128)(2,1)} %bitcast.16), calls=%async_computation.4 | async-start | bytes 6291456 | tf_op jit(solution)/shard_map/all_to_all | solution.py:472
  279.2 13.6 %collective-permute-start.21 = (bf16[32,4096]{1,0:T(8,128)(2,1)}, bf16[32,4096]{1,0:T(8,128)(2,1)S(1)}, u32[]{:S(2)}, u32[]{:S(2)}) collective-permute-start(bf16[32,4096]{1,0:T(8,128)(2,1)} %get-tuple-element.102), channel_id=1, source_target_pairs={{0,3},{1,2},{2,1},{3,0},{4,7},{5,6},{6,5},{7,4},{8,11},{9,10},{10,... | collective-permute-start | bytes 786440 | tf_op jit(solution)/shard_map/ppermute | solution.py:38
  279.4 53.7 %collective-permute-start.22 = (bf16[32,4096]{1,0:T(8,128)(2,1)}, bf16[32,4096]{1,0:T(8,128)(2,1)S(1)}, u32[]{:S(2)}, u32[]{:S(2)}) collective-permute-start(bf16[32,4096]{1,0:T(8,128)(2,1)} %get-tuple-element.111), channel_id=1, source_target_pairs={{0,1},{1,0},{2,3},{3,2},{4,5},{5,4},{6,7},{7,6},{8,9},{9,8},{10,11... | collective-permute-start | bytes 786440 | tf_op jit(solution)/shard_map/ppermute | solution.py:38
  280.6 52.6 %collective-permute-start.23 = (bf16[32,4096]{1,0:T(8,128)(2,1)}, bf16[32,4096]{1,0:T(8,128)(2,1)}, u32[]{:S(2)}, u32[]{:S(2)}) collective-permute-start(bf16[32,4096]{1,0:T(8,128)(2,1)} %get-tuple-element.112), channel_id=1, source_target_pairs={{0,2},{1,3},{2,0},{3,1},{4,6},{5,7},{6,4},{7,5},{8,10},{9,11},{10,... | collective-permute-start | bytes 786440 | tf_op jit(solution)/shard_map/ppermute | solution.py:38
  286.2 34.8 %collective-permute-start.25 = (bf16[32,4096]{1,0:T(8,128)(2,1)}, bf16[32,4096]{1,0:T(8,128)(2,1)}, u32[]{:S(2)}, u32[]{:S(2)}) collective-permute-start(bf16[32,4096]{1,0:T(8,128)(2,1)} %get-tuple-element.115), channel_id=1, source_target_pairs={{0,1},{1,0},{2,3},{3,2},{4,5},{5,4},{6,7},{7,6},{8,9},{9,8},{10,11... | collective-permute-start | bytes 786440 | tf_op jit(solution)/shard_map/ppermute | solution.py:38
  286.2 35.1 %collective-permute-start.26 = (bf16[32,4096]{1,0:T(8,128)(2,1)}, bf16[32,4096]{1,0:T(8,128)(2,1)}, u32[]{:S(2)}, u32[]{:S(2)}) collective-permute-start(bf16[32,4096]{1,0:T(8,128)(2,1)} %get-tuple-element.116), channel_id=1, source_target_pairs={{0,2},{1,3},{2,0},{3,1},{4,6},{5,7},{6,4},{7,5},{8,10},{9,11},{10,... | collective-permute-start | bytes 786440 | tf_op jit(solution)/shard_map/ppermute | solution.py:38
  292.8 39.0 %collective-permute-start.27 = (bf16[32,4096]{1,0:T(8,128)(2,1)}, bf16[32,4096]{1,0:T(8,128)(2,1)}, u32[]{:S(2)}, u32[]{:S(2)}) collective-permute-start(bf16[32,4096]{1,0:T(8,128)(2,1)} %get-tuple-element.117), channel_id=1, source_target_pairs={{0,3},{1,2},{2,1},{3,0},{4,7},{5,6},{6,5},{7,4},{8,11},{9,10},{10,... | collective-permute-start | bytes 786440 | tf_op jit(solution)/shard_map/ppermute | solution.py:38
  313.6 1.7 copy-start.1
  319.7 1.4 copy-start.23
  319.7 1.7 copy-start.21
  319.7 12.1 %copy-start.25 = (bf16[32,4096]{1,0:T(8,128)(2,1)S(1)}, bf16[32,4096]{1,0:T(8,128)(2,1)}, u32[]{:S(2)}) copy-start(bf16[32,4096]{1,0:T(8,128)(2,1)} %get-tuple-element.119) | copy-start | bytes 786436
  319.7 13.5 %copy-start.24 = (bf16[32,4096]{1,0:T(8,128)(2,1)S(1)}, bf16[32,4096]{1,0:T(8,128)(2,1)}, u32[]{:S(2)}) copy-start(bf16[32,4096]{1,0:T(8,128)(2,1)} %get-tuple-element.120) | copy-start | bytes 786436
  321.0 38.7 %copy-start.18 = (f32[32,4096]{1,0:T(8,128)S(1)}, f32[32,4096]{1,0:T(8,128)}, u32[]{:S(2)}) copy-start(f32[32,4096]{1,0:T(8,128)} %get-tuple-element.118) | copy-start | bytes 1572868
  321.0 38.8 %copy-start.3 = (f32[128,2048]{1,0:T(8,128)S(1)}, f32[128,2048]{1,0:T(8,128)}, u32[]{:S(2)}) copy-start(f32[128,2048]{1,0:T(8,128)} %get-tuple-element.121) | copy-start | bytes 3145732
  321.1 27.4 %collective-permute-start.24 = (bf16[32,4096]{1,0:T(8,128)(2,1)S(1)}, bf16[32,4096]{1,0:T(8,128)(2,1)S(1)}, u32[]{:S(2)}, u32[]{:S(2)}) collective-permute-start(bf16[32,4096]{1,0:T(8,128)(2,1)S(1)} %copy-done.23), channel_id=1, source_target_pairs={{0,3},{1,2},{2,1},{3,0},{4,7},{5,6},{6,5},{7,4},{8,11},{9,10},{10,... | collective-permute-start | bytes 786440 | tf_op jit(solution)/shard_map/ppermute | solution.py:38
  321.3 38.4 %collective-permute-start.28 = (bf16[32,4096]{1,0:T(8,128)(2,1)S(1)}, bf16[32,4096]{1,0:T(8,128)(2,1)S(1)}, u32[]{:S(2)}, u32[]{:S(2)}) collective-permute-start(bf16[32,4096]{1,0:T(8,128)(2,1)S(1)} %copy-done.21), channel_id=1, source_target_pairs={{0,1},{1,0},{2,3},{3,2},{4,5},{5,4},{6,7},{7,6},{8,9},{9,8},{10,11... | collective-permute-start | bytes 786440 | tf_op jit(solution)/shard_map/ppermute | solution.py:38
  331.7 20.9 %collective-permute-start.29 = (bf16[32,4096]{1,0:T(8,128)(2,1)S(1)}, bf16[32,4096]{1,0:T(8,128)(2,1)S(1)}, u32[]{:S(2)}, u32[]{:S(2)}) collective-permute-start(bf16[32,4096]{1,0:T(8,128)(2,1)S(1)} %copy-done.25), channel_id=1, source_target_pairs={{0,2},{1,3},{2,0},{3,1},{4,6},{5,7},{6,4},{7,5},{8,10},{9,11},{10,... | collective-permute-start | bytes 786440 | tf_op jit(solution)/shard_map/ppermute | solution.py:38
  333.1 26.6 %collective-permute-start.30 = (bf16[32,4096]{1,0:T(8,128)(2,1)S(1)}, bf16[32,4096]{1,0:T(8,128)(2,1)S(1)}, u32[]{:S(2)}, u32[]{:S(2)}) collective-permute-start(bf16[32,4096]{1,0:T(8,128)(2,1)S(1)} %copy-done.24), channel_id=1, source_target_pairs={{0,3},{1,2},{2,1},{3,0},{4,7},{5,6},{6,5},{7,4},{8,11},{9,10},{10,... | collective-permute-start | bytes 786440 | tf_op jit(solution)/shard_map/ppermute | solution.py:38
  333.2 26.6 %collective-permute-start.31 = (bf16[128,2048]{1,0:T(8,128)(2,1)}, bf16[128,2048]{1,0:T(8,128)(2,1)S(1)}, u32[]{:S(2)}, u32[]{:S(2)}) collective-permute-start(bf16[128,2048]{1,0:T(8,128)(2,1)} %get-tuple-element.122), channel_id=1, source_target_pairs={{0,16},{4,20},{8,24},{12,28},{16,0},{20,4},{24,8},{28,12},{1,17},{... | collective-permute-start | bytes 1572872 | tf_op jit(solution)/shard_map/ppermute | solution.py:38
  348.5 13.2 %collective-permute-start.34 = (bf16[128,2048]{1,0:T(8,128)(2,1)}, bf16[128,2048]{1,0:T(8,128)(2,1)S(1)}, u32[]{:S(2)}, u32[]{:S(2)}) collective-permute-start(bf16[128,2048]{1,0:T(8,128)(2,1)} %get-tuple-element.124), channel_id=1, source_target_pairs={{0,8},{4,12},{8,0},{12,4},{16,24},{20,28},{24,16},{28,20},{1,9},{5... | collective-permute-start | bytes 1572872 | tf_op jit(solution)/shard_map/ppermute | solution.py:38
  349.9 11.8 %copy-start.4 = (f32[128,2048]{1,0:T(8,128)S(1)}, f32[128,2048]{1,0:T(8,128)}, u32[]{:S(2)}) copy-start(f32[128,2048]{1,0:T(8,128)} %get-tuple-element.123) | copy-start | bytes 3145732
  360.0 7.5 %collective-permute-start.32 = (bf16[64,2048]{1,0:T(8,128)(2,1)S(1)}, bf16[64,2048]{1,0:T(8,128)(2,1)S(1)}, u32[]{:S(2)}, u32[]{:S(2)}) collective-permute-start(bf16[64,2048]{1,0:T(8,128)(2,1)S(1)} %split.57), channel_id=1, source_target_pairs={{0,8},{4,12},{8,0},{12,4},{16,24},{20,28},{24,16},{28,20},{1,9},{5... | collective-permute-start | bytes 786440 | tf_op jit(solution)/shard_map/ppermute | solution.py:38
  361.8 7.1 %collective-permute-start.35 = (bf16[64,2048]{1,0:T(8,128)(2,1)S(1)}, bf16[64,2048]{1,0:T(8,128)(2,1)S(1)}, u32[]{:S(2)}, u32[]{:S(2)}) collective-permute-start(bf16[64,2048]{1,0:T(8,128)(2,1)S(1)} %split.56), channel_id=1, source_target_pairs={{0,16},{4,20},{8,24},{12,28},{16,0},{20,4},{24,8},{28,12},{1,17},{... | collective-permute-start | bytes 786440 | tf_op jit(solution)/shard_map/ppermute | solution.py:38
  367.6 3.2 collective-permute-start.33
  369.0 2.7 collective-permute-start.36
  (4 other events, 3.3 us)

commit v10 on v9

--- a/solution.py
+++ b/solution.py
@@ -530,7 +530,7 @@
     out0, tie = fence([out0, ids], [arrived12] + arrived3)
     landed0 = to_experts(out0)
     size = slots // peers
-    sizes = [size] * (peers - 2) + [size * 2 // 3, size // 3] * 2
+    sizes = [size] * (peers - 2) + [size // 2] * 4
     last2, last1 = peers - 2, peers - 1
     out3 = list(expert([own3] + arrived3, tie, *weights, sizes=sizes))
     landed3 = out3[:1] + swaps(out3, "local", 1, last1)
@@ -553,9 +553,10 @@
     cross = mix_cross(mixing3a, mixing3b, landed3)
 
     own2, parts2 = mix(mixing2, landed2)
-    own0, own1, *cross = fence([own0, own1] + list(cross), parts2[:1])
+    own1, *cross = fence([own1] + list(cross), parts2[:1])
     parts2 = swaps([None] + parts2, "local", 1, peers)
     sums3 = halve(*cross[:2], "node", bits_a[-1]), halve(*cross[2:], "node", bits_b[-1])
+    (own2,) = fence([own2], [sums3[0]])
     piece0, piece1 = total(own0, parts0), total(own1, parts1)
     piece3 = [sum_halving(s, "node", bits[:-1]) for s, bits in zip(sums3, (bits_a, bits_b))]
     piece3 = jnp.concatenate(piece3, axis=1)

time: 375 us -> 377 us (level)
  starting transfers between devices: 79 us -> 86.5 us
  waiting for transfers between devices: 167 us -> 160 us
    all_to_all x5, waiting for transfers between devices: 14.4 us -> 0.01 us  [to_experts(): return lax.all_to_all(rows, 'node', 0, 0, tiled=True)]
    ppermute x31, waiting for transfers between devices: 136 us -> 144 us  [swap(): return lax.ppermute(array, axis, [(i, i ^ bits) for i in range(size)])]
    ppermute x31, starting transfers between devices: 31.7 us -> 39.3 us  [swap(): return lax.ppermute(array, axis, [(i, i ^ bits) for i in range(size)])]
  transfers between devices with their start and end apart: 42 -> 42, of which waited for: 22 -> 21; matrix products, arithmetic and copies ran while one was open for 3% -> 4% of each run, Pallas kernels for 27% -> 27%
where the time goes in v10:
time: 377 us; the launch traced here: 375 us
  waiting for transfers between devices  160 us (42%)
  Pallas kernels  104 us (28%)
  starting transfers between devices  86.5 us (23%)
  other arithmetic  19.1 us (5%)
  local copies, waits for them, and re-layouts  5.39 us (1%)
    ppermute x31, waiting for transfers between devices, swap(): return lax.ppermute(array, axis, [(i, i ^ bits) for i in range(size)])  144 us
    pallas_call x4, Pallas kernels, expert(): pl.pallas_call(functools.partial(expert_kernel, len(parts), first_tiles,...  63.2 us
    ppermute x31, starting transfers between devices, swap(): return lax.ppermute(array, axis, [(i, i ^ bits) for i in range(size)])  39.3 us
    all_to_all x5, starting transfers between devices, to_experts(): return lax.all_to_all(rows, 'node', 0, 0, tiled=True)  29.5 us
    ppermute x6, starting transfers between devices, chain_step(): lax.ppermute(a, axis, way)  17.8 us
    ppermute x6, waiting for transfers between devices, chain_step(): lax.ppermute(a, axis, way)  16.2 us
    pallas_call x3, Pallas kernels, mix(): pl.pallas_call(mix_kernel, grid=(TILES,), out_shape=[jax.ShapeDtypeStruct...  13.1 us
    pallas_call x2, Pallas kernels, pick(): pl.pallas_call(functools.partial(pick_kernel, len(parts), blocks, peers,...  12.9 us
  transfers between devices with their start and end apart: 42, of which 21 were waited for; matrix products, arithmetic and copies ran while one was open for 4% of the time, Pallas kernels for 27%

profile of v10, /device:TPU:9, one launch (start us, length us, event | category | flops | bytes accessed | tf_op | source)
XLA Modules:
  0.0 375.3 jit_solution(5415369188802805556)
XLA Ops:
  0.0 2.9 shard_map.262
  2.9 1.3 collective-permute-start.2
  9.1 1.3 collective-permute-start.4
  10.4 1.3 collective-permute-start.5
  11.7 10.6 %collective-permute-done.2.refs_3_.refs_7_ = bf16[32,4224]{1,0:T(8,128)(2,1)S(1)} collective-permute-done((bf16[32,4224]{1,0:T(8,128)(2,1)}, bf16[32,4224]{1,0:T(8,128)(2,1)S(1)}, u32[]{:S(2)}, u32[]{:S(2)}) %collective-permute-start.2) | collective-permute-done | bytes 270368 | tf_op jit(solution)/shard_map/ppermute | solution.py:38
  22.3 4.8 %collective-permute-done.1.refs_2_.refs_6_ = bf16[32,4224]{1,0:T(8,128)(2,1)S(1)} collective-permute-done((bf16[32,4224]{1,0:T(8,128)(2,1)}, bf16[32,4224]{1,0:T(8,128)(2,1)S(1)}, u32[]{:S(2)}, u32[]{:S(2)}) %collective-permute-start.1) | collective-permute-done | bytes 270368 | tf_op jit(solution)/shard_map/ppermute | solution.py:38
  29.4 4.1 %collective-permute-start.9 = (bf16[64,4224]{1,0:T(8,128)(2,1)}, bf16[64,4224]{1,0:T(8,128)(2,1)S(1)}, u32[]{:S(2)}, u32[]{:S(2)}) collective-permute-start(bf16[64,4224]{1,0:T(8,128)(2,1)} %get-tuple-element.71.refs_0_.refs_7_), channel_id=1, source_target_pairs={{3,2},{2,1},{1,0},{7,6},{6,5},{5,4},{11,10},{10,9},{9,8},{15,14},{... | collective-permute-start | bytes 1622024 | tf_op jit(solution)/shard_map/ppermute | solution.py:54
  33.5 1.9 collective-permute-start.8
  35.4 1.3 collective-permute-start.7
  38.6 5.2 %shard_map.263 = (bf16[8,1,48,4096]{3,2,1,0:T(8,128)(2,1)}, bf16[128,384]{1,0:T(8,128)(2,1)}) custom-call(s32[2]{0:T(128)} %pad_add_fusion.ids.tie.refs_1_, bf16[32,4224]{1,0:T(8,128)(2,1)} %get-tuple-element.64.refs_0_.refs_4_, bf16[32,4224]{1,0:T(8,128)(2,1)} %copy-done.11, bf16[32,4224]{1,0:T(8,128)(2,1)} %copy-done.10, bf16[32,4224]{1,0:T(8,128)(2,1)} %copy-done.9, ...), custom_call_target="tpu_custom_call" | custom-call | flops 402653184 | bytes 4194304 | tf_op jit(solution)/shard_map/pallas_call | solution.py:182
  44.0 3.7 collective-permute-done.8.refs_1_.refs_8_
  49.4 6.4 %all-to-all-start = ((bf16[8,1,48,4096]{3,2,1,0:T(8,128)(2,1)}), bf16[8,1,48,4096]{3,2,1,0:T(8,128)(2,1)S(1)}, u32[]{:S(2)}, u32[]{:S(2)}) async-start(bf16[8,1,48,4096]{3,2,1,0:T(8,128)(2,1)} %get-tuple-element.72), calls=%async_computation | async-start | bytes 6291456 | tf_op jit(solution)/shard_map/all_to_all | solution.py:472
  55.8 3.4 collective-permute-start.11
  59.2 2.7 collective-permute-start.10
  61.9 9.7 %collective-permute-done.11.refs_4_.refs_11_ = bf16[64,4224]{1,0:T(8,128)(2,1)S(1)} collective-permute-done((bf16[64,4224]{1,0:T(8,128)(2,1)}, bf16[64,4224]{1,0:T(8,128)(2,1)S(1)}, u32[]{:S(2)}, u32[]{:S(2)}) %collective-permute-start.11) | collective-permute-done | bytes 540704 | tf_op jit(solution)/shard_map/ppermute | solution.py:54
  71.6 4.2 %collective-permute-start.13 = (bf16[64,4224]{1,0:T(8,128)(2,1)S(1)}, bf16[64,4224]{1,0:T(8,128)(2,1)}, u32[]{:S(2)}, u32[]{:S(2)}) collective-permute-start(bf16[64,4224]{1,0:T(8,128)(2,1)S(1)} %collective-permute-done.11.refs_4_.refs_11_), channel_id=1, source_target_pairs={{1,0},{5,4},{9,8},{13,12},{17,16},{21,20},{25,24},{29,28}} | collective-permute-start | bytes 1622024 | tf_op jit(solution)/shard_map/ppermute | solution.py:54
  75.8 1.5 collective-permute-start.12
  77.3 5.9 %shard_map.268 = (bf16[96,4096]{1,0:T(8,128)(2,1)}, bf16[96,4096]{1,0:T(8,128)(2,1)}, bf16[96,4096]{1,0:T(8,128)(2,1)}, bf16[96,4096]{1,0:T(8,128)(2,1)}, bf16[2...) custom-call(s32[2]{0:T(128)} %pad_add_fusion.ids.tie.refs_1_, bf16[128,2048]{1,0:T(8,128)(2,1)} %get-tuple-element.69.a0, ...), custom_call_target="tpu_custom_call" | custom-call | flops 805306368 | bytes 5242880 | tf_op jit(solution)/shard_map/pallas_call | solution.py:260
  83.1 2.5 collective-permute-done.13.refs_6_.refs_13_
  85.6 7.7 %shard_map.267 = (bf16[8,2,48,4096]{3,2,1,0:T(8,128)(2,1)}, bf16[128,384]{1,0:T(8,128)(2,1)}, bf16[128,384]{1,0:T(8,128)(2,1)}) custom-call(s32[2]{0:T(128)} %pad_add_fusion.ids.tie.refs_1_, bf16[64,4224]{1,0:T(8,128)(2,1)} %get-tuple-element.71.refs_0_.refs_7_, bf16[64,4224]{1,0:T(8,128)(2,1)} %copy-done.6, bf16[64,4224]{1,0:T(8,128)(2,1)} %copy-done.5, ...), custom_call_target="tpu_custom_call" | custom-call | flops 1409286144 | bytes 9961472 | tf_op jit(solution)/shard_map/pallas_call | solution.py:182
  95.0 6.7 %all-to-all-start.1 = ((bf16[8,2,48,4096]{3,2,1,0:T(8,128)(2,1)}), bf16[8,2,48,4096]{3,2,1,0:T(8,128)(2,1)}, u32[]{:S(2)}, u32[]{:S(2)}) async-start(bf16[8,2,48,4096]{3,2,1,0:T(8,128)(2,1)} %get-tuple-element.79), calls=%async_computation.1 | async-start | bytes 12582912 | tf_op jit(solution)/shard_map/all_to_all | solution.py:472
  101.6 2.3 collective-permute-start.14
  104.0 2.0 collective-permute-start.15
  106.3 15.9 %shard_map.266.refs_0_ = bf16[384,4096]{1,0:T(8,128)(2,1)} custom-call(s32[2]{0:T(128)} %pad_add_fusion.ids.tie.refs_1_, bf16[384,4096]{1,0:T(8,128)(2,1)} %bitcast.36, bf16[4096,768]{1,0:T(8,128)(2,1)} %bitcast.18, bf16[4096,768]{1,0:T(8,128)(2,1)} %bitcast.22, bf16[768,4096]{1,0:T(8,128)(2,1)} %bitcast.26), custom_call_target="tpu_custom_call" | custom-call | flops 7247757312 | bytes 25165824 | tf_op jit(solution)/shard_map/pallas_call | solution.py:404
  122.2 14.9 %collective-permute-done.14.refs_1_ = bf16[96,4096]{1,0:T(8,128)(2,1)S(1)} collective-permute-done((bf16[96,4096]{1,0:T(8,128)(2,1)S(1)}, bf16[96,4096]{1,0:T(8,128)(2,1)S(1)}, u32[]{:S(2)}, u32[]{:S(2)}) %collective-permute-start.14) | collective-permute-done | bytes 786464 | tf_op jit(solution)/shard_map/ppermute | solution.py:38
  137.1 19.4 %collective-permute-done.15.refs_2_ = bf16[96,4096]{1,0:T(8,128)(2,1)} collective-permute-done((bf16[96,4096]{1,0:T(8,128)(2,1)S(1)}, bf16[96,4096]{1,0:T(8,128)(2,1)}, u32[]{:S(2)}, u32[]{:S(2)}) %collective-permute-start.15) | collective-permute-done | bytes 786464 | tf_op jit(solution)/shard_map/ppermute | solution.py:38
  156.5 17.9 %collective-permute-done.16.refs_3_ = bf16[96,4096]{1,0:T(8,128)(2,1)} collective-permute-done((bf16[96,4096]{1,0:T(8,128)(2,1)S(1)}, bf16[96,4096]{1,0:T(8,128)(2,1)}, u32[]{:S(2)}, u32[]{:S(2)}) %collective-permute-start.16) | collective-permute-done | bytes 786464 | tf_op jit(solution)/shard_map/ppermute | solution.py:38
  174.4 1.3 convert_add_fusion.4.refs_2_
  175.7 4.9 %all-to-all-start.2 = ((bf16[8,48,4096]{2,1,0:T(8,128)(2,1)}), bf16[8,48,4096]{2,1,0:T(8,128)(2,1)S(1)}, u32[]{:S(2)}, u32[]{:S(2)}) async-start(bf16[8,48,4096]{2,1,0:T(8,128)(2,1)} %bitcast.34), calls=%async_computation.2 | async-start | bytes 6291456 | tf_op jit(solution)/shard_map/all_to_all | solution.py:472
  180.6 16.1 %shard_map.271 = (bf16[96,4096]{1,0:T(8,128)(2,1)}, bf16[96,4096]{1,0:T(8,128)(2,1)}, bf16[48,4096]{1,0:T(8,128)(2,1)}, bf16[48,4096]{1,0:T(8,128)(2,1)}, bf16[4...) custom-call(s32[2]{0:T(128)} %get-tuple-element.83.tie.refs_0_, bf16[96,4096]{1,0:T(8,128)(2,1)} %get-tuple-element.84.refs_0_, ...), custom_call_target="tpu_custom_call" | custom-call | flops 7247757312 | bytes 25165824 | tf_op jit(solution)/shard_map/pallas_call | solution.py:404
  196.8 1.3 slice_convert_fusion.7.refs_1_
  198.1 2.4 collective-permute-start.18
  200.5 15.6 %shard_map.273.refs_0_ = bf16[384,4096]{1,0:T(8,128)(2,1)} custom-call(s32[2]{0:T(128)} %shard_map.272.tie.refs_3_, bf16[8,2,48,4096]{3,2,1,0:T(8,128)(2,1)} %all-to-all-done.1.refs_0_, bf16[4096,768]{1,0:T(8,128)(2,1)} %bitcast.20, bf16[4096,768]{1,0:T(8,128)(2,1)} %bitcast.24, bf16[768,4096]{1,0:T(8,128)(2,1)} %bitcast.28), custom_call_target="tpu_custom_call" | custom-call | flops 7247757312 | bytes 25165824 | tf_op jit(solution)/shard_map/pallas_call | solution.py:404
  216.1 9.5 %collective-permute-done.18.refs_2_ = bf16[48,4096]{1,0:T(8,128)(2,1)S(1)} collective-permute-done((bf16[48,4096]{1,0:T(8,128)(2,1)}, bf16[48,4096]{1,0:T(8,128)(2,1)S(1)}, u32[]{:S(2)}, u32[]{:S(2)}) %collective-permute-start.18) | collective-permute-done | bytes 393248 | tf_op jit(solution)/shard_map/ppermute | solution.py:38
  225.6 1.7 convert_add_fusion.3.refs_4_
  227.4 4.6 %all-to-all-start.3 = ((bf16[8,48,4096]{2,1,0:T(8,128)(2,1)}), bf16[8,48,4096]{2,1,0:T(8,128)(2,1)S(1)}, u32[]{:S(2)}, u32[]{:S(2)}) async-start(bf16[8,48,4096]{2,1,0:T(8,128)(2,1)} %bitcast.17), calls=%async_computation.3 | async-start | bytes 6291456 | tf_op jit(solution)/shard_map/all_to_all | solution.py:472
  233.0 15.6 %shard_map.275.refs_0_ = bf16[384,4096]{1,0:T(8,128)(2,1)} custom-call(s32[2]{0:T(128)} %get-tuple-element.91.tie, bf16[8,2,48,4096]{3,2,1,0:T(8,128)(2,1)} %all-to-all-done.1.refs_0_, bf16[4096,768]{1,0:T(8,128)(2,1)} %bitcast.21, bf16[4096,768]{1,0:T(8,128)(2,1)} %bitcast.25, bf16[768,4096]{1,0:T(8,128)(2,1)} %bitcast.29), custom_call_target="tpu_custom_call" | custom-call | flops 7247757312 | bytes 25165824 | tf_op jit(solution)/shard_map/pallas_call | solution.py:404
  248.6 1.3 slice_convert_fusion.4.refs_1_
  249.9 4.3 %shard_map.277 = (f32[32,4096]{1,0:T(8,128)}, bf16[32,4096]{1,0:T(8,128)(2,1)}, bf16[32,4096]{1,0:T(8,128)(2,1)}, bf16[32,4096]{1,0:T(8,128)(2,1)}) custom-call(bf16[128,384]{1,0:T(8,128)(2,1)} %shard_map.276.mixing, bf16[384,4096]{1,0:T(8,128)(2,1)} %bitcast.33), custom_call_target="tpu_custom_call" | custom-call | flops 402653184 | bytes 4194304 | tf_op jit(solution)/shard_map/pallas_call | solution.py:295
  254.2 4.7 %collective-permute-done.22.refs_3_ = bf16[48,4096]{1,0:T(8,128)(2,1)S(1)} collective-permute-done((bf16[48,4096]{1,0:T(8,128)(2,1)}, bf16[48,4096]{1,0:T(8,128)(2,1)S(1)}, u32[]{:S(2)}, u32[]{:S(2)}) %collective-permute-start.22) | collective-permute-done | bytes 393248 | tf_op jit(solution)/shard_map/ppermute | solution.py:38
  258.9 8.4 %collective-permute-done.23.refs_4_ = bf16[48,4096]{1,0:T(8,128)(2,1)} collective-permute-done((bf16[48,4096]{1,0:T(8,128)(2,1)}, bf16[48,4096]{1,0:T(8,128)(2,1)}, u32[]{:S(2)}, u32[]{:S(2)}) %collective-permute-start.23) | collective-permute-done | bytes 393248 | tf_op jit(solution)/shard_map/ppermute | solution.py:38
  267.3 1.6 convert_add_fusion.2.refs_2_
  269.0 7.0 %all-to-all-start.4 = ((bf16[8,48,4096]{2,1,0:T(8,128)(2,1)}), bf16[8,48,4096]{2,1,0:T(8,128)(2,1)}, u32[]{:S(2)}, u32[]{:S(2)}) async-start(bf16[8,48,4096]{2,1,0:T(8,128)(2,1)} %bitcast.16), calls=%async_computation.4 | async-start | bytes 6291456 | tf_op jit(solution)/shard_map/all_to_all | solution.py:472
  276.0 1.4 collective-permute-start.20
  278.8 7.7 %collective-permute-done.19 = bf16[32,4096]{1,0:T(8,128)(2,1)S(1)} collective-permute-done((bf16[32,4096]{1,0:T(8,128)(2,1)}, bf16[32,4096]{1,0:T(8,128)(2,1)S(1)}, u32[]{:S(2)}, u32[]{:S(2)}) %collective-permute-start.19) | collective-permute-done | bytes 262176 | tf_op jit(solution)/shard_map/ppermute | solution.py:38
  286.5 3.0 collective-permute-done.20
  289.5 20.7 %collective-permute-done.21 = bf16[32,4096]{1,0:T(8,128)(2,1)S(1)} collective-permute-done((bf16[32,4096]{1,0:T(8,128)(2,1)}, bf16[32,4096]{1,0:T(8,128)(2,1)S(1)}, u32[]{:S(2)}, u32[]{:S(2)}) %collective-permute-start.21) | collective-permute-done | bytes 262176 | tf_op jit(solution)/shard_map/ppermute | solution.py:38
  311.4 4.4 %shard_map.278 = (f32[32,4096]{1,0:T(8,128)}, bf16[32,4096]{1,0:T(8,128)(2,1)}, bf16[32,4096]{1,0:T(8,128)(2,1)}, bf16[32,4096]{1,0:T(8,128)(2,1)}) custom-call(bf16[128,384]{1,0:T(8,128)(2,1)} %get-tuple-element.96.mixing, bf16[384,4096]{1,0:T(8,128)(2,1)} %bitcast.31), custom_call_target="tpu_custom_call" | custom-call | flops 402653184 | bytes 4194304 | tf_op jit(solution)/shard_map/pallas_call | solution.py:295
  315.7 1.4 collective-permute-start.26
  317.1 1.3 collective-permute-start.27
  319.3 5.6 %shard_map.280 = (f32[128,2048]{1,0:T(8,128)}, bf16[128,2048]{1,0:T(8,128)(2,1)}, f32[128,2048]{1,0:T(8,128)}, bf16[128,2048]{1,0:T(8,128)(2,1)}) custom-call(bf16[256,384]{1,0:T(8,128)(2,1)} %get-tuple-element.99.mixing_a, bf16[256,384]{1,0:T(8,128)(2,1)} %get-tuple-element.100.mixing_b, bf16[96,4096]{1,0:T(8,128)(2,1)} %get-tuple-element.85.refs_0_, ...), custom_call_target="tpu_custom_call" | custom-call | flops 805306368 | bytes 5242880 | tf_op jit(solution)/shard_map/pallas_call | solution.py:337
  325.0 4.4 %shard_map.281 = (f32[32,4096]{1,0:T(8,128)}, bf16[32,4096]{1,0:T(8,128)(2,1)}, bf16[32,4096]{1,0:T(8,128)(2,1)}, bf16[32,4096]{1,0:T(8,128)(2,1)}) custom-call(bf16[128,384]{1,0:T(8,128)(2,1)} %get-tuple-element.109.mixing, bf16[384,4096]{1,0:T(8,128)(2,1)} %bitcast.15.landed), custom_call_target="tpu_custom_call" | custom-call | flops 402653184 | bytes 4194304 | tf_op jit(solution)/shard_map/pallas_call | solution.py:295
  330.7 1.3 slice_convert_fusion.6.refs_5_
  332.0 1.3 collective-permute-start.31
  333.3 1.3 collective-permute-start.28
  334.6 12.4 %collective-permute-done.27 = bf16[32,4096]{1,0:T(8,128)(2,1)S(1)} collective-permute-done((bf16[32,4096]{1,0:T(8,128)(2,1)}, bf16[32,4096]{1,0:T(8,128)(2,1)S(1)}, u32[]{:S(2)}, u32[]{:S(2)}) %collective-permute-start.27) | collective-permute-done | bytes 262176 | tf_op jit(solution)/shard_map/ppermute | solution.py:38
  346.9 1.3 collective-permute-start.34
  349.4 1.3 convert_add_fusion.1
  351.6 3.9 %collective-permute-done.34 = bf16[128,2048]{1,0:T(8,128)(2,1)S(1)} collective-permute-done((bf16[128,2048]{1,0:T(8,128)(2,1)}, bf16[128,2048]{1,0:T(8,128)(2,1)S(1)}, u32[]{:S(2)}, u32[]{:S(2)}) %collective-permute-start.34) | collective-permute-done | bytes 524320 | tf_op jit(solution)/shard_map/ppermute | solution.py:38
  356.3 1.3 collective-permute-start.35
  357.7 4.9 %collective-permute-done.31 = bf16[32,4096]{1,0:T(8,128)(2,1)} collective-permute-done((bf16[32,4096]{1,0:T(8,128)(2,1)}, bf16[32,4096]{1,0:T(8,128)(2,1)}, u32[]{:S(2)}, u32[]{:S(2)}) %collective-permute-start.31) | collective-permute-done | bytes 262176 | tf_op jit(solution)/shard_map/ppermute | solution.py:38
  362.6 1.4 add_convert_fusion
  364.1 5.5 %collective-permute-start.33 = (bf16[32,2048]{1,0:T(8,128)(2,1)S(1)}, bf16[32,2048]{1,0:T(8,128)(2,1)S(1)}, u32[]{:S(2)}, u32[]{:S(2)}) collective-permute-start(bf16[32,2048]{1,0:T(8,128)(2,1)S(1)} %split.59), channel_id=1, source_target_pairs={{0,4},{4,0},{8,12},{12,8},{16,20},{20,16},{24,28},{28,24},{1,5},{5... | collective-permute-start | bytes 393224 | tf_op jit(solution)/shard_map/ppermute | solution.py:38
  369.7 3.6 collective-permute-start.36
  (111 shorter events, 24.2 us)
Async XLA Ops:
  2.9 19.3 %collective-permute-start.2 = (bf16[32,4224]{1,0:T(8,128)(2,1)}, bf16[32,4224]{1,0:T(8,128)(2,1)S(1)}, u32[]{:S(2)}, u32[]{:S(2)}) collective-permute-start(bf16[32,4224]{1,0:T(8,128)(2,1)} %get-tuple-element.64.refs_0_.refs_4_), channel_id=1, source_target_pairs={{0,3},{1,2},{2,1},{3,0},{4,7},{5,6},{6,5},{7,4},{8,11},{9,10},{10,... | collective-permute-start | bytes 811016 | tf_op jit(solution)/shard_map/ppermute | solution.py:38
  4.2 22.8 %collective-permute-start.1 = (bf16[32,4224]{1,0:T(8,128)(2,1)}, bf16[32,4224]{1,0:T(8,128)(2,1)S(1)}, u32[]{:S(2)}, u32[]{:S(2)}) collective-permute-start(bf16[32,4224]{1,0:T(8,128)(2,1)} %get-tuple-element.64.refs_0_.refs_4_), channel_id=1, source_target_pairs={{0,2},{1,3},{2,0},{3,1},{4,6},{5,7},{6,4},{7,5},{8,10},{9,11},{10,... | collective-permute-start | bytes 811016 | tf_op jit(solution)/shard_map/ppermute | solution.py:38
  5.2 21.8 %collective-permute-start = (bf16[32,4224]{1,0:T(8,128)(2,1)}, bf16[32,4224]{1,0:T(8,128)(2,1)S(1)}, u32[]{:S(2)}, u32[]{:S(2)}) collective-permute-start(bf16[32,4224]{1,0:T(8,128)(2,1)} %get-tuple-element.64.refs_0_.refs_4_), channel_id=1, source_target_pairs={{0,1},{1,0},{2,3},{3,2},{4,5},{5,4},{6,7},{7,6},{8,9},{9,8},{10,11... | collective-permute-start | bytes 811016 | tf_op jit(solution)/shard_map/ppermute | solution.py:38
  6.4 2.6 collective-permute-start.3
  9.1 18.6 %collective-permute-start.4 = (bf16[64,2048]{1,0:T(8,128)(2,1)S(1)}, bf16[64,2048]{1,0:T(8,128)(2,1)S(1)}, u32[]{:S(2)}, u32[]{:S(2)}) collective-permute-start(bf16[64,2048]{1,0:T(8,128)(2,1)S(1)} %slice.92), channel_id=1, source_target_pairs={{0,8},{4,12},{8,0},{12,4},{16,24},{20,28},{24,16},{28,20},{1,9},{5... | collective-permute-start | bytes 786440 | tf_op jit(solution)/shard_map/ppermute | solution.py:38
  10.4 18.2 %collective-permute-start.5 = (bf16[64,2176]{1,0:T(8,128)(2,1)S(1)}, bf16[64,2176]{1,0:T(8,128)(2,1)S(1)}, u32[]{:S(2)}, u32[]{:S(2)}) collective-permute-start(bf16[64,2176]{1,0:T(8,128)(2,1)S(1)} %slice.93), channel_id=1, source_target_pairs={{0,16},{4,20},{8,24},{12,28},{16,0},{20,4},{24,8},{28,12},{1,17},{... | collective-permute-start | bytes 835592 | tf_op jit(solution)/shard_map/ppermute | solution.py:38
  22.3 16.3 %copy-start.9 = (bf16[32,4224]{1,0:T(8,128)(2,1)}, bf16[32,4224]{1,0:T(8,128)(2,1)S(1)}, u32[]{:S(2)}) copy-start(bf16[32,4224]{1,0:T(8,128)(2,1)S(1)} %collective-permute-done.2.refs_3_.refs_7_) | copy-start | bytes 811012
  27.1 11.5 %copy-start.10 = (bf16[32,4224]{1,0:T(8,128)(2,1)}, bf16[32,4224]{1,0:T(8,128)(2,1)S(1)}, u32[]{:S(2)}) copy-start(bf16[32,4224]{1,0:T(8,128)(2,1)S(1)} %collective-permute-done.1.refs_2_.refs_6_) | copy-start | bytes 811012
  27.1 11.5 %copy-start.11 = (bf16[32,4224]{1,0:T(8,128)(2,1)}, bf16[32,4224]{1,0:T(8,128)(2,1)S(1)}, u32[]{:S(2)}) copy-start(bf16[32,4224]{1,0:T(8,128)(2,1)S(1)} %collective-permute-done.refs_1_.refs_5_) | copy-start | bytes 811012
  29.4 14.6 %collective-permute-start.9 = (bf16[64,4224]{1,0:T(8,128)(2,1)}, bf16[64,4224]{1,0:T(8,128)(2,1)S(1)}, u32[]{:S(2)}, u32[]{:S(2)}) collective-permute-start(bf16[64,4224]{1,0:T(8,128)(2,1)} %get-tuple-element.71.refs_0_.refs_7_), channel_id=1, source_target_pairs={{3,2},{2,1},{1,0},{7,6},{6,5},{5,4},{11,10},{10,9},{9,8},{15,14},{... | collective-permute-start | bytes 1622024 | tf_op jit(solution)/shard_map/ppermute | solution.py:54
  33.5 14.2 %collective-permute-start.8 = (bf16[64,4224]{1,0:T(8,128)(2,1)}, bf16[64,4224]{1,0:T(8,128)(2,1)S(1)}, u32[]{:S(2)}, u32[]{:S(2)}) collective-permute-start(bf16[64,4224]{1,0:T(8,128)(2,1)} %get-tuple-element.71.refs_0_.refs_7_), channel_id=1, source_target_pairs={{0,1},{1,2},{2,3},{4,5},{5,6},{6,7},{8,9},{9,10},{10,11},{12,13},{... | collective-permute-start | bytes 1622024 | tf_op jit(solution)/shard_map/ppermute | solution.py:54
  35.4 13.0 %collective-permute-start.7 = (bf16[128,2176]{1,0:T(8,128)(2,1)}, bf16[128,2176]{1,0:T(8,128)(2,1)S(1)}, u32[]{:S(2)}, u32[]{:S(2)}) collective-permute-start(bf16[128,2176]{1,0:T(8,128)(2,1)} %get-tuple-element.70.b0.t0), channel_id=1, source_target_pairs={{0,8},{4,12},{8,0},{12,4},{16,24},{20,28},{24,16},{28,20},{1,9},{5... | collective-permute-start | bytes 1671176 | tf_op jit(solution)/shard_map/ppermute | solution.py:38
  36.7 11.7 %collective-permute-start.6 = (bf16[128,2048]{1,0:T(8,128)(2,1)}, bf16[128,2048]{1,0:T(8,128)(2,1)S(1)}, u32[]{:S(2)}, u32[]{:S(2)}) collective-permute-start(bf16[128,2048]{1,0:T(8,128)(2,1)} %get-tuple-element.69.a0), channel_id=1, source_target_pairs={{0,16},{4,20},{8,24},{12,28},{16,0},{20,4},{24,8},{28,12},{1,17},{... | collective-permute-start | bytes 1572872 | tf_op jit(solution)/shard_map/ppermute | solution.py:38
  44.0 5.4 %copy-start.5 = (bf16[64,4224]{1,0:T(8,128)(2,1)}, bf16[64,4224]{1,0:T(8,128)(2,1)S(1)}, u32[]{:S(2)}) copy-start(bf16[64,4224]{1,0:T(8,128)(2,1)S(1)} %collective-permute-done.9.refs_2_.refs_9_) | copy-start | bytes 1622020
  47.7 1.6 copy-start.6
  48.4 0.8 copy-start.8
  48.4 1.0 copy-start.2
  49.4 44.0 %all-to-all-start = ((bf16[8,1,48,4096]{3,2,1,0:T(8,128)(2,1)}), bf16[8,1,48,4096]{3,2,1,0:T(8,128)(2,1)S(1)}, u32[]{:S(2)}, u32[]{:S(2)}) async-start(bf16[8,1,48,4096]{3,2,1,0:T(8,128)(2,1)} %get-tuple-element.72), calls=%async_computation | async-start | bytes 6291456 | tf_op jit(solution)/shard_map/all_to_all | solution.py:472
  55.8 15.8 %collective-permute-start.11 = (bf16[64,4224]{1,0:T(8,128)(2,1)}, bf16[64,4224]{1,0:T(8,128)(2,1)S(1)}, u32[]{:S(2)}, u32[]{:S(2)}) collective-permute-start(bf16[64,4224]{1,0:T(8,128)(2,1)} %copy-done.5), channel_id=1, source_target_pairs={{2,1},{1,0},{6,5},{5,4},{10,9},{9,8},{14,13},{13,12},{18,17},{17,1... | collective-permute-start | bytes 1622024 | tf_op jit(solution)/shard_map/ppermute | solution.py:54
  59.2 16.6 %collective-permute-start.10 = (bf16[64,4224]{1,0:T(8,128)(2,1)}, bf16[64,4224]{1,0:T(8,128)(2,1)}, u32[]{:S(2)}, u32[]{:S(2)}) collective-permute-start(bf16[64,4224]{1,0:T(8,128)(2,1)} %copy-done.6), channel_id=1, source_target_pairs={{1,2},{2,3},{5,6},{6,7},{9,10},{10,11},{13,14},{14,15},{17,18},{18... | collective-permute-start | bytes 1622024 | tf_op jit(solution)/shard_map/ppermute | solution.py:54
  71.6 14.0 %copy-start.7 = (bf16[64,4224]{1,0:T(8,128)(2,1)}, bf16[64,4224]{1,0:T(8,128)(2,1)S(1)}, u32[]{:S(2)}) copy-start(bf16[64,4224]{1,0:T(8,128)(2,1)S(1)} %collective-permute-done.11.refs_4_.refs_11_) | copy-start | bytes 1622020
  71.6 14.0 %collective-permute-start.13 = (bf16[64,4224]{1,0:T(8,128)(2,1)S(1)}, bf16[64,4224]{1,0:T(8,128)(2,1)}, u32[]{:S(2)}, u32[]{:S(2)}) collective-permute-start(bf16[64,4224]{1,0:T(8,128)(2,1)S(1)} %collective-permute-done.11.refs_4_.refs_11_), channel_id=1, source_target_pairs={{1,0},{5,4},{9,8},{13,12},{17,16},{21,20},{25,24},{29,28}} | collective-permute-start | bytes 1622024 | tf_op jit(solution)/shard_map/ppermute | solution.py:54
  75.8 9.8 %collective-permute-start.12 = (bf16[64,4224]{1,0:T(8,128)(2,1)}, bf16[64,4224]{1,0:T(8,128)(2,1)}, u32[]{:S(2)}, u32[]{:S(2)}) collective-permute-start(bf16[64,4224]{1,0:T(8,128)(2,1)} %collective-permute-done.10.refs_3_.refs_10_), channel_id=1, source_target_pairs={{2,3},{6,7},{10,11},{14,15},{18,19},{22,23},{26,27},{30,31}} | collective-permute-start | bytes 1622024 | tf_op jit(solution)/shard_map/ppermute | solution.py:54
  93.4 1.6 copy-start.4
  95.0 6.7 %copy-start.12 = (bf16[96,4096]{1,0:T(8,128)(2,1)S(1)}, bf16[96,4096]{1,0:T(8,128)(2,1)}, u32[]{:S(2)}) copy-start(bf16[96,4096]{1,0:T(8,128)(2,1)} %get-tuple-element.80) | copy-start | bytes 2359300
  95.0 9.0 %copy-start.13 = (bf16[96,4096]{1,0:T(8,128)(2,1)S(1)}, bf16[96,4096]{1,0:T(8,128)(2,1)}, u32[]{:S(2)}) copy-start(bf16[96,4096]{1,0:T(8,128)(2,1)} %get-tuple-element.81) | copy-start | bytes 2359300
  95.0 11.0 %copy-start.14 = (bf16[96,4096]{1,0:T(8,128)(2,1)S(1)}, bf16[96,4096]{1,0:T(8,128)(2,1)}, u32[]{:S(2)}) copy-start(bf16[96,4096]{1,0:T(8,128)(2,1)} %get-tuple-element.82) | copy-start | bytes 2359300
  95.0 79.4 %all-to-all-start.1 = ((bf16[8,2,48,4096]{3,2,1,0:T(8,128)(2,1)}), bf16[8,2,48,4096]{3,2,1,0:T(8,128)(2,1)}, u32[]{:S(2)}, u32[]{:S(2)}) async-start(bf16[8,2,48,4096]{3,2,1,0:T(8,128)(2,1)} %get-tuple-element.79), calls=%async_computation.1 | async-start | bytes 12582912 | tf_op jit(solution)/shard_map/all_to_all | solution.py:472
  101.6 35.5 %collective-permute-start.14 = (bf16[96,4096]{1,0:T(8,128)(2,1)S(1)}, bf16[96,4096]{1,0:T(8,128)(2,1)S(1)}, u32[]{:S(2)}, u32[]{:S(2)}) collective-permute-start(bf16[96,4096]{1,0:T(8,128)(2,1)S(1)} %copy-done.12), channel_id=1, source_target_pairs={{0,1},{1,0},{2,3},{3,2},{4,5},{5,4},{6,7},{7,6},{8,9},{9,8},{10,11... | collective-permute-start | bytes 2359304 | tf_op jit(solution)/shard_map/ppermute | solution.py:38
  104.0 52.5 %collective-permute-start.15 = (bf16[96,4096]{1,0:T(8,128)(2,1)S(1)}, bf16[96,4096]{1,0:T(8,128)(2,1)}, u32[]{:S(2)}, u32[]{:S(2)}) collective-permute-start(bf16[96,4096]{1,0:T(8,128)(2,1)S(1)} %copy-done.13), channel_id=1, source_target_pairs={{0,2},{1,3},{2,0},{3,1},{4,6},{5,7},{6,4},{7,5},{8,10},{9,11},{10,... | collective-permute-start | bytes 2359304 | tf_op jit(solution)/shard_map/ppermute | solution.py:38
  106.0 68.4 %collective-permute-start.16 = (bf16[96,4096]{1,0:T(8,128)(2,1)S(1)}, bf16[96,4096]{1,0:T(8,128)(2,1)}, u32[]{:S(2)}, u32[]{:S(2)}) collective-permute-start(bf16[96,4096]{1,0:T(8,128)(2,1)S(1)} %copy-done.14), channel_id=1, source_target_pairs={{0,3},{1,2},{2,1},{3,0},{4,7},{5,6},{6,5},{7,4},{8,11},{9,10},{10,... | collective-permute-start | bytes 2359304 | tf_op jit(solution)/shard_map/ppermute | solution.py:38
  137.1 38.6 %copy-start.18 = (bf16[96,4096]{1,0:T(8,128)(2,1)}, bf16[96,4096]{1,0:T(8,128)(2,1)S(1)}, u32[]{:S(2)}) copy-start(bf16[96,4096]{1,0:T(8,128)(2,1)S(1)} %collective-permute-done.14.refs_1_) | copy-start | bytes 2359300
  175.7 49.8 %all-to-all-start.2 = ((bf16[8,48,4096]{2,1,0:T(8,128)(2,1)}), bf16[8,48,4096]{2,1,0:T(8,128)(2,1)S(1)}, u32[]{:S(2)}, u32[]{:S(2)}) async-start(bf16[8,48,4096]{2,1,0:T(8,128)(2,1)} %bitcast.34), calls=%async_computation.2 | async-start | bytes 6291456 | tf_op jit(solution)/shard_map/all_to_all | solution.py:472
  196.7 28.8 %collective-permute-start.17 = (bf16[96,4096]{1,0:T(8,128)(2,1)}, bf16[96,4096]{1,0:T(8,128)(2,1)}, u32[]{:S(2)}, u32[]{:S(2)}) collective-permute-start(bf16[96,4096]{1,0:T(8,128)(2,1)} %get-tuple-element.89), channel_id=1, source_target_pairs={{0,1},{1,0},{2,3},{3,2},{4,5},{5,4},{6,7},{7,6},{8,9},{9,8},{10,11... | collective-permute-start | bytes 2359304 | tf_op jit(solution)/shard_map/ppermute | solution.py:38
  198.1 27.5 %collective-permute-start.18 = (bf16[48,4096]{1,0:T(8,128)(2,1)}, bf16[48,4096]{1,0:T(8,128)(2,1)S(1)}, u32[]{:S(2)}, u32[]{:S(2)}) collective-permute-start(bf16[48,4096]{1,0:T(8,128)(2,1)} %get-tuple-element.90), channel_id=1, source_target_pairs={{0,2},{1,3},{2,0},{3,1},{4,6},{5,7},{6,4},{7,5},{8,10},{9,11},{10,... | collective-permute-start | bytes 1179656 | tf_op jit(solution)/shard_map/ppermute | solution.py:38
  225.5 1.9 copy-start.15
  225.6 1.8 copy-start.1
  227.4 39.9 %all-to-all-start.3 = ((bf16[8,48,4096]{2,1,0:T(8,128)(2,1)}), bf16[8,48,4096]{2,1,0:T(8,128)(2,1)S(1)}, u32[]{:S(2)}, u32[]{:S(2)}) async-start(bf16[8,48,4096]{2,1,0:T(8,128)(2,1)} %bitcast.17), calls=%async_computation.3 | async-start | bytes 6291456 | tf_op jit(solution)/shard_map/all_to_all | solution.py:472
  232.0 26.8 %collective-permute-start.22 = (bf16[48,4096]{1,0:T(8,128)(2,1)}, bf16[48,4096]{1,0:T(8,128)(2,1)S(1)}, u32[]{:S(2)}, u32[]{:S(2)}) collective-permute-start(bf16[48,4096]{1,0:T(8,128)(2,1)} %get-tuple-element.101), channel_id=1, source_target_pairs={{0,2},{1,3},{2,0},{3,1},{4,6},{5,7},{6,4},{7,5},{8,10},{9,11},{10,... | collective-permute-start | bytes 1179656 | tf_op jit(solution)/shard_map/ppermute | solution.py:38
  233.0 34.3 %collective-permute-start.23 = (bf16[48,4096]{1,0:T(8,128)(2,1)}, bf16[48,4096]{1,0:T(8,128)(2,1)}, u32[]{:S(2)}, u32[]{:S(2)}) collective-permute-start(bf16[48,4096]{1,0:T(8,128)(2,1)} %get-tuple-element.102), channel_id=1, source_target_pairs={{0,3},{1,2},{2,1},{3,0},{4,7},{5,6},{6,5},{7,4},{8,11},{9,10},{10,... | collective-permute-start | bytes 1179656 | tf_op jit(solution)/shard_map/ppermute | solution.py:38
  258.9 10.0 %copy-start.16 = (bf16[48,4096]{1,0:T(8,128)(2,1)}, bf16[48,4096]{1,0:T(8,128)(2,1)S(1)}, u32[]{:S(2)}) copy-start(bf16[48,4096]{1,0:T(8,128)(2,1)S(1)} %collective-permute-done.22.refs_3_) | copy-start | bytes 1179652
  267.3 1.7 copy-start
  269.0 55.9 %all-to-all-start.4 = ((bf16[8,48,4096]{2,1,0:T(8,128)(2,1)}), bf16[8,48,4096]{2,1,0:T(8,128)(2,1)}, u32[]{:S(2)}, u32[]{:S(2)}) async-start(bf16[8,48,4096]{2,1,0:T(8,128)(2,1)} %bitcast.16), calls=%async_computation.4 | async-start | bytes 6291456 | tf_op jit(solution)/shard_map/all_to_all | solution.py:472
  276.0 10.6 %collective-permute-start.19 = (bf16[32,4096]{1,0:T(8,128)(2,1)}, bf16[32,4096]{1,0:T(8,128)(2,1)S(1)}, u32[]{:S(2)}, u32[]{:S(2)}) collective-permute-start(bf16[32,4096]{1,0:T(8,128)(2,1)} %get-tuple-element.93), channel_id=1, source_target_pairs={{0,1},{1,0},{2,3},{3,2},{4,5},{5,4},{6,7},{7,6},{8,9},{9,8},{10,11... | collective-permute-start | bytes 786440 | tf_op jit(solution)/shard_map/ppermute | solution.py:38
  276.0 13.5 %collective-permute-start.20 = (bf16[32,4096]{1,0:T(8,128)(2,1)}, bf16[32,4096]{1,0:T(8,128)(2,1)S(1)}, u32[]{:S(2)}, u32[]{:S(2)}) collective-permute-start(bf16[32,4096]{1,0:T(8,128)(2,1)} %get-tuple-element.94), channel_id=1, source_target_pairs={{0,2},{1,3},{2,0},{3,1},{4,6},{5,7},{6,4},{7,5},{8,10},{9,11},{10,... | collective-permute-start | bytes 786440 | tf_op jit(solution)/shard_map/ppermute | solution.py:38
  277.4 32.8 %collective-permute-start.21 = (bf16[32,4096]{1,0:T(8,128)(2,1)}, bf16[32,4096]{1,0:T(8,128)(2,1)S(1)}, u32[]{:S(2)}, u32[]{:S(2)}) collective-permute-start(bf16[32,4096]{1,0:T(8,128)(2,1)} %get-tuple-element.95), channel_id=1, source_target_pairs={{0,3},{1,2},{2,1},{3,0},{4,7},{5,6},{6,5},{7,4},{8,11},{9,10},{10,... | collective-permute-start | bytes 786440 | tf_op jit(solution)/shard_map/ppermute | solution.py:38
  278.6 39.9 %collective-permute-start.24 = (bf16[48,4096]{1,0:T(8,128)(2,1)}, bf16[48,4096]{1,0:T(8,128)(2,1)S(1)}, u32[]{:S(2)}, u32[]{:S(2)}) collective-permute-start(bf16[48,4096]{1,0:T(8,128)(2,1)} %get-tuple-element.104), channel_id=1, source_target_pairs={{0,3},{1,2},{2,1},{3,0},{4,7},{5,6},{6,5},{7,4},{8,11},{9,10},{10,... | collective-permute-start | bytes 1179656 | tf_op jit(solution)/shard_map/ppermute | solution.py:38
  315.7 16.3 %collective-permute-start.25 = (bf16[32,4096]{1,0:T(8,128)(2,1)}, bf16[32,4096]{1,0:T(8,128)(2,1)S(1)}, u32[]{:S(2)}, u32[]{:S(2)}) collective-permute-start(bf16[32,4096]{1,0:T(8,128)(2,1)} %get-tuple-element.113), channel_id=1, source_target_pairs={{0,1},{1,0},{2,3},{3,2},{4,5},{5,4},{6,7},{7,6},{8,9},{9,8},{10,11... | collective-permute-start | bytes 786440 | tf_op jit(solution)/shard_map/ppermute | solution.py:38
  315.7 17.6 %collective-permute-start.26 = (bf16[32,4096]{1,0:T(8,128)(2,1)}, bf16[32,4096]{1,0:T(8,128)(2,1)S(1)}, u32[]{:S(2)}, u32[]{:S(2)}) collective-permute-start(bf16[32,4096]{1,0:T(8,128)(2,1)} %get-tuple-element.114), channel_id=1, source_target_pairs={{0,2},{1,3},{2,0},{3,1},{4,6},{5,7},{6,4},{7,5},{8,10},{9,11},{10,... | collective-permute-start | bytes 786440 | tf_op jit(solution)/shard_map/ppermute | solution.py:38
  317.1 29.8 %collective-permute-start.27 = (bf16[32,4096]{1,0:T(8,128)(2,1)}, bf16[32,4096]{1,0:T(8,128)(2,1)S(1)}, u32[]{:S(2)}, u32[]{:S(2)}) collective-permute-start(bf16[32,4096]{1,0:T(8,128)(2,1)} %get-tuple-element.115), channel_id=1, source_target_pairs={{0,3},{1,2},{2,1},{3,0},{4,7},{5,6},{6,5},{7,4},{8,11},{9,10},{10,... | collective-permute-start | bytes 786440 | tf_op jit(solution)/shard_map/ppermute | solution.py:38
  318.5 0.8 copy-start.17
  329.3 28.3 %collective-permute-start.30 = (bf16[32,4096]{1,0:T(8,128)(2,1)}, bf16[32,4096]{1,0:T(8,128)(2,1)}, u32[]{:S(2)}, u32[]{:S(2)}) collective-permute-start(bf16[32,4096]{1,0:T(8,128)(2,1)} %get-tuple-element.119), channel_id=1, source_target_pairs={{0,2},{1,3},{2,0},{3,1},{4,6},{5,7},{6,4},{7,5},{8,10},{9,11},{10,... | collective-permute-start | bytes 786440 | tf_op jit(solution)/shard_map/ppermute | solution.py:38
  330.1 32.5 %collective-permute-start.29 = (bf16[32,4096]{1,0:T(8,128)(2,1)}, bf16[32,4096]{1,0:T(8,128)(2,1)}, u32[]{:S(2)}, u32[]{:S(2)}) collective-permute-start(bf16[32,4096]{1,0:T(8,128)(2,1)} %get-tuple-element.111), channel_id=1, source_target_pairs={{0,1},{1,0},{2,3},{3,2},{4,5},{5,4},{6,7},{7,6},{8,9},{9,8},{10,11... | collective-permute-start | bytes 786440 | tf_op jit(solution)/shard_map/ppermute | solution.py:38
  332.0 23.4 %copy-start.3 = (f32[128,2048]{1,0:T(8,128)S(1)}, f32[128,2048]{1,0:T(8,128)}, u32[]{:S(2)}) copy-start(f32[128,2048]{1,0:T(8,128)} %get-tuple-element.121) | copy-start | bytes 3145732
  332.0 30.6 %collective-permute-start.31 = (bf16[32,4096]{1,0:T(8,128)(2,1)}, bf16[32,4096]{1,0:T(8,128)(2,1)}, u32[]{:S(2)}, u32[]{:S(2)}) collective-permute-start(bf16[32,4096]{1,0:T(8,128)(2,1)} %get-tuple-element.120), channel_id=1, source_target_pairs={{0,3},{1,2},{2,1},{3,0},{4,7},{5,6},{6,5},{7,4},{8,11},{9,10},{10,... | collective-permute-start | bytes 786440 | tf_op jit(solution)/shard_map/ppermute | solution.py:38
  333.3 16.1 %collective-permute-start.28 = (bf16[128,2048]{1,0:T(8,128)(2,1)}, bf16[128,2048]{1,0:T(8,128)(2,1)S(1)}, u32[]{:S(2)}, u32[]{:S(2)}) collective-permute-start(bf16[128,2048]{1,0:T(8,128)(2,1)} %get-tuple-element.118), channel_id=1, source_target_pairs={{0,16},{4,20},{8,24},{12,28},{16,0},{20,4},{24,8},{28,12},{1,17},{... | collective-permute-start | bytes 1572872 | tf_op jit(solution)/shard_map/ppermute | solution.py:38
  346.9 8.5 %collective-permute-start.34 = (bf16[128,2048]{1,0:T(8,128)(2,1)}, bf16[128,2048]{1,0:T(8,128)(2,1)S(1)}, u32[]{:S(2)}, u32[]{:S(2)}) collective-permute-start(bf16[128,2048]{1,0:T(8,128)(2,1)} %get-tuple-element.122), channel_id=1, source_target_pairs={{0,8},{4,12},{8,0},{12,4},{16,24},{20,28},{24,16},{28,20},{1,9},{5... | collective-permute-start | bytes 1572872 | tf_op jit(solution)/shard_map/ppermute | solution.py:38
  351.4 12.6 %collective-permute-start.32 = (bf16[64,2048]{1,0:T(8,128)(2,1)S(1)}, bf16[64,2048]{1,0:T(8,128)(2,1)S(1)}, u32[]{:S(2)}, u32[]{:S(2)}) collective-permute-start(bf16[64,2048]{1,0:T(8,128)(2,1)S(1)} %split.57), channel_id=1, source_target_pairs={{0,8},{4,12},{8,0},{12,4},{16,24},{20,28},{24,16},{28,20},{1,9},{5... | collective-permute-start | bytes 786440 | tf_op jit(solution)/shard_map/ppermute | solution.py:38
  356.3 13.3 %collective-permute-start.35 = (bf16[64,2048]{1,0:T(8,128)(2,1)}, bf16[64,2048]{1,0:T(8,128)(2,1)S(1)}, u32[]{:S(2)}, u32[]{:S(2)}) collective-permute-start(bf16[64,2048]{1,0:T(8,128)(2,1)} %split.56), channel_id=1, source_target_pairs={{0,16},{4,20},{8,24},{12,28},{16,0},{20,4},{24,8},{28,12},{1,17},{... | collective-permute-start | bytes 786440 | tf_op jit(solution)/shard_map/ppermute | solution.py:38
  364.1 9.2 %collective-permute-start.33 = (bf16[32,2048]{1,0:T(8,128)(2,1)S(1)}, bf16[32,2048]{1,0:T(8,128)(2,1)S(1)}, u32[]{:S(2)}, u32[]{:S(2)}) collective-permute-start(bf16[32,2048]{1,0:T(8,128)(2,1)S(1)} %split.59), channel_id=1, source_target_pairs={{0,4},{4,0},{8,12},{12,8},{16,20},{20,16},{24,28},{28,24},{1,5},{5... | collective-permute-start | bytes 393224 | tf_op jit(solution)/shard_map/ppermute | solution.py:38
  369.7 4.5 %collective-permute-start.36 = (bf16[32,2048]{1,0:T(8,128)(2,1)S(1)}, bf16[32,2048]{1,0:T(8,128)(2,1)S(1)}, u32[]{:S(2)}, u32[]{:S(2)}) collective-permute-start(bf16[32,2048]{1,0:T(8,128)(2,1)S(1)} %split.58), channel_id=1, source_target_pairs={{0,4},{4,0},{8,12},{12,8},{16,20},{20,16},{24,28},{28,24},{1,5},{5... | collective-permute-start | bytes 393224 | tf_op jit(solution)/shard_map/ppermute | solution.py:38

commit v11 on v10

--- a/solution.py
+++ b/solution.py
@@ -549,6 +549,7 @@
     landed2 = to_experts(out2)
     landed3.append(swap(part3, "local", last1))
     own1, parts1 = mix(mixing1, landed1)
+    (own0,) = fence([own0], parts1[:1])
     parts1 = swaps([None] + parts1, "local", 1, peers)
     cross = mix_cross(mixing3a, mixing3b, landed3)
 

time: 377 us -> 389 us (1.032)
  waiting for transfers between devices: 160 us -> 168 us
    ppermute x31, waiting for transfers between devices: 144 us -> 152 us  [swap(): return lax.ppermute(array, axis, [(i, i ^ bits) for i in range(size)])]
  transfers between devices with their start and end apart: 42 -> 42, of which waited for: 21 -> 20; matrix products, arithmetic and copies ran while one was open for 4% -> 4% of each run, Pallas kernels for 27% -> 26%
where the time goes in v11:
time: 389 us; the launch traced here: 386 us
  waiting for transfers between devices  168 us (43%)
  Pallas kernels  104 us (27%)
  starting transfers between devices  85.4 us (22%)
  other arithmetic  20.5 us (5%)
  local copies, waits for them, and re-layouts  7.64 us (2%)
    ppermute x31, waiting for transfers between devices, swap(): return lax.ppermute(array, axis, [(i, i ^ bits) for i in range(size)])  152 us
    pallas_call x4, Pallas kernels, expert(): pl.pallas_call(functools.partial(expert_kernel, len(parts), first_tiles,...  63.3 us
    ppermute x31, starting transfers between devices, swap(): return lax.ppermute(array, axis, [(i, i ^ bits) for i in range(size)])  37.9 us
    all_to_all x5, starting transfers between devices, to_experts(): return lax.all_to_all(rows, 'node', 0, 0, tiled=True)  29.6 us
    ppermute x6, starting transfers between devices, chain_step(): lax.ppermute(a, axis, way)  17.8 us
    ppermute x6, waiting for transfers between devices, chain_step(): lax.ppermute(a, axis, way)  16.2 us
    pallas_call x3, Pallas kernels, mix(): pl.pallas_call(mix_kernel, grid=(TILES,), out_shape=[jax.ShapeDtypeStruct...  13.2 us
    pallas_call x2, Pallas kernels, pick(): pl.pallas_call(functools.partial(pick_kernel, len(parts), blocks, peers,...  12.8 us
  transfers between devices with their start and end apart: 42, of which 20 were waited for; matrix products, arithmetic and copies ran while one was open for 4% of the time, Pallas kernels for 26%

profile of v11, /device:TPU:9, one launch (start us, length us, event | category | flops | bytes accessed | tf_op | source)
XLA Modules:
  0.0 385.6 jit_solution(11721286045685725126)
XLA Ops:
  0.0 2.9 shard_map.262
  2.9 1.3 collective-permute-start.2
  9.1 1.3 collective-permute-start.4
  10.4 1.3 collective-permute-start.5
  11.7 10.6 %collective-permute-done.2.refs_3_.refs_7_ = bf16[32,4224]{1,0:T(8,128)(2,1)S(1)} collective-permute-done((bf16[32,4224]{1,0:T(8,128)(2,1)}, bf16[32,4224]{1,0:T(8,128)(2,1)S(1)}, u32[]{:S(2)}, u32[]{:S(2)}) %collective-permute-start.2) | collective-permute-done | bytes 270368 | tf_op jit(solution)/shard_map/ppermute | solution.py:38
  22.3 4.8 %collective-permute-done.1.refs_2_.refs_6_ = bf16[32,4224]{1,0:T(8,128)(2,1)S(1)} collective-permute-done((bf16[32,4224]{1,0:T(8,128)(2,1)}, bf16[32,4224]{1,0:T(8,128)(2,1)S(1)}, u32[]{:S(2)}, u32[]{:S(2)}) %collective-permute-start.1) | collective-permute-done | bytes 270368 | tf_op jit(solution)/shard_map/ppermute | solution.py:38
  29.4 4.1 %collective-permute-start.9 = (bf16[64,4224]{1,0:T(8,128)(2,1)}, bf16[64,4224]{1,0:T(8,128)(2,1)S(1)}, u32[]{:S(2)}, u32[]{:S(2)}) collective-permute-start(bf16[64,4224]{1,0:T(8,128)(2,1)} %get-tuple-element.71.refs_0_.refs_7_), channel_id=1, source_target_pairs={{3,2},{2,1},{1,0},{7,6},{6,5},{5,4},{11,10},{10,9},{9,8},{15,14},{... | collective-permute-start | bytes 1622024 | tf_op jit(solution)/shard_map/ppermute | solution.py:54
  33.5 1.9 collective-permute-start.8
  35.4 1.3 collective-permute-start.7
  36.7 1.2 collective-permute-start.6
  38.6 5.1 %shard_map.263 = (bf16[8,1,48,4096]{3,2,1,0:T(8,128)(2,1)}, bf16[128,384]{1,0:T(8,128)(2,1)}) custom-call(s32[2]{0:T(128)} %pad_add_fusion.ids.tie.refs_1_, bf16[32,4224]{1,0:T(8,128)(2,1)} %get-tuple-element.64.refs_0_.refs_4_, bf16[32,4224]{1,0:T(8,128)(2,1)} %copy-done.11, bf16[32,4224]{1,0:T(8,128)(2,1)} %copy-done.10, bf16[32,4224]{1,0:T(8,128)(2,1)} %copy-done.9, ...), custom_call_target="tpu_custom_call" | custom-call | flops 402653184 | bytes 4194304 | tf_op jit(solution)/shard_map/pallas_call | solution.py:182
  44.0 3.7 collective-permute-done.8.refs_1_.refs_8_
  49.5 6.4 %all-to-all-start = ((bf16[8,1,48,4096]{3,2,1,0:T(8,128)(2,1)}), bf16[8,1,48,4096]{3,2,1,0:T(8,128)(2,1)S(1)}, u32[]{:S(2)}, u32[]{:S(2)}) async-start(bf16[8,1,48,4096]{3,2,1,0:T(8,128)(2,1)} %get-tuple-element.72), calls=%async_computation | async-start | bytes 6291456 | tf_op jit(solution)/shard_map/all_to_all | solution.py:472
  55.9 3.4 collective-permute-start.11
  59.2 2.7 collective-permute-start.10
  62.0 9.7 %collective-permute-done.11.refs_4_.refs_11_ = bf16[64,4224]{1,0:T(8,128)(2,1)S(1)} collective-permute-done((bf16[64,4224]{1,0:T(8,128)(2,1)}, bf16[64,4224]{1,0:T(8,128)(2,1)S(1)}, u32[]{:S(2)}, u32[]{:S(2)}) %collective-permute-start.11) | collective-permute-done | bytes 540704 | tf_op jit(solution)/shard_map/ppermute | solution.py:54
  71.7 4.2 %collective-permute-start.13 = (bf16[64,4224]{1,0:T(8,128)(2,1)S(1)}, bf16[64,4224]{1,0:T(8,128)(2,1)}, u32[]{:S(2)}, u32[]{:S(2)}) collective-permute-start(bf16[64,4224]{1,0:T(8,128)(2,1)S(1)} %collective-permute-done.11.refs_4_.refs_11_), channel_id=1, source_target_pairs={{1,0},{5,4},{9,8},{13,12},{17,16},{21,20},{25,24},{29,28}} | collective-permute-start | bytes 1622024 | tf_op jit(solution)/shard_map/ppermute | solution.py:54
  75.9 1.5 collective-permute-start.12
  77.4 5.9 %shard_map.268 = (bf16[96,4096]{1,0:T(8,128)(2,1)}, bf16[96,4096]{1,0:T(8,128)(2,1)}, bf16[96,4096]{1,0:T(8,128)(2,1)}, bf16[96,4096]{1,0:T(8,128)(2,1)}, bf16[2...) custom-call(s32[2]{0:T(128)} %pad_add_fusion.ids.tie.refs_1_, bf16[128,2048]{1,0:T(8,128)(2,1)} %get-tuple-element.69.a0, ...), custom_call_target="tpu_custom_call" | custom-call | flops 805306368 | bytes 5242880 | tf_op jit(solution)/shard_map/pallas_call | solution.py:260
  83.3 2.4 collective-permute-done.13.refs_6_.refs_13_
  85.7 7.7 %shard_map.267 = (bf16[8,2,48,4096]{3,2,1,0:T(8,128)(2,1)}, bf16[128,384]{1,0:T(8,128)(2,1)}, bf16[128,384]{1,0:T(8,128)(2,1)}) custom-call(s32[2]{0:T(128)} %pad_add_fusion.ids.tie.refs_1_, bf16[64,4224]{1,0:T(8,128)(2,1)} %get-tuple-element.71.refs_0_.refs_7_, bf16[64,4224]{1,0:T(8,128)(2,1)} %copy-done.6, bf16[64,4224]{1,0:T(8,128)(2,1)} %copy-done.5, ...), custom_call_target="tpu_custom_call" | custom-call | flops 1409286144 | bytes 9961472 | tf_op jit(solution)/shard_map/pallas_call | solution.py:182
  95.1 6.7 %all-to-all-start.1 = ((bf16[8,2,48,4096]{3,2,1,0:T(8,128)(2,1)}), bf16[8,2,48,4096]{3,2,1,0:T(8,128)(2,1)}, u32[]{:S(2)}, u32[]{:S(2)}) async-start(bf16[8,2,48,4096]{3,2,1,0:T(8,128)(2,1)} %get-tuple-element.79), calls=%async_computation.1 | async-start | bytes 12582912 | tf_op jit(solution)/shard_map/all_to_all | solution.py:472
  101.8 2.3 collective-permute-start.14
  104.1 2.0 collective-permute-start.15
  106.4 15.9 %shard_map.266.refs_0_ = bf16[384,4096]{1,0:T(8,128)(2,1)} custom-call(s32[2]{0:T(128)} %pad_add_fusion.ids.tie.refs_1_, bf16[384,4096]{1,0:T(8,128)(2,1)} %bitcast.35, bf16[4096,768]{1,0:T(8,128)(2,1)} %bitcast.18, bf16[4096,768]{1,0:T(8,128)(2,1)} %bitcast.22, bf16[768,4096]{1,0:T(8,128)(2,1)} %bitcast.26), custom_call_target="tpu_custom_call" | custom-call | flops 7247757312 | bytes 25165824 | tf_op jit(solution)/shard_map/pallas_call | solution.py:404
  122.4 14.9 %collective-permute-done.14.refs_1_ = bf16[96,4096]{1,0:T(8,128)(2,1)S(1)} collective-permute-done((bf16[96,4096]{1,0:T(8,128)(2,1)S(1)}, bf16[96,4096]{1,0:T(8,128)(2,1)S(1)}, u32[]{:S(2)}, u32[]{:S(2)}) %collective-permute-start.14) | collective-permute-done | bytes 786464 | tf_op jit(solution)/shard_map/ppermute | solution.py:38
  137.3 19.4 %collective-permute-done.15.refs_2_ = bf16[96,4096]{1,0:T(8,128)(2,1)} collective-permute-done((bf16[96,4096]{1,0:T(8,128)(2,1)S(1)}, bf16[96,4096]{1,0:T(8,128)(2,1)}, u32[]{:S(2)}, u32[]{:S(2)}) %collective-permute-start.15) | collective-permute-done | bytes 786464 | tf_op jit(solution)/shard_map/ppermute | solution.py:38
  156.6 17.9 %collective-permute-done.16.refs_3_ = bf16[96,4096]{1,0:T(8,128)(2,1)} collective-permute-done((bf16[96,4096]{1,0:T(8,128)(2,1)S(1)}, bf16[96,4096]{1,0:T(8,128)(2,1)}, u32[]{:S(2)}, u32[]{:S(2)}) %collective-permute-start.16) | collective-permute-done | bytes 786464 | tf_op jit(solution)/shard_map/ppermute | solution.py:38
  174.5 1.3 convert_add_fusion.4.refs_2_
  175.8 4.9 %all-to-all-start.2 = ((bf16[8,48,4096]{2,1,0:T(8,128)(2,1)}), bf16[8,48,4096]{2,1,0:T(8,128)(2,1)S(1)}, u32[]{:S(2)}, u32[]{:S(2)}) async-start(bf16[8,48,4096]{2,1,0:T(8,128)(2,1)} %bitcast.33), calls=%async_computation.2 | async-start | bytes 6291456 | tf_op jit(solution)/shard_map/all_to_all | solution.py:472
  180.7 16.2 %shard_map.271 = (bf16[96,4096]{1,0:T(8,128)(2,1)}, bf16[96,4096]{1,0:T(8,128)(2,1)}, bf16[48,4096]{1,0:T(8,128)(2,1)}, bf16[48,4096]{1,0:T(8,128)(2,1)}, bf16[4...) custom-call(s32[2]{0:T(128)} %get-tuple-element.83.tie.refs_0_, bf16[96,4096]{1,0:T(8,128)(2,1)} %get-tuple-element.84.refs_0_, ...), custom_call_target="tpu_custom_call" | custom-call | flops 7247757312 | bytes 25165824 | tf_op jit(solution)/shard_map/pallas_call | solution.py:404
  197.0 1.3 slice_convert_fusion.8.refs_1_
  198.2 2.4 collective-permute-start.18
  200.7 15.6 %shard_map.273.refs_0_ = bf16[384,4096]{1,0:T(8,128)(2,1)} custom-call(s32[2]{0:T(128)} %shard_map.272.tie.refs_3_, bf16[8,2,48,4096]{3,2,1,0:T(8,128)(2,1)} %all-to-all-done.1.refs_0_, bf16[4096,768]{1,0:T(8,128)(2,1)} %bitcast.20, bf16[4096,768]{1,0:T(8,128)(2,1)} %bitcast.24, bf16[768,4096]{1,0:T(8,128)(2,1)} %bitcast.28), custom_call_target="tpu_custom_call" | custom-call | flops 7247757312 | bytes 25165824 | tf_op jit(solution)/shard_map/pallas_call | solution.py:404
  216.2 9.5 %collective-permute-done.18.refs_2_ = bf16[48,4096]{1,0:T(8,128)(2,1)S(1)} collective-permute-done((bf16[48,4096]{1,0:T(8,128)(2,1)}, bf16[48,4096]{1,0:T(8,128)(2,1)S(1)}, u32[]{:S(2)}, u32[]{:S(2)}) %collective-permute-start.18) | collective-permute-done | bytes 393248 | tf_op jit(solution)/shard_map/ppermute | solution.py:38
  225.8 1.7 convert_add_fusion.3.refs_4_
  227.5 5.3 %all-to-all-start.3 = ((bf16[8,48,4096]{2,1,0:T(8,128)(2,1)}), bf16[8,48,4096]{2,1,0:T(8,128)(2,1)}, u32[]{:S(2)}, u32[]{:S(2)}) async-start(bf16[8,48,4096]{2,1,0:T(8,128)(2,1)} %bitcast.17), calls=%async_computation.3 | async-start | bytes 6291456 | tf_op jit(solution)/shard_map/all_to_all | solution.py:472
  233.8 15.6 %shard_map.275.refs_0_ = bf16[384,4096]{1,0:T(8,128)(2,1)} custom-call(s32[2]{0:T(128)} %get-tuple-element.91.tie, bf16[8,2,48,4096]{3,2,1,0:T(8,128)(2,1)} %all-to-all-done.1.refs_0_, bf16[4096,768]{1,0:T(8,128)(2,1)} %bitcast.21, bf16[4096,768]{1,0:T(8,128)(2,1)} %bitcast.25, bf16[768,4096]{1,0:T(8,128)(2,1)} %bitcast.29), custom_call_target="tpu_custom_call" | custom-call | flops 7247757312 | bytes 25165824 | tf_op jit(solution)/shard_map/pallas_call | solution.py:404
  249.4 1.3 slice_convert_fusion.4.refs_1_
  250.7 4.3 %shard_map.277 = (f32[32,4096]{1,0:T(8,128)}, bf16[32,4096]{1,0:T(8,128)(2,1)}, bf16[32,4096]{1,0:T(8,128)(2,1)}, bf16[32,4096]{1,0:T(8,128)(2,1)}) custom-call(bf16[128,384]{1,0:T(8,128)(2,1)} %shard_map.276.mixing, bf16[384,4096]{1,0:T(8,128)(2,1)} %bitcast.31), custom_call_target="tpu_custom_call" | custom-call | flops 402653184 | bytes 4194304 | tf_op jit(solution)/shard_map/pallas_call | solution.py:295
  255.0 4.6 %collective-permute-done.22.refs_3_ = bf16[48,4096]{1,0:T(8,128)(2,1)S(1)} collective-permute-done((bf16[48,4096]{1,0:T(8,128)(2,1)}, bf16[48,4096]{1,0:T(8,128)(2,1)S(1)}, u32[]{:S(2)}, u32[]{:S(2)}) %collective-permute-start.22) | collective-permute-done | bytes 393248 | tf_op jit(solution)/shard_map/ppermute | solution.py:38
  259.6 8.4 %collective-permute-done.23.refs_4_ = bf16[48,4096]{1,0:T(8,128)(2,1)S(1)} collective-permute-done((bf16[48,4096]{1,0:T(8,128)(2,1)}, bf16[48,4096]{1,0:T(8,128)(2,1)S(1)}, u32[]{:S(2)}, u32[]{:S(2)}) %collective-permute-start.23) | collective-permute-done | bytes 393248 | tf_op jit(solution)/shard_map/ppermute | solution.py:38
  268.0 1.3 convert_add_fusion.2.refs_2_
  269.4 6.4 %all-to-all-start.4 = ((bf16[8,48,4096]{2,1,0:T(8,128)(2,1)}), bf16[8,48,4096]{2,1,0:T(8,128)(2,1)S(1)}, u32[]{:S(2)}, u32[]{:S(2)}) async-start(bf16[8,48,4096]{2,1,0:T(8,128)(2,1)} %bitcast.16), calls=%async_computation.4 | async-start | bytes 6291456 | tf_op jit(solution)/shard_map/all_to_all | solution.py:472
  275.7 1.5 collective-permute-start.20
  278.4 4.5 %shard_map.278 = (f32[32,4096]{1,0:T(8,128)}, bf16[32,4096]{1,0:T(8,128)(2,1)}, bf16[32,4096]{1,0:T(8,128)(2,1)}, bf16[32,4096]{1,0:T(8,128)(2,1)}) custom-call(bf16[128,384]{1,0:T(8,128)(2,1)} %get-tuple-element.93.mixing, bf16[384,4096]{1,0:T(8,128)(2,1)} %bitcast.13.landed), custom_call_target="tpu_custom_call" | custom-call | flops 402653184 | bytes 4194304 | tf_op jit(solution)/shard_map/pallas_call | solution.py:295
  283.8 1.3 slice_convert_fusion.7.refs_1_
  286.4 1.5 collective-permute-start.27
  287.9 1.7 collective-permute-done.20
  290.6 30.6 %collective-permute-done.21 = bf16[32,4096]{1,0:T(8,128)(2,1)} collective-permute-done((bf16[32,4096]{1,0:T(8,128)(2,1)}, bf16[32,4096]{1,0:T(8,128)(2,1)}, u32[]{:S(2)}, u32[]{:S(2)}) %collective-permute-start.21) | collective-permute-done | bytes 262176 | tf_op jit(solution)/shard_map/ppermute | solution.py:38
  321.2 1.4 add_convert_fusion.2
  322.6 18.2 %collective-permute-done.24.refs_5_ = bf16[48,4096]{1,0:T(8,128)(2,1)S(1)} collective-permute-done((bf16[48,4096]{1,0:T(8,128)(2,1)}, bf16[48,4096]{1,0:T(8,128)(2,1)S(1)}, u32[]{:S(2)}, u32[]{:S(2)}) %collective-permute-start.24) | collective-permute-done | bytes 393248 | tf_op jit(solution)/shard_map/ppermute | solution.py:38
  341.6 5.6 %shard_map.281 = (f32[128,2048]{1,0:T(8,128)}, bf16[128,2048]{1,0:T(8,128)(2,1)}, f32[128,2048]{1,0:T(8,128)}, bf16[128,2048]{1,0:T(8,128)(2,1)}) custom-call(bf16[256,384]{1,0:T(8,128)(2,1)} %get-tuple-element.100.mixing_a, bf16[256,384]{1,0:T(8,128)(2,1)} %get-tuple-element.101.mixing_b, bf16[96,4096]{1,0:T(8,128)(2,1)} %get-tuple-element.85.refs_0_, ...), custom_call_target="tpu_custom_call" | custom-call | flops 805306368 | bytes 5242880 | tf_op jit(solution)/shard_map/pallas_call | solution.py:337
  347.2 1.6 copy-done.1
  348.8 4.4 %shard_map.282 = (f32[32,4096]{1,0:T(8,128)}, bf16[32,4096]{1,0:T(8,128)(2,1)}, bf16[32,4096]{1,0:T(8,128)(2,1)}, bf16[32,4096]{1,0:T(8,128)(2,1)}) custom-call(bf16[128,384]{1,0:T(8,128)(2,1)} %get-tuple-element.110.mixing, bf16[384,4096]{1,0:T(8,128)(2,1)} %bitcast.32), custom_call_target="tpu_custom_call" | custom-call | flops 402653184 | bytes 4194304 | tf_op jit(solution)/shard_map/pallas_call | solution.py:295
  353.2 1.6 collective-permute-start.29
  354.8 1.3 slice_convert_fusion.6.refs_5_
  359.6 1.4 add_convert_fusion.1
  361.0 7.8 %collective-permute-done.28 = bf16[128,2048]{1,0:T(8,128)(2,1)S(1)} collective-permute-done((bf16[128,2048]{1,0:T(8,128)(2,1)}, bf16[128,2048]{1,0:T(8,128)(2,1)S(1)}, u32[]{:S(2)}, u32[]{:S(2)}) %collective-permute-start.28) | collective-permute-done | bytes 524320 | tf_op jit(solution)/shard_map/ppermute | solution.py:38
  368.8 1.3 convert_add_fusion.1
  374.6 1.7 collective-permute-done.31
  376.3 1.4 add_convert_fusion
  377.7 3.4 collective-permute-start.33
  381.2 2.3 collective-permute-start.36
  (117 shorter events, 28.3 us)
Async XLA Ops:
  2.9 19.3 %collective-permute-start.2 = (bf16[32,4224]{1,0:T(8,128)(2,1)}, bf16[32,4224]{1,0:T(8,128)(2,1)S(1)}, u32[]{:S(2)}, u32[]{:S(2)}) collective-permute-start(bf16[32,4224]{1,0:T(8,128)(2,1)} %get-tuple-element.64.refs_0_.refs_4_), channel_id=1, source_target_pairs={{0,3},{1,2},{2,1},{3,0},{4,7},{5,6},{6,5},{7,4},{8,11},{9,10},{10,... | collective-permute-start | bytes 811016 | tf_op jit(solution)/shard_map/ppermute | solution.py:38
  4.2 22.8 %collective-permute-start.1 = (bf16[32,4224]{1,0:T(8,128)(2,1)}, bf16[32,4224]{1,0:T(8,128)(2,1)S(1)}, u32[]{:S(2)}, u32[]{:S(2)}) collective-permute-start(bf16[32,4224]{1,0:T(8,128)(2,1)} %get-tuple-element.64.refs_0_.refs_4_), channel_id=1, source_target_pairs={{0,2},{1,3},{2,0},{3,1},{4,6},{5,7},{6,4},{7,5},{8,10},{9,11},{10,... | collective-permute-start | bytes 811016 | tf_op jit(solution)/shard_map/ppermute | solution.py:38
  5.2 21.8 %collective-permute-start = (bf16[32,4224]{1,0:T(8,128)(2,1)}, bf16[32,4224]{1,0:T(8,128)(2,1)S(1)}, u32[]{:S(2)}, u32[]{:S(2)}) collective-permute-start(bf16[32,4224]{1,0:T(8,128)(2,1)} %get-tuple-element.64.refs_0_.refs_4_), channel_id=1, source_target_pairs={{0,1},{1,0},{2,3},{3,2},{4,5},{5,4},{6,7},{7,6},{8,9},{9,8},{10,11... | collective-permute-start | bytes 811016 | tf_op jit(solution)/shard_map/ppermute | solution.py:38
  6.4 2.6 collective-permute-start.3
  9.1 18.6 %collective-permute-start.4 = (bf16[64,2048]{1,0:T(8,128)(2,1)S(1)}, bf16[64,2048]{1,0:T(8,128)(2,1)S(1)}, u32[]{:S(2)}, u32[]{:S(2)}) collective-permute-start(bf16[64,2048]{1,0:T(8,128)(2,1)S(1)} %slice.96), channel_id=1, source_target_pairs={{0,8},{4,12},{8,0},{12,4},{16,24},{20,28},{24,16},{28,20},{1,9},{5... | collective-permute-start | bytes 786440 | tf_op jit(solution)/shard_map/ppermute | solution.py:38
  10.4 18.2 %collective-permute-start.5 = (bf16[64,2176]{1,0:T(8,128)(2,1)S(1)}, bf16[64,2176]{1,0:T(8,128)(2,1)S(1)}, u32[]{:S(2)}, u32[]{:S(2)}) collective-permute-start(bf16[64,2176]{1,0:T(8,128)(2,1)S(1)} %slice.97), channel_id=1, source_target_pairs={{0,16},{4,20},{8,24},{12,28},{16,0},{20,4},{24,8},{28,12},{1,17},{... | collective-permute-start | bytes 835592 | tf_op jit(solution)/shard_map/ppermute | solution.py:38
  22.3 16.3 %copy-start.9 = (bf16[32,4224]{1,0:T(8,128)(2,1)}, bf16[32,4224]{1,0:T(8,128)(2,1)S(1)}, u32[]{:S(2)}) copy-start(bf16[32,4224]{1,0:T(8,128)(2,1)S(1)} %collective-permute-done.2.refs_3_.refs_7_) | copy-start | bytes 811012
  27.1 11.5 %copy-start.10 = (bf16[32,4224]{1,0:T(8,128)(2,1)}, bf16[32,4224]{1,0:T(8,128)(2,1)S(1)}, u32[]{:S(2)}) copy-start(bf16[32,4224]{1,0:T(8,128)(2,1)S(1)} %collective-permute-done.1.refs_2_.refs_6_) | copy-start | bytes 811012
  27.1 11.5 %copy-start.11 = (bf16[32,4224]{1,0:T(8,128)(2,1)}, bf16[32,4224]{1,0:T(8,128)(2,1)S(1)}, u32[]{:S(2)}) copy-start(bf16[32,4224]{1,0:T(8,128)(2,1)S(1)} %collective-permute-done.refs_1_.refs_5_) | copy-start | bytes 811012
  29.4 14.6 %collective-permute-start.9 = (bf16[64,4224]{1,0:T(8,128)(2,1)}, bf16[64,4224]{1,0:T(8,128)(2,1)S(1)}, u32[]{:S(2)}, u32[]{:S(2)}) collective-permute-start(bf16[64,4224]{1,0:T(8,128)(2,1)} %get-tuple-element.71.refs_0_.refs_7_), channel_id=1, source_target_pairs={{3,2},{2,1},{1,0},{7,6},{6,5},{5,4},{11,10},{10,9},{9,8},{15,14},{... | collective-permute-start | bytes 1622024 | tf_op jit(solution)/shard_map/ppermute | solution.py:54
  33.5 14.2 %collective-permute-start.8 = (bf16[64,4224]{1,0:T(8,128)(2,1)}, bf16[64,4224]{1,0:T(8,128)(2,1)S(1)}, u32[]{:S(2)}, u32[]{:S(2)}) collective-permute-start(bf16[64,4224]{1,0:T(8,128)(2,1)} %get-tuple-element.71.refs_0_.refs_7_), channel_id=1, source_target_pairs={{0,1},{1,2},{2,3},{4,5},{5,6},{6,7},{8,9},{9,10},{10,11},{12,13},{... | collective-permute-start | bytes 1622024 | tf_op jit(solution)/shard_map/ppermute | solution.py:54
  35.4 13.0 %collective-permute-start.7 = (bf16[128,2176]{1,0:T(8,128)(2,1)}, bf16[128,2176]{1,0:T(8,128)(2,1)S(1)}, u32[]{:S(2)}, u32[]{:S(2)}) collective-permute-start(bf16[128,2176]{1,0:T(8,128)(2,1)} %get-tuple-element.70.b0.t0), channel_id=1, source_target_pairs={{0,8},{4,12},{8,0},{12,4},{16,24},{20,28},{24,16},{28,20},{1,9},{5... | collective-permute-start | bytes 1671176 | tf_op jit(solution)/shard_map/ppermute | solution.py:38
  36.7 11.7 %collective-permute-start.6 = (bf16[128,2048]{1,0:T(8,128)(2,1)}, bf16[128,2048]{1,0:T(8,128)(2,1)S(1)}, u32[]{:S(2)}, u32[]{:S(2)}) collective-permute-start(bf16[128,2048]{1,0:T(8,128)(2,1)} %get-tuple-element.69.a0), channel_id=1, source_target_pairs={{0,16},{4,20},{8,24},{12,28},{16,0},{20,4},{24,8},{28,12},{1,17},{... | collective-permute-start | bytes 1572872 | tf_op jit(solution)/shard_map/ppermute | solution.py:38
  44.0 5.5 %copy-start.5 = (bf16[64,4224]{1,0:T(8,128)(2,1)}, bf16[64,4224]{1,0:T(8,128)(2,1)S(1)}, u32[]{:S(2)}) copy-start(bf16[64,4224]{1,0:T(8,128)(2,1)S(1)} %collective-permute-done.9.refs_2_.refs_9_) | copy-start | bytes 1622020
  47.7 1.7 copy-start.6
  48.4 0.8 copy-start.8
  48.4 1.0 copy-start.2
  49.5 44.0 %all-to-all-start = ((bf16[8,1,48,4096]{3,2,1,0:T(8,128)(2,1)}), bf16[8,1,48,4096]{3,2,1,0:T(8,128)(2,1)S(1)}, u32[]{:S(2)}, u32[]{:S(2)}) async-start(bf16[8,1,48,4096]{3,2,1,0:T(8,128)(2,1)} %get-tuple-element.72), calls=%async_computation | async-start | bytes 6291456 | tf_op jit(solution)/shard_map/all_to_all | solution.py:472
  55.9 15.8 %collective-permute-start.11 = (bf16[64,4224]{1,0:T(8,128)(2,1)}, bf16[64,4224]{1,0:T(8,128)(2,1)S(1)}, u32[]{:S(2)}, u32[]{:S(2)}) collective-permute-start(bf16[64,4224]{1,0:T(8,128)(2,1)} %copy-done.5), channel_id=1, source_target_pairs={{2,1},{1,0},{6,5},{5,4},{10,9},{9,8},{14,13},{13,12},{18,17},{17,1... | collective-permute-start | bytes 1622024 | tf_op jit(solution)/shard_map/ppermute | solution.py:54
  59.2 16.6 %collective-permute-start.10 = (bf16[64,4224]{1,0:T(8,128)(2,1)}, bf16[64,4224]{1,0:T(8,128)(2,1)}, u32[]{:S(2)}, u32[]{:S(2)}) collective-permute-start(bf16[64,4224]{1,0:T(8,128)(2,1)} %copy-done.6), channel_id=1, source_target_pairs={{1,2},{2,3},{5,6},{6,7},{9,10},{10,11},{13,14},{14,15},{17,18},{18... | collective-permute-start | bytes 1622024 | tf_op jit(solution)/shard_map/ppermute | solution.py:54
  71.7 14.0 %copy-start.7 = (bf16[64,4224]{1,0:T(8,128)(2,1)}, bf16[64,4224]{1,0:T(8,128)(2,1)S(1)}, u32[]{:S(2)}) copy-start(bf16[64,4224]{1,0:T(8,128)(2,1)S(1)} %collective-permute-done.11.refs_4_.refs_11_) | copy-start | bytes 1622020
  71.7 14.0 %collective-permute-start.13 = (bf16[64,4224]{1,0:T(8,128)(2,1)S(1)}, bf16[64,4224]{1,0:T(8,128)(2,1)}, u32[]{:S(2)}, u32[]{:S(2)}) collective-permute-start(bf16[64,4224]{1,0:T(8,128)(2,1)S(1)} %collective-permute-done.11.refs_4_.refs_11_), channel_id=1, source_target_pairs={{1,0},{5,4},{9,8},{13,12},{17,16},{21,20},{25,24},{29,28}} | collective-permute-start | bytes 1622024 | tf_op jit(solution)/shard_map/ppermute | solution.py:54
  75.9 9.8 %collective-permute-start.12 = (bf16[64,4224]{1,0:T(8,128)(2,1)}, bf16[64,4224]{1,0:T(8,128)(2,1)}, u32[]{:S(2)}, u32[]{:S(2)}) collective-permute-start(bf16[64,4224]{1,0:T(8,128)(2,1)} %collective-permute-done.10.refs_3_.refs_10_), channel_id=1, source_target_pairs={{2,3},{6,7},{10,11},{14,15},{18,19},{22,23},{26,27},{30,31}} | collective-permute-start | bytes 1622024 | tf_op jit(solution)/shard_map/ppermute | solution.py:54
  93.4 1.7 copy-start.4
  95.1 6.7 %copy-start.12 = (bf16[96,4096]{1,0:T(8,128)(2,1)S(1)}, bf16[96,4096]{1,0:T(8,128)(2,1)}, u32[]{:S(2)}) copy-start(bf16[96,4096]{1,0:T(8,128)(2,1)} %get-tuple-element.80) | copy-start | bytes 2359300
  95.1 9.0 %copy-start.13 = (bf16[96,4096]{1,0:T(8,128)(2,1)S(1)}, bf16[96,4096]{1,0:T(8,128)(2,1)}, u32[]{:S(2)}) copy-start(bf16[96,4096]{1,0:T(8,128)(2,1)} %get-tuple-element.81) | copy-start | bytes 2359300
  95.1 11.1 %copy-start.14 = (bf16[96,4096]{1,0:T(8,128)(2,1)S(1)}, bf16[96,4096]{1,0:T(8,128)(2,1)}, u32[]{:S(2)}) copy-start(bf16[96,4096]{1,0:T(8,128)(2,1)} %get-tuple-element.82) | copy-start | bytes 2359300
  95.1 79.5 %all-to-all-start.1 = ((bf16[8,2,48,4096]{3,2,1,0:T(8,128)(2,1)}), bf16[8,2,48,4096]{3,2,1,0:T(8,128)(2,1)}, u32[]{:S(2)}, u32[]{:S(2)}) async-start(bf16[8,2,48,4096]{3,2,1,0:T(8,128)(2,1)} %get-tuple-element.79), calls=%async_computation.1 | async-start | bytes 12582912 | tf_op jit(solution)/shard_map/all_to_all | solution.py:472
  101.8 35.5 %collective-permute-start.14 = (bf16[96,4096]{1,0:T(8,128)(2,1)S(1)}, bf16[96,4096]{1,0:T(8,128)(2,1)S(1)}, u32[]{:S(2)}, u32[]{:S(2)}) collective-permute-start(bf16[96,4096]{1,0:T(8,128)(2,1)S(1)} %copy-done.12), channel_id=1, source_target_pairs={{0,1},{1,0},{2,3},{3,2},{4,5},{5,4},{6,7},{7,6},{8,9},{9,8},{10,11... | collective-permute-start | bytes 2359304 | tf_op jit(solution)/shard_map/ppermute | solution.py:38
  104.1 52.5 %collective-permute-start.15 = (bf16[96,4096]{1,0:T(8,128)(2,1)S(1)}, bf16[96,4096]{1,0:T(8,128)(2,1)}, u32[]{:S(2)}, u32[]{:S(2)}) collective-permute-start(bf16[96,4096]{1,0:T(8,128)(2,1)S(1)} %copy-done.13), channel_id=1, source_target_pairs={{0,2},{1,3},{2,0},{3,1},{4,6},{5,7},{6,4},{7,5},{8,10},{9,11},{10,... | collective-permute-start | bytes 2359304 | tf_op jit(solution)/shard_map/ppermute | solution.py:38
  106.1 68.4 %collective-permute-start.16 = (bf16[96,4096]{1,0:T(8,128)(2,1)S(1)}, bf16[96,4096]{1,0:T(8,128)(2,1)}, u32[]{:S(2)}, u32[]{:S(2)}) collective-permute-start(bf16[96,4096]{1,0:T(8,128)(2,1)S(1)} %copy-done.14), channel_id=1, source_target_pairs={{0,3},{1,2},{2,1},{3,0},{4,7},{5,6},{6,5},{7,4},{8,11},{9,10},{10,... | collective-permute-start | bytes 2359304 | tf_op jit(solution)/shard_map/ppermute | solution.py:38
  137.3 38.6 %copy-start.20 = (bf16[96,4096]{1,0:T(8,128)(2,1)}, bf16[96,4096]{1,0:T(8,128)(2,1)S(1)}, u32[]{:S(2)}) copy-start(bf16[96,4096]{1,0:T(8,128)(2,1)S(1)} %collective-permute-done.14.refs_1_) | copy-start | bytes 2359300
  175.8 49.9 %all-to-all-start.2 = ((bf16[8,48,4096]{2,1,0:T(8,128)(2,1)}), bf16[8,48,4096]{2,1,0:T(8,128)(2,1)S(1)}, u32[]{:S(2)}, u32[]{:S(2)}) async-start(bf16[8,48,4096]{2,1,0:T(8,128)(2,1)} %bitcast.33), calls=%async_computation.2 | async-start | bytes 6291456 | tf_op jit(solution)/shard_map/all_to_all | solution.py:472
  196.9 28.9 %collective-permute-start.17 = (bf16[96,4096]{1,0:T(8,128)(2,1)}, bf16[96,4096]{1,0:T(8,128)(2,1)}, u32[]{:S(2)}, u32[]{:S(2)}) collective-permute-start(bf16[96,4096]{1,0:T(8,128)(2,1)} %get-tuple-element.89), channel_id=1, source_target_pairs={{0,1},{1,0},{2,3},{3,2},{4,5},{5,4},{6,7},{7,6},{8,9},{9,8},{10,11... | collective-permute-start | bytes 2359304 | tf_op jit(solution)/shard_map/ppermute | solution.py:38
  198.2 27.5 %collective-permute-start.18 = (bf16[48,4096]{1,0:T(8,128)(2,1)}, bf16[48,4096]{1,0:T(8,128)(2,1)S(1)}, u32[]{:S(2)}, u32[]{:S(2)}) collective-permute-start(bf16[48,4096]{1,0:T(8,128)(2,1)} %get-tuple-element.90), channel_id=1, source_target_pairs={{0,2},{1,3},{2,0},{3,1},{4,6},{5,7},{6,4},{7,5},{8,10},{9,11},{10,... | collective-permute-start | bytes 1179656 | tf_op jit(solution)/shard_map/ppermute | solution.py:38
  225.7 1.8 copy-start.15
  225.7 1.8 copy-start
  227.5 40.5 %all-to-all-start.3 = ((bf16[8,48,4096]{2,1,0:T(8,128)(2,1)}), bf16[8,48,4096]{2,1,0:T(8,128)(2,1)}, u32[]{:S(2)}, u32[]{:S(2)}) async-start(bf16[8,48,4096]{2,1,0:T(8,128)(2,1)} %bitcast.17), calls=%async_computation.3 | async-start | bytes 6291456 | tf_op jit(solution)/shard_map/all_to_all | solution.py:472
  232.8 26.8 %collective-permute-start.22 = (bf16[48,4096]{1,0:T(8,128)(2,1)}, bf16[48,4096]{1,0:T(8,128)(2,1)S(1)}, u32[]{:S(2)}, u32[]{:S(2)}) collective-permute-start(bf16[48,4096]{1,0:T(8,128)(2,1)} %get-tuple-element.102), channel_id=1, source_target_pairs={{0,2},{1,3},{2,0},{3,1},{4,6},{5,7},{6,4},{7,5},{8,10},{9,11},{10,... | collective-permute-start | bytes 1179656 | tf_op jit(solution)/shard_map/ppermute | solution.py:38
  233.8 34.3 %collective-permute-start.23 = (bf16[48,4096]{1,0:T(8,128)(2,1)}, bf16[48,4096]{1,0:T(8,128)(2,1)S(1)}, u32[]{:S(2)}, u32[]{:S(2)}) collective-permute-start(bf16[48,4096]{1,0:T(8,128)(2,1)} %get-tuple-element.103), channel_id=1, source_target_pairs={{0,3},{1,2},{2,1},{3,0},{4,7},{5,6},{6,5},{7,4},{8,11},{9,10},{10,... | collective-permute-start | bytes 1179656 | tf_op jit(solution)/shard_map/ppermute | solution.py:38
  259.6 9.8 %copy-start.16 = (bf16[48,4096]{1,0:T(8,128)(2,1)}, bf16[48,4096]{1,0:T(8,128)(2,1)S(1)}, u32[]{:S(2)}) copy-start(bf16[48,4096]{1,0:T(8,128)(2,1)S(1)} %collective-permute-done.22.refs_3_) | copy-start | bytes 1179652
  268.0 1.3 copy-start.17
  269.4 77.8 %all-to-all-start.4 = ((bf16[8,48,4096]{2,1,0:T(8,128)(2,1)}), bf16[8,48,4096]{2,1,0:T(8,128)(2,1)S(1)}, u32[]{:S(2)}, u32[]{:S(2)}) async-start(bf16[8,48,4096]{2,1,0:T(8,128)(2,1)} %bitcast.16), calls=%async_computation.4 | async-start | bytes 6291456 | tf_op jit(solution)/shard_map/all_to_all | solution.py:472
  275.7 10.7 %collective-permute-start.19 = (bf16[32,4096]{1,0:T(8,128)(2,1)}, bf16[32,4096]{1,0:T(8,128)(2,1)S(1)}, u32[]{:S(2)}, u32[]{:S(2)}) collective-permute-start(bf16[32,4096]{1,0:T(8,128)(2,1)} %get-tuple-element.96), channel_id=1, source_target_pairs={{0,1},{1,0},{2,3},{3,2},{4,5},{5,4},{6,7},{7,6},{8,9},{9,8},{10,11... | collective-permute-start | bytes 786440 | tf_op jit(solution)/shard_map/ppermute | solution.py:38
  275.7 13.8 %collective-permute-start.20 = (bf16[32,4096]{1,0:T(8,128)(2,1)}, bf16[32,4096]{1,0:T(8,128)(2,1)}, u32[]{:S(2)}, u32[]{:S(2)}) collective-permute-start(bf16[32,4096]{1,0:T(8,128)(2,1)} %get-tuple-element.97), channel_id=1, source_target_pairs={{0,2},{1,3},{2,0},{3,1},{4,6},{5,7},{6,4},{7,5},{8,10},{9,11},{10,... | collective-permute-start | bytes 786440 | tf_op jit(solution)/shard_map/ppermute | solution.py:38
  277.2 44.0 %collective-permute-start.21 = (bf16[32,4096]{1,0:T(8,128)(2,1)}, bf16[32,4096]{1,0:T(8,128)(2,1)}, u32[]{:S(2)}, u32[]{:S(2)}) collective-permute-start(bf16[32,4096]{1,0:T(8,128)(2,1)} %get-tuple-element.98), channel_id=1, source_target_pairs={{0,3},{1,2},{2,1},{3,0},{4,7},{5,6},{6,5},{7,4},{8,11},{9,10},{10,... | collective-permute-start | bytes 786440 | tf_op jit(solution)/shard_map/ppermute | solution.py:38
  282.9 75.6 %collective-permute-start.25 = (bf16[32,4096]{1,0:T(8,128)(2,1)}, bf16[32,4096]{1,0:T(8,128)(2,1)}, u32[]{:S(2)}, u32[]{:S(2)}) collective-permute-start(bf16[32,4096]{1,0:T(8,128)(2,1)} %get-tuple-element.95), channel_id=1, source_target_pairs={{0,1},{1,0},{2,3},{3,2},{4,5},{5,4},{6,7},{7,6},{8,9},{9,8},{10,11... | collective-permute-start | bytes 786440 | tf_op jit(solution)/shard_map/ppermute | solution.py:38
  285.1 71.1 %collective-permute-start.26 = (bf16[32,4096]{1,0:T(8,128)(2,1)}, bf16[32,4096]{1,0:T(8,128)(2,1)}, u32[]{:S(2)}, u32[]{:S(2)}) collective-permute-start(bf16[32,4096]{1,0:T(8,128)(2,1)} %get-tuple-element.114), channel_id=1, source_target_pairs={{0,2},{1,3},{2,0},{3,1},{4,6},{5,7},{6,4},{7,5},{8,10},{9,11},{10,... | collective-permute-start | bytes 786440 | tf_op jit(solution)/shard_map/ppermute | solution.py:38
  286.4 4.2 %copy-start.19 = (bf16[32,4096]{1,0:T(8,128)(2,1)}, bf16[32,4096]{1,0:T(8,128)(2,1)S(1)}, u32[]{:S(2)}) copy-start(bf16[32,4096]{1,0:T(8,128)(2,1)S(1)} %collective-permute-done.19) | copy-start | bytes 786436
  286.4 70.8 %collective-permute-start.27 = (bf16[32,4096]{1,0:T(8,128)(2,1)}, bf16[32,4096]{1,0:T(8,128)(2,1)}, u32[]{:S(2)}, u32[]{:S(2)}) collective-permute-start(bf16[32,4096]{1,0:T(8,128)(2,1)} %get-tuple-element.115), channel_id=1, source_target_pairs={{0,3},{1,2},{2,1},{3,0},{4,7},{5,6},{6,5},{7,4},{8,11},{9,10},{10,... | collective-permute-start | bytes 786440 | tf_op jit(solution)/shard_map/ppermute | solution.py:38
  289.6 51.2 %collective-permute-start.24 = (bf16[48,4096]{1,0:T(8,128)(2,1)}, bf16[48,4096]{1,0:T(8,128)(2,1)S(1)}, u32[]{:S(2)}, u32[]{:S(2)}) collective-permute-start(bf16[48,4096]{1,0:T(8,128)(2,1)} %get-tuple-element.105), channel_id=1, source_target_pairs={{0,3},{1,2},{2,1},{3,0},{4,7},{5,6},{6,5},{7,4},{8,11},{9,10},{10,... | collective-permute-start | bytes 1179656 | tf_op jit(solution)/shard_map/ppermute | solution.py:38
  340.8 0.8 copy-start.18
  347.2 1.6 copy-start.1
  353.2 21.4 %collective-permute-start.30 = (bf16[32,4096]{1,0:T(8,128)(2,1)}, bf16[32,4096]{1,0:T(8,128)(2,1)}, u32[]{:S(2)}, u32[]{:S(2)}) collective-permute-start(bf16[32,4096]{1,0:T(8,128)(2,1)} %get-tuple-element.119), channel_id=1, source_target_pairs={{0,2},{1,3},{2,0},{3,1},{4,6},{5,7},{6,4},{7,5},{8,10},{9,11},{10,... | collective-permute-start | bytes 786440 | tf_op jit(solution)/shard_map/ppermute | solution.py:38
  353.2 23.0 %collective-permute-start.29 = (bf16[32,4096]{1,0:T(8,128)(2,1)}, bf16[32,4096]{1,0:T(8,128)(2,1)}, u32[]{:S(2)}, u32[]{:S(2)}) collective-permute-start(bf16[32,4096]{1,0:T(8,128)(2,1)} %get-tuple-element.112), channel_id=1, source_target_pairs={{0,1},{1,0},{2,3},{3,2},{4,5},{5,4},{6,7},{7,6},{8,9},{9,8},{10,11... | collective-permute-start | bytes 786440 | tf_op jit(solution)/shard_map/ppermute | solution.py:38
  356.1 16.4 %copy-start.3 = (f32[128,2048]{1,0:T(8,128)S(1)}, f32[128,2048]{1,0:T(8,128)}, u32[]{:S(2)}) copy-start(f32[128,2048]{1,0:T(8,128)} %get-tuple-element.121) | copy-start | bytes 3145732
  356.1 20.1 %collective-permute-start.31 = (bf16[32,4096]{1,0:T(8,128)(2,1)}, bf16[32,4096]{1,0:T(8,128)(2,1)}, u32[]{:S(2)}, u32[]{:S(2)}) collective-permute-start(bf16[32,4096]{1,0:T(8,128)(2,1)} %get-tuple-element.120), channel_id=1, source_target_pairs={{0,3},{1,2},{2,1},{3,0},{4,7},{5,6},{6,5},{7,4},{8,11},{9,10},{10,... | collective-permute-start | bytes 786440 | tf_op jit(solution)/shard_map/ppermute | solution.py:38
  357.2 11.6 %collective-permute-start.28 = (bf16[128,2048]{1,0:T(8,128)(2,1)}, bf16[128,2048]{1,0:T(8,128)(2,1)S(1)}, u32[]{:S(2)}, u32[]{:S(2)}) collective-permute-start(bf16[128,2048]{1,0:T(8,128)(2,1)} %get-tuple-element.118), channel_id=1, source_target_pairs={{0,16},{4,20},{8,24},{12,28},{16,0},{20,4},{24,8},{28,12},{1,17},{... | collective-permute-start | bytes 1572872 | tf_op jit(solution)/shard_map/ppermute | solution.py:38
  358.4 14.1 %collective-permute-start.34 = (bf16[128,2048]{1,0:T(8,128)(2,1)}, bf16[128,2048]{1,0:T(8,128)(2,1)S(1)}, u32[]{:S(2)}, u32[]{:S(2)}) collective-permute-start(bf16[128,2048]{1,0:T(8,128)(2,1)} %get-tuple-element.122), channel_id=1, source_target_pairs={{0,8},{4,12},{8,0},{12,4},{16,24},{20,28},{24,16},{28,20},{1,9},{5... | collective-permute-start | bytes 1572872 | tf_op jit(solution)/shard_map/ppermute | solution.py:38
  371.5 6.2 %collective-permute-start.32 = (bf16[64,2048]{1,0:T(8,128)(2,1)}, bf16[64,2048]{1,0:T(8,128)(2,1)S(1)}, u32[]{:S(2)}, u32[]{:S(2)}) collective-permute-start(bf16[64,2048]{1,0:T(8,128)(2,1)} %split.57), channel_id=1, source_target_pairs={{0,8},{4,12},{8,0},{12,4},{16,24},{20,28},{24,16},{28,20},{1,9},{5... | collective-permute-start | bytes 786440 | tf_op jit(solution)/shard_map/ppermute | solution.py:38
  373.4 7.8 %collective-permute-start.35 = (bf16[64,2048]{1,0:T(8,128)(2,1)}, bf16[64,2048]{1,0:T(8,128)(2,1)S(1)}, u32[]{:S(2)}, u32[]{:S(2)}) collective-permute-start(bf16[64,2048]{1,0:T(8,128)(2,1)} %split.56), channel_id=1, source_target_pairs={{0,16},{4,20},{8,24},{12,28},{16,0},{20,4},{24,8},{28,12},{1,17},{... | collective-permute-start | bytes 786440 | tf_op jit(solution)/shard_map/ppermute | solution.py:38
  377.7 5.8 %collective-permute-start.33 = (bf16[32,2048]{1,0:T(8,128)(2,1)S(1)}, bf16[32,2048]{1,0:T(8,128)(2,1)S(1)}, u32[]{:S(2)}, u32[]{:S(2)}) collective-permute-start(bf16[32,2048]{1,0:T(8,128)(2,1)S(1)} %split.59), channel_id=1, source_target_pairs={{0,4},{4,0},{8,12},{12,8},{16,20},{20,16},{24,28},{28,24},{1,5},{5... | collective-permute-start | bytes 393224 | tf_op jit(solution)/shard_map/ppermute | solution.py:38
  381.2 3.3 collective-permute-start.36

commit v12 on v10

--- a/solution.py
+++ b/solution.py
@@ -553,7 +553,7 @@
     cross = mix_cross(mixing3a, mixing3b, landed3)
 
     own2, parts2 = mix(mixing2, landed2)
-    own1, *cross = fence([own1] + list(cross), parts2[:1])
+    own0, own1, *cross = fence([own0, own1] + list(cross), parts2[:1])
     parts2 = swaps([None] + parts2, "local", 1, peers)
     sums3 = halve(*cross[:2], "node", bits_a[-1]), halve(*cross[2:], "node", bits_b[-1])
     (own2,) = fence([own2], [sums3[0]])

time: 377 us -> 379 us (level)
  no operation moved by 1% of the time
where the time goes in v12:
time: 379 us; the launch traced here: 376 us
  waiting for transfers between devices  163 us (43%)
  Pallas kernels  104 us (27%)
  starting transfers between devices  84.8 us (22%)
  other arithmetic  18 us (5%)
  local copies, waits for them, and re-layouts  6.81 us (2%)
    ppermute x31, waiting for transfers between devices, swap(): return lax.ppermute(array, axis, [(i, i ^ bits) for i in range(size)])  144 us
    pallas_call x4, Pallas kernels, expert(): pl.pallas_call(functools.partial(expert_kernel, len(parts), first_tiles,...  63.2 us
    ppermute x31, starting transfers between devices, swap(): return lax.ppermute(array, axis, [(i, i ^ bits) for i in range(size)])  37.5 us
    all_to_all x5, starting transfers between devices, to_experts(): return lax.all_to_all(rows, 'node', 0, 0, tiled=True)  29.6 us
    ppermute x6, starting transfers between devices, chain_step(): lax.ppermute(a, axis, way)  17.8 us
    ppermute x6, waiting for transfers between devices, chain_step(): lax.ppermute(a, axis, way)  16.1 us
    pallas_call x3, Pallas kernels, mix(): pl.pallas_call(mix_kernel, grid=(TILES,), out_shape=[jax.ShapeDtypeStruct...  13.1 us
    pallas_call x2, Pallas kernels, pick(): pl.pallas_call(functools.partial(pick_kernel, len(parts), blocks, peers,...  12.9 us
  transfers between devices with their start and end apart: 42, of which 21 were waited for; matrix products, arithmetic and copies ran while one was open for 4% of the time, Pallas kernels for 27%

profile of v12, /device:TPU:9, one launch (start us, length us, event | category | flops | bytes accessed | tf_op | source)
XLA Modules:
  0.0 376.4 jit_solution(16591317152898933485)
XLA Ops:
  0.0 2.9 shard_map.262
  2.9 1.3 collective-permute-start.2
  9.1 1.3 collective-permute-start.4
  10.4 1.3 collective-permute-start.5
  11.7 10.6 %collective-permute-done.2.refs_3_.refs_7_ = bf16[32,4224]{1,0:T(8,128)(2,1)S(1)} collective-permute-done((bf16[32,4224]{1,0:T(8,128)(2,1)}, bf16[32,4224]{1,0:T(8,128)(2,1)S(1)}, u32[]{:S(2)}, u32[]{:S(2)}) %collective-permute-start.2) | collective-permute-done | bytes 270368 | tf_op jit(solution)/shard_map/ppermute | solution.py:38
  22.3 4.8 %collective-permute-done.1.refs_2_.refs_6_ = bf16[32,4224]{1,0:T(8,128)(2,1)S(1)} collective-permute-done((bf16[32,4224]{1,0:T(8,128)(2,1)}, bf16[32,4224]{1,0:T(8,128)(2,1)S(1)}, u32[]{:S(2)}, u32[]{:S(2)}) %collective-permute-start.1) | collective-permute-done | bytes 270368 | tf_op jit(solution)/shard_map/ppermute | solution.py:38
  29.4 4.1 %collective-permute-start.9 = (bf16[64,4224]{1,0:T(8,128)(2,1)}, bf16[64,4224]{1,0:T(8,128)(2,1)S(1)}, u32[]{:S(2)}, u32[]{:S(2)}) collective-permute-start(bf16[64,4224]{1,0:T(8,128)(2,1)} %get-tuple-element.72.refs_0_.refs_7_), channel_id=1, source_target_pairs={{3,2},{2,1},{1,0},{7,6},{6,5},{5,4},{11,10},{10,9},{9,8},{15,14},{... | collective-permute-start | bytes 1622024 | tf_op jit(solution)/shard_map/ppermute | solution.py:54
  33.5 1.9 collective-permute-start.8
  35.4 1.3 collective-permute-start.7
  38.6 5.2 %shard_map.263 = (bf16[8,1,48,4096]{3,2,1,0:T(8,128)(2,1)}, bf16[128,384]{1,0:T(8,128)(2,1)}) custom-call(s32[2]{0:T(128)} %pad_add_fusion.ids.tie.refs_1_, bf16[32,4224]{1,0:T(8,128)(2,1)} %get-tuple-element.65.refs_0_.refs_4_, bf16[32,4224]{1,0:T(8,128)(2,1)} %copy-done.12, bf16[32,4224]{1,0:T(8,128)(2,1)} %copy-done.11, bf16[32,4224]{1,0:T(8,128)(2,1)} %copy-done.10, ...), custom_call_target="tpu_custom_call" | custom-call | flops 402653184 | bytes 4194304 | tf_op jit(solution)/shard_map/pallas_call | solution.py:182
  44.0 3.7 collective-permute-done.8.refs_1_.refs_8_
  49.4 6.4 %all-to-all-start = ((bf16[8,1,48,4096]{3,2,1,0:T(8,128)(2,1)}), bf16[8,1,48,4096]{3,2,1,0:T(8,128)(2,1)S(1)}, u32[]{:S(2)}, u32[]{:S(2)}) async-start(bf16[8,1,48,4096]{3,2,1,0:T(8,128)(2,1)} %get-tuple-element.73), calls=%async_computation | async-start | bytes 6291456 | tf_op jit(solution)/shard_map/all_to_all | solution.py:472
  55.8 3.4 collective-permute-start.11
  59.2 2.8 collective-permute-start.10
  62.0 9.7 %collective-permute-done.11.refs_4_.refs_11_ = bf16[64,4224]{1,0:T(8,128)(2,1)S(1)} collective-permute-done((bf16[64,4224]{1,0:T(8,128)(2,1)}, bf16[64,4224]{1,0:T(8,128)(2,1)S(1)}, u32[]{:S(2)}, u32[]{:S(2)}) %collective-permute-start.11) | collective-permute-done | bytes 540704 | tf_op jit(solution)/shard_map/ppermute | solution.py:54
  71.7 4.2 %collective-permute-start.13 = (bf16[64,4224]{1,0:T(8,128)(2,1)S(1)}, bf16[64,4224]{1,0:T(8,128)(2,1)}, u32[]{:S(2)}, u32[]{:S(2)}) collective-permute-start(bf16[64,4224]{1,0:T(8,128)(2,1)S(1)} %collective-permute-done.11.refs_4_.refs_11_), channel_id=1, source_target_pairs={{1,0},{5,4},{9,8},{13,12},{17,16},{21,20},{25,24},{29,28}} | collective-permute-start | bytes 1622024 | tf_op jit(solution)/shard_map/ppermute | solution.py:54
  75.9 1.5 collective-permute-start.12
  77.3 5.8 %shard_map.268 = (bf16[96,4096]{1,0:T(8,128)(2,1)}, bf16[96,4096]{1,0:T(8,128)(2,1)}, bf16[96,4096]{1,0:T(8,128)(2,1)}, bf16[96,4096]{1,0:T(8,128)(2,1)}, bf16[2...) custom-call(s32[2]{0:T(128)} %pad_add_fusion.ids.tie.refs_1_, bf16[128,2048]{1,0:T(8,128)(2,1)} %get-tuple-element.70.a0, ...), custom_call_target="tpu_custom_call" | custom-call | flops 805306368 | bytes 5242880 | tf_op jit(solution)/shard_map/pallas_call | solution.py:260
  83.2 2.5 collective-permute-done.13.refs_6_.refs_13_
  85.7 7.7 %shard_map.267 = (bf16[8,2,48,4096]{3,2,1,0:T(8,128)(2,1)}, bf16[128,384]{1,0:T(8,128)(2,1)}, bf16[128,384]{1,0:T(8,128)(2,1)}) custom-call(s32[2]{0:T(128)} %pad_add_fusion.ids.tie.refs_1_, bf16[64,4224]{1,0:T(8,128)(2,1)} %get-tuple-element.72.refs_0_.refs_7_, bf16[64,4224]{1,0:T(8,128)(2,1)} %copy-done.7, bf16[64,4224]{1,0:T(8,128)(2,1)} %copy-done.6, ...), custom_call_target="tpu_custom_call" | custom-call | flops 1409286144 | bytes 9961472 | tf_op jit(solution)/shard_map/pallas_call | solution.py:182
  95.1 6.6 %all-to-all-start.1 = ((bf16[8,2,48,4096]{3,2,1,0:T(8,128)(2,1)}), bf16[8,2,48,4096]{3,2,1,0:T(8,128)(2,1)}, u32[]{:S(2)}, u32[]{:S(2)}) async-start(bf16[8,2,48,4096]{3,2,1,0:T(8,128)(2,1)} %get-tuple-element.80), calls=%async_computation.1 | async-start | bytes 12582912 | tf_op jit(solution)/shard_map/all_to_all | solution.py:472
  101.8 2.3 collective-permute-start.14
  104.1 2.0 collective-permute-start.15
  106.4 15.9 %shard_map.266.refs_0_ = bf16[384,4096]{1,0:T(8,128)(2,1)} custom-call(s32[2]{0:T(128)} %pad_add_fusion.ids.tie.refs_1_, bf16[384,4096]{1,0:T(8,128)(2,1)} %bitcast.35, bf16[4096,768]{1,0:T(8,128)(2,1)} %bitcast.18, bf16[4096,768]{1,0:T(8,128)(2,1)} %bitcast.22, bf16[768,4096]{1,0:T(8,128)(2,1)} %bitcast.26), custom_call_target="tpu_custom_call" | custom-call | flops 7247757312 | bytes 25165824 | tf_op jit(solution)/shard_map/pallas_call | solution.py:404
  122.3 14.9 %collective-permute-done.14.refs_1_ = bf16[96,4096]{1,0:T(8,128)(2,1)S(1)} collective-permute-done((bf16[96,4096]{1,0:T(8,128)(2,1)S(1)}, bf16[96,4096]{1,0:T(8,128)(2,1)S(1)}, u32[]{:S(2)}, u32[]{:S(2)}) %collective-permute-start.14) | collective-permute-done | bytes 786464 | tf_op jit(solution)/shard_map/ppermute | solution.py:38
  137.2 19.4 %collective-permute-done.15.refs_2_ = bf16[96,4096]{1,0:T(8,128)(2,1)} collective-permute-done((bf16[96,4096]{1,0:T(8,128)(2,1)S(1)}, bf16[96,4096]{1,0:T(8,128)(2,1)}, u32[]{:S(2)}, u32[]{:S(2)}) %collective-permute-start.15) | collective-permute-done | bytes 786464 | tf_op jit(solution)/shard_map/ppermute | solution.py:38
  156.6 17.9 %collective-permute-done.16.refs_3_ = bf16[96,4096]{1,0:T(8,128)(2,1)} collective-permute-done((bf16[96,4096]{1,0:T(8,128)(2,1)S(1)}, bf16[96,4096]{1,0:T(8,128)(2,1)}, u32[]{:S(2)}, u32[]{:S(2)}) %collective-permute-start.16) | collective-permute-done | bytes 786464 | tf_op jit(solution)/shard_map/ppermute | solution.py:38
  174.5 1.3 convert_add_fusion.4.refs_2_
  175.8 4.9 %all-to-all-start.2 = ((bf16[8,48,4096]{2,1,0:T(8,128)(2,1)}), bf16[8,48,4096]{2,1,0:T(8,128)(2,1)S(1)}, u32[]{:S(2)}, u32[]{:S(2)}) async-start(bf16[8,48,4096]{2,1,0:T(8,128)(2,1)} %bitcast.33), calls=%async_computation.2 | async-start | bytes 6291456 | tf_op jit(solution)/shard_map/all_to_all | solution.py:472
  180.7 16.2 %shard_map.271 = (bf16[96,4096]{1,0:T(8,128)(2,1)}, bf16[96,4096]{1,0:T(8,128)(2,1)}, bf16[48,4096]{1,0:T(8,128)(2,1)}, bf16[48,4096]{1,0:T(8,128)(2,1)}, bf16[4...) custom-call(s32[2]{0:T(128)} %get-tuple-element.84.tie.refs_0_, bf16[96,4096]{1,0:T(8,128)(2,1)} %get-tuple-element.85.refs_0_, ...), custom_call_target="tpu_custom_call" | custom-call | flops 7247757312 | bytes 25165824 | tf_op jit(solution)/shard_map/pallas_call | solution.py:404
  196.9 1.3 slice_convert_fusion.7.refs_1_
  198.2 2.4 collective-permute-start.18
  200.6 15.6 %shard_map.273.refs_0_ = bf16[384,4096]{1,0:T(8,128)(2,1)} custom-call(s32[2]{0:T(128)} %shard_map.272.tie.refs_3_, bf16[8,2,48,4096]{3,2,1,0:T(8,128)(2,1)} %all-to-all-done.1.refs_0_, bf16[4096,768]{1,0:T(8,128)(2,1)} %bitcast.20, bf16[4096,768]{1,0:T(8,128)(2,1)} %bitcast.24, bf16[768,4096]{1,0:T(8,128)(2,1)} %bitcast.28), custom_call_target="tpu_custom_call" | custom-call | flops 7247757312 | bytes 25165824 | tf_op jit(solution)/shard_map/pallas_call | solution.py:404
  216.2 9.5 %collective-permute-done.18.refs_2_ = bf16[48,4096]{1,0:T(8,128)(2,1)S(1)} collective-permute-done((bf16[48,4096]{1,0:T(8,128)(2,1)}, bf16[48,4096]{1,0:T(8,128)(2,1)S(1)}, u32[]{:S(2)}, u32[]{:S(2)}) %collective-permute-start.18) | collective-permute-done | bytes 393248 | tf_op jit(solution)/shard_map/ppermute | solution.py:38
  225.7 1.7 convert_add_fusion.3.refs_4_
  227.5 5.3 %all-to-all-start.3 = ((bf16[8,48,4096]{2,1,0:T(8,128)(2,1)}), bf16[8,48,4096]{2,1,0:T(8,128)(2,1)}, u32[]{:S(2)}, u32[]{:S(2)}) async-start(bf16[8,48,4096]{2,1,0:T(8,128)(2,1)} %bitcast.17), calls=%async_computation.3 | async-start | bytes 6291456 | tf_op jit(solution)/shard_map/all_to_all | solution.py:472
  233.7 15.6 %shard_map.275.refs_0_ = bf16[384,4096]{1,0:T(8,128)(2,1)} custom-call(s32[2]{0:T(128)} %get-tuple-element.92.tie, bf16[8,2,48,4096]{3,2,1,0:T(8,128)(2,1)} %all-to-all-done.1.refs_0_, bf16[4096,768]{1,0:T(8,128)(2,1)} %bitcast.21, bf16[4096,768]{1,0:T(8,128)(2,1)} %bitcast.25, bf16[768,4096]{1,0:T(8,128)(2,1)} %bitcast.29), custom_call_target="tpu_custom_call" | custom-call | flops 7247757312 | bytes 25165824 | tf_op jit(solution)/shard_map/pallas_call | solution.py:404
  249.3 1.3 slice_convert_fusion.4.refs_1_
  250.6 4.4 %shard_map.277 = (f32[32,4096]{1,0:T(8,128)}, bf16[32,4096]{1,0:T(8,128)(2,1)}, bf16[32,4096]{1,0:T(8,128)(2,1)}, bf16[32,4096]{1,0:T(8,128)(2,1)}) custom-call(bf16[128,384]{1,0:T(8,128)(2,1)} %shard_map.276.mixing, bf16[384,4096]{1,0:T(8,128)(2,1)} %bitcast.31), custom_call_target="tpu_custom_call" | custom-call | flops 402653184 | bytes 4194304 | tf_op jit(solution)/shard_map/pallas_call | solution.py:295
  255.0 4.6 %collective-permute-done.19.refs_3_ = bf16[48,4096]{1,0:T(8,128)(2,1)S(1)} collective-permute-done((bf16[48,4096]{1,0:T(8,128)(2,1)}, bf16[48,4096]{1,0:T(8,128)(2,1)S(1)}, u32[]{:S(2)}, u32[]{:S(2)}) %collective-permute-start.19) | collective-permute-done | bytes 393248 | tf_op jit(solution)/shard_map/ppermute | solution.py:38
  259.6 8.4 %collective-permute-done.20.refs_4_ = bf16[48,4096]{1,0:T(8,128)(2,1)S(1)} collective-permute-done((bf16[48,4096]{1,0:T(8,128)(2,1)}, bf16[48,4096]{1,0:T(8,128)(2,1)S(1)}, u32[]{:S(2)}, u32[]{:S(2)}) %collective-permute-start.20) | collective-permute-done | bytes 393248 | tf_op jit(solution)/shard_map/ppermute | solution.py:38
  268.0 1.3 convert_add_fusion.2.refs_2_
  269.3 6.4 %all-to-all-start.4 = ((bf16[8,48,4096]{2,1,0:T(8,128)(2,1)}), bf16[8,48,4096]{2,1,0:T(8,128)(2,1)S(1)}, u32[]{:S(2)}, u32[]{:S(2)}) async-start(bf16[8,48,4096]{2,1,0:T(8,128)(2,1)} %bitcast.16), calls=%async_computation.4 | async-start | bytes 6291456 | tf_op jit(solution)/shard_map/all_to_all | solution.py:472
  276.0 1.8 collective-permute-start.22
  278.3 4.4 %shard_map.278 = (f32[32,4096]{1,0:T(8,128)}, bf16[32,4096]{1,0:T(8,128)(2,1)}, bf16[32,4096]{1,0:T(8,128)(2,1)}, bf16[32,4096]{1,0:T(8,128)(2,1)}) custom-call(bf16[128,384]{1,0:T(8,128)(2,1)} %get-tuple-element.94.mixing, bf16[384,4096]{1,0:T(8,128)(2,1)} %bitcast.13.landed), custom_call_target="tpu_custom_call" | custom-call | flops 402653184 | bytes 4194304 | tf_op jit(solution)/shard_map/pallas_call | solution.py:295
  282.7 1.9 collective-permute-start.26
  284.6 16.2 %collective-permute-done.21.refs_5_ = bf16[48,4096]{1,0:T(8,128)(2,1)S(1)} collective-permute-done((bf16[48,4096]{1,0:T(8,128)(2,1)}, bf16[48,4096]{1,0:T(8,128)(2,1)S(1)}, u32[]{:S(2)}, u32[]{:S(2)}) %collective-permute-start.21) | collective-permute-done | bytes 393248 | tf_op jit(solution)/shard_map/ppermute | solution.py:38
  301.5 5.7 %shard_map.280 = (f32[128,2048]{1,0:T(8,128)}, bf16[128,2048]{1,0:T(8,128)(2,1)}, f32[128,2048]{1,0:T(8,128)}, bf16[128,2048]{1,0:T(8,128)(2,1)}) custom-call(bf16[256,384]{1,0:T(8,128)(2,1)} %get-tuple-element.97.mixing_a, bf16[256,384]{1,0:T(8,128)(2,1)} %get-tuple-element.98.mixing_b, bf16[96,4096]{1,0:T(8,128)(2,1)} %get-tuple-element.86.refs_0_, ...), custom_call_target="tpu_custom_call" | custom-call | flops 805306368 | bytes 5242880 | tf_op jit(solution)/shard_map/pallas_call | solution.py:337
  307.2 2.9 all-to-all-done.4
  310.1 1.7 copy-done.1
  311.8 4.4 %shard_map.281 = (f32[32,4096]{1,0:T(8,128)}, bf16[32,4096]{1,0:T(8,128)(2,1)}, bf16[32,4096]{1,0:T(8,128)(2,1)}, bf16[32,4096]{1,0:T(8,128)(2,1)}) custom-call(bf16[128,384]{1,0:T(8,128)(2,1)} %get-tuple-element.107.mixing, bf16[384,4096]{1,0:T(8,128)(2,1)} %bitcast.32), custom_call_target="tpu_custom_call" | custom-call | flops 402653184 | bytes 4194304 | tf_op jit(solution)/shard_map/pallas_call | solution.py:295
  316.1 1.3 slice_convert_fusion.6.refs_6_
  317.9 6.3 %collective-permute-done.26 = bf16[32,4096]{1,0:T(8,128)(2,1)} collective-permute-done((bf16[32,4096]{1,0:T(8,128)(2,1)}, bf16[32,4096]{1,0:T(8,128)(2,1)}, u32[]{:S(2)}, u32[]{:S(2)}) %collective-permute-start.26) | collective-permute-done | bytes 262176 | tf_op jit(solution)/shard_map/ppermute | solution.py:38
  324.2 5.9 %collective-permute-start.29 = (bf16[32,4096]{1,0:T(8,128)(2,1)}, bf16[32,4096]{1,0:T(8,128)(2,1)}, u32[]{:S(2)}, u32[]{:S(2)}) collective-permute-start(bf16[32,4096]{1,0:T(8,128)(2,1)} %get-tuple-element.109), channel_id=1, source_target_pairs={{0,1},{1,0},{2,3},{3,2},{4,5},{5,4},{6,7},{7,6},{8,9},{9,8},{10,11... | collective-permute-start | bytes 786440 | tf_op jit(solution)/shard_map/ppermute | solution.py:38
  330.0 4.4 %collective-permute-done.27 = bf16[32,4096]{1,0:T(8,128)(2,1)} collective-permute-done((bf16[32,4096]{1,0:T(8,128)(2,1)}, bf16[32,4096]{1,0:T(8,128)(2,1)}, u32[]{:S(2)}, u32[]{:S(2)}) %collective-permute-start.27) | collective-permute-done | bytes 262176 | tf_op jit(solution)/shard_map/ppermute | solution.py:38
  334.5 1.5 add_convert_fusion.1
  337.5 13.7 %collective-permute-done.24 = bf16[32,4096]{1,0:T(8,128)(2,1)S(1)} collective-permute-done((bf16[32,4096]{1,0:T(8,128)(2,1)S(1)}, bf16[32,4096]{1,0:T(8,128)(2,1)S(1)}, u32[]{:S(2)}, u32[]{:S(2)}) %collective-permute-start.24) | collective-permute-done | bytes 262176 | tf_op jit(solution)/shard_map/ppermute | solution.py:38
  351.2 1.4 collective-permute-start.34
  354.8 9.6 %collective-permute-done.34 = bf16[128,2048]{1,0:T(8,128)(2,1)S(1)} collective-permute-done((bf16[128,2048]{1,0:T(8,128)(2,1)}, bf16[128,2048]{1,0:T(8,128)(2,1)S(1)}, u32[]{:S(2)}, u32[]{:S(2)}) %collective-permute-start.34) | collective-permute-done | bytes 524320 | tf_op jit(solution)/shard_map/ppermute | solution.py:38
  365.3 1.4 collective-permute-start.35
  366.6 1.4 add_convert_fusion
  368.0 2.0 collective-permute-done.32
  370.1 1.4 collective-permute-start.33
  371.6 2.7 collective-permute-start.36
  (117 shorter events, 22.9 us)
Async XLA Ops:
  2.9 19.3 %collective-permute-start.2 = (bf16[32,4224]{1,0:T(8,128)(2,1)}, bf16[32,4224]{1,0:T(8,128)(2,1)S(1)}, u32[]{:S(2)}, u32[]{:S(2)}) collective-permute-start(bf16[32,4224]{1,0:T(8,128)(2,1)} %get-tuple-element.65.refs_0_.refs_4_), channel_id=1, source_target_pairs={{0,3},{1,2},{2,1},{3,0},{4,7},{5,6},{6,5},{7,4},{8,11},{9,10},{10,... | collective-permute-start | bytes 811016 | tf_op jit(solution)/shard_map/ppermute | solution.py:38
  4.2 22.8 %collective-permute-start.1 = (bf16[32,4224]{1,0:T(8,128)(2,1)}, bf16[32,4224]{1,0:T(8,128)(2,1)S(1)}, u32[]{:S(2)}, u32[]{:S(2)}) collective-permute-start(bf16[32,4224]{1,0:T(8,128)(2,1)} %get-tuple-element.65.refs_0_.refs_4_), channel_id=1, source_target_pairs={{0,2},{1,3},{2,0},{3,1},{4,6},{5,7},{6,4},{7,5},{8,10},{9,11},{10,... | collective-permute-start | bytes 811016 | tf_op jit(solution)/shard_map/ppermute | solution.py:38
  5.2 21.8 %collective-permute-start = (bf16[32,4224]{1,0:T(8,128)(2,1)}, bf16[32,4224]{1,0:T(8,128)(2,1)S(1)}, u32[]{:S(2)}, u32[]{:S(2)}) collective-permute-start(bf16[32,4224]{1,0:T(8,128)(2,1)} %get-tuple-element.65.refs_0_.refs_4_), channel_id=1, source_target_pairs={{0,1},{1,0},{2,3},{3,2},{4,5},{5,4},{6,7},{7,6},{8,9},{9,8},{10,11... | collective-permute-start | bytes 811016 | tf_op jit(solution)/shard_map/ppermute | solution.py:38
  6.4 2.6 collective-permute-start.3
  9.1 18.6 %collective-permute-start.4 = (bf16[64,2048]{1,0:T(8,128)(2,1)S(1)}, bf16[64,2048]{1,0:T(8,128)(2,1)S(1)}, u32[]{:S(2)}, u32[]{:S(2)}) collective-permute-start(bf16[64,2048]{1,0:T(8,128)(2,1)S(1)} %slice.92), channel_id=1, source_target_pairs={{0,8},{4,12},{8,0},{12,4},{16,24},{20,28},{24,16},{28,20},{1,9},{5... | collective-permute-start | bytes 786440 | tf_op jit(solution)/shard_map/ppermute | solution.py:38
  10.4 18.2 %collective-permute-start.5 = (bf16[64,2176]{1,0:T(8,128)(2,1)S(1)}, bf16[64,2176]{1,0:T(8,128)(2,1)S(1)}, u32[]{:S(2)}, u32[]{:S(2)}) collective-permute-start(bf16[64,2176]{1,0:T(8,128)(2,1)S(1)} %slice.93), channel_id=1, source_target_pairs={{0,16},{4,20},{8,24},{12,28},{16,0},{20,4},{24,8},{28,12},{1,17},{... | collective-permute-start | bytes 835592 | tf_op jit(solution)/shard_map/ppermute | solution.py:38
  22.3 16.3 %copy-start.10 = (bf16[32,4224]{1,0:T(8,128)(2,1)}, bf16[32,4224]{1,0:T(8,128)(2,1)S(1)}, u32[]{:S(2)}) copy-start(bf16[32,4224]{1,0:T(8,128)(2,1)S(1)} %collective-permute-done.2.refs_3_.refs_7_) | copy-start | bytes 811012
  27.1 11.5 %copy-start.11 = (bf16[32,4224]{1,0:T(8,128)(2,1)}, bf16[32,4224]{1,0:T(8,128)(2,1)S(1)}, u32[]{:S(2)}) copy-start(bf16[32,4224]{1,0:T(8,128)(2,1)S(1)} %collective-permute-done.1.refs_2_.refs_6_) | copy-start | bytes 811012
  27.1 11.5 %copy-start.12 = (bf16[32,4224]{1,0:T(8,128)(2,1)}, bf16[32,4224]{1,0:T(8,128)(2,1)S(1)}, u32[]{:S(2)}) copy-start(bf16[32,4224]{1,0:T(8,128)(2,1)S(1)} %collective-permute-done.refs_1_.refs_5_) | copy-start | bytes 811012
  29.4 14.6 %collective-permute-start.9 = (bf16[64,4224]{1,0:T(8,128)(2,1)}, bf16[64,4224]{1,0:T(8,128)(2,1)S(1)}, u32[]{:S(2)}, u32[]{:S(2)}) collective-permute-start(bf16[64,4224]{1,0:T(8,128)(2,1)} %get-tuple-element.72.refs_0_.refs_7_), channel_id=1, source_target_pairs={{3,2},{2,1},{1,0},{7,6},{6,5},{5,4},{11,10},{10,9},{9,8},{15,14},{... | collective-permute-start | bytes 1622024 | tf_op jit(solution)/shard_map/ppermute | solution.py:54
  33.5 14.2 %collective-permute-start.8 = (bf16[64,4224]{1,0:T(8,128)(2,1)}, bf16[64,4224]{1,0:T(8,128)(2,1)S(1)}, u32[]{:S(2)}, u32[]{:S(2)}) collective-permute-start(bf16[64,4224]{1,0:T(8,128)(2,1)} %get-tuple-element.72.refs_0_.refs_7_), channel_id=1, source_target_pairs={{0,1},{1,2},{2,3},{4,5},{5,6},{6,7},{8,9},{9,10},{10,11},{12,13},{... | collective-permute-start | bytes 1622024 | tf_op jit(solution)/shard_map/ppermute | solution.py:54
  35.4 13.0 %collective-permute-start.7 = (bf16[128,2176]{1,0:T(8,128)(2,1)}, bf16[128,2176]{1,0:T(8,128)(2,1)S(1)}, u32[]{:S(2)}, u32[]{:S(2)}) collective-permute-start(bf16[128,2176]{1,0:T(8,128)(2,1)} %get-tuple-element.71.b0.t0), channel_id=1, source_target_pairs={{0,8},{4,12},{8,0},{12,4},{16,24},{20,28},{24,16},{28,20},{1,9},{5... | collective-permute-start | bytes 1671176 | tf_op jit(solution)/shard_map/ppermute | solution.py:38
  36.7 11.7 %collective-permute-start.6 = (bf16[128,2048]{1,0:T(8,128)(2,1)}, bf16[128,2048]{1,0:T(8,128)(2,1)S(1)}, u32[]{:S(2)}, u32[]{:S(2)}) collective-permute-start(bf16[128,2048]{1,0:T(8,128)(2,1)} %get-tuple-element.70.a0), channel_id=1, source_target_pairs={{0,16},{4,20},{8,24},{12,28},{16,0},{20,4},{24,8},{28,12},{1,17},{... | collective-permute-start | bytes 1572872 | tf_op jit(solution)/shard_map/ppermute | solution.py:38
  44.0 5.4 %copy-start.6 = (bf16[64,4224]{1,0:T(8,128)(2,1)}, bf16[64,4224]{1,0:T(8,128)(2,1)S(1)}, u32[]{:S(2)}) copy-start(bf16[64,4224]{1,0:T(8,128)(2,1)S(1)} %collective-permute-done.9.refs_2_.refs_9_) | copy-start | bytes 1622020
  47.7 1.7 copy-start.7
  48.4 0.8 copy-start.9
  48.4 1.0 copy-start.2
  49.4 44.0 %all-to-all-start = ((bf16[8,1,48,4096]{3,2,1,0:T(8,128)(2,1)}), bf16[8,1,48,4096]{3,2,1,0:T(8,128)(2,1)S(1)}, u32[]{:S(2)}, u32[]{:S(2)}) async-start(bf16[8,1,48,4096]{3,2,1,0:T(8,128)(2,1)} %get-tuple-element.73), calls=%async_computation | async-start | bytes 6291456 | tf_op jit(solution)/shard_map/all_to_all | solution.py:472
  55.8 15.8 %collective-permute-start.11 = (bf16[64,4224]{1,0:T(8,128)(2,1)}, bf16[64,4224]{1,0:T(8,128)(2,1)S(1)}, u32[]{:S(2)}, u32[]{:S(2)}) collective-permute-start(bf16[64,4224]{1,0:T(8,128)(2,1)} %copy-done.6), channel_id=1, source_target_pairs={{2,1},{1,0},{6,5},{5,4},{10,9},{9,8},{14,13},{13,12},{18,17},{17,1... | collective-permute-start | bytes 1622024 | tf_op jit(solution)/shard_map/ppermute | solution.py:54
  59.2 16.6 %collective-permute-start.10 = (bf16[64,4224]{1,0:T(8,128)(2,1)}, bf16[64,4224]{1,0:T(8,128)(2,1)}, u32[]{:S(2)}, u32[]{:S(2)}) collective-permute-start(bf16[64,4224]{1,0:T(8,128)(2,1)} %copy-done.7), channel_id=1, source_target_pairs={{1,2},{2,3},{5,6},{6,7},{9,10},{10,11},{13,14},{14,15},{17,18},{18... | collective-permute-start | bytes 1622024 | tf_op jit(solution)/shard_map/ppermute | solution.py:54
  71.7 14.0 %copy-start.8 = (bf16[64,4224]{1,0:T(8,128)(2,1)}, bf16[64,4224]{1,0:T(8,128)(2,1)S(1)}, u32[]{:S(2)}) copy-start(bf16[64,4224]{1,0:T(8,128)(2,1)S(1)} %collective-permute-done.11.refs_4_.refs_11_) | copy-start | bytes 1622020
  71.7 14.0 %collective-permute-start.13 = (bf16[64,4224]{1,0:T(8,128)(2,1)S(1)}, bf16[64,4224]{1,0:T(8,128)(2,1)}, u32[]{:S(2)}, u32[]{:S(2)}) collective-permute-start(bf16[64,4224]{1,0:T(8,128)(2,1)S(1)} %collective-permute-done.11.refs_4_.refs_11_), channel_id=1, source_target_pairs={{1,0},{5,4},{9,8},{13,12},{17,16},{21,20},{25,24},{29,28}} | collective-permute-start | bytes 1622024 | tf_op jit(solution)/shard_map/ppermute | solution.py:54
  75.9 9.8 %collective-permute-start.12 = (bf16[64,4224]{1,0:T(8,128)(2,1)}, bf16[64,4224]{1,0:T(8,128)(2,1)}, u32[]{:S(2)}, u32[]{:S(2)}) collective-permute-start(bf16[64,4224]{1,0:T(8,128)(2,1)} %collective-permute-done.10.refs_3_.refs_10_), channel_id=1, source_target_pairs={{2,3},{6,7},{10,11},{14,15},{18,19},{22,23},{26,27},{30,31}} | collective-permute-start | bytes 1622024 | tf_op jit(solution)/shard_map/ppermute | solution.py:54
  93.4 1.7 copy-start.5
  95.1 6.6 %copy-start.13 = (bf16[96,4096]{1,0:T(8,128)(2,1)S(1)}, bf16[96,4096]{1,0:T(8,128)(2,1)}, u32[]{:S(2)}) copy-start(bf16[96,4096]{1,0:T(8,128)(2,1)} %get-tuple-element.81) | copy-start | bytes 2359300
  95.1 8.9 %copy-start.14 = (bf16[96,4096]{1,0:T(8,128)(2,1)S(1)}, bf16[96,4096]{1,0:T(8,128)(2,1)}, u32[]{:S(2)}) copy-start(bf16[96,4096]{1,0:T(8,128)(2,1)} %get-tuple-element.82) | copy-start | bytes 2359300
  95.1 11.0 %copy-start.15 = (bf16[96,4096]{1,0:T(8,128)(2,1)S(1)}, bf16[96,4096]{1,0:T(8,128)(2,1)}, u32[]{:S(2)}) copy-start(bf16[96,4096]{1,0:T(8,128)(2,1)} %get-tuple-element.83) | copy-start | bytes 2359300
  95.1 79.4 %all-to-all-start.1 = ((bf16[8,2,48,4096]{3,2,1,0:T(8,128)(2,1)}), bf16[8,2,48,4096]{3,2,1,0:T(8,128)(2,1)}, u32[]{:S(2)}, u32[]{:S(2)}) async-start(bf16[8,2,48,4096]{3,2,1,0:T(8,128)(2,1)} %get-tuple-element.80), calls=%async_computation.1 | async-start | bytes 12582912 | tf_op jit(solution)/shard_map/all_to_all | solution.py:472
  101.8 35.5 %collective-permute-start.14 = (bf16[96,4096]{1,0:T(8,128)(2,1)S(1)}, bf16[96,4096]{1,0:T(8,128)(2,1)S(1)}, u32[]{:S(2)}, u32[]{:S(2)}) collective-permute-start(bf16[96,4096]{1,0:T(8,128)(2,1)S(1)} %copy-done.13), channel_id=1, source_target_pairs={{0,1},{1,0},{2,3},{3,2},{4,5},{5,4},{6,7},{7,6},{8,9},{9,8},{10,11... | collective-permute-start | bytes 2359304 | tf_op jit(solution)/shard_map/ppermute | solution.py:38
  104.1 52.5 %collective-permute-start.15 = (bf16[96,4096]{1,0:T(8,128)(2,1)S(1)}, bf16[96,4096]{1,0:T(8,128)(2,1)}, u32[]{:S(2)}, u32[]{:S(2)}) collective-permute-start(bf16[96,4096]{1,0:T(8,128)(2,1)S(1)} %copy-done.14), channel_id=1, source_target_pairs={{0,2},{1,3},{2,0},{3,1},{4,6},{5,7},{6,4},{7,5},{8,10},{9,11},{10,... | collective-permute-start | bytes 2359304 | tf_op jit(solution)/shard_map/ppermute | solution.py:38
  106.1 68.4 %collective-permute-start.16 = (bf16[96,4096]{1,0:T(8,128)(2,1)S(1)}, bf16[96,4096]{1,0:T(8,128)(2,1)}, u32[]{:S(2)}, u32[]{:S(2)}) collective-permute-start(bf16[96,4096]{1,0:T(8,128)(2,1)S(1)} %copy-done.15), channel_id=1, source_target_pairs={{0,3},{1,2},{2,1},{3,0},{4,7},{5,6},{6,5},{7,4},{8,11},{9,10},{10,... | collective-permute-start | bytes 2359304 | tf_op jit(solution)/shard_map/ppermute | solution.py:38
  137.2 38.6 %copy-start.20 = (bf16[96,4096]{1,0:T(8,128)(2,1)}, bf16[96,4096]{1,0:T(8,128)(2,1)S(1)}, u32[]{:S(2)}) copy-start(bf16[96,4096]{1,0:T(8,128)(2,1)S(1)} %collective-permute-done.14.refs_1_) | copy-start | bytes 2359300
  175.8 49.9 %all-to-all-start.2 = ((bf16[8,48,4096]{2,1,0:T(8,128)(2,1)}), bf16[8,48,4096]{2,1,0:T(8,128)(2,1)S(1)}, u32[]{:S(2)}, u32[]{:S(2)}) async-start(bf16[8,48,4096]{2,1,0:T(8,128)(2,1)} %bitcast.33), calls=%async_computation.2 | async-start | bytes 6291456 | tf_op jit(solution)/shard_map/all_to_all | solution.py:472
  196.9 28.8 %collective-permute-start.17 = (bf16[96,4096]{1,0:T(8,128)(2,1)}, bf16[96,4096]{1,0:T(8,128)(2,1)}, u32[]{:S(2)}, u32[]{:S(2)}) collective-permute-start(bf16[96,4096]{1,0:T(8,128)(2,1)} %get-tuple-element.90), channel_id=1, source_target_pairs={{0,1},{1,0},{2,3},{3,2},{4,5},{5,4},{6,7},{7,6},{8,9},{9,8},{10,11... | collective-permute-start | bytes 2359304 | tf_op jit(solution)/shard_map/ppermute | solution.py:38
  198.2 27.5 %collective-permute-start.18 = (bf16[48,4096]{1,0:T(8,128)(2,1)}, bf16[48,4096]{1,0:T(8,128)(2,1)S(1)}, u32[]{:S(2)}, u32[]{:S(2)}) collective-permute-start(bf16[48,4096]{1,0:T(8,128)(2,1)} %get-tuple-element.91), channel_id=1, source_target_pairs={{0,2},{1,3},{2,0},{3,1},{4,6},{5,7},{6,4},{7,5},{8,10},{9,11},{10,... | collective-permute-start | bytes 1179656 | tf_op jit(solution)/shard_map/ppermute | solution.py:38
  225.7 1.8 copy-start.16
  225.7 1.8 copy-start
  227.5 40.5 %all-to-all-start.3 = ((bf16[8,48,4096]{2,1,0:T(8,128)(2,1)}), bf16[8,48,4096]{2,1,0:T(8,128)(2,1)}, u32[]{:S(2)}, u32[]{:S(2)}) async-start(bf16[8,48,4096]{2,1,0:T(8,128)(2,1)} %bitcast.17), calls=%async_computation.3 | async-start | bytes 6291456 | tf_op jit(solution)/shard_map/all_to_all | solution.py:472
  232.8 26.8 %collective-permute-start.19 = (bf16[48,4096]{1,0:T(8,128)(2,1)}, bf16[48,4096]{1,0:T(8,128)(2,1)S(1)}, u32[]{:S(2)}, u32[]{:S(2)}) collective-permute-start(bf16[48,4096]{1,0:T(8,128)(2,1)} %get-tuple-element.99), channel_id=1, source_target_pairs={{0,2},{1,3},{2,0},{3,1},{4,6},{5,7},{6,4},{7,5},{8,10},{9,11},{10,... | collective-permute-start | bytes 1179656 | tf_op jit(solution)/shard_map/ppermute | solution.py:38
  233.7 34.3 %collective-permute-start.20 = (bf16[48,4096]{1,0:T(8,128)(2,1)}, bf16[48,4096]{1,0:T(8,128)(2,1)S(1)}, u32[]{:S(2)}, u32[]{:S(2)}) collective-permute-start(bf16[48,4096]{1,0:T(8,128)(2,1)} %get-tuple-element.100), channel_id=1, source_target_pairs={{0,3},{1,2},{2,1},{3,0},{4,7},{5,6},{6,5},{7,4},{8,11},{9,10},{10,... | collective-permute-start | bytes 1179656 | tf_op jit(solution)/shard_map/ppermute | solution.py:38
  259.6 9.8 %copy-start.17 = (bf16[48,4096]{1,0:T(8,128)(2,1)}, bf16[48,4096]{1,0:T(8,128)(2,1)S(1)}, u32[]{:S(2)}) copy-start(bf16[48,4096]{1,0:T(8,128)(2,1)S(1)} %collective-permute-done.19.refs_3_) | copy-start | bytes 1179652
  268.0 1.3 copy-start.18
  269.3 40.7 %all-to-all-start.4 = ((bf16[8,48,4096]{2,1,0:T(8,128)(2,1)}), bf16[8,48,4096]{2,1,0:T(8,128)(2,1)S(1)}, u32[]{:S(2)}, u32[]{:S(2)}) async-start(bf16[8,48,4096]{2,1,0:T(8,128)(2,1)} %bitcast.16), calls=%async_computation.4 | async-start | bytes 6291456 | tf_op jit(solution)/shard_map/all_to_all | solution.py:472
  275.7 25.1 %collective-permute-start.21 = (bf16[48,4096]{1,0:T(8,128)(2,1)}, bf16[48,4096]{1,0:T(8,128)(2,1)S(1)}, u32[]{:S(2)}, u32[]{:S(2)}) collective-permute-start(bf16[48,4096]{1,0:T(8,128)(2,1)} %get-tuple-element.102), channel_id=1, source_target_pairs={{0,3},{1,2},{2,1},{3,0},{4,7},{5,6},{6,5},{7,4},{8,11},{9,10},{10,... | collective-permute-start | bytes 1179656 | tf_op jit(solution)/shard_map/ppermute | solution.py:38
  276.0 60.0 %collective-permute-start.22 = (bf16[32,4096]{1,0:T(8,128)(2,1)}, bf16[32,4096]{1,0:T(8,128)(2,1)S(1)}, u32[]{:S(2)}, u32[]{:S(2)}) collective-permute-start(bf16[32,4096]{1,0:T(8,128)(2,1)} %get-tuple-element.111), channel_id=1, source_target_pairs={{0,1},{1,0},{2,3},{3,2},{4,5},{5,4},{6,7},{7,6},{8,9},{9,8},{10,11... | collective-permute-start | bytes 786440 | tf_op jit(solution)/shard_map/ppermute | solution.py:38
  277.8 58.5 %collective-permute-start.23 = (bf16[32,4096]{1,0:T(8,128)(2,1)}, bf16[32,4096]{1,0:T(8,128)(2,1)}, u32[]{:S(2)}, u32[]{:S(2)}) collective-permute-start(bf16[32,4096]{1,0:T(8,128)(2,1)} %get-tuple-element.112), channel_id=1, source_target_pairs={{0,2},{1,3},{2,0},{3,1},{4,6},{5,7},{6,4},{7,5},{8,10},{9,11},{10,... | collective-permute-start | bytes 786440 | tf_op jit(solution)/shard_map/ppermute | solution.py:38
  282.7 34.8 %collective-permute-start.25 = (bf16[32,4096]{1,0:T(8,128)(2,1)}, bf16[32,4096]{1,0:T(8,128)(2,1)}, u32[]{:S(2)}, u32[]{:S(2)}) collective-permute-start(bf16[32,4096]{1,0:T(8,128)(2,1)} %get-tuple-element.115), channel_id=1, source_target_pairs={{0,1},{1,0},{2,3},{3,2},{4,5},{5,4},{6,7},{7,6},{8,9},{9,8},{10,11... | collective-permute-start | bytes 786440 | tf_op jit(solution)/shard_map/ppermute | solution.py:38
  282.7 41.5 %collective-permute-start.26 = (bf16[32,4096]{1,0:T(8,128)(2,1)}, bf16[32,4096]{1,0:T(8,128)(2,1)}, u32[]{:S(2)}, u32[]{:S(2)}) collective-permute-start(bf16[32,4096]{1,0:T(8,128)(2,1)} %get-tuple-element.116), channel_id=1, source_target_pairs={{0,2},{1,3},{2,0},{3,1},{4,6},{5,7},{6,4},{7,5},{8,10},{9,11},{10,... | collective-permute-start | bytes 786440 | tf_op jit(solution)/shard_map/ppermute | solution.py:38
  300.8 0.8 copy-start.19
  300.8 33.7 %collective-permute-start.27 = (bf16[32,4096]{1,0:T(8,128)(2,1)}, bf16[32,4096]{1,0:T(8,128)(2,1)}, u32[]{:S(2)}, u32[]{:S(2)}) collective-permute-start(bf16[32,4096]{1,0:T(8,128)(2,1)} %get-tuple-element.117), channel_id=1, source_target_pairs={{0,3},{1,2},{2,1},{3,0},{4,7},{5,6},{6,5},{7,4},{8,11},{9,10},{10,... | collective-permute-start | bytes 786440 | tf_op jit(solution)/shard_map/ppermute | solution.py:38
  310.1 1.7 copy-start.1
  316.1 1.3 copy-start.21
  317.5 36.4 %copy-start.3 = (f32[128,2048]{1,0:T(8,128)S(1)}, f32[128,2048]{1,0:T(8,128)}, u32[]{:S(2)}) copy-start(f32[128,2048]{1,0:T(8,128)} %get-tuple-element.119) | copy-start | bytes 3145732
  317.5 33.8 %collective-permute-start.24 = (bf16[32,4096]{1,0:T(8,128)(2,1)S(1)}, bf16[32,4096]{1,0:T(8,128)(2,1)S(1)}, u32[]{:S(2)}, u32[]{:S(2)}) collective-permute-start(bf16[32,4096]{1,0:T(8,128)(2,1)S(1)} %copy-done.21), channel_id=1, source_target_pairs={{0,3},{1,2},{2,1},{3,0},{4,7},{5,6},{6,5},{7,4},{8,11},{9,10},{10,... | collective-permute-start | bytes 786440 | tf_op jit(solution)/shard_map/ppermute | solution.py:38
  324.2 42.4 %collective-permute-start.29 = (bf16[32,4096]{1,0:T(8,128)(2,1)}, bf16[32,4096]{1,0:T(8,128)(2,1)}, u32[]{:S(2)}, u32[]{:S(2)}) collective-permute-start(bf16[32,4096]{1,0:T(8,128)(2,1)} %get-tuple-element.109), channel_id=1, source_target_pairs={{0,1},{1,0},{2,3},{3,2},{4,5},{5,4},{6,7},{7,6},{8,9},{9,8},{10,11... | collective-permute-start | bytes 786440 | tf_op jit(solution)/shard_map/ppermute | solution.py:38
  334.5 32.1 %collective-permute-start.30 = (bf16[32,4096]{1,0:T(8,128)(2,1)}, bf16[32,4096]{1,0:T(8,128)(2,1)}, u32[]{:S(2)}, u32[]{:S(2)}) collective-permute-start(bf16[32,4096]{1,0:T(8,128)(2,1)} %get-tuple-element.121), channel_id=1, source_target_pairs={{0,2},{1,3},{2,0},{3,1},{4,6},{5,7},{6,4},{7,5},{8,10},{9,11},{10,... | collective-permute-start | bytes 786440 | tf_op jit(solution)/shard_map/ppermute | solution.py:38
  334.5 29.9 %copy-start.4 = (f32[128,2048]{1,0:T(8,128)S(1)}, f32[128,2048]{1,0:T(8,128)}, u32[]{:S(2)}) copy-start(f32[128,2048]{1,0:T(8,128)} %get-tuple-element.123) | copy-start | bytes 3145732
  336.0 30.7 %collective-permute-start.31 = (bf16[32,4096]{1,0:T(8,128)(2,1)}, bf16[32,4096]{1,0:T(8,128)(2,1)}, u32[]{:S(2)}, u32[]{:S(2)}) collective-permute-start(bf16[32,4096]{1,0:T(8,128)(2,1)} %get-tuple-element.122), channel_id=1, source_target_pairs={{0,3},{1,2},{2,1},{3,0},{4,7},{5,6},{6,5},{7,4},{8,11},{9,10},{10,... | collective-permute-start | bytes 786440 | tf_op jit(solution)/shard_map/ppermute | solution.py:38
  336.3 17.6 %collective-permute-start.28 = (bf16[128,2048]{1,0:T(8,128)(2,1)}, bf16[128,2048]{1,0:T(8,128)(2,1)S(1)}, u32[]{:S(2)}, u32[]{:S(2)}) collective-permute-start(bf16[128,2048]{1,0:T(8,128)(2,1)} %get-tuple-element.120), channel_id=1, source_target_pairs={{0,16},{4,20},{8,24},{12,28},{16,0},{20,4},{24,8},{28,12},{1,17},{... | collective-permute-start | bytes 1572872 | tf_op jit(solution)/shard_map/ppermute | solution.py:38
  351.2 13.2 %collective-permute-start.34 = (bf16[128,2048]{1,0:T(8,128)(2,1)}, bf16[128,2048]{1,0:T(8,128)(2,1)S(1)}, u32[]{:S(2)}, u32[]{:S(2)}) collective-permute-start(bf16[128,2048]{1,0:T(8,128)(2,1)} %get-tuple-element.124), channel_id=1, source_target_pairs={{0,8},{4,12},{8,0},{12,4},{16,24},{20,28},{24,16},{28,20},{1,9},{5... | collective-permute-start | bytes 1572872 | tf_op jit(solution)/shard_map/ppermute | solution.py:38
  354.6 15.4 %collective-permute-start.32 = (bf16[64,2048]{1,0:T(8,128)(2,1)S(1)}, bf16[64,2048]{1,0:T(8,128)(2,1)S(1)}, u32[]{:S(2)}, u32[]{:S(2)}) collective-permute-start(bf16[64,2048]{1,0:T(8,128)(2,1)S(1)} %split.57), channel_id=1, source_target_pairs={{0,8},{4,12},{8,0},{12,4},{16,24},{20,28},{24,16},{28,20},{1,9},{5... | collective-permute-start | bytes 786440 | tf_op jit(solution)/shard_map/ppermute | solution.py:38
  365.3 6.3 %collective-permute-start.35 = (bf16[64,2048]{1,0:T(8,128)(2,1)}, bf16[64,2048]{1,0:T(8,128)(2,1)S(1)}, u32[]{:S(2)}, u32[]{:S(2)}) collective-permute-start(bf16[64,2048]{1,0:T(8,128)(2,1)} %split.56), channel_id=1, source_target_pairs={{0,16},{4,20},{8,24},{12,28},{16,0},{20,4},{24,8},{28,12},{1,17},{... | collective-permute-start | bytes 786440 | tf_op jit(solution)/shard_map/ppermute | solution.py:38
  370.1 4.2 %collective-permute-start.33 = (bf16[32,2048]{1,0:T(8,128)(2,1)S(1)}, bf16[32,2048]{1,0:T(8,128)(2,1)S(1)}, u32[]{:S(2)}, u32[]{:S(2)}) collective-permute-start(bf16[32,2048]{1,0:T(8,128)(2,1)S(1)} %split.59), channel_id=1, source_target_pairs={{0,4},{4,0},{8,12},{12,8},{16,20},{20,16},{24,28},{28,24},{1,5},{5... | collective-permute-start | bytes 393224 | tf_op jit(solution)/shard_map/ppermute | solution.py:38
  371.6 3.7 collective-permute-start.36

commit v13 on v9

--- a/solution.py
+++ b/solution.py
@@ -530,7 +530,7 @@
     out0, tie = fence([out0, ids], [arrived12] + arrived3)
     landed0 = to_experts(out0)
     size = slots // peers
-    sizes = [size] * (peers - 2) + [size * 2 // 3, size // 3] * 2
+    sizes = [size] * (peers - 2) + [size * 2 // 3, size // 3, size - 16, 16]
     last2, last1 = peers - 2, peers - 1
     out3 = list(expert([own3] + arrived3, tie, *weights, sizes=sizes))
     landed3 = out3[:1] + swaps(out3, "local", 1, last1)

time: 375 us -> 374 us (level)
  waiting for transfers between devices: 167 us -> 161 us
  starting transfers between devices: 79 us -> 83.1 us
    ppermute x31, waiting for transfers between devices: 136 us -> 127 us  [swap(): return lax.ppermute(array, axis, [(i, i ^ bits) for i in range(size)])]
    ppermute x31, starting transfers between devices: 31.7 us -> 37.4 us  [swap(): return lax.ppermute(array, axis, [(i, i ^ bits) for i in range(size)])]
    all_to_all x5, waiting for transfers between devices: 14.4 us -> 18.7 us  [to_experts(): return lax.all_to_all(rows, 'node', 0, 0, tiled=True)]
  transfers between devices with their start and end apart: 42 -> 42, of which waited for: 22 -> 19; matrix products, arithmetic and copies ran while one was open for 3% -> 3% of each run, Pallas kernels for 27% -> 27%
where the time goes in v13:
time: 374 us; the launch traced here: 371 us
  waiting for transfers between devices  161 us (43%)
  Pallas kernels  104 us (28%)
  starting transfers between devices  83.1 us (22%)
  other arithmetic  16.7 us (4%)
  local copies, waits for them, and re-layouts  6.11 us (2%)
    ppermute x31, waiting for transfers between devices, swap(): return lax.ppermute(array, axis, [(i, i ^ bits) for i in range(size)])  127 us
    pallas_call x4, Pallas kernels, expert(): pl.pallas_call(functools.partial(expert_kernel, len(parts), first_tiles,...  63.3 us
    ppermute x31, starting transfers between devices, swap(): return lax.ppermute(array, axis, [(i, i ^ bits) for i in range(size)])  37.4 us
    all_to_all x5, starting transfers between devices, to_experts(): return lax.all_to_all(rows, 'node', 0, 0, tiled=True)  27.9 us
    all_to_all x5, waiting for transfers between devices, to_experts(): return lax.all_to_all(rows, 'node', 0, 0, tiled=True)  18.7 us
    ppermute x6, starting transfers between devices, chain_step(): lax.ppermute(a, axis, way)  17.8 us
    ppermute x6, waiting for transfers between devices, chain_step(): lax.ppermute(a, axis, way)  16.2 us
    pallas_call x3, Pallas kernels, mix(): pl.pallas_call(mix_kernel, grid=(TILES,), out_shape=[jax.ShapeDtypeStruct...  13.2 us
  transfers between devices with their start and end apart: 42, of which 19 were waited for; matrix products, arithmetic and copies ran while one was open for 3% of the time, Pallas kernels for 27%

profile of v13, /device:TPU:9, one launch (start us, length us, event | category | flops | bytes accessed | tf_op | source)
XLA Modules:
  0.0 371.5 jit_solution(18226932143054974639)
XLA Ops:
  0.0 2.9 shard_map.262
  2.9 1.3 collective-permute-start.2
  9.1 1.3 collective-permute-start.4
  10.4 1.3 collective-permute-start.5
  11.7 10.6 %collective-permute-done.2.refs_3_.refs_7_ = bf16[32,4224]{1,0:T(8,128)(2,1)S(1)} collective-permute-done((bf16[32,4224]{1,0:T(8,128)(2,1)}, bf16[32,4224]{1,0:T(8,128)(2,1)S(1)}, u32[]{:S(2)}, u32[]{:S(2)}) %collective-permute-start.2) | collective-permute-done | bytes 270368 | tf_op jit(solution)/shard_map/ppermute | solution.py:38
  22.2 4.8 %collective-permute-done.1.refs_2_.refs_6_ = bf16[32,4224]{1,0:T(8,128)(2,1)S(1)} collective-permute-done((bf16[32,4224]{1,0:T(8,128)(2,1)}, bf16[32,4224]{1,0:T(8,128)(2,1)S(1)}, u32[]{:S(2)}, u32[]{:S(2)}) %collective-permute-start.1) | collective-permute-done | bytes 270368 | tf_op jit(solution)/shard_map/ppermute | solution.py:38
  29.4 4.1 %collective-permute-start.9 = (bf16[64,4224]{1,0:T(8,128)(2,1)}, bf16[64,4224]{1,0:T(8,128)(2,1)S(1)}, u32[]{:S(2)}, u32[]{:S(2)}) collective-permute-start(bf16[64,4224]{1,0:T(8,128)(2,1)} %get-tuple-element.72.refs_0_.refs_7_), channel_id=1, source_target_pairs={{3,2},{2,1},{1,0},{7,6},{6,5},{5,4},{11,10},{10,9},{9,8},{15,14},{... | collective-permute-start | bytes 1622024 | tf_op jit(solution)/shard_map/ppermute | solution.py:54
  33.5 1.9 collective-permute-start.8
  35.4 1.3 collective-permute-start.7
  38.6 5.1 %shard_map.263 = (bf16[8,1,48,4096]{3,2,1,0:T(8,128)(2,1)}, bf16[128,384]{1,0:T(8,128)(2,1)}) custom-call(s32[2]{0:T(128)} %pad_add_fusion.ids.tie.refs_1_, bf16[32,4224]{1,0:T(8,128)(2,1)} %get-tuple-element.65.refs_0_.refs_4_, bf16[32,4224]{1,0:T(8,128)(2,1)} %copy-done.12, bf16[32,4224]{1,0:T(8,128)(2,1)} %copy-done.11, bf16[32,4224]{1,0:T(8,128)(2,1)} %copy-done.10, ...), custom_call_target="tpu_custom_call" | custom-call | flops 402653184 | bytes 4194304 | tf_op jit(solution)/shard_map/pallas_call | solution.py:182
  44.0 3.7 %collective-permute-done.8.refs_1_.refs_8_ = bf16[64,4224]{1,0:T(8,128)(2,1)S(1)} collective-permute-done((bf16[64,4224]{1,0:T(8,128)(2,1)}, bf16[64,4224]{1,0:T(8,128)(2,1)S(1)}, u32[]{:S(2)}, u32[]{:S(2)}) %collective-permute-start.8) | collective-permute-done | bytes 540704 | tf_op jit(solution)/shard_map/ppermute | solution.py:54
  49.4 6.4 %all-to-all-start = ((bf16[8,1,48,4096]{3,2,1,0:T(8,128)(2,1)}), bf16[8,1,48,4096]{3,2,1,0:T(8,128)(2,1)S(1)}, u32[]{:S(2)}, u32[]{:S(2)}) async-start(bf16[8,1,48,4096]{3,2,1,0:T(8,128)(2,1)} %get-tuple-element.73), calls=%async_computation | async-start | bytes 6291456 | tf_op jit(solution)/shard_map/all_to_all | solution.py:472
  55.8 3.4 collective-permute-start.11
  59.2 2.8 collective-permute-start.10
  62.0 9.7 %collective-permute-done.11.refs_4_.refs_11_ = bf16[64,4224]{1,0:T(8,128)(2,1)S(1)} collective-permute-done((bf16[64,4224]{1,0:T(8,128)(2,1)}, bf16[64,4224]{1,0:T(8,128)(2,1)S(1)}, u32[]{:S(2)}, u32[]{:S(2)}) %collective-permute-start.11) | collective-permute-done | bytes 540704 | tf_op jit(solution)/shard_map/ppermute | solution.py:54
  71.7 4.2 %collective-permute-start.13 = (bf16[64,4224]{1,0:T(8,128)(2,1)S(1)}, bf16[64,4224]{1,0:T(8,128)(2,1)}, u32[]{:S(2)}, u32[]{:S(2)}) collective-permute-start(bf16[64,4224]{1,0:T(8,128)(2,1)S(1)} %collective-permute-done.11.refs_4_.refs_11_), channel_id=1, source_target_pairs={{1,0},{5,4},{9,8},{13,12},{17,16},{21,20},{25,24},{29,28}} | collective-permute-start | bytes 1622024 | tf_op jit(solution)/shard_map/ppermute | solution.py:54
  75.9 1.5 collective-permute-start.12
  77.3 5.8 %shard_map.268 = (bf16[96,4096]{1,0:T(8,128)(2,1)}, bf16[96,4096]{1,0:T(8,128)(2,1)}, bf16[96,4096]{1,0:T(8,128)(2,1)}, bf16[96,4096]{1,0:T(8,128)(2,1)}, bf16[2...) custom-call(s32[2]{0:T(128)} %pad_add_fusion.ids.tie.refs_1_, bf16[128,2048]{1,0:T(8,128)(2,1)} %get-tuple-element.70.a0, ...), custom_call_target="tpu_custom_call" | custom-call | flops 805306368 | bytes 5242880 | tf_op jit(solution)/shard_map/pallas_call | solution.py:260
  83.2 2.5 collective-permute-done.13.refs_6_.refs_13_
  85.7 7.8 %shard_map.267 = (bf16[8,2,48,4096]{3,2,1,0:T(8,128)(2,1)}, bf16[128,384]{1,0:T(8,128)(2,1)}, bf16[128,384]{1,0:T(8,128)(2,1)}) custom-call(s32[2]{0:T(128)} %pad_add_fusion.ids.tie.refs_1_, bf16[64,4224]{1,0:T(8,128)(2,1)} %get-tuple-element.72.refs_0_.refs_7_, bf16[64,4224]{1,0:T(8,128)(2,1)} %copy-done.7, bf16[64,4224]{1,0:T(8,128)(2,1)} %copy-done.6, ...), custom_call_target="tpu_custom_call" | custom-call | flops 1409286144 | bytes 9961472 | tf_op jit(solution)/shard_map/pallas_call | solution.py:182
  95.1 6.6 %all-to-all-start.1 = ((bf16[8,2,48,4096]{3,2,1,0:T(8,128)(2,1)}), bf16[8,2,48,4096]{3,2,1,0:T(8,128)(2,1)}, u32[]{:S(2)}, u32[]{:S(2)}) async-start(bf16[8,2,48,4096]{3,2,1,0:T(8,128)(2,1)} %get-tuple-element.80), calls=%async_computation.1 | async-start | bytes 12582912 | tf_op jit(solution)/shard_map/all_to_all | solution.py:472
  101.8 2.3 collective-permute-start.14
  104.1 2.0 collective-permute-start.15
  106.4 16.0 %shard_map.266.refs_0_ = bf16[384,4096]{1,0:T(8,128)(2,1)} custom-call(s32[2]{0:T(128)} %pad_add_fusion.ids.tie.refs_1_, bf16[384,4096]{1,0:T(8,128)(2,1)} %bitcast.35, bf16[4096,768]{1,0:T(8,128)(2,1)} %bitcast.18, bf16[4096,768]{1,0:T(8,128)(2,1)} %bitcast.22, bf16[768,4096]{1,0:T(8,128)(2,1)} %bitcast.26), custom_call_target="tpu_custom_call" | custom-call | flops 7247757312 | bytes 25165824 | tf_op jit(solution)/shard_map/pallas_call | solution.py:404
  122.4 14.8 %collective-permute-done.14.refs_1_ = bf16[96,4096]{1,0:T(8,128)(2,1)S(1)} collective-permute-done((bf16[96,4096]{1,0:T(8,128)(2,1)S(1)}, bf16[96,4096]{1,0:T(8,128)(2,1)S(1)}, u32[]{:S(2)}, u32[]{:S(2)}) %collective-permute-start.14) | collective-permute-done | bytes 786464 | tf_op jit(solution)/shard_map/ppermute | solution.py:38
  137.3 19.4 %collective-permute-done.15.refs_2_ = bf16[96,4096]{1,0:T(8,128)(2,1)} collective-permute-done((bf16[96,4096]{1,0:T(8,128)(2,1)S(1)}, bf16[96,4096]{1,0:T(8,128)(2,1)}, u32[]{:S(2)}, u32[]{:S(2)}) %collective-permute-start.15) | collective-permute-done | bytes 786464 | tf_op jit(solution)/shard_map/ppermute | solution.py:38
  156.6 17.9 %collective-permute-done.16.refs_3_ = bf16[96,4096]{1,0:T(8,128)(2,1)} collective-permute-done((bf16[96,4096]{1,0:T(8,128)(2,1)S(1)}, bf16[96,4096]{1,0:T(8,128)(2,1)}, u32[]{:S(2)}, u32[]{:S(2)}) %collective-permute-start.16) | collective-permute-done | bytes 786464 | tf_op jit(solution)/shard_map/ppermute | solution.py:38
  174.5 1.3 convert_add_fusion.4.refs_2_
  175.8 4.9 %all-to-all-start.2 = ((bf16[8,48,4096]{2,1,0:T(8,128)(2,1)}), bf16[8,48,4096]{2,1,0:T(8,128)(2,1)S(1)}, u32[]{:S(2)}, u32[]{:S(2)}) async-start(bf16[8,48,4096]{2,1,0:T(8,128)(2,1)} %bitcast.33), calls=%async_computation.2 | async-start | bytes 6291456 | tf_op jit(solution)/shard_map/all_to_all | solution.py:472
  180.7 16.1 %shard_map.271 = (bf16[96,4096]{1,0:T(8,128)(2,1)}, bf16[96,4096]{1,0:T(8,128)(2,1)}, bf16[64,4096]{1,0:T(8,128)(2,1)}, bf16[32,4096]{1,0:T(8,128)(2,1)}, bf16[8...) custom-call(s32[2]{0:T(128)} %get-tuple-element.84.tie.refs_0_, bf16[96,4096]{1,0:T(8,128)(2,1)} %get-tuple-element.85.refs_0_, ...), custom_call_target="tpu_custom_call" | custom-call | flops 7247757312 | bytes 25165824 | tf_op jit(solution)/shard_map/pallas_call | solution.py:404
  196.9 1.3 slice_convert_fusion.7.refs_1_
  198.2 2.4 collective-permute-start.18
  200.6 15.6 %shard_map.273.refs_0_ = bf16[384,4096]{1,0:T(8,128)(2,1)} custom-call(s32[2]{0:T(128)} %shard_map.272.tie.refs_3_, bf16[8,2,48,4096]{3,2,1,0:T(8,128)(2,1)} %all-to-all-done.1.refs_0_, bf16[4096,768]{1,0:T(8,128)(2,1)} %bitcast.20, bf16[4096,768]{1,0:T(8,128)(2,1)} %bitcast.24, bf16[768,4096]{1,0:T(8,128)(2,1)} %bitcast.28), custom_call_target="tpu_custom_call" | custom-call | flops 7247757312 | bytes 25165824 | tf_op jit(solution)/shard_map/pallas_call | solution.py:404
  216.2 12.3 %collective-permute-done.18.refs_2_ = bf16[64,4096]{1,0:T(8,128)(2,1)S(1)} collective-permute-done((bf16[64,4096]{1,0:T(8,128)(2,1)}, bf16[64,4096]{1,0:T(8,128)(2,1)S(1)}, u32[]{:S(2)}, u32[]{:S(2)}) %collective-permute-start.18) | collective-permute-done | bytes 524320 | tf_op jit(solution)/shard_map/ppermute | solution.py:38
  229.3 1.6 convert_add_fusion.3.refs_4_
  231.0 5.3 %all-to-all-start.3 = ((bf16[8,48,4096]{2,1,0:T(8,128)(2,1)}), bf16[8,48,4096]{2,1,0:T(8,128)(2,1)}, u32[]{:S(2)}, u32[]{:S(2)}) async-start(bf16[8,48,4096]{2,1,0:T(8,128)(2,1)} %bitcast.17), calls=%async_computation.3 | async-start | bytes 6291456 | tf_op jit(solution)/shard_map/all_to_all | solution.py:472
  236.5 15.6 %shard_map.275.refs_0_ = bf16[384,4096]{1,0:T(8,128)(2,1)} custom-call(s32[2]{0:T(128)} %get-tuple-element.92.tie, bf16[8,2,48,4096]{3,2,1,0:T(8,128)(2,1)} %all-to-all-done.1.refs_0_, bf16[4096,768]{1,0:T(8,128)(2,1)} %bitcast.21, bf16[4096,768]{1,0:T(8,128)(2,1)} %bitcast.25, bf16[768,4096]{1,0:T(8,128)(2,1)} %bitcast.29), custom_call_target="tpu_custom_call" | custom-call | flops 7247757312 | bytes 25165824 | tf_op jit(solution)/shard_map/pallas_call | solution.py:404
  252.1 1.3 slice_convert_fusion.4.refs_1_
  253.4 4.4 %shard_map.277 = (f32[32,4096]{1,0:T(8,128)}, bf16[32,4096]{1,0:T(8,128)(2,1)}, bf16[32,4096]{1,0:T(8,128)(2,1)}, bf16[32,4096]{1,0:T(8,128)(2,1)}) custom-call(bf16[128,384]{1,0:T(8,128)(2,1)} %shard_map.276.mixing, bf16[384,4096]{1,0:T(8,128)(2,1)} %bitcast.31), custom_call_target="tpu_custom_call" | custom-call | flops 402653184 | bytes 4194304 | tf_op jit(solution)/shard_map/pallas_call | solution.py:295
  257.8 4.2 %collective-permute-done.19.refs_3_ = bf16[32,4096]{1,0:T(8,128)(2,1)S(1)} collective-permute-done((bf16[32,4096]{1,0:T(8,128)(2,1)}, bf16[32,4096]{1,0:T(8,128)(2,1)S(1)}, u32[]{:S(2)}, u32[]{:S(2)}) %collective-permute-start.19) | collective-permute-done | bytes 262176 | tf_op jit(solution)/shard_map/ppermute | solution.py:38
  262.0 15.0 %collective-permute-done.20.refs_4_ = bf16[80,4096]{1,0:T(8,128)(2,1)S(1)} collective-permute-done((bf16[80,4096]{1,0:T(8,128)(2,1)}, bf16[80,4096]{1,0:T(8,128)(2,1)S(1)}, u32[]{:S(2)}, u32[]{:S(2)}) %collective-permute-start.20) | collective-permute-done | bytes 655392 | tf_op jit(solution)/shard_map/ppermute | solution.py:38
  277.0 1.3 convert_add_fusion.2.refs_2_
  278.4 4.7 %all-to-all-start.4 = ((bf16[8,48,4096]{2,1,0:T(8,128)(2,1)}), bf16[8,48,4096]{2,1,0:T(8,128)(2,1)S(1)}, u32[]{:S(2)}, u32[]{:S(2)}) async-start(bf16[8,48,4096]{2,1,0:T(8,128)(2,1)} %bitcast.16), calls=%async_computation.4 | async-start | bytes 6291456 | tf_op jit(solution)/shard_map/all_to_all | solution.py:472
  283.1 1.5 collective-permute-start.21
  284.5 1.2 collective-permute-start.23
  285.8 1.4 collective-permute-start.24
  287.2 4.4 %shard_map.278 = (f32[32,4096]{1,0:T(8,128)}, bf16[32,4096]{1,0:T(8,128)(2,1)}, bf16[32,4096]{1,0:T(8,128)(2,1)}, bf16[32,4096]{1,0:T(8,128)(2,1)}) custom-call(bf16[128,384]{1,0:T(8,128)(2,1)} %get-tuple-element.94.mixing, bf16[384,4096]{1,0:T(8,128)(2,1)} %bitcast.13.landed), custom_call_target="tpu_custom_call" | custom-call | flops 402653184 | bytes 4194304 | tf_op jit(solution)/shard_map/pallas_call | solution.py:295
  293.2 5.6 %shard_map.280 = (f32[128,2048]{1,0:T(8,128)}, bf16[128,2048]{1,0:T(8,128)(2,1)}, f32[128,2048]{1,0:T(8,128)}, bf16[128,2048]{1,0:T(8,128)(2,1)}) custom-call(bf16[256,384]{1,0:T(8,128)(2,1)} %get-tuple-element.97.mixing_a, bf16[256,384]{1,0:T(8,128)(2,1)} %get-tuple-element.98.mixing_b, bf16[96,4096]{1,0:T(8,128)(2,1)} %get-tuple-element.86.refs_0_, ...), custom_call_target="tpu_custom_call" | custom-call | flops 805306368 | bytes 5242880 | tf_op jit(solution)/shard_map/pallas_call | solution.py:337
  298.8 18.7 %all-to-all-done.4 = bf16[8,48,4096]{2,1,0:T(8,128)(2,1)S(1)} async-done(((bf16[8,48,4096]{2,1,0:T(8,128)(2,1)}), bf16[8,48,4096]{2,1,0:T(8,128)(2,1)S(1)}, u32[]{:S(2)}, u32[]{:S(2)}) %all-to-all-start.4) | async-done | bytes 3145760 | tf_op jit(solution)/shard_map/all_to_all | solution.py:472
  317.5 1.7 copy-done.1
  319.2 4.4 %shard_map.281 = (f32[32,4096]{1,0:T(8,128)}, bf16[32,4096]{1,0:T(8,128)(2,1)}, bf16[32,4096]{1,0:T(8,128)(2,1)}, bf16[32,4096]{1,0:T(8,128)(2,1)}) custom-call(bf16[128,384]{1,0:T(8,128)(2,1)} %get-tuple-element.107.mixing, bf16[384,4096]{1,0:T(8,128)(2,1)} %bitcast.32), custom_call_target="tpu_custom_call" | custom-call | flops 402653184 | bytes 4194304 | tf_op jit(solution)/shard_map/pallas_call | solution.py:295
  323.6 1.4 slice_convert_fusion.6.refs_6_
  325.0 1.5 collective-permute-start.27
  326.6 1.3 collective-permute-start.29
  327.8 1.4 add_convert_fusion.2
  329.2 1.4 collective-permute-start.30
  331.8 3.2 collective-permute-done.27
  335.0 3.2 collective-permute-start.34
  338.1 1.3 add_convert_fusion.1
  339.5 11.3 %collective-permute-done.29 = bf16[32,4096]{1,0:T(8,128)(2,1)S(1)} collective-permute-done((bf16[32,4096]{1,0:T(8,128)(2,1)S(1)}, bf16[32,4096]{1,0:T(8,128)(2,1)S(1)}, u32[]{:S(2)}, u32[]{:S(2)}) %collective-permute-start.29) | collective-permute-done | bytes 262176 | tf_op jit(solution)/shard_map/ppermute | solution.py:38
  350.8 5.6 %collective-permute-done.30 = bf16[32,4096]{1,0:T(8,128)(2,1)S(1)} collective-permute-done((bf16[32,4096]{1,0:T(8,128)(2,1)S(1)}, bf16[32,4096]{1,0:T(8,128)(2,1)S(1)}, u32[]{:S(2)}, u32[]{:S(2)}) %collective-permute-start.30) | collective-permute-done | bytes 262176 | tf_op jit(solution)/shard_map/ppermute | solution.py:38
  356.7 3.6 collective-permute-start.32
  360.6 6.0 %collective-permute-done.32 = bf16[64,2048]{1,0:T(8,128)(2,1)S(1)} collective-permute-done((bf16[64,2048]{1,0:T(8,128)(2,1)S(1)}, bf16[64,2048]{1,0:T(8,128)(2,1)S(1)}, u32[]{:S(2)}, u32[]{:S(2)}) %collective-permute-start.32) | collective-permute-done | bytes 262176 | tf_op jit(solution)/shard_map/ppermute | solution.py:38
  367.8 1.6 collective-permute-start.36
  (125 shorter events, 20.7 us)
Async XLA Ops:
  2.9 19.3 %collective-permute-start.2 = (bf16[32,4224]{1,0:T(8,128)(2,1)}, bf16[32,4224]{1,0:T(8,128)(2,1)S(1)}, u32[]{:S(2)}, u32[]{:S(2)}) collective-permute-start(bf16[32,4224]{1,0:T(8,128)(2,1)} %get-tuple-element.65.refs_0_.refs_4_), channel_id=1, source_target_pairs={{0,3},{1,2},{2,1},{3,0},{4,7},{5,6},{6,5},{7,4},{8,11},{9,10},{10,... | collective-permute-start | bytes 811016 | tf_op jit(solution)/shard_map/ppermute | solution.py:38
  4.2 22.8 %collective-permute-start.1 = (bf16[32,4224]{1,0:T(8,128)(2,1)}, bf16[32,4224]{1,0:T(8,128)(2,1)S(1)}, u32[]{:S(2)}, u32[]{:S(2)}) collective-permute-start(bf16[32,4224]{1,0:T(8,128)(2,1)} %get-tuple-element.65.refs_0_.refs_4_), channel_id=1, source_target_pairs={{0,2},{1,3},{2,0},{3,1},{4,6},{5,7},{6,4},{7,5},{8,10},{9,11},{10,... | collective-permute-start | bytes 811016 | tf_op jit(solution)/shard_map/ppermute | solution.py:38
  5.2 21.8 %collective-permute-start = (bf16[32,4224]{1,0:T(8,128)(2,1)}, bf16[32,4224]{1,0:T(8,128)(2,1)S(1)}, u32[]{:S(2)}, u32[]{:S(2)}) collective-permute-start(bf16[32,4224]{1,0:T(8,128)(2,1)} %get-tuple-element.65.refs_0_.refs_4_), channel_id=1, source_target_pairs={{0,1},{1,0},{2,3},{3,2},{4,5},{5,4},{6,7},{7,6},{8,9},{9,8},{10,11... | collective-permute-start | bytes 811016 | tf_op jit(solution)/shard_map/ppermute | solution.py:38
  6.4 2.6 collective-permute-start.3
  9.1 18.6 %collective-permute-start.4 = (bf16[64,2048]{1,0:T(8,128)(2,1)S(1)}, bf16[64,2048]{1,0:T(8,128)(2,1)S(1)}, u32[]{:S(2)}, u32[]{:S(2)}) collective-permute-start(bf16[64,2048]{1,0:T(8,128)(2,1)S(1)} %slice.88), channel_id=1, source_target_pairs={{0,8},{4,12},{8,0},{12,4},{16,24},{20,28},{24,16},{28,20},{1,9},{5... | collective-permute-start | bytes 786440 | tf_op jit(solution)/shard_map/ppermute | solution.py:38
  10.4 18.2 %collective-permute-start.5 = (bf16[64,2176]{1,0:T(8,128)(2,1)S(1)}, bf16[64,2176]{1,0:T(8,128)(2,1)S(1)}, u32[]{:S(2)}, u32[]{:S(2)}) collective-permute-start(bf16[64,2176]{1,0:T(8,128)(2,1)S(1)} %slice.89), channel_id=1, source_target_pairs={{0,16},{4,20},{8,24},{12,28},{16,0},{20,4},{24,8},{28,12},{1,17},{... | collective-permute-start | bytes 835592 | tf_op jit(solution)/shard_map/ppermute | solution.py:38
  22.2 16.4 %copy-start.10 = (bf16[32,4224]{1,0:T(8,128)(2,1)}, bf16[32,4224]{1,0:T(8,128)(2,1)S(1)}, u32[]{:S(2)}) copy-start(bf16[32,4224]{1,0:T(8,128)(2,1)S(1)} %collective-permute-done.2.refs_3_.refs_7_) | copy-start | bytes 811012
  27.0 11.6 %copy-start.11 = (bf16[32,4224]{1,0:T(8,128)(2,1)}, bf16[32,4224]{1,0:T(8,128)(2,1)S(1)}, u32[]{:S(2)}) copy-start(bf16[32,4224]{1,0:T(8,128)(2,1)S(1)} %collective-permute-done.1.refs_2_.refs_6_) | copy-start | bytes 811012
  27.0 11.6 %copy-start.12 = (bf16[32,4224]{1,0:T(8,128)(2,1)}, bf16[32,4224]{1,0:T(8,128)(2,1)S(1)}, u32[]{:S(2)}) copy-start(bf16[32,4224]{1,0:T(8,128)(2,1)S(1)} %collective-permute-done.refs_1_.refs_5_) | copy-start | bytes 811012
  29.4 14.6 %collective-permute-start.9 = (bf16[64,4224]{1,0:T(8,128)(2,1)}, bf16[64,4224]{1,0:T(8,128)(2,1)S(1)}, u32[]{:S(2)}, u32[]{:S(2)}) collective-permute-start(bf16[64,4224]{1,0:T(8,128)(2,1)} %get-tuple-element.72.refs_0_.refs_7_), channel_id=1, source_target_pairs={{3,2},{2,1},{1,0},{7,6},{6,5},{5,4},{11,10},{10,9},{9,8},{15,14},{... | collective-permute-start | bytes 1622024 | tf_op jit(solution)/shard_map/ppermute | solution.py:54
  33.5 14.2 %collective-permute-start.8 = (bf16[64,4224]{1,0:T(8,128)(2,1)}, bf16[64,4224]{1,0:T(8,128)(2,1)S(1)}, u32[]{:S(2)}, u32[]{:S(2)}) collective-permute-start(bf16[64,4224]{1,0:T(8,128)(2,1)} %get-tuple-element.72.refs_0_.refs_7_), channel_id=1, source_target_pairs={{0,1},{1,2},{2,3},{4,5},{5,6},{6,7},{8,9},{9,10},{10,11},{12,13},{... | collective-permute-start | bytes 1622024 | tf_op jit(solution)/shard_map/ppermute | solution.py:54
  35.4 13.0 %collective-permute-start.7 = (bf16[128,2176]{1,0:T(8,128)(2,1)}, bf16[128,2176]{1,0:T(8,128)(2,1)S(1)}, u32[]{:S(2)}, u32[]{:S(2)}) collective-permute-start(bf16[128,2176]{1,0:T(8,128)(2,1)} %get-tuple-element.71.b0.t0), channel_id=1, source_target_pairs={{0,8},{4,12},{8,0},{12,4},{16,24},{20,28},{24,16},{28,20},{1,9},{5... | collective-permute-start | bytes 1671176 | tf_op jit(solution)/shard_map/ppermute | solution.py:38
  36.7 11.7 %collective-permute-start.6 = (bf16[128,2048]{1,0:T(8,128)(2,1)}, bf16[128,2048]{1,0:T(8,128)(2,1)S(1)}, u32[]{:S(2)}, u32[]{:S(2)}) collective-permute-start(bf16[128,2048]{1,0:T(8,128)(2,1)} %get-tuple-element.70.a0), channel_id=1, source_target_pairs={{0,16},{4,20},{8,24},{12,28},{16,0},{20,4},{24,8},{28,12},{1,17},{... | collective-permute-start | bytes 1572872 | tf_op jit(solution)/shard_map/ppermute | solution.py:38
  44.0 5.4 %copy-start.6 = (bf16[64,4224]{1,0:T(8,128)(2,1)}, bf16[64,4224]{1,0:T(8,128)(2,1)S(1)}, u32[]{:S(2)}) copy-start(bf16[64,4224]{1,0:T(8,128)(2,1)S(1)} %collective-permute-done.9.refs_2_.refs_9_) | copy-start | bytes 1622020
  47.7 1.7 copy-start.7
  49.4 44.0 %all-to-all-start = ((bf16[8,1,48,4096]{3,2,1,0:T(8,128)(2,1)}), bf16[8,1,48,4096]{3,2,1,0:T(8,128)(2,1)S(1)}, u32[]{:S(2)}, u32[]{:S(2)}) async-start(bf16[8,1,48,4096]{3,2,1,0:T(8,128)(2,1)} %get-tuple-element.73), calls=%async_computation | async-start | bytes 6291456 | tf_op jit(solution)/shard_map/all_to_all | solution.py:472
  55.8 15.8 %collective-permute-start.11 = (bf16[64,4224]{1,0:T(8,128)(2,1)}, bf16[64,4224]{1,0:T(8,128)(2,1)S(1)}, u32[]{:S(2)}, u32[]{:S(2)}) collective-permute-start(bf16[64,4224]{1,0:T(8,128)(2,1)} %copy-done.6), channel_id=1, source_target_pairs={{2,1},{1,0},{6,5},{5,4},{10,9},{9,8},{14,13},{13,12},{18,17},{17,1... | collective-permute-start | bytes 1622024 | tf_op jit(solution)/shard_map/ppermute | solution.py:54
  59.2 16.7 %collective-permute-start.10 = (bf16[64,4224]{1,0:T(8,128)(2,1)}, bf16[64,4224]{1,0:T(8,128)(2,1)}, u32[]{:S(2)}, u32[]{:S(2)}) collective-permute-start(bf16[64,4224]{1,0:T(8,128)(2,1)} %copy-done.7), channel_id=1, source_target_pairs={{1,2},{2,3},{5,6},{6,7},{9,10},{10,11},{13,14},{14,15},{17,18},{18... | collective-permute-start | bytes 1622024 | tf_op jit(solution)/shard_map/ppermute | solution.py:54
  71.7 14.0 %copy-start.8 = (bf16[64,4224]{1,0:T(8,128)(2,1)}, bf16[64,4224]{1,0:T(8,128)(2,1)S(1)}, u32[]{:S(2)}) copy-start(bf16[64,4224]{1,0:T(8,128)(2,1)S(1)} %collective-permute-done.11.refs_4_.refs_11_) | copy-start | bytes 1622020
  71.7 14.0 %collective-permute-start.13 = (bf16[64,4224]{1,0:T(8,128)(2,1)S(1)}, bf16[64,4224]{1,0:T(8,128)(2,1)}, u32[]{:S(2)}, u32[]{:S(2)}) collective-permute-start(bf16[64,4224]{1,0:T(8,128)(2,1)S(1)} %collective-permute-done.11.refs_4_.refs_11_), channel_id=1, source_target_pairs={{1,0},{5,4},{9,8},{13,12},{17,16},{21,20},{25,24},{29,28}} | collective-permute-start | bytes 1622024 | tf_op jit(solution)/shard_map/ppermute | solution.py:54
  75.9 9.8 %collective-permute-start.12 = (bf16[64,4224]{1,0:T(8,128)(2,1)}, bf16[64,4224]{1,0:T(8,128)(2,1)}, u32[]{:S(2)}, u32[]{:S(2)}) collective-permute-start(bf16[64,4224]{1,0:T(8,128)(2,1)} %collective-permute-done.10.refs_3_.refs_10_), channel_id=1, source_target_pairs={{2,3},{6,7},{10,11},{14,15},{18,19},{22,23},{26,27},{30,31}} | collective-permute-start | bytes 1622024 | tf_op jit(solution)/shard_map/ppermute | solution.py:54
  93.5 1.7 copy-start.5
  95.1 6.7 %copy-start.13 = (bf16[96,4096]{1,0:T(8,128)(2,1)S(1)}, bf16[96,4096]{1,0:T(8,128)(2,1)}, u32[]{:S(2)}) copy-start(bf16[96,4096]{1,0:T(8,128)(2,1)} %get-tuple-element.81) | copy-start | bytes 2359300
  95.1 9.0 %copy-start.14 = (bf16[96,4096]{1,0:T(8,128)(2,1)S(1)}, bf16[96,4096]{1,0:T(8,128)(2,1)}, u32[]{:S(2)}) copy-start(bf16[96,4096]{1,0:T(8,128)(2,1)} %get-tuple-element.82) | copy-start | bytes 2359300
  95.1 11.0 %copy-start.15 = (bf16[96,4096]{1,0:T(8,128)(2,1)S(1)}, bf16[96,4096]{1,0:T(8,128)(2,1)}, u32[]{:S(2)}) copy-start(bf16[96,4096]{1,0:T(8,128)(2,1)} %get-tuple-element.83) | copy-start | bytes 2359300
  95.1 79.4 %all-to-all-start.1 = ((bf16[8,2,48,4096]{3,2,1,0:T(8,128)(2,1)}), bf16[8,2,48,4096]{3,2,1,0:T(8,128)(2,1)}, u32[]{:S(2)}, u32[]{:S(2)}) async-start(bf16[8,2,48,4096]{3,2,1,0:T(8,128)(2,1)} %get-tuple-element.80), calls=%async_computation.1 | async-start | bytes 12582912 | tf_op jit(solution)/shard_map/all_to_all | solution.py:472
  101.8 35.5 %collective-permute-start.14 = (bf16[96,4096]{1,0:T(8,128)(2,1)S(1)}, bf16[96,4096]{1,0:T(8,128)(2,1)S(1)}, u32[]{:S(2)}, u32[]{:S(2)}) collective-permute-start(bf16[96,4096]{1,0:T(8,128)(2,1)S(1)} %copy-done.13), channel_id=1, source_target_pairs={{0,1},{1,0},{2,3},{3,2},{4,5},{5,4},{6,7},{7,6},{8,9},{9,8},{10,11... | collective-permute-start | bytes 2359304 | tf_op jit(solution)/shard_map/ppermute | solution.py:38
  104.1 52.5 %collective-permute-start.15 = (bf16[96,4096]{1,0:T(8,128)(2,1)S(1)}, bf16[96,4096]{1,0:T(8,128)(2,1)}, u32[]{:S(2)}, u32[]{:S(2)}) collective-permute-start(bf16[96,4096]{1,0:T(8,128)(2,1)S(1)} %copy-done.14), channel_id=1, source_target_pairs={{0,2},{1,3},{2,0},{3,1},{4,6},{5,7},{6,4},{7,5},{8,10},{9,11},{10,... | collective-permute-start | bytes 2359304 | tf_op jit(solution)/shard_map/ppermute | solution.py:38
  106.1 68.4 %collective-permute-start.16 = (bf16[96,4096]{1,0:T(8,128)(2,1)S(1)}, bf16[96,4096]{1,0:T(8,128)(2,1)}, u32[]{:S(2)}, u32[]{:S(2)}) collective-permute-start(bf16[96,4096]{1,0:T(8,128)(2,1)S(1)} %copy-done.15), channel_id=1, source_target_pairs={{0,3},{1,2},{2,1},{3,0},{4,7},{5,6},{6,5},{7,4},{8,11},{9,10},{10,... | collective-permute-start | bytes 2359304 | tf_op jit(solution)/shard_map/ppermute | solution.py:38
  137.3 38.6 %copy-start.23 = (bf16[96,4096]{1,0:T(8,128)(2,1)}, bf16[96,4096]{1,0:T(8,128)(2,1)S(1)}, u32[]{:S(2)}) copy-start(bf16[96,4096]{1,0:T(8,128)(2,1)S(1)} %collective-permute-done.14.refs_1_) | copy-start | bytes 2359300
  175.8 53.5 %all-to-all-start.2 = ((bf16[8,48,4096]{2,1,0:T(8,128)(2,1)}), bf16[8,48,4096]{2,1,0:T(8,128)(2,1)S(1)}, u32[]{:S(2)}, u32[]{:S(2)}) async-start(bf16[8,48,4096]{2,1,0:T(8,128)(2,1)} %bitcast.33), calls=%async_computation.2 | async-start | bytes 6291456 | tf_op jit(solution)/shard_map/all_to_all | solution.py:472
  196.8 32.5 %collective-permute-start.17 = (bf16[96,4096]{1,0:T(8,128)(2,1)}, bf16[96,4096]{1,0:T(8,128)(2,1)}, u32[]{:S(2)}, u32[]{:S(2)}) collective-permute-start(bf16[96,4096]{1,0:T(8,128)(2,1)} %get-tuple-element.90), channel_id=1, source_target_pairs={{0,1},{1,0},{2,3},{3,2},{4,5},{5,4},{6,7},{7,6},{8,9},{9,8},{10,11... | collective-permute-start | bytes 2359304 | tf_op jit(solution)/shard_map/ppermute | solution.py:38
  198.2 30.3 %collective-permute-start.18 = (bf16[64,4096]{1,0:T(8,128)(2,1)}, bf16[64,4096]{1,0:T(8,128)(2,1)S(1)}, u32[]{:S(2)}, u32[]{:S(2)}) collective-permute-start(bf16[64,4096]{1,0:T(8,128)(2,1)} %get-tuple-element.91), channel_id=1, source_target_pairs={{0,2},{1,3},{2,0},{3,1},{4,6},{5,7},{6,4},{7,5},{8,10},{9,11},{10,... | collective-permute-start | bytes 1572872 | tf_op jit(solution)/shard_map/ppermute | solution.py:38
  229.3 1.7 copy-start
  231.0 46.0 %all-to-all-start.3 = ((bf16[8,48,4096]{2,1,0:T(8,128)(2,1)}), bf16[8,48,4096]{2,1,0:T(8,128)(2,1)}, u32[]{:S(2)}, u32[]{:S(2)}) async-start(bf16[8,48,4096]{2,1,0:T(8,128)(2,1)} %bitcast.17), calls=%async_computation.3 | async-start | bytes 6291456 | tf_op jit(solution)/shard_map/all_to_all | solution.py:472
  236.3 25.7 %collective-permute-start.19 = (bf16[32,4096]{1,0:T(8,128)(2,1)}, bf16[32,4096]{1,0:T(8,128)(2,1)S(1)}, u32[]{:S(2)}, u32[]{:S(2)}) collective-permute-start(bf16[32,4096]{1,0:T(8,128)(2,1)} %get-tuple-element.99), channel_id=1, source_target_pairs={{0,2},{1,3},{2,0},{3,1},{4,6},{5,7},{6,4},{7,5},{8,10},{9,11},{10,... | collective-permute-start | bytes 786440 | tf_op jit(solution)/shard_map/ppermute | solution.py:38
  236.5 40.5 %collective-permute-start.20 = (bf16[80,4096]{1,0:T(8,128)(2,1)}, bf16[80,4096]{1,0:T(8,128)(2,1)S(1)}, u32[]{:S(2)}, u32[]{:S(2)}) collective-permute-start(bf16[80,4096]{1,0:T(8,128)(2,1)} %get-tuple-element.100), channel_id=1, source_target_pairs={{0,3},{1,2},{2,1},{3,0},{4,7},{5,6},{6,5},{7,4},{8,11},{9,10},{10,... | collective-permute-start | bytes 1966088 | tf_op jit(solution)/shard_map/ppermute | solution.py:38
  262.0 16.3 %copy-start.19 = (bf16[32,4096]{1,0:T(8,128)(2,1)}, bf16[32,4096]{1,0:T(8,128)(2,1)S(1)}, u32[]{:S(2)}) copy-start(bf16[32,4096]{1,0:T(8,128)(2,1)S(1)} %collective-permute-done.19.refs_3_) | copy-start | bytes 786436
  278.3 4.7 %copy-start.21 = (bf16[16,4096]{1,0:T(8,128)(2,1)S(1)}, bf16[16,4096]{1,0:T(8,128)(2,1)}, u32[]{:S(2)}) copy-start(bf16[16,4096]{1,0:T(8,128)(2,1)} %get-tuple-element.102) | copy-start | bytes 393220
  278.4 39.1 %all-to-all-start.4 = ((bf16[8,48,4096]{2,1,0:T(8,128)(2,1)}), bf16[8,48,4096]{2,1,0:T(8,128)(2,1)S(1)}, u32[]{:S(2)}, u32[]{:S(2)}) async-start(bf16[8,48,4096]{2,1,0:T(8,128)(2,1)} %bitcast.16), calls=%async_computation.4 | async-start | bytes 6291456 | tf_op jit(solution)/shard_map/all_to_all | solution.py:472
  283.1 9.5 %collective-permute-start.21 = (bf16[16,4096]{1,0:T(8,128)(2,1)S(1)}, bf16[16,4096]{1,0:T(8,128)(2,1)S(1)}, u32[]{:S(2)}, u32[]{:S(2)}) collective-permute-start(bf16[16,4096]{1,0:T(8,128)(2,1)S(1)} %copy-done.21), channel_id=1, source_target_pairs={{0,3},{1,2},{2,1},{3,0},{4,7},{5,6},{6,5},{7,4},{8,11},{9,10},{10,... | collective-permute-start | bytes 393224 | tf_op jit(solution)/shard_map/ppermute | solution.py:38
  284.5 40.4 %collective-permute-start.22 = (bf16[32,4096]{1,0:T(8,128)(2,1)}, bf16[32,4096]{1,0:T(8,128)(2,1)}, u32[]{:S(2)}, u32[]{:S(2)}) collective-permute-start(bf16[32,4096]{1,0:T(8,128)(2,1)} %get-tuple-element.111), channel_id=1, source_target_pairs={{0,1},{1,0},{2,3},{3,2},{4,5},{5,4},{6,7},{7,6},{8,9},{9,8},{10,11... | collective-permute-start | bytes 786440 | tf_op jit(solution)/shard_map/ppermute | solution.py:38
  284.5 42.0 %collective-permute-start.23 = (bf16[32,4096]{1,0:T(8,128)(2,1)}, bf16[32,4096]{1,0:T(8,128)(2,1)}, u32[]{:S(2)}, u32[]{:S(2)}) collective-permute-start(bf16[32,4096]{1,0:T(8,128)(2,1)} %get-tuple-element.112), channel_id=1, source_target_pairs={{0,2},{1,3},{2,0},{3,1},{4,6},{5,7},{6,4},{7,5},{8,10},{9,11},{10,... | collective-permute-start | bytes 786440 | tf_op jit(solution)/shard_map/ppermute | solution.py:38
  285.8 40.8 %collective-permute-start.24 = (bf16[32,4096]{1,0:T(8,128)(2,1)}, bf16[32,4096]{1,0:T(8,128)(2,1)}, u32[]{:S(2)}, u32[]{:S(2)}) collective-permute-start(bf16[32,4096]{1,0:T(8,128)(2,1)} %get-tuple-element.113), channel_id=1, source_target_pairs={{0,3},{1,2},{2,1},{3,0},{4,7},{5,6},{6,5},{7,4},{8,11},{9,10},{10,... | collective-permute-start | bytes 786440 | tf_op jit(solution)/shard_map/ppermute | solution.py:38
  291.6 37.6 %collective-permute-start.25 = (bf16[32,4096]{1,0:T(8,128)(2,1)}, bf16[32,4096]{1,0:T(8,128)(2,1)S(1)}, u32[]{:S(2)}, u32[]{:S(2)}) collective-permute-start(bf16[32,4096]{1,0:T(8,128)(2,1)} %get-tuple-element.115), channel_id=1, source_target_pairs={{0,1},{1,0},{2,3},{3,2},{4,5},{5,4},{6,7},{7,6},{8,9},{9,8},{10,11... | collective-permute-start | bytes 786440 | tf_op jit(solution)/shard_map/ppermute | solution.py:38
  292.5 38.2 %collective-permute-start.26 = (bf16[32,4096]{1,0:T(8,128)(2,1)}, bf16[32,4096]{1,0:T(8,128)(2,1)}, u32[]{:S(2)}, u32[]{:S(2)}) collective-permute-start(bf16[32,4096]{1,0:T(8,128)(2,1)} %get-tuple-element.116), channel_id=1, source_target_pairs={{0,2},{1,3},{2,0},{3,1},{4,6},{5,7},{6,4},{7,5},{8,10},{9,11},{10,... | collective-permute-start | bytes 786440 | tf_op jit(solution)/shard_map/ppermute | solution.py:38
  317.5 1.7 copy-start.1
  323.6 1.4 copy-start.24
  323.6 3.0 copy-start.22
  323.6 3.0 copy-start.26
  323.6 5.6 %copy-start.25 = (bf16[32,4096]{1,0:T(8,128)(2,1)S(1)}, bf16[32,4096]{1,0:T(8,128)(2,1)}, u32[]{:S(2)}) copy-start(bf16[32,4096]{1,0:T(8,128)(2,1)} %get-tuple-element.120) | copy-start | bytes 786436
  325.0 31.4 %copy-start.18 = (f32[32,4096]{1,0:T(8,128)S(1)}, f32[32,4096]{1,0:T(8,128)}, u32[]{:S(2)}) copy-start(f32[32,4096]{1,0:T(8,128)} %get-tuple-element.118) | copy-start | bytes 1572868
  325.0 31.6 %copy-start.3 = (f32[128,2048]{1,0:T(8,128)S(1)}, f32[128,2048]{1,0:T(8,128)}, u32[]{:S(2)}) copy-start(f32[128,2048]{1,0:T(8,128)} %get-tuple-element.121) | copy-start | bytes 3145732
  325.0 10.0 %collective-permute-start.27 = (bf16[32,4096]{1,0:T(8,128)(2,1)S(1)}, bf16[32,4096]{1,0:T(8,128)(2,1)S(1)}, u32[]{:S(2)}, u32[]{:S(2)}) collective-permute-start(bf16[32,4096]{1,0:T(8,128)(2,1)S(1)} %copy-done.24), channel_id=1, source_target_pairs={{0,3},{1,2},{2,1},{3,0},{4,7},{5,6},{6,5},{7,4},{8,11},{9,10},{10,... | collective-permute-start | bytes 786440 | tf_op jit(solution)/shard_map/ppermute | solution.py:38
  326.5 29.9 %collective-permute-start.28 = (bf16[32,4096]{1,0:T(8,128)(2,1)S(1)}, bf16[32,4096]{1,0:T(8,128)(2,1)S(1)}, u32[]{:S(2)}, u32[]{:S(2)}) collective-permute-start(bf16[32,4096]{1,0:T(8,128)(2,1)S(1)} %copy-done.22), channel_id=1, source_target_pairs={{0,1},{1,0},{2,3},{3,2},{4,5},{5,4},{6,7},{7,6},{8,9},{9,8},{10,11... | collective-permute-start | bytes 786440 | tf_op jit(solution)/shard_map/ppermute | solution.py:38
  326.6 24.2 %collective-permute-start.29 = (bf16[32,4096]{1,0:T(8,128)(2,1)S(1)}, bf16[32,4096]{1,0:T(8,128)(2,1)S(1)}, u32[]{:S(2)}, u32[]{:S(2)}) collective-permute-start(bf16[32,4096]{1,0:T(8,128)(2,1)S(1)} %copy-done.26), channel_id=1, source_target_pairs={{0,2},{1,3},{2,0},{3,1},{4,6},{5,7},{6,4},{7,5},{8,10},{9,11},{10,... | collective-permute-start | bytes 786440 | tf_op jit(solution)/shard_map/ppermute | solution.py:38
  329.2 27.2 %collective-permute-start.30 = (bf16[32,4096]{1,0:T(8,128)(2,1)S(1)}, bf16[32,4096]{1,0:T(8,128)(2,1)S(1)}, u32[]{:S(2)}, u32[]{:S(2)}) collective-permute-start(bf16[32,4096]{1,0:T(8,128)(2,1)S(1)} %copy-done.25), channel_id=1, source_target_pairs={{0,3},{1,2},{2,1},{3,0},{4,7},{5,6},{6,5},{7,4},{8,11},{9,10},{10,... | collective-permute-start | bytes 786440 | tf_op jit(solution)/shard_map/ppermute | solution.py:38
  330.7 25.9 %collective-permute-start.31 = (bf16[128,2048]{1,0:T(8,128)(2,1)}, bf16[128,2048]{1,0:T(8,128)(2,1)S(1)}, u32[]{:S(2)}, u32[]{:S(2)}) collective-permute-start(bf16[128,2048]{1,0:T(8,128)(2,1)} %get-tuple-element.122), channel_id=1, source_target_pairs={{0,16},{4,20},{8,24},{12,28},{16,0},{20,4},{24,8},{28,12},{1,17},{... | collective-permute-start | bytes 1572872 | tf_op jit(solution)/shard_map/ppermute | solution.py:38
  335.0 25.4 %collective-permute-start.34 = (bf16[128,2048]{1,0:T(8,128)(2,1)}, bf16[128,2048]{1,0:T(8,128)(2,1)S(1)}, u32[]{:S(2)}, u32[]{:S(2)}) collective-permute-start(bf16[128,2048]{1,0:T(8,128)(2,1)} %get-tuple-element.124), channel_id=1, source_target_pairs={{0,8},{4,12},{8,0},{12,4},{16,24},{20,28},{24,16},{28,20},{1,9},{5... | collective-permute-start | bytes 1572872 | tf_op jit(solution)/shard_map/ppermute | solution.py:38
  338.1 22.2 %copy-start.4 = (f32[128,2048]{1,0:T(8,128)S(1)}, f32[128,2048]{1,0:T(8,128)}, u32[]{:S(2)}) copy-start(f32[128,2048]{1,0:T(8,128)} %get-tuple-element.123) | copy-start | bytes 3145732
  356.7 9.9 %collective-permute-start.32 = (bf16[64,2048]{1,0:T(8,128)(2,1)S(1)}, bf16[64,2048]{1,0:T(8,128)(2,1)S(1)}, u32[]{:S(2)}, u32[]{:S(2)}) collective-permute-start(bf16[64,2048]{1,0:T(8,128)(2,1)S(1)} %split.57), channel_id=1, source_target_pairs={{0,8},{4,12},{8,0},{12,4},{16,24},{20,28},{24,16},{28,20},{1,9},{5... | collective-permute-start | bytes 786440 | tf_op jit(solution)/shard_map/ppermute | solution.py:38
  360.5 7.2 %collective-permute-start.35 = (bf16[64,2048]{1,0:T(8,128)(2,1)S(1)}, bf16[64,2048]{1,0:T(8,128)(2,1)S(1)}, u32[]{:S(2)}, u32[]{:S(2)}) collective-permute-start(bf16[64,2048]{1,0:T(8,128)(2,1)S(1)} %split.56), channel_id=1, source_target_pairs={{0,16},{4,20},{8,24},{12,28},{16,0},{20,4},{24,8},{28,12},{1,17},{... | collective-permute-start | bytes 786440 | tf_op jit(solution)/shard_map/ppermute | solution.py:38
  366.6 2.8 collective-permute-start.33
  367.8 2.6 collective-permute-start.36
  (5 other events, 4.6 us)
